TPU v7x, 32 devices: a whole 2x2x4 slice. The times are simulated.
32 devices in a mesh: dp: 8 (over y, x, core), tensor: 4 (over z).
Axes of the slice: x: 2, y: 2, z: 4, core: 2. Of those that a mesh axis runs over, the one named last changes fastest.
Arguments:
- block_input: float32 [8192, 2048], P(('dp', 'tensor')), may hold values from -6 to 6
- out_grad: float32 [8192, 2048], P(('dp', 'tensor')), may hold values from -6 to 6
- seq_lengths: int32 [8, 4], P('dp'), may hold values from 0 to 1024, as said below
- in_weight: float32 [2048, 7, 2048], P('dp', None, 'tensor'), may hold values from -0.125 to 0.125
- down_weight: float32 [5, 2048, 2048], P(None, 'tensor', 'dp'), may hold values from -0.35355339 to 0.35355339
- column_bias: float32 [7, 2048], P(None, ('tensor', 'dp')), may hold values from -1.75 to 1.75
- vector_params: float32 [3, 2048], P(None, 'dp'), may hold values from -1.2 to 1.4
- in_first: float32 [2048, 7, 2048], P('dp', None, 'tensor'), may hold values from -40 to 40
- in_second: float32 [2048, 7, 2048], P('dp', None, 'tensor'), may hold values from 106.496 to 1720.32
- down_first: float32 [5, 2048, 2048], P(None, 'tensor', 'dp'), may hold values from -24 to 24
- down_second: float32 [5, 2048, 2048], P(None, 'tensor', 'dp'), may hold values from 34.4064 to 548.864
- bias_first: float32 [7, 2048], P(None, ('tensor', 'dp')), may hold values from -40 to 40
- bias_second: float32 [7, 2048], P(None, ('tensor', 'dp')), may hold values from 106.496 to 1720.32
- vector_first: float32 [3, 2048], P(None, 'dp'), may hold values from -96 to 96
- vector_second: float32 [3, 2048], P(None, 'dp'), may hold values from 483.328 to 7782.4
Outputs:
- block_out: float32 [8192, 2048], P(('dp', 'tensor'))
- input_grad: float32 [8192, 2048], P(('dp', 'tensor'))
- in_weight_new: float32 [2048, 7, 2048], P('dp', None, 'tensor')
- in_first_new: float32 [2048, 7, 2048], P('dp', None, 'tensor')
- in_second_new: float32 [2048, 7, 2048], P('dp', None, 'tensor')
- down_weight_new: float32 [5, 2048, 2048], P(None, 'tensor', 'dp')
- down_first_new: float32 [5, 2048, 2048], P(None, 'tensor', 'dp')
- down_second_new: float32 [5, 2048, 2048], P(None, 'tensor', 'dp')
- bias_new: float32 [7, 2048], P(None, ('tensor', 'dp'))
- bias_first_new: float32 [7, 2048], P(None, ('tensor', 'dp'))
- bias_second_new: float32 [7, 2048], P(None, ('tensor', 'dp'))
- vector_new: float32 [3, 2048], P(None, 'dp')
- vector_first_new: float32 [3, 2048], P(None, 'dp')
- vector_second_new: float32 [3, 2048], P(None, 'dp')
Inputs may be any that keep to these rules, and one draw needn't show every extreme that they name: `seq_lengths`: row i lists, in order, the lengths of the sequences packed from the first of data shard i's 1024 slots; a zero is an unused entry and follows all used ones; a row holds one to three sequences, each of 256 tokens or more, and sums to 512 or more, the slots after its sum being padding; in every draw some shard holds one sequence of 1024 tokens.
All inputs are finite; a program needn't handle non-finite values.
Results may differ from a plain program's by a relative error of at most 0.0098.
Values may be sent and summed in bfloat16 or wider, within the bound.
A program may use at most 256 MiB of HBM per device.

v0:
```python
from functools import partial

import jax
import jax.numpy as jnp
from jax import lax
from jax.sharding import PartitionSpec as P

HEAD = 64
ROT = 32
STEP = 8


norm_eps = 1e-05
beta_first = 0.9
beta_second = 0.95
adam_eps = 1e-08
masked_score = -1000000000.0
rate_in = 0.02
rate_down = 0.05
rate_vector = 0.2
weight_decay = 0.1


def layout(lengths, group_size):
    seq_ends = jnp.cumsum(lengths)
    places = jnp.arange(group_size, dtype=jnp.int32)
    segment = jnp.sum((places[:, None] >= seq_ends[None, :]).astype(jnp.int32), axis=1)
    starts = jnp.concatenate([jnp.zeros((1,), jnp.int32), seq_ends])
    picked = segment[:, None] == jnp.arange(lengths.shape[0] + 1, dtype=jnp.int32)[None, :]
    seq_begin = jnp.sum(jnp.where(picked, starts[None, :], 0), axis=1)
    position = places - seq_begin
    live_mask = (segment < lengths.shape[0]).astype(jnp.int32)
    return (segment, position, live_mask)


def rotary_tables(position):
    half_rot = ROT // 2
    frequency = 10000.0 ** (-2.0 * jnp.arange(half_rot, dtype=jnp.float32) / ROT)
    angles = position.astype(jnp.float32)[:, None] * frequency[None, :]
    return (jnp.cos(angles)[:, None, :], jnp.sin(angles)[:, None, :])


def rotate(values, cosine, sine_table):
    half_rot = ROT // 2
    first_half = values[..., :half_rot]
    second_half = values[..., half_rot:ROT]
    return jnp.concatenate(
        [
            first_half * cosine - second_half * sine_table,
            second_half * cosine + first_half * sine_table,
            values[..., ROT:],
        ],
        axis=-1,
    )


def rotate_back(grads, cosine, sine_table):
    half_rot = ROT // 2
    first_half = grads[..., :half_rot]
    second_half = grads[..., half_rot:ROT]
    return jnp.concatenate(
        [
            first_half * cosine + second_half * sine_table,
            second_half * cosine - first_half * sine_table,
            grads[..., ROT:],
        ],
        axis=-1,
    )


def normalize(group_rows, gain_row, shift_row):
    centered = group_rows - jnp.mean(group_rows, axis=-1, keepdims=True)
    inv_scale = lax.rsqrt(jnp.mean(centered * centered, axis=-1, keepdims=True) + norm_eps)
    return centered * inv_scale * gain_row + shift_row


def causal_mask(segment, row_start, block_size, row_stop):
    query_place = row_start + jnp.arange(block_size, dtype=jnp.int32)
    key_place = jnp.arange(row_stop, dtype=jnp.int32)
    same_seq = segment[row_start:row_stop][:, None] == segment[:row_stop][None, :]
    return same_seq & (key_place[None, :] <= query_place[:, None])


def block_scores(queries, key_rows, allowed):
    scores = jnp.einsum(
        "qhe,khe->hqk", queries, key_rows, preferred_element_type=jnp.float32
    ) * HEAD ** (-0.5)
    return jnp.where(allowed[None], scores, masked_score)


def attend_forward(queries, key_rows, values, segment, block_size):
    total_rows = queries.shape[0]
    outputs = []
    log_sums = []
    for row_start in range(0, total_rows, block_size):
        row_stop = row_start + block_size
        scores = block_scores(
            queries[row_start:row_stop],
            key_rows[:row_stop],
            causal_mask(segment, row_start, block_size, row_stop),
        )
        row_max = jnp.max(scores, axis=-1, keepdims=True)
        exp_scores = jnp.exp(scores - row_max)
        exp_total = jnp.sum(exp_scores, axis=-1, keepdims=True)
        attn_probs = (exp_scores / exp_total).astype(jnp.bfloat16)
        outputs.append(
            jnp.einsum(
                "hqk,khe->qhe", attn_probs, values[:row_stop], preferred_element_type=jnp.float32
            )
        )
        log_sums.append(row_max + jnp.log(exp_total))
    return (jnp.concatenate(outputs, axis=0), log_sums)


def attend_backward(queries, key_rows, values, segment, block_size, log_sums, out_rows):
    block_count = queries.shape[0] // block_size
    part_shape = (block_size,) + key_rows.shape[1:]
    query_grads = []
    key_parts = [jnp.zeros(part_shape, jnp.float32) for key_block in range(block_count)]
    value_parts = [jnp.zeros(part_shape, jnp.float32) for key_block in range(block_count)]
    for query_block in range(block_count):
        row_start = query_block * block_size
        row_stop = row_start + block_size
        chosen_rows = queries[row_start:row_stop]
        prefix_keys = key_rows[:row_stop]
        grad_rows = out_rows[row_start:row_stop]
        scores = block_scores(
            chosen_rows, prefix_keys, causal_mask(segment, row_start, block_size, row_stop)
        )
        attn_probs = jnp.exp(scores - log_sums[query_block])
        value_step = jnp.einsum(
            "hqk,qhe->khe",
            attn_probs.astype(jnp.bfloat16),
            grad_rows,
            preferred_element_type=jnp.float32,
        )
        prob_grad = jnp.einsum(
            "qhe,khe->hqk", grad_rows, values[:row_stop], preferred_element_type=jnp.float32
        )
        score_grad = (
            attn_probs * (prob_grad - jnp.sum(attn_probs * prob_grad, axis=-1, keepdims=True))
        ).astype(jnp.bfloat16)
        query_grads.append(
            jnp.einsum("hqk,khe->qhe", score_grad, prefix_keys, preferred_element_type=jnp.float32)
            * HEAD ** (-0.5)
        )
        key_step = jnp.einsum(
            "hqk,qhe->khe", score_grad, chosen_rows, preferred_element_type=jnp.float32
        ) * HEAD ** (-0.5)
        for key_block in range(query_block + 1):
            lower = key_block * block_size
            key_parts[key_block] = key_parts[key_block] + key_step[lower : lower + block_size]
            value_parts[key_block] = value_parts[key_block] + value_step[lower : lower + block_size]
    return (
        jnp.concatenate(query_grads, axis=0),
        jnp.concatenate(key_parts, axis=0),
        jnp.concatenate(value_parts, axis=0),
    )


def adam_update(weight, moment_one, moment_two, gradient, step_rate, decay_factor):
    first_new = beta_first * moment_one + (1.0 - beta_first) * gradient
    second_new = beta_second * moment_two + (1.0 - beta_second) * gradient * gradient
    corrected = first_new / (1.0 - beta_first**STEP)
    spread = jnp.sqrt(second_new / (1.0 - beta_second**STEP))
    return (
        weight - step_rate * (corrected / (spread + adam_eps) + decay_factor * weight),
        first_new,
        second_new,
    )


def per_device(
    block_input,
    out_grad,
    seq_lengths,
    in_weight,
    down_weight,
    column_bias,
    vector_params,
    in_first,
    in_second,
    down_first,
    down_second,
    bias_first,
    bias_second,
    vector_first,
    vector_second,
):
    own_rows = block_input.shape[0]
    group_size = own_rows * lax.axis_size("tensor")
    proj_width = in_weight.shape[1]
    local_width = in_weight.shape[2]
    local_heads = local_width // HEAD
    block_size = min(512, group_size)
    segment, position, live_mask = layout(seq_lengths[0], group_size)
    own_live = lax.dynamic_slice_in_dim(
        live_mask, lax.axis_index("tensor") * own_rows, own_rows
    ).astype(jnp.float32)
    in_low = in_weight.astype(jnp.bfloat16)
    down_low = down_weight.astype(jnp.bfloat16)
    in_full, bias_full, vector_full, down_full = (
        lax.all_gather(in_low, "dp", axis=0, tiled=True),
        lax.all_gather(column_bias.astype(jnp.bfloat16), "dp", axis=1, tiled=True),
        lax.all_gather(vector_params.astype(jnp.bfloat16), "dp", axis=1, tiled=True),
        lax.all_gather(down_low, "dp", axis=2, tiled=True),
    )
    bias_vals = bias_full.astype(jnp.float32)
    vector_vals = vector_full.astype(jnp.float32)
    normed, norm_pull = jax.vjp(normalize, block_input, vector_vals[0], vector_vals[1])
    normed_all = lax.all_gather(normed.astype(jnp.bfloat16), "tensor", axis=0, tiled=True)
    model_width = normed_all.shape[1]
    in_flat = in_full.reshape(model_width, proj_width * local_width)
    projected = (
        jnp.dot(normed_all, in_flat, preferred_element_type=jnp.float32).reshape(
            group_size, proj_width, local_width
        )
        + bias_vals
    )
    cosine, sine_table = rotary_tables(position)
    queries = rotate(
        projected[:, 0].reshape(group_size, local_heads, HEAD), cosine, sine_table
    ).astype(jnp.bfloat16)
    key_rows = rotate(
        projected[:, 1].reshape(group_size, local_heads, HEAD), cosine, sine_table
    ).astype(jnp.bfloat16)
    values = projected[:, 2].reshape(group_size, local_heads, HEAD).astype(jnp.bfloat16)
    attended, log_sums = attend_forward(queries, key_rows, values, segment, block_size)
    attended_low = attended.reshape(group_size, local_width).astype(jnp.bfloat16)
    hidden, gelu_pull = jax.vjp(partial(jax.nn.gelu, approximate=True), projected[:, 3:])
    hidden_low = hidden.astype(jnp.bfloat16)
    mlp_rows = lax.slice_in_dim(hidden_low, 0, own_rows * lax.axis_size("tensor"), axis=0)
    attn_part = jnp.dot(attended_low, down_full[0], preferred_element_type=jnp.float32)
    mixed = (
        lax.psum_scatter(
            (
                attn_part
                + jnp.einsum(
                    "grc,rcd->gd", mlp_rows, down_full[1:], preferred_element_type=jnp.float32
                )
            ).astype(jnp.bfloat16),
            "tensor",
            scatter_dimension=0,
            tiled=True,
        ).astype(jnp.float32)
        + vector_vals[2]
    )
    block_out = block_input + mixed
    cot_live = out_grad * own_live[:, None]
    cot_low = cot_live.astype(jnp.bfloat16)
    cot_all = lax.all_gather(cot_low, "tensor", axis=0, tiled=True)
    in_back, down_back = (
        lax.all_gather(in_low, "dp", axis=0, tiled=True),
        lax.all_gather(down_low, "dp", axis=2, tiled=True),
    )
    down_grad = jnp.concatenate(
        [
            jnp.einsum("gc,gd->cd", attended_low, cot_all, preferred_element_type=jnp.float32)[
                None
            ],
            jnp.einsum("grc,gd->rcd", hidden_low, cot_all, preferred_element_type=jnp.float32),
        ],
        axis=0,
    )
    attn_grad = jnp.einsum(
        "gd,cd->gc", cot_all, down_back[0], preferred_element_type=jnp.float32
    ).astype(jnp.bfloat16)
    hidden_grad = jnp.einsum(
        "gd,rcd->grc", cot_all, down_back[1:], preferred_element_type=jnp.float32
    )
    pre_grad = gelu_pull(hidden_grad)[0]
    query_grad, key_grad, value_grad = attend_backward(
        queries,
        key_rows,
        values,
        segment,
        block_size,
        log_sums,
        attn_grad.reshape(group_size, local_heads, HEAD),
    )
    proj_grad = jnp.concatenate(
        [
            rotate_back(query_grad, cosine, sine_table).reshape(group_size, 1, local_width),
            rotate_back(key_grad, cosine, sine_table).reshape(group_size, 1, local_width),
            value_grad.reshape(group_size, 1, local_width),
            pre_grad,
        ],
        axis=1,
    ).astype(jnp.bfloat16)
    bias_grad = jnp.sum(proj_grad, axis=0, dtype=jnp.float32)
    proj_flat = proj_grad.reshape(group_size, proj_width * local_width)
    in_grad = jnp.einsum(
        "gd,gk->dk", normed_all, proj_flat, preferred_element_type=jnp.float32
    ).reshape(model_width, proj_width, local_width)
    back_flat = in_back.reshape(model_width, proj_width * local_width)
    normed_grad = lax.psum_scatter(
        jnp.einsum("gk,dk->gd", proj_flat, back_flat, preferred_element_type=jnp.float32).astype(
            jnp.bfloat16
        ),
        "tensor",
        scatter_dimension=0,
        tiled=True,
    ).astype(jnp.float32)
    input_part, gain_grad, shift_grad = norm_pull(normed_grad)
    input_grad = cot_live + input_part
    outbias_grad = jnp.sum(cot_low, axis=0, dtype=jnp.float32)
    vector_grad = jnp.stack([gain_grad, shift_grad, outbias_grad])
    in_reduced, bias_reduced, vector_reduced, down_reduced = (
        lax.psum_scatter(in_grad, "dp", scatter_dimension=0, tiled=True),
        lax.psum_scatter(bias_grad, "dp", scatter_dimension=1, tiled=True),
        lax.psum_scatter(vector_grad, "dp", scatter_dimension=1, tiled=True),
        lax.psum_scatter(down_grad, "dp", scatter_dimension=2, tiled=True),
    )
    vector_reduced = lax.psum(vector_reduced, "tensor")
    in_new, in_one, in_two = adam_update(
        in_weight, in_first, in_second, in_reduced, rate_in, weight_decay
    )
    down_new, down_one, down_two = adam_update(
        down_weight, down_first, down_second, down_reduced, rate_down, weight_decay
    )
    bias_new, bias_one, bias_two = adam_update(
        column_bias, bias_first, bias_second, bias_reduced, rate_vector, 0.0
    )
    vector_new, vector_one, vector_two = adam_update(
        vector_params, vector_first, vector_second, vector_reduced, rate_vector, 0.0
    )
    return (
        block_out,
        input_grad,
        in_new,
        in_one,
        in_two,
        down_new,
        down_one,
        down_two,
        bias_new,
        bias_one,
        bias_two,
        vector_new,
        vector_one,
        vector_two,
    )


def solution(mesh):
    return jax.shard_map(
        per_device,
        mesh=mesh,
        in_specs=(
            P(("dp", "tensor"), None),
            P(("dp", "tensor"), None),
            P("dp", None),
            P("dp", None, "tensor"),
            P(None, "tensor", "dp"),
            P(None, ("tensor", "dp")),
            P(None, "dp"),
            P("dp", None, "tensor"),
            P("dp", None, "tensor"),
            P(None, "tensor", "dp"),
            P(None, "tensor", "dp"),
            P(None, ("tensor", "dp")),
            P(None, ("tensor", "dp")),
            P(None, "dp"),
            P(None, "dp"),
        ),
        out_specs=(
            P(("dp", "tensor"), None),
            P(("dp", "tensor"), None),
            P("dp", None, "tensor"),
            P("dp", None, "tensor"),
            P("dp", None, "tensor"),
            P(None, "tensor", "dp"),
            P(None, "tensor", "dp"),
            P(None, "tensor", "dp"),
            P(None, ("tensor", "dp")),
            P(None, ("tensor", "dp")),
            P(None, ("tensor", "dp")),
            P(None, "dp"),
            P(None, "dp"),
            P(None, "dp"),
        ),
        check_vma=False,
    )
```

profile of v0, /device:TPU:24, one launch (start us, length us, event | category | flops | bytes accessed | tf_op | source)
XLA Modules:
  0.0 1036.5 jit_solution(4642176177468012025)
XLA Ops:
  11.2 8.9 all_gather.20
  27.8 8.9 all-gather
  39.4 53.7 %all-gather.8.cloned.1.call-done = bf16[2048,7,512]{2,0,1:T(8,128)(2,1)} async-done(((bf16[256,7,512]{2,0,1:T(8,128)(2,1)}), bf16[2048,7,512]{2,0,1:T(8,128)(2,1)}) %all-gather.8.cloned.1.call-update) | async-done | bytes 14680080 | tf_op jit(solution)/shard_map/all_gather | solution.py:203
  93.1 19.5 %copy.63 = bf16[2048,7,512]{0,2,1:T(8,128)(2,1)} copy(bf16[2048,7,512]{2,0,1:T(8,128)(2,1)} %all-gather.8.cloned.1.call-done) | data formatting | bytes 29360128 | tf_op jit(solution)/shard_map/all_gather | solution.py:203
  112.6 60.7 %all-gather.6.cloned.1.call-done = bf16[1024,2048]{1,0:T(8,128)(2,1)} async-done(((bf16[256,2048]{1,0:T(8,128)(2,1)}), bf16[1024,2048]{1,0:T(8,128)(2,1)}) %all-gather.6.cloned.1.call-update) | async-done | bytes 4194320 | tf_op jit(solution)/shard_map/all_gather | solution.py:211
  173.3 20.6 %fusion.86 = (bf16[1024,7,512]{0,2,1:T(8,128)(2,1)}, f32[1024,7,512]{0,2,1:T(8,128)S(1)}) fusion(f32[7,512]{1,0:T(8,128)S(1)} %bitcast.154, bf16[2048,7,512]{0,2,1:T(8,128)(2,1)} %copy.63, bf16[1024,2048]{1,0:T(8,128)(2,1)} %all-gather.6.cloned.1.call-done), kind=kOutput, calls=%fused_computation.163 | convolution fusion | flops 15039725568 | bytes 40908800 | tf_op jit(solution)/shard_map/dot_general | solution.py:215
  216.8 38.0 %all-gather.12.cloned.1.call-done = bf16[1024,2048]{1,0:T(8,128)(2,1)} async-done(((bf16[256,2048]{1,0:T(8,128)(2,1)}), bf16[1024,2048]{1,0:T(8,128)(2,1)}) %all-gather.12.cloned.1.call-update) | async-done | bytes 4194320 | tf_op jit(solution)/shard_map/all_gather | solution.py:251
  254.8 13.1 %fusion.30 = f32[4,512,2048]{2,1,0:T(8,128)S(1)} fusion(bf16[1024,2048]{1,0:T(8,128)(2,1)} %all-gather.12.cloned.1.call-done, f32[1024,7,512]{0,2,1:T(8,128)} %copy-done.15), kind=kOutput, calls=%fused_computation.45 | convolution fusion | flops 8608808960 | bytes 29360128 | tf_op jit(solution)/shard_map/grc,gd->rcd/dot_general | solution.py:261
  272.7 7.6 pad_maximum_fusion
  280.4 137.3 %reduce-scatter.17.cloned.1.call-done = f32[5,512,256]{2,1,0:T(8,128)} async-done(((f32[5,512,2048]{2,1,0:T(8,128)}), f32[5,512,256]{2,1,0:T(8,128)}) %reduce-scatter.17.cloned.1.call-update) | async-done | bytes 2621456 | tf_op jit(solution)/shard_map/reduce_scatter | solution.py:312
  417.7 7.9 multiply_subtract_fusion.1
  425.8 65.3 %all-gather.10.cloned.1.call-done = bf16[5,512,2048]{2,1,0:T(8,128)(2,1)} async-done(((bf16[5,512,256]{2,1,0:T(8,128)(2,1)}), bf16[5,512,2048]{2,1,0:T(8,128)(2,1)}) %all-gather.10.cloned.1.call-update) | async-done | bytes 10485776 | tf_op jit(solution)/shard_map/all_gather | solution.py:206
  491.1 5.2 fusion.50
  496.4 8.6 fusion.47
  505.9 5.8 fusion.58
  511.7 9.1 multiply_reduce_fusion.1
  520.8 9.9 multiply_reduce_fusion
  530.7 10.2 multiply_convert_fusion
  540.9 6.2 fusion.57
  547.1 5.1 multiply_bitcast_fusion
  558.9 19.4 %fusion.12 = bf16[1024,4,512]{0,2,1:T(8,128)(2,1)} fusion(f32[1024,7,512]{0,2,1:T(8,128)} %copy-done.15, bf16[5,512,2048]{2,1,0:T(8,128)(2,1)} %all-gather.10.cloned.1.call-done, bf16[1024,2048]{1,0:T(8,128)(2,1)} %all-gather.12.cloned.1.call-done), kind=kOutput, calls=%fused_computation.21 | convolution fusion | flops 8631877632 | bytes 25165824 | tf_op jit(solution)/shard_map/gd,rcd->grc/dot_general | solution.py:268
  585.3 17.2 %bitcast_convert_fusion = bf16[1024,2048]{1,0:T(8,128)(2,1)} fusion(bf16[1024,7,512]{0,2,1:T(8,128)(2,1)S(1)} %get-tuple-element.26, bf16[2048,7,512]{2,0,1:T(8,128)(2,1)S(1)} %bitcast.120), kind=kOutput, calls=%fused_computation.23 | convolution fusion | flops 15034482688 | bytes 26214400 | tf_op jit(solution)/shard_map/gk,dk->gd/dot_general | solution.py:297
  604.3 16.3 %fusion.21 = f32[1024,2048,1]{1,0,2:T(8,128)S(1)} fusion(bf16[5,512,2048]{2,1,0:T(8,128)(2,1)} %all-gather.10.cloned.1.call-done, f32[1024,7,512]{0,2,1:T(8,128)} %copy-done.15), kind=kOutput, calls=%fused_computation.38 | convolution fusion | flops 8608808960 | bytes 25165824 | tf_op jit(solution)/shard_map/grc,rcd->gd/dot_general | solution.py:238
  620.6 6.2 fusion.15
  627.0 51.8 %reduce-scatter.13.cloned.1.call-done = bf16[256,2048]{1,0:T(8,128)(2,1)} async-done(((bf16[1024,2048]{1,0:T(8,128)(2,1)}), bf16[256,2048]{1,0:T(8,128)(2,1)}) %reduce-scatter.13.cloned.1.call-update) | async-done | bytes 1048592 | tf_op jit(solution)/shard_map/reduce_scatter | solution.py:296
  684.2 24.8 %fusion.23 = f32[2048,7,512]{2,0,1:T(8,128)} fusion(bf16[1024,7,512]{0,2,1:T(8,128)(2,1)} %copy-done.5, bf16[1024,2048]{1,0:T(8,128)(2,1)} %all-gather.6.cloned.1.call-done), kind=kOutput, calls=%fused_computation.40 | convolution fusion | flops 15032385536 | bytes 40894464 | tf_op jit(solution)/shard_map/gd,gk->dk/dot_general | solution.py:292
  709.0 8.6 reduce-scatter.19.cloned.1.call-done
  719.0 76.9 %reduce-scatter.11.cloned.1.call-done = bf16[256,2048]{1,0:T(8,128)(2,1)} async-done(((bf16[1024,2048]{1,0:T(8,128)(2,1)}), bf16[256,2048]{1,0:T(8,128)(2,1)}) %reduce-scatter.11.cloned.1.call-update) | async-done | bytes 1048592 | tf_op jit(solution)/shard_map/reduce_scatter | solution.py:235
  800.8 36.5 %reduce-scatter.21.cloned.1.call-done = f32[256,3]{1,0:T(8,128)} async-done(((f32[2048,3]{1,0:T(8,128)}), f32[256,3]{1,0:T(8,128)}) %reduce-scatter.21.cloned.1.call-update) | async-done | bytes 3088
  838.3 8.1 psum.7
  847.0 173.0 %reduce-scatter.15.cloned.1.call-done = f32[256,7,512]{2,0,1:T(8,128)} async-done(((f32[2048,7,512]{2,0,1:T(8,128)}), f32[256,7,512]{2,0,1:T(8,128)}) %reduce-scatter.15.cloned.1.call-update) | async-done | bytes 3670032 | tf_op jit(solution)/shard_map/reduce_scatter | solution.py:309
  1020.0 9.2 multiply_subtract_fusion
  (208 shorter events, 71.5 us)
Async XLA Ops:
  7.2 85.9 %all-gather.8.cloned.1.call-start = ((), (), s32[]{:S(2)}) async-start(), calls=%async_computation.7 | async-start | bytes 16515072 | tf_op jit(solution)/shard_map/all_gather | solution.py:203
  10.9 162.4 %all-gather.6.cloned.1.call-start = ((), (), s32[]{:S(2)}) async-start(), calls=%async_computation.6 | async-start | bytes 5242880 | tf_op jit(solution)/shard_map/all_gather | solution.py:211
  23.7 231.1 %all-gather.12.cloned.1.call-start = ((), (), s32[]{:S(2)}) async-start(), calls=%async_computation.10 | async-start | bytes 5242880 | tf_op jit(solution)/shard_map/all_gather | solution.py:251
  27.5 390.2 %reduce-scatter.17.cloned.1.call-start = ((), (), s32[]{:S(2)}) async-start(), calls=%async_computation.13 | async-start | bytes 23592960 | tf_op jit(solution)/shard_map/reduce_scatter | solution.py:312
  38.0 156.4 %copy-start.11 = (f32[1024,16]{0,1:T(8,128)}, f32[1024,16]{0,1:T(8,128)S(1)}, u32[]{:S(2)}) copy-start(f32[1024,16]{0,1:T(8,128)S(1)} %get-tuple-element.56) | copy-start | bytes 196612
  38.0 156.4 %copy-start.13 = (f32[1024,16]{0,1:T(8,128)}, f32[1024,16]{0,1:T(8,128)S(1)}, u32[]{:S(2)}) copy-start(f32[1024,16]{0,1:T(8,128)S(1)} %get-tuple-element.57) | copy-start | bytes 196612
  215.7 52.2 %copy-start.19 = (bf16[8,64,512]{2,1,0:T(8,128)(2,1)}, bf16[8,64,512]{2,1,0:T(8,128)(2,1)S(1)}, u32[]{:S(2)}) copy-start(bf16[8,64,512]{2,1,0:T(8,128)(2,1)S(1)} %fusion.62) | copy-start | bytes 1572868
  280.4 210.7 %all-gather.10.cloned.1.call-start = ((), (), s32[]{:S(2)}) async-start(), calls=%async_computation.8 | async-start | bytes 11796480 | tf_op jit(solution)/shard_map/all_gather | solution.py:206
  425.7 253.1 %reduce-scatter.13.cloned.1.call-start = ((), (), s32[]{:S(2)}) async-start(), calls=%async_computation.11 | async-start | bytes 5242880 | tf_op jit(solution)/shard_map/reduce_scatter | solution.py:296
  425.7 80.2 %copy-start.22 = (f32[8,512]{1,0:T(8,128)}, f32[8,512]{1,0:T(8,128)S(1)}, u32[]{:S(2)}) copy-start(f32[8,512]{1,0:T(8,128)S(1)} %log_add_fusion.1) | copy-start | bytes 49156
  496.4 24.4 %slice-start = ((s8[16777216]{0:T(1024)(128)(4,1)}), s8[4194304]{0:T(1024)(128)(4,1)S(1)}, s32[]{:S(2)}) async-start(s8[16777216]{0:T(1024)(128)(4,1)} %bitcast.113), calls=%async_computation.16 | async-start | bytes 8388608
  496.4 24.4 %slice-start.1 = ((s8[16777216]{0:T(1024)(128)(4,1)}), s8[4194304]{0:T(1024)(128)(4,1)S(1)}, s32[]{:S(2)}) async-start(s8[16777216]{0:T(1024)(128)(4,1)} %bitcast.113), calls=%async_computation.17 | async-start | bytes 8388608
  558.6 26.7 %slice-start.8 = ((s8[14680064]{0:T(1024)(128)(4,1)}), s8[4194304]{0:T(1024)(128)(4,1)S(1)}, s32[]{:S(2)}) async-start(s8[14680064]{0:T(1024)(128)(4,1)} %bitcast.119), calls=%async_computation.24 | async-start | bytes 8388608
  558.9 26.4 %slice-start.9 = ((s8[14680064]{0:T(1024)(128)(4,1)}), s8[4194304]{0:T(1024)(128)(4,1)S(1)}, s32[]{:S(2)}) async-start(s8[14680064]{0:T(1024)(128)(4,1)} %bitcast.119), calls=%async_computation.25 | async-start | bytes 8388608
  558.9 26.4 %slice-start.10 = ((s8[14680064]{0:T(1024)(128)(4,1)}), s8[4194304]{0:T(1024)(128)(4,1)S(1)}, s32[]{:S(2)}) async-start(s8[14680064]{0:T(1024)(128)(4,1)} %bitcast.119), calls=%async_computation.26 | async-start | bytes 8388608
  558.9 26.4 %slice-start.11 = ((s8[14680064]{0:T(1024)(128)(4,1)}), s8[2097152]{0:T(1024)(128)(4,1)S(1)}, s32[]{:S(2)}) async-start(s8[14680064]{0:T(1024)(128)(4,1)} %bitcast.119), calls=%async_computation.27 | async-start | bytes 4194304
  602.6 114.9 %reduce-scatter.19.cloned.1.call-start = ((), (), s32[]{:S(2)}) async-start(), calls=%async_computation.14 | async-start | bytes 294912
  604.2 191.7 %reduce-scatter.11.cloned.1.call-start = ((), (), s32[]{:S(2)}) async-start(), calls=%async_computation.9 | async-start | bytes 5242880 | tf_op jit(solution)/shard_map/reduce_scatter | solution.py:235
  626.8 51.9 %copy-start.3 = (f32[256,2048]{1,0:T(8,128)S(1)}, f32[256,2048]{1,0:T(8,128)}, u32[]{:S(2)}) copy-start(f32[256,2048]{1,0:T(8,128)} %param.15) | copy-start | bytes 6291460
  626.8 51.9 %copy-start.25 = (f32[1,2048]{1,0:T(1,128)S(1)}, f32[1,2048]{1,0:T(1,128)}, u32[]{:S(2)}) copy-start(f32[1,2048]{1,0:T(1,128)} %copy-done.24) | copy-start | bytes 24580
  626.9 51.9 %copy-start.29 = (f32[256]{0:T(256)S(1)}, f32[256]{0:T(256)}, u32[]{:S(2)}) copy-start(f32[256]{0:T(256)} %copy-done.28) | copy-start | bytes 3076
  626.9 53.6 %copy-start.39 = (f32[256]{0:T(256)S(1)}, f32[256]{0:T(256)}, u32[]{:S(2)}) copy-start(f32[256]{0:T(256)} %copy-done.38) | copy-start | bytes 3076
  626.9 53.6 %copy-start.33 = (f32[256]{0:T(256)S(1)}, f32[256]{0:T(256)}, u32[]{:S(2)}) copy-start(f32[256]{0:T(256)} %copy-done.32) | copy-start | bytes 3076
  626.9 55.8 %copy-start.30 = (f32[2048]{0:T(1024)S(1)}, f32[2048]{0:T(1024)}, u32[]{:S(2)}) copy-start(f32[2048]{0:T(1024)} %get-tuple-element.20) | copy-start | bytes 24580
  626.9 210.4 %reduce-scatter.21.cloned.1.call-start = ((), (), s32[]{:S(2)}) async-start(), calls=%async_computation.15 | async-start | bytes 1179648
  684.1 335.9 %reduce-scatter.15.cloned.1.call-start = ((), (), s32[]{:S(2)}) async-start(), calls=%async_computation.12 | async-start | bytes 33030144 | tf_op jit(solution)/shard_map/reduce_scatter | solution.py:309
  708.9 87.0 %copy-start.4 = (bf16[256,2048]{1,0:T(8,128)(2,1)S(1)}, bf16[256,2048]{1,0:T(8,128)(2,1)}, u32[]{:S(2)}) copy-start(bf16[256,2048]{1,0:T(8,128)(2,1)} %reduce-scatter.13.cloned.1.call-done) | copy-start | bytes 3145732
  709.0 87.0 %copy-start.31 = (f32[1,2048]{1,0:T(1,128)S(1)}, f32[1,2048]{1,0:T(1,128)}, u32[]{:S(2)}) copy-start(f32[1,2048]{1,0:T(1,128)} %get-tuple-element.53) | copy-start | bytes 24580
  709.0 86.9 %copy-start.41 = (f32[256]{0:T(256)S(1)}, f32[256]{0:T(256)}, u32[]{:S(2)}) copy-start(f32[256]{0:T(256)} %copy-done.40) | copy-start | bytes 3076
  795.9 50.5 %copy-start.37 = (f32[3,256]{1,0:T(4,128)S(1)}, f32[3,256]{1,0:T(4,128)}, u32[]{:S(2)}) copy-start(f32[3,256]{1,0:T(4,128)} %param.21) | copy-start | bytes 9220
  795.9 50.5 %copy-start.44 = (f32[3,256]{1,0:T(4,128)S(1)}, f32[3,256]{1,0:T(4,128)}, u32[]{:S(2)}) copy-start(f32[3,256]{1,0:T(4,128)} %param.28) | copy-start | bytes 9220
  795.9 50.5 %copy-start.45 = (f32[3,256]{1,0:T(4,128)S(1)}, f32[3,256]{1,0:T(4,128)}, u32[]{:S(2)}) copy-start(f32[3,256]{1,0:T(4,128)} %param.29) | copy-start | bytes 9220
  (37 other events, 236.0 us)
Sparse Core Ops, SparseCore 0:
  11.0 82.0 all-gather.7
  95.2 78.0 all-gather.5
  175.5 79.2 all-gather.11
  280.5 137.2 reduce-scatter.16
  425.8 65.2 all-gather.9
  602.7 75.9 reduce-scatter.12
  682.7 34.8 reduce-scatter.18
  719.9 75.9 reduce-scatter.10
  800.0 37.2 reduce-scatter.20
  841.2 178.7 reduce-scatter.14
where the time goes:
time: 1040 us
  waiting for transfers between devices  702 us (68%)
  matrix products  185 us (18%)
  other arithmetic  71.4 us (7%)
  local copies, waits for them, and re-layouts  36.3 us (3%)
  blocking collectives  25.9 us (2%)
  between operations  15.5 us (1%)
    reduce_scatter x1, waiting for transfers between devices, per_device(): lax.psum_scatter(in_grad, 'dp', scatter_dimension=0, tiled=True)  173 us
    reduce_scatter x1, waiting for transfers between devices, per_device(): lax.psum_scatter(down_grad, 'dp', scatter_dimension=2, tiled=True)  137 us
    reduce_scatter x1, waiting for transfers between devices, per_device(): lax.psum_scatter((attn_part + jnp.einsum('grc,rcd->gd', mlp_rows, down_fu...  76.9 us
    all_gather x1, waiting for transfers between devices, per_device(): lax.all_gather(down_low, 'dp', axis=2, tiled=True)  65.3 us
    all_gather x1, waiting for transfers between devices, per_device(): lax.all_gather(normed.astype(jnp.bfloat16), 'tensor', axis=0, tiled=True)  60.7 us
    all_gather x1, waiting for transfers between devices, per_device(): lax.all_gather(in_low, 'dp', axis=0, tiled=True)  53.7 us
    reduce_scatter x1, waiting for transfers between devices, per_device(): lax.psum_scatter(jnp.einsum('gk,dk->gd', proj_flat, back_flat, preferred_...  51.8 us
    unnamed x12, waiting for transfers between devices  45.2 us
  transfers between devices with their start and end apart: 10, of which 10 were waited for; matrix products, arithmetic and copies ran while one was open for 13% of the time, Pallas kernels for 0%

commit v1 on v0

v1 whole, which is shorter than its diff:
```python
from functools import partial

import jax
import jax.numpy as jnp
from jax import lax
from jax.experimental import pallas as pl
from jax.experimental.pallas import tpu as pltpu
from jax.sharding import PartitionSpec as P

HEAD = 64
ROT = 32
STEP = 8
LANES = 128
QUERY_ROWS = 256

norm_eps = 1e-05
beta_first = 0.9
beta_second = 0.95
adam_eps = 1e-08
masked_score = -1000000000.0
rate_in = 0.02
rate_down = 0.05
rate_vector = 0.2
weight_decay = 0.1

bf16 = jnp.bfloat16
f32 = jnp.float32


def layout(lengths, group_size):
    seq_ends = jnp.cumsum(lengths)
    places = jnp.arange(group_size, dtype=jnp.int32)
    segment = jnp.sum((places[:, None] >= seq_ends[None, :]).astype(jnp.int32), axis=1)
    starts = jnp.concatenate([jnp.zeros((1,), jnp.int32), seq_ends])
    picked = segment[:, None] == jnp.arange(lengths.shape[0] + 1, dtype=jnp.int32)[None, :]
    seq_begin = jnp.sum(jnp.where(picked, starts[None, :], 0), axis=1)
    live_mask = (segment < lengths.shape[0]).astype(f32)
    return seq_begin, places - seq_begin, live_mask


def rotary_tables(position):
    half_rot = ROT // 2
    frequency = 10000.0 ** (-2.0 * jnp.arange(half_rot, dtype=f32) / ROT)
    angles = position.astype(f32)[:, None] * frequency[None, :]
    cosine, sine = jnp.cos(angles), jnp.sin(angles)
    rows = position.shape[0]
    none = jnp.zeros((rows, half_rot), f32)
    rest = jnp.zeros((rows, HEAD - ROT), f32)
    own = jnp.concatenate([cosine, cosine, rest + 1.0], axis=1)
    ahead = jnp.concatenate([-sine, none, rest], axis=1)
    behind = jnp.concatenate([none, sine, rest], axis=1)
    return tuple(jnp.concatenate([t] * (LANES // HEAD), axis=1) for t in (own, ahead, behind))


def attend_mask(begin, row_start, rows, stop):
    key_place = lax.broadcasted_iota(jnp.int32, (rows, stop), 1)
    query_place = row_start + lax.broadcasted_iota(jnp.int32, (rows, stop), 0)
    return (key_place <= query_place) & (key_place >= begin)


def head_lanes(rows, head):
    lane = lax.broadcasted_iota(jnp.int32, (rows, LANES), 1)
    return (lane >= head * HEAD) & (lane < (head + 1) * HEAD)


def dot_t(a, b):
    return lax.dot_general(a, b, (((1,), (1,)), ((), ())), preferred_element_type=f32)


def dot_n(a, b):
    return lax.dot_general(a, b, (((1,), (0,)), ((), ())), preferred_element_type=f32)


def dot_s(a, b):
    return lax.dot_general(a, b, (((0,), (0,)), ((), ())), preferred_element_type=f32)


def turn(x, own, ahead, behind, sign):
    half = ROT // 2
    return x * own + sign * (
        pltpu.roll(x, LANES - half, 1) * ahead + pltpu.roll(x, half, 1) * behind
    )


def attend_forward_kernel(q_in, k_in, v_in, own, ahead, behind, begin, out, q_out, k_out, v_out, lse):
    total = q_in.shape[0]
    rows = min(QUERY_ROWS, total)
    q_out[...] = turn(q_in[...], own[...], ahead[...], behind[...], 1.0).astype(bf16)
    k_out[...] = turn(k_in[...], own[...], ahead[...], behind[...], 1.0).astype(bf16)
    v_out[...] = v_in[...].astype(bf16)
    for start in range(0, total, rows):
        stop = start + rows
        place = pl.ds(start, rows)
        allowed = attend_mask(begin[place, :], start, rows, stop)
        query = q_out[place, :]
        results, sums = [], []
        for head in range(LANES // HEAD):
            mine = head_lanes(rows, head)
            chosen = jnp.where(mine, query, jnp.zeros_like(query)) * HEAD ** (-0.5)
            scores = jnp.where(allowed, dot_t(chosen.astype(bf16), k_out[:stop, :]), masked_score)
            top = jnp.max(scores, axis=1, keepdims=True)
            weights = jnp.exp(scores - top)
            total_weight = jnp.sum(weights, axis=1, keepdims=True)
            results.append(dot_n(weights.astype(bf16), v_out[:stop, :]) / total_weight)
            sums.append(top + jnp.log(total_weight))
        first = head_lanes(rows, 0)
        out[place, :] = jnp.where(first, results[0], results[1]).astype(bf16)
        lse[place, :] = jnp.where(first, sums[0], sums[1])


def attend_forward(q, k, v, tables, begin):
    total, width = q.shape
    tile = pl.BlockSpec((total, LANES), lambda p: (0, p))
    fixed = pl.BlockSpec((total, LANES), lambda p: (0, 0))
    return pl.pallas_call(
        attend_forward_kernel,
        grid=(width // LANES,),
        in_specs=[tile] * 3 + [fixed] * 3 + [pl.BlockSpec((total, 1), lambda p: (0, 0))],
        out_specs=[tile] * 5,
        out_shape=[jax.ShapeDtypeStruct((total, width), bf16)] * 4
        + [jax.ShapeDtypeStruct((total, width), f32)],
        compiler_params=pltpu.CompilerParams(vmem_limit_bytes=48 << 20),
        cost_estimate=pl.CostEstimate(
            flops=8 * total * total * width, bytes_accessed=24 * total * width, transcendentals=0
        ),
    )(q, k, v, *tables, begin)


def attend_backward_kernel(q_in, k_in, v_in, grad, lse, own, ahead, behind, begin, dq, dk, dv, k_sum, v_sum):
    total = q_in.shape[0]
    rows = min(QUERY_ROWS, total)
    k_sum[...] = jnp.zeros_like(k_sum)
    v_sum[...] = jnp.zeros_like(v_sum)
    scale = HEAD ** (-0.5)
    for start in range(0, total, rows):
        stop = start + rows
        place = pl.ds(start, rows)
        allowed = attend_mask(begin[place, :], start, rows, stop)
        q_sum = jnp.zeros((rows, LANES), f32)
        for head in range(LANES // HEAD):
            mine = head_lanes(rows, head)
            query = jnp.where(mine, q_in[place, :], jnp.zeros((rows, LANES), bf16)) * scale
            query = query.astype(bf16)
            cot = jnp.where(mine, grad[place, :], jnp.zeros((rows, LANES), bf16))
            scores = dot_t(query, k_in[:stop, :]) - lse[place, head * HEAD : head * HEAD + 1]
            probs = jnp.where(allowed, jnp.exp(scores), 0.0)
            prob_grad = dot_t(cot, v_in[:stop, :])
            mean = jnp.sum(probs * prob_grad, axis=1, keepdims=True)
            score_grad = (probs * (prob_grad - mean)).astype(bf16)
            q_step = dot_n(score_grad, k_in[:stop, :])
            q_sum = jnp.where(mine, q_step * scale, q_sum)
            k_sum[:stop, :] += dot_s(score_grad, query)
            v_sum[:stop, :] += dot_s(probs.astype(bf16), cot)
        dq[place, :] = turn(
            q_sum, own[place, :], ahead[place, :], behind[place, :], -1.0
        ).astype(bf16)
    dk[...] = turn(k_sum[...], own[...], ahead[...], behind[...], -1.0).astype(bf16)
    dv[...] = v_sum[...].astype(bf16)


def attend_backward(q, k, v, grad, lse, tables, begin):
    total, width = q.shape
    tile = pl.BlockSpec((total, LANES), lambda p: (0, p))
    fixed = pl.BlockSpec((total, LANES), lambda p: (0, 0))
    return pl.pallas_call(
        attend_backward_kernel,
        grid=(width // LANES,),
        in_specs=[tile] * 5 + [fixed] * 3 + [pl.BlockSpec((total, 1), lambda p: (0, 0))],
        out_specs=[tile] * 3,
        out_shape=[jax.ShapeDtypeStruct((total, width), bf16)] * 3,
        scratch_shapes=[pltpu.VMEM((total, LANES), f32)] * 2,
        compiler_params=pltpu.CompilerParams(vmem_limit_bytes=48 << 20),
        cost_estimate=pl.CostEstimate(
            flops=20 * total * total * width, bytes_accessed=20 * total * width, transcendentals=0
        ),
    )(q, k, v, grad, lse, *tables, begin)


def after(value, *others):
    return lax.optimization_barrier((value,) + others)[0]


def line_gather(own, axis):
    n = lax.axis_size(axis)
    me = lax.axis_index(axis)
    rows = own.shape[0]
    up, down = [own], [own]
    for step in range(1, n):
        up.append(lax.ppermute(up[-1], axis, [(j, j + 1) for j in range(step - 1, n - 1)]))
        down.append(lax.ppermute(down[-1], axis, [(j, j - 1) for j in range(1, n - step + 1)]))
    full = jnp.zeros((n * rows,) + own.shape[1:], own.dtype)
    for step in range(n):
        part = own if step == 0 else jnp.where(me >= step, up[step], down[n - step])
        full = lax.dynamic_update_slice_in_dim(full, part, lax.rem(me - step + n, n) * rows, 0)
    return full, (up[-1], down[-1])


def line_scatter(partials, axis):
    n = lax.axis_size(axis)
    me = lax.axis_index(axis)
    rows = partials.shape[0] // n

    def part(owner):
        owner = jnp.clip(owner, 0, n - 1)
        return lax.dynamic_slice_in_dim(partials, owner * rows, rows, 0)

    up = down = None
    for step in range(n - 1):
        to_up = part(me + n - 1 - step)
        to_down = part(me - n + 1 + step)
        if step:
            to_up = (to_up.astype(f32) + up.astype(f32)).astype(bf16)
            to_down = (to_down.astype(f32) + down.astype(f32)).astype(bf16)
        up = lax.ppermute(to_up, axis, [(j, j + 1) for j in range(0, min(step, n - 2) + 1)])
        down = lax.ppermute(to_down, axis, [(j, j - 1) for j in range(n - 1 - step, n)])
    return part(me).astype(f32) + up.astype(f32) + down.astype(f32)


def flip(value, axis, bit):
    return lax.ppermute(value, axis, [(j, j ^ bit) for j in range(lax.axis_size(axis))])


def low_bit(mask):
    return mask & -mask


def high_bit(mask):
    return 1 << (mask.bit_length() - 1)


def cube_gather(own, axis):
    n = lax.axis_size(axis)
    half = own.shape[0] // 2
    whole = {0: own}
    parts = {0: (own[:half], own[half:])}
    for mask in sorted(range(2, n, 2), key=lambda m: m.bit_count()):
        if mask.bit_count() == 1:
            whole[mask] = flip(own, axis, mask)
            parts[mask] = (whole[mask][:half], whole[mask][half:])
        else:
            last, other = high_bit(mask), low_bit(mask)
            parts[mask] = (
                flip(parts[mask ^ last][0], axis, last),
                flip(parts[mask ^ other][1], axis, other),
            )
    if n > 1:
        for mask in range(0, n, 2):
            if mask in whole:
                whole[mask | 1] = flip(whole[mask], axis, 1)
            else:
                parts[mask | 1] = tuple(flip(p, axis, 1) for p in parts[mask])
    return whole, parts


def cube_assemble(gathered, axis, dim):
    whole, parts = gathered
    n = lax.axis_size(axis)
    me = lax.axis_index(axis)
    shape = list(whole[0].shape)
    step, half = shape[dim], shape[0] // 2
    shape[dim] *= n
    full = jnp.zeros(shape, whole[0].dtype)
    for mask in range(n):
        owner = jnp.bitwise_xor(me, mask)
        pieces = [(0, whole[mask])] if mask in whole else [(0, parts[mask][0]), (half, parts[mask][1])]
        for row, piece in pieces:
            start = [0] * len(shape)
            start[0] = row
            start[dim] = start[dim] + owner * step
            full = lax.dynamic_update_slice(full, piece, start)
    return full


def cube_scatter(send, keep, axis):
    n = lax.axis_size(axis)
    got = flip(send, axis, 1)
    total = {2 * j: (keep[j].astype(f32) + got[j].astype(f32)).astype(bf16) for j in range(n // 2)}
    half = keep.shape[1] // 2
    bits = [1 << b for b in range(1, n.bit_length() - 1)]
    results = []
    for rows, order in ((slice(0, half), bits), (slice(half, None), bits[::-1])):
        held = {m: t[rows] for m, t in total.items()}
        for bit in order:
            away = [m for m in sorted(held) if m & bit]
            came = flip(jnp.stack([held[m] for m in away]), axis, bit)
            held = {
                m ^ bit: held[m ^ bit].astype(f32) + came[j].astype(f32) for j, m in enumerate(away)
            }
            if bit != order[-1]:
                held = {m: t.astype(bf16) for m, t in held.items()}
        results.append(held[0].astype(f32))
    return jnp.concatenate(results, axis=0)


def adam_update(weight, moment_one, moment_two, gradient, step_rate, decay_factor):
    first_new = beta_first * moment_one + (1.0 - beta_first) * gradient
    second_new = beta_second * moment_two + (1.0 - beta_second) * gradient * gradient
    corrected = first_new / (1.0 - beta_first**STEP)
    spread = jnp.sqrt(second_new / (1.0 - beta_second**STEP))
    return (
        weight - step_rate * (corrected / (spread + adam_eps) + decay_factor * weight),
        first_new,
        second_new,
    )


def mm(a, b):
    return jnp.dot(a, b, preferred_element_type=f32)


def columns_of(full, axis, masks, step):
    me = lax.axis_index(axis)
    return jnp.concatenate(
        [
            lax.dynamic_slice_in_dim(full, jnp.bitwise_xor(me, m) * step, step, 1)
            for m in masks
        ],
        axis=1,
    )


def per_device(
    block_input,
    out_grad,
    seq_lengths,
    in_weight,
    down_weight,
    column_bias,
    vector_params,
    in_first,
    in_second,
    down_first,
    down_second,
    bias_first,
    bias_second,
    vector_first,
    vector_second,
):
    n_dp = lax.axis_size("dp")
    n_tensor = lax.axis_size("tensor")
    own_rows, model = block_input.shape
    group = own_rows * n_tensor
    in_rows, widths, local = in_weight.shape
    out_cols = down_weight.shape[2]
    n_mlp = widths - 3
    attn_width, mlp_width = 3 * local, n_mlp * local

    in_attn = in_weight[:, :3].astype(bf16).reshape(in_rows, attn_width)
    in_mlp = in_weight[:, 3:].astype(bf16).reshape(in_rows, mlp_width)
    down_low = down_weight.astype(bf16).reshape(widths_down(down_weight), out_cols)

    centered = block_input - jnp.mean(block_input, axis=-1, keepdims=True)
    inv_scale = lax.rsqrt(jnp.mean(centered * centered, axis=-1, keepdims=True) + norm_eps)
    xhat = centered * inv_scale
    begin, position, live = layout(seq_lengths[0], group)
    own_live = lax.dynamic_slice_in_dim(live, lax.axis_index("tensor") * own_rows, own_rows)
    cot_live = out_grad * own_live[:, None]
    cot_low = cot_live.astype(bf16)

    xhat_all, xhat_last = line_gather(xhat.astype(bf16), "tensor")
    attn_pieces = cube_gather(in_attn, "dp")
    in_mlp = after(in_mlp, attn_pieces[0][min(2, n_dp - 1)])
    mlp_pieces = cube_gather(in_mlp, "dp")
    small = lax.all_gather(
        jnp.concatenate([column_bias.astype(bf16).reshape(-1), vector_params.astype(bf16).reshape(-1)]),
        "dp",
        axis=0,
    )
    n_bias = column_bias.size
    bias_vals = (
        small[:, :n_bias].reshape((n_dp,) + column_bias.shape).transpose(1, 0, 2).reshape(widths, local)
    ).astype(f32)
    vector_vals = (
        small[:, n_bias:].reshape((n_dp,) + vector_params.shape).transpose(1, 0, 2).reshape(3, model)
    ).astype(f32)
    gain, shift, out_bias = vector_vals[0], vector_vals[1], vector_vals[2]

    cot_low = after(cot_low, *xhat_last)
    cot_all, _ = line_gather(cot_low, "tensor")
    down_low = after(down_low, mlp_pieces[0][min(2, n_dp - 1)])
    down_pieces = cube_gather(down_low, "dp")

    w_attn = cube_assemble(attn_pieces, "dp", 0)
    w_mlp = cube_assemble(mlp_pieces, "dp", 0)
    w_down = cube_assemble(down_pieces, "dp", 1)

    tables = rotary_tables(position)
    begin_col = begin[:, None]
    normed = (xhat_all.astype(f32) * gain + shift).astype(bf16)

    bias_flat = bias_vals.reshape(-1)
    proj_attn = mm(normed, w_attn) + bias_flat[:attn_width]
    attended, q_low, k_low, v_low, lse = attend_forward(
        proj_attn[:, :local],
        proj_attn[:, local : 2 * local],
        proj_attn[:, 2 * local :],
        tables,
        begin_col,
    )
    pre = mm(normed, w_mlp) + bias_flat[attn_width:]
    hidden, gelu_pull = jax.vjp(partial(jax.nn.gelu, approximate=True), pre)
    hidden = hidden.astype(bf16)
    out_part = (mm(attended, w_down[:local]) + mm(hidden, w_down[local:])).astype(bf16)
    mixed = line_scatter(out_part, "tensor")
    block_out = block_input + (mixed + out_bias)

    attn_grad = dot_t(cot_all, w_down[:local]).astype(bf16)
    pre_grad = gelu_pull(dot_t(cot_all, w_down[local:]))[0].astype(bf16)

    keep_masks = list(range(0, n_dp, 2))
    send_masks = [m + 1 for m in keep_masks]
    cot_send = columns_of(cot_all, "dp", send_masks, out_cols)
    cot_keep = columns_of(cot_all, "dp", keep_masks, out_cols)
    normed_send = columns_of(normed, "dp", send_masks, in_rows)
    normed_keep = columns_of(normed, "dp", keep_masks, in_rows)

    def down_part(cot):
        parts = jnp.concatenate([dot_s(attended, cot).astype(bf16), dot_s(hidden, cot).astype(bf16)], axis=0)
        return parts.reshape(parts.shape[0], n_dp // 2, out_cols).transpose(1, 0, 2)

    def in_part(rows, grads):
        return dot_s(rows, grads).astype(bf16).reshape(n_dp // 2, in_rows, grads.shape[1])

    down_reduced = cube_scatter(down_part(cot_send), down_part(cot_keep), "dp")
    in_mlp_reduced = cube_scatter(in_part(normed_send, pre_grad), in_part(normed_keep, pre_grad), "dp")

    dq, dk, dv = attend_backward(q_low, k_low, v_low, attn_grad, lse, tables, begin_col)
    qkv_grad = jnp.concatenate([dq, dk, dv], axis=1)
    dh_part = dot_t(qkv_grad, w_attn) + dot_t(pre_grad, w_mlp)
    dh = line_scatter(dh_part.astype(bf16), "tensor")
    in_attn_reduced = cube_scatter(in_part(normed_send, qkv_grad), in_part(normed_keep, qkv_grad), "dp")

    bias_grad = jnp.concatenate(
        [jnp.sum(qkv_grad, axis=0, dtype=f32), jnp.sum(pre_grad, axis=0, dtype=f32)]
    ).reshape(widths, n_dp, column_bias.shape[1])
    gain_part = jnp.sum(dh_part * xhat_all.astype(f32), axis=0)
    shift_part = jnp.sum(dh_part, axis=0)
    outbias_part = jnp.sum(cot_low.astype(f32), axis=0)
    vector_grad = jnp.stack([gain_part, shift_part, outbias_part]).reshape(3, n_dp, vector_params.shape[1])
    small_grad = jnp.concatenate(
        [
            bias_grad.transpose(1, 0, 2).reshape(n_dp, -1),
            vector_grad.transpose(1, 0, 2).reshape(n_dp, -1),
        ],
        axis=1,
    )
    small_reduced = lax.psum_scatter(small_grad, "dp", scatter_dimension=0, tiled=True)[0]
    bias_reduced = small_reduced[:n_bias].reshape(column_bias.shape)
    vector_reduced = lax.psum(small_reduced[n_bias:], "tensor").reshape(vector_params.shape)

    dxhat = dh * gain
    input_grad = cot_live + inv_scale * (
        dxhat
        - jnp.mean(dxhat, axis=-1, keepdims=True)
        - xhat * jnp.mean(dxhat * xhat, axis=-1, keepdims=True)
    )

    in_reduced = jnp.concatenate(
        [
            in_attn_reduced.reshape(in_rows, 3, local),
            in_mlp_reduced.reshape(in_rows, n_mlp, local),
        ],
        axis=1,
    )
    down_reduced = down_reduced.reshape(down_weight.shape)
    in_new, in_one, in_two = adam_update(
        in_weight, in_first, in_second, in_reduced, rate_in, weight_decay
    )
    down_new, down_one, down_two = adam_update(
        down_weight, down_first, down_second, down_reduced, rate_down, weight_decay
    )
    bias_new, bias_one, bias_two = adam_update(
        column_bias, bias_first, bias_second, bias_reduced, rate_vector, 0.0
    )
    vector_new, vector_one, vector_two = adam_update(
        vector_params, vector_first, vector_second, vector_reduced, rate_vector, 0.0
    )
    return (
        block_out,
        input_grad,
        in_new,
        in_one,
        in_two,
        down_new,
        down_one,
        down_two,
        bias_new,
        bias_one,
        bias_two,
        vector_new,
        vector_one,
        vector_two,
    )


def widths_down(down_weight):
    return down_weight.shape[0] * down_weight.shape[1]


def solution(mesh):
    return jax.shard_map(
        per_device,
        mesh=mesh,
        in_specs=(
            P(("dp", "tensor"), None),
            P(("dp", "tensor"), None),
            P("dp", None),
            P("dp", None, "tensor"),
            P(None, "tensor", "dp"),
            P(None, ("tensor", "dp")),
            P(None, "dp"),
            P("dp", None, "tensor"),
            P("dp", None, "tensor"),
            P(None, "tensor", "dp"),
            P(None, "tensor", "dp"),
            P(None, ("tensor", "dp")),
            P(None, ("tensor", "dp")),
            P(None, "dp"),
            P(None, "dp"),
        ),
        out_specs=(
            P(("dp", "tensor"), None),
            P(("dp", "tensor"), None),
            P("dp", None, "tensor"),
            P("dp", None, "tensor"),
            P("dp", None, "tensor"),
            P(None, "tensor", "dp"),
            P(None, "tensor", "dp"),
            P(None, "tensor", "dp"),
            P(None, ("tensor", "dp")),
            P(None, ("tensor", "dp")),
            P(None, ("tensor", "dp")),
            P(None, "dp"),
            P(None, "dp"),
            P(None, "dp"),
        ),
        check_vma=False,
    )
```

time: 1040 us -> 748 us (0.72)
  waiting for transfers between devices: 702 us -> 221 us
  starting transfers between devices: 0.42 us -> 122 us
  matrix products: 185 us -> 126 us
  local copies, waits for them, and re-layouts: 36.3 us -> 92.8 us
  Pallas kernels: 0 us -> 45.8 us
  blocking collectives: 25.9 us -> 65.6 us
  other arithmetic: 71.4 us -> 59 us
  between operations: 15.5 us -> 3.75 us
    reduce_scatter x4 -> x0, waiting for transfers between devices: 439 us -> none  [the longest x1 173 us: per_device(): lax.psum_scatter(in_grad, 'dp', scatter_dimension=0, tiled=True)]
    ppermute x0 -> x66, waiting for transfers between devices: none -> 221 us  [the longest x42 124 us: flip(): lax.ppermute(value, axis, [(j, j ^ bit) for j in range(lax.axis_size(axis...]
    all_gather x4 -> x0, waiting for transfers between devices: 218 us -> none  [the longest x1 65.3 us: per_device(): lax.all_gather(down_low, 'dp', axis=2, tiled=True)]
    ppermute x0 -> x66, starting transfers between devices: none -> 122 us  [the longest x6 56.5 us: line_scatter(): lax.ppermute(to_down, axis, [(j, j - 1) for j in range(n - 1 - step, n)])]
    dot_general x21 -> x16, matrix products: 185 us -> 126 us  [the longest x4 47.1 us: dot_t(): lax.dot_general(a, b, (((1,), (1,)), ((), ())), preferred_element_type=f32)]
    unnamed x0 -> x2, blocking collectives: none -> 57.5 us
    pallas_call x0 -> x2, Pallas kernels: none -> 45.8 us  [the longest x1 26.3 us: attend_backward(): pl.pallas_call(attend_backward_kernel, grid=(width // LANES,), in_specs=[...]
    unnamed x12 -> x0, waiting for transfers between devices: 45.2 us -> none
  transfers between devices with their start and end apart: 10 -> 66, of which waited for: 10 -> 22; matrix products, arithmetic and copies ran while one was open for 13% -> 21% of each run, Pallas kernels for 0% -> 3%
where the time goes in v1:
time: 748 us; the launch traced here: 736 us
  waiting for transfers between devices  221 us (30%)
  matrix products  126 us (17%)
  starting transfers between devices  122 us (16%)
  local copies, waits for them, and re-layouts  92.8 us (12%)
  blocking collectives  65.6 us (9%)
  other arithmetic  59 us (8%)
  Pallas kernels  45.8 us (6%)
    ppermute x42, waiting for transfers between devices, flip(): lax.ppermute(value, axis, [(j, j ^ bit) for j in range(lax.axis_size(axis...  124 us
    ppermute x6, waiting for transfers between devices, line_gather(): lax.ppermute(up[-1], axis, [(j, j + 1) for j in range(step - 1, n - 1)])  73.4 us
    unnamed x2, blocking collectives  57.5 us
    ppermute x6, starting transfers between devices, line_scatter(): lax.ppermute(to_down, axis, [(j, j - 1) for j in range(n - 1 - step, n)])  56.5 us
    dot_general x4, matrix products, dot_t(): lax.dot_general(a, b, (((1,), (1,)), ((), ())), preferred_element_type=f32)  47.1 us
    dot_general x4, matrix products, mm(): return jnp.dot(a, b, preferred_element_type=f32)  42 us
    dot_general x8, matrix products, dot_s(): lax.dot_general(a, b, (((0,), (0,)), ((), ())), preferred_element_type=f32)  36.7 us
    ppermute x42, starting transfers between devices, flip(): lax.ppermute(value, axis, [(j, j ^ bit) for j in range(lax.axis_size(axis...  34.5 us
  transfers between devices with their start and end apart: 66, of which 22 were waited for; matrix products, arithmetic and copies ran while one was open for 21% of the time, Pallas kernels for 3%

profile of v1, /device:TPU:24, one launch (start us, length us, event | category | flops | bytes accessed | tf_op | source)
XLA Modules:
  0.0 735.6 jit_solution(15858430956415777593)
XLA Ops:
  9.9 5.5 collective-permute-start.1
  22.9 33.1 %all-reduce = bf16[9728]{0:T(1024)(128)(2,1)S(1)} all-reduce(bf16[9728]{0:T(1024)(128)(2,1)S(1)} %dynamic-update-slice), channel_id=2, replica_groups=mesh['dp'=8,'tensor'=4] {'dp'}, use_global_device_ids=true, to_apply=%add | all-reduce | flops 9728 | bytes 38912
  87.0 25.7 %collective-permute-done.11 = bf16[128,1536]{0,1:T(8,128)(2,1)S(1)} collective-permute-done((bf16[128,1536]{0,1:T(8,128)(2,1)S(1)}, bf16[128,1536]{0,1:T(8,128)(2,1)S(1)}, u32[]{:S(2)}, u32[]{:S(2)}) %collective-permute-start.11) | collective-permute-done | bytes 393248 | tf_op jit(solution)/shard_map/ppermute | solution.py:220
  126.1 19.3 %collective-permute-done.4 = bf16[256,2048]{1,0:T(8,128)(2,1)S(1)} collective-permute-done((bf16[256,2048]{1,0:T(8,128)(2,1)}, bf16[256,2048]{1,0:T(8,128)(2,1)S(1)}, u32[]{:S(2)}, u32[]{:S(2)}) %collective-permute-start.4) | collective-permute-done | bytes 1048608 | tf_op jit(solution)/shard_map/ppermute | solution.py:189
  150.4 22.4 %collective-permute-done.5 = bf16[256,2048]{1,0:T(8,128)(2,1)S(1)} collective-permute-done((bf16[256,2048]{1,0:T(8,128)(2,1)S(1)}, bf16[256,2048]{1,0:T(8,128)(2,1)S(1)}, u32[]{:S(2)}, u32[]{:S(2)}) %collective-permute-start.5) | collective-permute-done | bytes 1048608 | tf_op jit(solution)/shard_map/ppermute | solution.py:189
  184.7 13.3 %multiply_convert_fusion = (bf16[1024,2048]{1,0:T(8,128)(2,1)}, f32[1024,2048]{1,0:T(8,128)}) fusion(f32[2048]{0:T(1024)S(1)} %add.488, bf16[1024,2048]{1,0:T(8,128)(2,1)S(1)} %fusion.1, bf16[2048,2048]{0,1:T(8,128)(2,1)S(1)} %constant_dynamic-update-slice_fusion.1), kind=kOutput, calls=%fused_computation.16 | convolution fusion | flops 8610906112 | bytes 25174016 | tf_op jit(solution)/shard_map/dot_general | solution.py:308
  201.3 8.8 %convolution_add_fusion = f32[1024,1536]{1,0:T(8,128)S(1)} fusion(bf16[1024,2048]{1,0:T(8,128)(2,1)S(1)} %fusion.1, bf16[2048,1536]{0,1:T(8,128)(2,1)} %constant_dynamic-update-slice_fusion.19, f32[1536]{0:T(1024)S(1)} %add.484), kind=kOutput, calls=%fused_computation.27 | convolution fusion | flops 6444023808 | bytes 16783360 | tf_op jit(solution)/shard_map/dot_general | solution.py:308
  217.0 19.5 %shard_map.254 = (bf16[1024,512]{1,0:T(8,128)(2,1)S(1)}, bf16[1024,512]{1,0:T(8,128)(2,1)S(1)}, bf16[1024,512]{1,0:T(8,128)(2,1)S(1)}, bf16[1024,512]{1,0:T(8,128)(2,1)}, f32[1024,512]{1,0:T(8,128)}) custom-call(f32[1024,512]{1,0:T(8,128)} %get-tuple-element.69.q_in, f32[1024,512]{1,0:T(8,128)} %get-tuple-element.68.k_in, ...), custom_call_target="tpu_custom_call" | custom-call | flops 4294967296 | bytes 12582912 | tf_op jit(solution)/shard_map/pallas_call | solution.py:115
  240.4 31.2 %collective-permute-done.44 = bf16[256,2048]{1,0:T(8,128)(2,1)S(1)} collective-permute-done((bf16[256,2048]{1,0:T(8,128)(2,1)}, bf16[256,2048]{1,0:T(8,128)(2,1)S(1)}, u32[]{:S(2)}, u32[]{:S(2)}) %collective-permute-start.44) | collective-permute-done | bytes 1048608 | tf_op jit(solution)/shard_map/ppermute | solution.py:189
  287.1 6.6 convolution_convert_fusion.3
  302.9 25.9 %collective-permute-done.62 = bf16[2,1280,256]{2,1,0:T(8,128)(2,1)S(1)} collective-permute-done((bf16[2,1280,256]{2,1,0:T(8,128)(2,1)S(1)}, bf16[2,1280,256]{2,1,0:T(8,128)(2,1)S(1)}, u32[]{:S(2)}, u32[]{:S(2)}) %collective-permute-start.62) | collective-permute-done | bytes 1310752 | tf_op jit(solution)/shard_map/ppermute | solution.py:220
  333.3 11.8 %collective-permute-done.63 = bf16[1,1280,256]{2,1,0:T(8,128)(2,1)S(1)} collective-permute-done((bf16[1,1280,256]{2,1,0:T(8,128)(2,1)S(1)}, bf16[1,1280,256]{2,1,0:T(8,128)(2,1)S(1)}, u32[]{:S(2)}, u32[]{:S(2)}) %collective-permute-start.63) | collective-permute-done | bytes 655392 | tf_op jit(solution)/shard_map/ppermute | solution.py:220
  358.7 24.9 %collective-permute-done.17 = bf16[2560,256]{1,0:T(8,128)(2,1)} collective-permute-done((bf16[2560,256]{1,0:T(8,128)(2,1)}, bf16[2560,256]{1,0:T(8,128)(2,1)}, u32[]{:S(2)}, u32[]{:S(2)}) %collective-permute-start.17) | collective-permute-done | bytes 1310752 | tf_op jit(solution)/shard_map/ppermute | solution.py:220
  387.3 5.3 broadcast_in_dim.27
  404.4 9.1 %collective-permute-done.21 = bf16[1280,256]{1,0:T(8,128)(2,1)S(1)} collective-permute-done((bf16[1280,256]{1,0:T(8,128)(2,1)S(1)}, bf16[1280,256]{1,0:T(8,128)(2,1)S(1)}, u32[]{:S(2)}, u32[]{:S(2)}) %collective-permute-start.21) | collective-permute-done | bytes 655392 | tf_op jit(solution)/shard_map/ppermute | solution.py:220
  429.1 13.3 %fusion.12 = f32[1024,2048]{1,0:T(8,128)} fusion(bf16[1024,2048]{1,0:T(8,128)(2,1)S(1)} %copy-done.73, bf16[2560,2048]{1,0:T(8,128)(2,1)} %constant_dynamic-update-slice_fusion.33), kind=kOutput, calls=%fused_computation.19 | convolution fusion | flops 8589934592 | bytes 20971520 | tf_op jit(solution)/shard_map/dot_general | solution.py:308
  442.4 19.5 %convert_reduce_fusion = (f32[2048]{0:T(1024)S(1)}, bf16[1024,2048]{1,0:T(8,128)(2,1)}) fusion(f32[1024,2048]{1,0:T(8,128)} %get-tuple-element.118, f32[2048]{0:T(1024)S(1)} %add.488, bf16[1024,2048]{1,0:T(8,128)(2,1)S(1)} %copy-done.12, bf16[2560,2048]{1,0:T(8,128)(2,1)} %constant_dynamic-update-slice_fusion.33), kind=kOutput, calls=%fused_computation.14 | convolution fusion | flops 8638167040 | bytes 25182208 | tf_op jit(solution)/shard_map/dot_general | solution.py:67
  461.9 12.7 %fusion.65 = f32[1024,2048]{1,0:T(8,128)} fusion(bf16[1024,2048]{1,0:T(8,128)(2,1)} %get-tuple-element.121, bf16[2048,2048]{0,1:T(8,128)(2,1)S(1)} %bitcast.194), kind=kOutput, calls=%fused_computation.261 | convolution fusion | flops 8589934592 | bytes 20971520 | tf_op jit(solution)/shard_map/dot_general | solution.py:67
  474.6 26.3 %shard_map.255 = (bf16[1024,512]{1,0:T(8,128)(2,1)S(1)}, bf16[1024,512]{1,0:T(8,128)(2,1)S(1)}, bf16[1024,512]{1,0:T(8,128)(2,1)S(1)}) custom-call(bf16[1024,512]{1,0:T(8,128)(2,1)} %copy-done, bf16[1024,512]{1,0:T(8,128)(2,1)} %copy-done.1, bf16[1024,512]{1,0:T(8,128)(2,1)} %get-tuple-element.30.v_in, bf16[1024,512]{1,0:T(8,128)(2,1)} %fusion.30.grad, ...), custom_call_target="tpu_custom_call" | custom-call | flops 10737418240 | bytes 10485760 | tf_op jit(solution)/shard_map/pallas_call | solution.py:165
  505.0 6.6 convolution_convert_fusion.4
  516.7 9.8 %fusion.2 = (f32[2048]{0:T(1024)S(1)}, f32[2048]{0:T(1024)S(1)}, bf16[1024,2048]{1,0:T(8,128)(2,1)S(1)}) fusion(bf16[1024,2048]{1,0:T(8,128)(2,1)S(1)} %copy-done.9, f32[1024,2048]{1,0:T(8,128)} %fusion.65, bf16[1024,1536]{1,0:T(8,128)(2,1)S(1)} %constant_dynamic-update-slice_fusion.30, bf16[2048,1536]{0,1:T(8,128)(2,1)S(1)} %bitcast.197), kind=kOutput, calls=%fused_computation.6 | convolution fusion | flops 6455029760 | bytes 26230784 | tf_op jit(solution)/shard_map/dot_general | solution.py:67
  532.6 6.5 add_convert_fusion
  545.1 6.7 convolution_convert_fusion.5
  552.5 24.3 %all-reduce.1 = f32[8,1216]{1,0:T(8,128)S(1)} all-reduce(f32[8,1216]{1,0:T(8,128)S(1)} %pad_maximum_fusion.24), channel_id=3, replica_groups=mesh['dp'=8,'tensor'=4] {'dp'}, use_global_device_ids=true, to_apply=%region_12.13.clone | all-reduce | flops 9728 | bytes 77824
  579.0 8.1 %psum.7 = f32[3,256]{1,0:T(4,128)S(1)} all-reduce(f32[3,256]{1,0:T(4,128)S(1)} %reshape.299), channel_id=1, replica_groups=mesh['dp'=8,'tensor'=4] {'tensor'}, use_global_device_ids=true, to_apply=%region_13.14 | all-reduce | flops 768 | bytes 6144 | tf_op jit(solution)/shard_map/psum | solution.py:449
  599.6 23.5 %collective-permute-start.49 = (bf16[256,2048]{1,0:T(8,128)(2,1)S(1)}, bf16[256,2048]{1,0:T(8,128)(2,1)S(1)}, u32[]{:S(2)}, u32[]{:S(2)}) collective-permute-start(bf16[256,2048]{1,0:T(8,128)(2,1)S(1)} %get-tuple-element.87), channel_id=1, source_target_pairs={{2,1},{3,2},{6,5},{7,6},{10,9},{11,10},{14,13},{15,14},{18,17},{19... | collective-permute-start | bytes 3145736 | tf_op jit(solution)/shard_map/ppermute | solution.py:215
  626.5 19.1 %collective-permute-start.37 = (bf16[256,2048]{1,0:T(8,128)(2,1)S(1)}, bf16[256,2048]{1,0:T(8,128)(2,1)S(1)}, u32[]{:S(2)}, u32[]{:S(2)}) collective-permute-start(bf16[256,2048]{1,0:T(8,128)(2,1)S(1)} %get-tuple-element.91), channel_id=1, source_target_pairs={{2,1},{3,2},{6,5},{7,6},{10,9},{11,10},{14,13},{15,14},{18,17},{19... | collective-permute-start | bytes 3145736 | tf_op jit(solution)/shard_map/ppermute | solution.py:215
  650.7 7.1 collective-permute-done.37
  667.0 6.9 collective-permute-done.54
  694.1 9.4 %collective-permute-done.38 = bf16[256,2048]{1,0:T(8,128)(2,1)S(1)} collective-permute-done((bf16[256,2048]{1,0:T(8,128)(2,1)S(1)}, bf16[256,2048]{1,0:T(8,128)(2,1)S(1)}, u32[]{:S(2)}, u32[]{:S(2)}) %collective-permute-start.38) | collective-permute-done | bytes 1048608 | tf_op jit(solution)/shard_map/ppermute | solution.py:215
  706.5 5.3 collective-permute-done.57
  729.6 5.5 multiply_subtract_fusion
  (450 shorter events, 258.7 us)
Async XLA Ops:
  8.5 70.5 %collective-permute-start = (bf16[256,2048]{1,0:T(8,128)(2,1)}, bf16[256,2048]{1,0:T(8,128)(2,1)}, u32[]{:S(2)}, u32[]{:S(2)}) collective-permute-start(bf16[256,2048]{1,0:T(8,128)(2,1)} %get-tuple-element.53), channel_id=1, source_target_pairs={{0,1},{1,2},{2,3},{4,5},{5,6},{6,7},{8,9},{9,10},{10,11},{12,13},{... | collective-permute-start | bytes 3145736 | tf_op jit(solution)/shard_map/ppermute | solution.py:189
  9.9 70.7 %collective-permute-start.1 = (bf16[256,2048]{1,0:T(8,128)(2,1)}, bf16[256,2048]{1,0:T(8,128)(2,1)}, u32[]{:S(2)}, u32[]{:S(2)}) collective-permute-start(bf16[256,2048]{1,0:T(8,128)(2,1)} %get-tuple-element.53), channel_id=1, source_target_pairs={{1,0},{2,1},{3,2},{5,4},{6,5},{7,6},{9,8},{10,9},{11,10},{13,12},{... | collective-permute-start | bytes 3145736 | tf_op jit(solution)/shard_map/ppermute | solution.py:190
  18.1 42.8 %collective-permute-start.7 = (bf16[256,1536]{0,1:T(8,128)(2,1)}, bf16[256,1536]{0,1:T(8,128)(2,1)}, u32[]{:S(2)}, u32[]{:S(2)}) collective-permute-start(bf16[256,1536]{0,1:T(8,128)(2,1)} %bitcast.4), channel_id=1, source_target_pairs={{0,8},{4,12},{8,0},{12,4},{16,24},{20,28},{24,16},{28,20},{1,9},{5... | collective-permute-start | bytes 2359304 | tf_op jit(solution)/shard_map/ppermute | solution.py:220
  19.6 54.7 %collective-permute-start.6 = (bf16[256,1536]{0,1:T(8,128)(2,1)}, bf16[256,1536]{0,1:T(8,128)(2,1)}, u32[]{:S(2)}, u32[]{:S(2)}) collective-permute-start(bf16[256,1536]{0,1:T(8,128)(2,1)} %bitcast.4), channel_id=1, source_target_pairs={{0,4},{4,0},{8,12},{12,8},{16,20},{20,16},{24,28},{28,24},{1,5},{5... | collective-permute-start | bytes 2359304 | tf_op jit(solution)/shard_map/ppermute | solution.py:220
  19.6 54.7 %collective-permute-start.9 = (bf16[256,1536]{0,1:T(8,128)(2,1)}, bf16[256,1536]{0,1:T(8,128)(2,1)}, u32[]{:S(2)}, u32[]{:S(2)}) collective-permute-start(bf16[256,1536]{0,1:T(8,128)(2,1)} %bitcast.4), channel_id=1, source_target_pairs={{0,16},{4,20},{8,24},{12,28},{16,0},{20,4},{24,8},{28,12},{1,17},{... | collective-permute-start | bytes 2359304 | tf_op jit(solution)/shard_map/ppermute | solution.py:220
  74.3 44.8 %collective-permute-start.15 = (bf16[256,2048]{0,1:T(8,128)(2,1)S(1)}, bf16[256,2048]{0,1:T(8,128)(2,1)S(1)}, u32[]{:S(2)}, u32[]{:S(2)}) collective-permute-start(bf16[256,2048]{0,1:T(8,128)(2,1)S(1)} %bitcast.201), channel_id=1, source_target_pairs={{0,8},{4,12},{8,0},{12,4},{16,24},{20,28},{24,16},{28,20},{1,9},{5... | collective-permute-start | bytes 3145736 | tf_op jit(solution)/shard_map/ppermute | solution.py:220
  74.4 41.2 %collective-permute-start.10 = (bf16[256,1536]{0,1:T(8,128)(2,1)}, bf16[256,1536]{0,1:T(8,128)(2,1)S(1)}, u32[]{:S(2)}, u32[]{:S(2)}) collective-permute-start(bf16[256,1536]{0,1:T(8,128)(2,1)} %collective-permute-done.9), channel_id=1, source_target_pairs={{0,4},{4,0},{8,12},{12,8},{16,20},{20,16},{24,28},{28,24},{1,5},{5... | collective-permute-start | bytes 2359304 | tf_op jit(solution)/shard_map/ppermute | solution.py:220
  79.0 40.2 %collective-permute-start.27 = (bf16[256,2048]{0,1:T(8,128)(2,1)S(1)}, bf16[256,2048]{0,1:T(8,128)(2,1)S(1)}, u32[]{:S(2)}, u32[]{:S(2)}) collective-permute-start(bf16[256,2048]{0,1:T(8,128)(2,1)S(1)} %bitcast.202), channel_id=1, source_target_pairs={{0,16},{4,20},{8,24},{12,28},{16,0},{20,4},{24,8},{28,12},{1,17},{... | collective-permute-start | bytes 3145736 | tf_op jit(solution)/shard_map/ppermute | solution.py:220
  80.6 32.0 %collective-permute-start.11 = (bf16[128,1536]{0,1:T(8,128)(2,1)S(1)}, bf16[128,1536]{0,1:T(8,128)(2,1)S(1)}, u32[]{:S(2)}, u32[]{:S(2)}) collective-permute-start(bf16[128,1536]{0,1:T(8,128)(2,1)S(1)} %slice.364), channel_id=1, source_target_pairs={{0,16},{4,20},{8,24},{12,28},{16,0},{20,4},{24,8},{28,12},{1,17},{... | collective-permute-start | bytes 1179656 | tf_op jit(solution)/shard_map/ppermute | solution.py:220
  81.1 31.5 %collective-permute-start.12 = (bf16[128,1536]{0,1:T(8,128)(2,1)S(1)}, bf16[128,1536]{0,1:T(8,128)(2,1)S(1)}, u32[]{:S(2)}, u32[]{:S(2)}) collective-permute-start(bf16[128,1536]{0,1:T(8,128)(2,1)S(1)} %slice.365), channel_id=1, source_target_pairs={{0,8},{4,12},{8,0},{12,4},{16,24},{20,28},{24,16},{28,20},{1,9},{5... | collective-permute-start | bytes 1179656 | tf_op jit(solution)/shard_map/ppermute | solution.py:220
  172.8 37.4 %collective-permute-start.39 = (bf16[256,2048]{1,0:T(8,128)(2,1)S(1)}, bf16[256,2048]{1,0:T(8,128)(2,1)S(1)}, u32[]{:S(2)}, u32[]{:S(2)}) collective-permute-start(bf16[256,2048]{1,0:T(8,128)(2,1)S(1)} %copy-done.15), channel_id=1, source_target_pairs={{0,1},{1,2},{2,3},{4,5},{5,6},{6,7},{8,9},{9,10},{10,11},{12,13},{... | collective-permute-start | bytes 3145736 | tf_op jit(solution)/shard_map/ppermute | solution.py:189
  237.0 34.5 %collective-permute-start.44 = (bf16[256,2048]{1,0:T(8,128)(2,1)}, bf16[256,2048]{1,0:T(8,128)(2,1)S(1)}, u32[]{:S(2)}, u32[]{:S(2)}) collective-permute-start(bf16[256,2048]{1,0:T(8,128)(2,1)} %collective-permute-done.43), channel_id=1, source_target_pairs={{2,3},{6,7},{10,11},{14,15},{18,19},{22,23},{26,27},{30,31}} | collective-permute-start | bytes 3145736 | tf_op jit(solution)/shard_map/ppermute | solution.py:189
  298.5 30.3 %collective-permute-start.62 = (bf16[2,1280,256]{2,1,0:T(8,128)(2,1)S(1)}, bf16[2,1280,256]{2,1,0:T(8,128)(2,1)S(1)}, u32[]{:S(2)}, u32[]{:S(2)}) collective-permute-start(bf16[2,1280,256]{2,1,0:T(8,128)(2,1)S(1)} %pad_maximum_fusion.10), channel_id=1, source_target_pairs={{0,8},{4,12},{8,0},{12,4},{16,24},{20,28},{24,16},{28,20},{1,9},{5... | collective-permute-start | bytes 3932168 | tf_op jit(solution)/shard_map/ppermute | solution.py:220
  300.5 30.7 %collective-permute-start.64 = (bf16[2,1280,256]{2,1,0:T(8,128)(2,1)S(1)}, bf16[2,1280,256]{2,1,0:T(8,128)(2,1)S(1)}, u32[]{:S(2)}, u32[]{:S(2)}) collective-permute-start(bf16[2,1280,256]{2,1,0:T(8,128)(2,1)S(1)} %pad_maximum_fusion.11), channel_id=1, source_target_pairs={{0,16},{4,20},{8,24},{12,28},{16,0},{20,4},{24,8},{28,12},{1,17},{... | collective-permute-start | bytes 3932168 | tf_op jit(solution)/shard_map/ppermute | solution.py:220
  354.9 28.6 %collective-permute-start.17 = (bf16[2560,256]{1,0:T(8,128)(2,1)}, bf16[2560,256]{1,0:T(8,128)(2,1)}, u32[]{:S(2)}, u32[]{:S(2)}) collective-permute-start(bf16[2560,256]{1,0:T(8,128)(2,1)} %bitcast.9), channel_id=1, source_target_pairs={{0,8},{4,12},{8,0},{12,4},{16,24},{20,28},{24,16},{28,20},{1,9},{5... | collective-permute-start | bytes 3932168 | tf_op jit(solution)/shard_map/ppermute | solution.py:220
  356.4 40.8 %collective-permute-start.19 = (bf16[2560,256]{1,0:T(8,128)(2,1)}, bf16[2560,256]{1,0:T(8,128)(2,1)}, u32[]{:S(2)}, u32[]{:S(2)}) collective-permute-start(bf16[2560,256]{1,0:T(8,128)(2,1)} %bitcast.9), channel_id=1, source_target_pairs={{0,16},{4,20},{8,24},{12,28},{16,0},{20,4},{24,8},{28,12},{1,17},{... | collective-permute-start | bytes 3932168 | tf_op jit(solution)/shard_map/ppermute | solution.py:220
  356.7 42.5 %collective-permute-start.16 = (bf16[2560,256]{1,0:T(8,128)(2,1)}, bf16[2560,256]{1,0:T(8,128)(2,1)}, u32[]{:S(2)}, u32[]{:S(2)}) collective-permute-start(bf16[2560,256]{1,0:T(8,128)(2,1)} %bitcast.9), channel_id=1, source_target_pairs={{0,4},{4,0},{8,12},{12,8},{16,20},{20,16},{24,28},{28,24},{1,5},{5... | collective-permute-start | bytes 3932168 | tf_op jit(solution)/shard_map/ppermute | solution.py:220
  383.6 31.7 %collective-permute-start.18 = (bf16[2560,256]{1,0:T(8,128)(2,1)}, bf16[2560,256]{1,0:T(8,128)(2,1)S(1)}, u32[]{:S(2)}, u32[]{:S(2)}) collective-permute-start(bf16[2560,256]{1,0:T(8,128)(2,1)} %collective-permute-done.17), channel_id=1, source_target_pairs={{0,4},{4,0},{8,12},{12,8},{16,20},{20,16},{24,28},{28,24},{1,5},{5... | collective-permute-start | bytes 3932168 | tf_op jit(solution)/shard_map/ppermute | solution.py:220
  528.2 59.5 %collective-permute-start.45 = (bf16[256,2048]{1,0:T(8,128)(2,1)}, bf16[256,2048]{1,0:T(8,128)(2,1)}, u32[]{:S(2)}, u32[]{:S(2)}) collective-permute-start(bf16[256,2048]{1,0:T(8,128)(2,1)} %get-tuple-element.88), channel_id=1, source_target_pairs={{0,1},{4,5},{8,9},{12,13},{16,17},{20,21},{24,25},{28,29}} | collective-permute-start | bytes 3145736 | tf_op jit(solution)/shard_map/ppermute | solution.py:214
  530.1 67.2 %collective-permute-start.48 = (bf16[256,2048]{1,0:T(8,128)(2,1)}, bf16[256,2048]{1,0:T(8,128)(2,1)}, u32[]{:S(2)}, u32[]{:S(2)}) collective-permute-start(bf16[256,2048]{1,0:T(8,128)(2,1)} %get-tuple-element.89), channel_id=1, source_target_pairs={{3,2},{7,6},{11,10},{15,14},{19,18},{23,22},{27,26},{31,30}} | collective-permute-start | bytes 3145736 | tf_op jit(solution)/shard_map/ppermute | solution.py:215
  540.7 49.7 %collective-permute-start.33 = (bf16[256,2048]{1,0:T(8,128)(2,1)}, bf16[256,2048]{1,0:T(8,128)(2,1)}, u32[]{:S(2)}, u32[]{:S(2)}) collective-permute-start(bf16[256,2048]{1,0:T(8,128)(2,1)} %get-tuple-element.92), channel_id=1, source_target_pairs={{0,1},{4,5},{8,9},{12,13},{16,17},{20,21},{24,25},{28,29}} | collective-permute-start | bytes 3145736 | tf_op jit(solution)/shard_map/ppermute | solution.py:214
  542.4 80.7 %collective-permute-start.36 = (bf16[256,2048]{1,0:T(8,128)(2,1)}, bf16[256,2048]{1,0:T(8,128)(2,1)}, u32[]{:S(2)}, u32[]{:S(2)}) collective-permute-start(bf16[256,2048]{1,0:T(8,128)(2,1)} %get-tuple-element.93), channel_id=1, source_target_pairs={{3,2},{7,6},{11,10},{15,14},{19,18},{23,22},{27,26},{31,30}} | collective-permute-start | bytes 3145736 | tf_op jit(solution)/shard_map/ppermute | solution.py:215
  544.7 100.9 %collective-permute-start.51 = (bf16[4,256,1536]{2,1,0:T(8,128)(2,1)}, bf16[4,256,1536]{2,1,0:T(8,128)(2,1)}, u32[]{:S(2)}, u32[]{:S(2)}) collective-permute-start(bf16[4,256,1536]{2,1,0:T(8,128)(2,1)} %bitcast.11), channel_id=1, source_target_pairs={{0,4},{4,0},{8,12},{12,8},{16,20},{20,16},{24,28},{28,24},{1,5},{5... | collective-permute-start | bytes 9437192 | tf_op jit(solution)/shard_map/ppermute | solution.py:220
  592.4 32.0 %collective-permute-start.34 = (bf16[256,2048]{1,0:T(8,128)(2,1)S(1)}, bf16[256,2048]{1,0:T(8,128)(2,1)S(1)}, u32[]{:S(2)}, u32[]{:S(2)}) collective-permute-start(bf16[256,2048]{1,0:T(8,128)(2,1)S(1)} %add_convert_fusion.12), channel_id=1, source_target_pairs={{0,1},{1,2},{4,5},{5,6},{8,9},{9,10},{12,13},{13,14},{16,17},{17,1... | collective-permute-start | bytes 3145736 | tf_op jit(solution)/shard_map/ppermute | solution.py:214
  597.3 81.2 %collective-permute-start.56 = (bf16[4,256,2048]{2,1,0:T(8,128)(2,1)S(1)}, bf16[4,256,2048]{2,1,0:T(8,128)(2,1)S(1)}, u32[]{:S(2)}, u32[]{:S(2)}) collective-permute-start(bf16[4,256,2048]{2,1,0:T(8,128)(2,1)S(1)} %bitcast.217), channel_id=1, source_target_pairs={{0,4},{4,0},{8,12},{12,8},{16,20},{20,16},{24,28},{28,24},{1,5},{5... | collective-permute-start | bytes 12582920 | tf_op jit(solution)/shard_map/ppermute | solution.py:220
  599.6 50.6 %collective-permute-start.49 = (bf16[256,2048]{1,0:T(8,128)(2,1)S(1)}, bf16[256,2048]{1,0:T(8,128)(2,1)S(1)}, u32[]{:S(2)}, u32[]{:S(2)}) collective-permute-start(bf16[256,2048]{1,0:T(8,128)(2,1)S(1)} %get-tuple-element.87), channel_id=1, source_target_pairs={{2,1},{3,2},{6,5},{7,6},{10,9},{11,10},{14,13},{15,14},{18,17},{19... | collective-permute-start | bytes 3145736 | tf_op jit(solution)/shard_map/ppermute | solution.py:215
  623.1 58.9 %collective-permute-start.47 = (bf16[256,2048]{1,0:T(8,128)(2,1)S(1)}, bf16[256,2048]{1,0:T(8,128)(2,1)S(1)}, u32[]{:S(2)}, u32[]{:S(2)}) collective-permute-start(bf16[256,2048]{1,0:T(8,128)(2,1)S(1)} %get-tuple-element.86), channel_id=1, source_target_pairs={{0,1},{1,2},{2,3},{4,5},{5,6},{6,7},{8,9},{9,10},{10,11},{12,13},{... | collective-permute-start | bytes 3145736 | tf_op jit(solution)/shard_map/ppermute | solution.py:214
  626.5 31.3 %collective-permute-start.37 = (bf16[256,2048]{1,0:T(8,128)(2,1)S(1)}, bf16[256,2048]{1,0:T(8,128)(2,1)S(1)}, u32[]{:S(2)}, u32[]{:S(2)}) collective-permute-start(bf16[256,2048]{1,0:T(8,128)(2,1)S(1)} %get-tuple-element.91), channel_id=1, source_target_pairs={{2,1},{3,2},{6,5},{7,6},{10,9},{11,10},{14,13},{15,14},{18,17},{19... | collective-permute-start | bytes 3145736 | tf_op jit(solution)/shard_map/ppermute | solution.py:215
  645.6 47.8 %collective-permute-start.35 = (bf16[256,2048]{1,0:T(8,128)(2,1)S(1)}, bf16[256,2048]{1,0:T(8,128)(2,1)S(1)}, u32[]{:S(2)}, u32[]{:S(2)}) collective-permute-start(bf16[256,2048]{1,0:T(8,128)(2,1)S(1)} %get-tuple-element.90), channel_id=1, source_target_pairs={{0,1},{1,2},{2,3},{4,5},{5,6},{6,7},{8,9},{9,10},{10,11},{12,13},{... | collective-permute-start | bytes 3145736 | tf_op jit(solution)/shard_map/ppermute | solution.py:214
  673.9 29.6 %collective-permute-start.38 = (bf16[256,2048]{1,0:T(8,128)(2,1)S(1)}, bf16[256,2048]{1,0:T(8,128)(2,1)S(1)}, u32[]{:S(2)}, u32[]{:S(2)}) collective-permute-start(bf16[256,2048]{1,0:T(8,128)(2,1)S(1)} %add_convert_fusion.9), channel_id=1, source_target_pairs={{1,0},{2,1},{3,2},{5,4},{6,5},{7,6},{9,8},{10,9},{11,10},{13,12},{... | collective-permute-start | bytes 3145736 | tf_op jit(solution)/shard_map/ppermute | solution.py:215
  678.5 37.6 %collective-permute-start.53 = (bf16[1,128,1536]{2,1,0:T(8,128)(2,1)S(1)}, bf16[1,128,1536]{2,1,0:T(8,128)(2,1)S(1)}, u32[]{:S(2)}, u32[]{:S(2)}) collective-permute-start(bf16[1,128,1536]{2,1,0:T(8,128)(2,1)S(1)} %fusion.43), channel_id=1, source_target_pairs={{0,16},{4,20},{8,24},{12,28},{16,0},{20,4},{24,8},{28,12},{1,17},{... | collective-permute-start | bytes 1179656 | tf_op jit(solution)/shard_map/ppermute | solution.py:220
  682.0 34.2 %collective-permute-start.55 = (bf16[1,128,1536]{2,1,0:T(8,128)(2,1)S(1)}, bf16[1,128,1536]{2,1,0:T(8,128)(2,1)S(1)}, u32[]{:S(2)}, u32[]{:S(2)}) collective-permute-start(bf16[1,128,1536]{2,1,0:T(8,128)(2,1)S(1)} %fusion.44), channel_id=1, source_target_pairs={{0,8},{4,12},{8,0},{12,4},{16,24},{20,28},{24,16},{28,20},{1,9},{5... | collective-permute-start | bytes 1179656 | tf_op jit(solution)/shard_map/ppermute | solution.py:220
  (112 other events, 2175.2 us)

commit v2 on v1

--- a/solution.py
+++ b/solution.py
@@ -80,50 +80,6 @@
     return x * own + sign * (
         pltpu.roll(x, LANES - half, 1) * ahead + pltpu.roll(x, half, 1) * behind
     )
-
-
-def attend_forward_kernel(q_in, k_in, v_in, own, ahead, behind, begin, out, q_out, k_out, v_out, lse):
-    total = q_in.shape[0]
-    rows = min(QUERY_ROWS, total)
-    q_out[...] = turn(q_in[...], own[...], ahead[...], behind[...], 1.0).astype(bf16)
-    k_out[...] = turn(k_in[...], own[...], ahead[...], behind[...], 1.0).astype(bf16)
-    v_out[...] = v_in[...].astype(bf16)
-    for start in range(0, total, rows):
-        stop = start + rows
-        place = pl.ds(start, rows)
-        allowed = attend_mask(begin[place, :], start, rows, stop)
-        query = q_out[place, :]
-        results, sums = [], []
-        for head in range(LANES // HEAD):
-            mine = head_lanes(rows, head)
-            chosen = jnp.where(mine, query, jnp.zeros_like(query)) * HEAD ** (-0.5)
-            scores = jnp.where(allowed, dot_t(chosen.astype(bf16), k_out[:stop, :]), masked_score)
-            top = jnp.max(scores, axis=1, keepdims=True)
-            weights = jnp.exp(scores - top)
-            total_weight = jnp.sum(weights, axis=1, keepdims=True)
-            results.append(dot_n(weights.astype(bf16), v_out[:stop, :]) / total_weight)
-            sums.append(top + jnp.log(total_weight))
-        first = head_lanes(rows, 0)
-        out[place, :] = jnp.where(first, results[0], results[1]).astype(bf16)
-        lse[place, :] = jnp.where(first, sums[0], sums[1])
-
-
-def attend_forward(q, k, v, tables, begin):
-    total, width = q.shape
-    tile = pl.BlockSpec((total, LANES), lambda p: (0, p))
-    fixed = pl.BlockSpec((total, LANES), lambda p: (0, 0))
-    return pl.pallas_call(
-        attend_forward_kernel,
-        grid=(width // LANES,),
-        in_specs=[tile] * 3 + [fixed] * 3 + [pl.BlockSpec((total, 1), lambda p: (0, 0))],
-        out_specs=[tile] * 5,
-        out_shape=[jax.ShapeDtypeStruct((total, width), bf16)] * 4
-        + [jax.ShapeDtypeStruct((total, width), f32)],
-        compiler_params=pltpu.CompilerParams(vmem_limit_bytes=48 << 20),
-        cost_estimate=pl.CostEstimate(
-            flops=8 * total * total * width, bytes_accessed=24 * total * width, transcendentals=0
-        ),
-    )(q, k, v, *tables, begin)
 
 
 def attend_backward_kernel(q_in, k_in, v_in, grad, lse, own, ahead, behind, begin, dq, dk, dv, k_sum, v_sum):
@@ -176,23 +132,414 @@
     )(q, k, v, grad, lse, *tables, begin)
 
 
+def low_bit(mask):
+    return mask & -mask
+
+
+def high_bit(mask):
+    return 1 << (mask.bit_length() - 1)
+
+
+def gelu_and_slope(a):
+    root = (2.0 / 3.141592653589793) ** 0.5
+    square = a * a
+    t = jnp.tanh(root * a * (1.0 + 0.044715 * square))
+    half = 0.5 * (1.0 + t)
+    return a * half, half + 0.5 * a * (1.0 - t * t) * (root * (1.0 + 3.0 * 0.044715 * square))
+
+
+class Plan:
+    def __init__(self, n_dp, n_line, rows, model, in_rows, local, n_mlp, out_cols):
+        self.n_dp, self.n_line = n_dp, n_line
+        self.rows, self.model = rows, model
+        self.group = rows * n_line
+        self.in_rows, self.local, self.n_mlp, self.out_cols = in_rows, local, n_mlp, out_cols
+        self.attn, self.mlp = 3 * local, n_mlp * local
+        self.down = (1 + n_mlp) * local
+        self.bias_cols = local // n_dp
+        self.bits = [1 << b for b in range(1, n_dp.bit_length() - 1)]
+        even = range(2, n_dp, 2)
+        self.single = [m for m in even if m.bit_count() == 1]
+        self.several = sorted((m for m in even if m.bit_count() > 1), key=lambda m: m.bit_count())
+        self.odd = list(range(1, n_dp, 2))
+
+    def hop(self, mask, half):
+        if mask & 1:
+            return 1
+        return high_bit(mask) if half == 0 else low_bit(mask)
+
+    def onward(self, mask, half):
+        if mask & 1:
+            return []
+        masks = [mask | 1] if self.n_dp > 1 else []
+        return masks + [
+            mask | b for b in self.bits if not mask & b and self.hop(mask | b, half) == b
+        ]
+
+
+def forward_kernel(
+    plan,
+    xhat_in, cot_in, wa_in, wm_in, wd_in, small_in, own, ahead, behind, begin,
+    wa_out, wm_out, wd_out, xhat_out, normed_out, cot_out, q_out, k_out, v_out, att_out, lse_out,
+    hidden_out, da_out, do_out, part_out,
+    wa, wm, wd, small, xs, ns, cs, q, k, v, att, lse, hidden, slope, do,
+    own_sem, out_sem, w_send, w_recv, up_send, up_recv, down_send, down_recv,
+):
+    n, line = plan.n_dp, plan.n_line
+    me, place = lax.axis_index("dp"), lax.axis_index("tensor")
+    rows, local = plan.rows, plan.local
+
+    def owner(mask):
+        index = me
+        for b in [1] + plan.bits:
+            if mask & b:
+                index = index + b - 2 * b * lax.rem(index // b, 2)
+        return index
+
+    def slot(flow, index, half):
+        if flow < 2:
+            step = plan.in_rows // 2
+            at = pl.multiple_of(index * plan.in_rows + half * step, step)
+            return (wa, wm)[flow].at[pl.ds(at, step), :]
+        if flow == 2:
+            step = plan.down // 2
+            at = pl.multiple_of(index * plan.out_cols, plan.out_cols)
+            return wd.at[pl.ds(half * step, step), pl.ds(at, plan.out_cols)]
+        return small.at[index]
+
+    def halves(flow):
+        return (0,) if flow == 3 else (0, 1)
+
+    def w_copy(flow, mask, half):
+        hop = plan.hop(mask, half)
+        piece = slot(flow, owner(mask ^ hop), half)
+        at = flow * 2 * n + 2 * mask + half
+        return pltpu.make_async_remote_copy(
+            src_ref=piece, dst_ref=piece, send_sem=w_send.at[at], recv_sem=w_recv.at[at],
+            device_id={"dp": owner(hop)}, device_id_type=pl.DeviceIdType.MESH,
+        )
+
+    def w_start(flow, mask=0):
+        for half in halves(flow):
+            for target in plan.onward(mask, half):
+                w_copy(flow, target, half).start()
+
+    def w_arrive(flow, masks):
+        for mask in masks:
+            for half in halves(flow):
+                piece = slot(flow, owner(mask), half)
+                at = flow * 2 * n + 2 * mask + half
+                pltpu.make_async_remote_copy(
+                    src_ref=piece, dst_ref=piece, send_sem=w_send.at[at], recv_sem=w_recv.at[at],
+                    device_id={"dp": owner(plan.hop(mask, half))}, device_id_type=pl.DeviceIdType.MESH,
+                ).wait_recv()
+                for target in plan.onward(mask, half):
+                    w_copy(flow, target, half).start()
+
+    def chunk(flow, index):
+        return (xs, cs)[flow].at[pl.ds(pl.multiple_of(index * rows, rows), rows), :]
+
+    def z_copy(flow, step, up):
+        piece = chunk(flow, place - (step - 1) if up else place + (step - 1))
+        at = flow * line + step
+        return pltpu.make_async_remote_copy(
+            src_ref=piece, dst_ref=piece,
+            send_sem=(up_send if up else down_send).at[at],
+            recv_sem=(up_recv if up else down_recv).at[at],
+            device_id={"tensor": place + 1 if up else place - 1}, device_id_type=pl.DeviceIdType.MESH,
+        )
+
+    def sends(step, up):
+        if up:
+            return (place < line - 1) & (place >= step - 1)
+        return (place > 0) & (place + step - 1 <= line - 1)
+
+    def z_start(flow, step):
+        for up in (True, False):
+            @pl.when(sends(step, up))
+            def _():
+                z_copy(flow, step, up).start()
+
+    def z_arrive(flow, step):
+        for up in (True, False):
+            @pl.when(place >= step if up else place + step <= line - 1)
+            def _():
+                piece = chunk(flow, place - step if up else place + step)
+                at = flow * line + step
+                pltpu.make_async_remote_copy(
+                    src_ref=piece, dst_ref=piece,
+                    send_sem=(up_send if up else down_send).at[at],
+                    recv_sem=(up_recv if up else down_recv).at[at],
+                    device_id={"tensor": place - 1 if up else place + 1},
+                    device_id_type=pl.DeviceIdType.MESH,
+                ).wait_recv()
+        if step + 1 < line:
+            z_start(flow, step + 1)
+
+    def z_sent(flow, step, up):
+        @pl.when(sends(step, up))
+        def _():
+            z_copy(flow, step, up).wait_send()
+
+    def cot_start(step):
+        for up in (True, False):
+            last = place == step - 1 if up else place == line - step
+            @pl.when(last & sends(1, up))
+            def _():
+                z_copy(0, step, up).wait_send()
+                z_copy(1, 1, up).start()
+
+    def at_distance(step, fn):
+        if step == 0:
+            fn(place)
+            return
+
+        def side(j, carry):
+            index = place - step + 2 * step * j
+
+            @pl.when((index >= 0) & (index < line))
+            def _():
+                fn(index)
+            return carry
+
+        lax.fori_loop(0, 2, side, 0)
+
+    def span(index):
+        return pl.ds(pl.multiple_of(index * rows, rows), rows)
+
+    outs = [
+        (wa, wa_out), (wm, wm_out), (wd, wd_out), (xs, xhat_out), (ns, normed_out), (cs, cot_out),
+        (q, q_out), (k, k_out), (v, v_out), (att, att_out), (lse, lse_out), (hidden, hidden_out),
+        (slope, da_out), (do, do_out), (xs, part_out),
+    ]
+
+    def out_copy(j):
+        return pltpu.make_async_copy(outs[j][0], outs[j][1], out_sem.at[j])
+
+    def write(*which):
+        for j in which:
+            out_copy(j).start()
+
+    loads = [
+        pltpu.make_async_copy(xhat_in, chunk(0, place), own_sem.at[0]),
+        pltpu.make_async_copy(wa_in, wa.at[pl.ds(pl.multiple_of(me * plan.in_rows, plan.in_rows), plan.in_rows), :], own_sem.at[1]),
+        pltpu.make_async_copy(small_in, small.at[me], own_sem.at[2]),
+        pltpu.make_async_copy(wm_in, wm.at[pl.ds(pl.multiple_of(me * plan.in_rows, plan.in_rows), plan.in_rows), :], own_sem.at[3]),
+        pltpu.make_async_copy(wd_in, wd.at[:, pl.ds(pl.multiple_of(me * plan.out_cols, plan.out_cols), plan.out_cols)], own_sem.at[4]),
+        pltpu.make_async_copy(cot_in, chunk(1, place), own_sem.at[5]),
+    ]
+    for load in loads:
+        load.start()
+    barrier = pltpu.get_barrier_semaphore()
+    for b in [1] + plan.bits if n > 1 else []:
+        pl.semaphore_signal(barrier, inc=1, device_id={"dp": owner(b)}, device_id_type=pl.DeviceIdType.MESH)
+
+    @pl.when(place < line - 1)
+    def _():
+        pl.semaphore_signal(barrier, inc=1, device_id={"tensor": place + 1}, device_id_type=pl.DeviceIdType.MESH)
+
+    @pl.when(place > 0)
+    def _():
+        pl.semaphore_signal(barrier, inc=1, device_id={"tensor": place - 1}, device_id_type=pl.DeviceIdType.MESH)
+
+    beside = (place + line - 1) // line + (2 * line - 2 - place) // line
+    pl.semaphore_wait(barrier, (1 + len(plan.bits) if n > 1 else 0) + beside)
+
+    def normalize_rows(index):
+        at = span(index)
+        gain = jnp.concatenate([small[o, 0:1, LANES:] for o in range(n)], axis=1).astype(f32)
+        shift = jnp.concatenate([small[o, 1:2, LANES:] for o in range(n)], axis=1).astype(f32)
+        ns[at, :] = (xs[at, :].astype(f32) * gain + shift).astype(bf16)
+
+    def bias_row(r, first, width):
+        per = LANES // plan.bias_cols
+        groups = []
+        for g in range(first // LANES, (first + width) // LANES):
+            total = small[g * per, r : r + 1, :LANES].astype(f32)
+            for o in range(1, per):
+                total = total + small[g * per + o, r : r + 1, :LANES].astype(f32)
+            groups.append(total)
+        return jnp.concatenate(groups, axis=1)
+
+    def attn_rows(index):
+        at = span(index)
+        normalize_rows(index)
+        for r, target in enumerate((q, k, v)):
+            proj = dot_n(ns[at, :], wa[:, r * local : (r + 1) * local]) + bias_row(r, 0, local)
+            if r == 2:
+                target[at, :] = proj.astype(bf16)
+            else:
+                for g in range(0, local, LANES):
+                    target[at, g : g + LANES] = turn(
+                        proj[:, g : g + LANES], own[at, :], ahead[at, :], behind[at, :], 1.0
+                    ).astype(bf16)
+
+    def mlp_rows(index):
+        at = span(index)
+        for r in range(plan.n_mlp):
+            cols = slice(r * local, (r + 1) * local)
+            pre = dot_n(ns[at, :], wm[:, cols]) + bias_row(3 + r, 0, local)
+            value, grad = gelu_and_slope(pre)
+            hidden[at, cols] = value.astype(bf16)
+            slope[at, cols] = grad.astype(bf16)
+
+    def attend(pair, carry):
+        total = plan.group
+        block = min(QUERY_ROWS, total)
+        lanes = pl.ds(pl.multiple_of(pair * LANES, LANES), LANES)
+        for start in range(0, total, block):
+            stop = start + block
+            here = pl.ds(start, block)
+            allowed = attend_mask(begin[here, :], start, block, stop)
+            query = q[here, lanes]
+            results, sums = [], []
+            for head in range(LANES // HEAD):
+                mine = head_lanes(block, head)
+                chosen = jnp.where(mine, query, jnp.zeros_like(query)) * HEAD ** (-0.5)
+                scores = jnp.where(allowed, dot_t(chosen.astype(bf16), k[:stop, lanes]), masked_score)
+                top = jnp.max(scores, axis=1, keepdims=True)
+                weights = jnp.exp(scores - top)
+                total_weight = jnp.sum(weights, axis=1, keepdims=True)
+                results.append(dot_n(weights.astype(bf16), v[:stop, lanes]) / total_weight)
+                sums.append(top + jnp.log(total_weight))
+            first = head_lanes(block, 0)
+            att[here, lanes] = jnp.where(first, results[0], results[1]).astype(bf16)
+            lse[here, lanes] = jnp.where(first, sums[0], sums[1])
+        return carry
+
+    tile = min(512, plan.model)
+    tall = min(512, plan.group)
+
+    def out_tile(j, carry):
+        cols = pl.ds(pl.multiple_of(lax.rem(j, plan.model // tile) * tile, tile), tile)
+        at = pl.ds(pl.multiple_of((j // (plan.model // tile)) * tall, tall), tall)
+        total = dot_n(att[at, :], wd[:local, cols]) + dot_n(hidden[at, :], wd[local:, cols])
+        xs[at, cols] = total.astype(bf16)
+        return carry
+
+    def back_rows(index):
+        at = span(index)
+        do[at, :] = dot_t(cs[at, :], wd[:local, :]).astype(bf16)
+        for r in range(plan.n_mlp):
+            cols = slice(r * local, (r + 1) * local)
+            grad = dot_t(cs[at, :], wd[(1 + r) * local : (2 + r) * local, :])
+            slope[at, cols] = (grad * slope[at, cols].astype(f32)).astype(bf16)
+
+    loads[0].wait()
+    z_start(0, 1)
+    loads[2].wait()
+    w_start(3)
+    loads[1].wait()
+    w_start(0)
+    loads[3].wait()
+    loads[4].wait()
+    loads[5].wait()
+    w_arrive(0, plan.single)
+    w_start(1)
+    w_arrive(3, plan.single)
+    if line > 1:
+        z_arrive(0, 1)
+        cot_start(1)
+    w_arrive(3, plan.several)
+    w_arrive(0, plan.several)
+    w_arrive(3, plan.odd)
+    w_arrive(0, plan.odd)
+    write(0)
+    at_distance(0, attn_rows)
+    if line > 2:
+        at_distance(1, attn_rows)
+    w_arrive(1, plan.single)
+    w_start(2)
+    for step in range(2, line - 1):
+        z_arrive(0, step)
+        cot_start(step)
+        at_distance(step, attn_rows)
+    w_arrive(1, plan.several)
+    w_arrive(1, plan.odd)
+    write(1)
+    near = max(line - 2, 0)
+    lax.fori_loop(
+        jnp.maximum(place - near, 0), jnp.minimum(place + near, line - 1) + 1,
+        lambda c, carry: (mlp_rows(c), carry)[1], 0,
+    )
+    if line > 1:
+        if line > 2:
+            z_arrive(0, line - 1)
+            cot_start(line - 1)
+        at_distance(line - 1, lambda c: (attn_rows(c), mlp_rows(c))[0])
+    write(3, 4, 6, 7, 8, 11)
+    pairs = local // LANES
+    lax.fori_loop(0, pairs // 2, attend, 0)
+    w_arrive(2, plan.single)
+    lax.fori_loop(pairs // 2, pairs, attend, 0)
+    write(9, 10)
+    if line > 1:
+        z_arrive(1, 1)
+    w_arrive(2, plan.several)
+    w_arrive(2, plan.odd)
+    write(2)
+    out_copy(3).wait()
+    for step in range(1, line):
+        for up in (True, False):
+            left = place != step - 1 if up else place != line - step
+            @pl.when(left & sends(step, up))
+            def _():
+                z_copy(0, step, up).wait_send()
+    lax.fori_loop(0, (plan.model // tile) * (plan.group // tall), out_tile, 0)
+    write(14)
+    at_distance(0, back_rows)
+    if line > 1:
+        at_distance(1, back_rows)
+    for step in range(2, line):
+        z_arrive(1, step)
+        at_distance(step, back_rows)
+    write(5, 12, 13)
+
+    for flow in range(4):
+        for mask in range(1, n):
+            for half in halves(flow):
+                w_copy(flow, mask, half).wait_send()
+    for step in range(1, line):
+        for up in (True, False):
+            z_sent(1, step, up)
+    for j in range(len(outs)):
+        if j != 3:
+            out_copy(j).wait()
+
+
+def forward(plan, xhat, cot, wa, wm, wd, small, tables, begin):
+    any_space = pl.BlockSpec(memory_space=pl.ANY)
+    vmem = pl.BlockSpec(memory_space=pltpu.VMEM)
+    n, line, group, model, local = plan.n_dp, plan.n_line, plan.group, plan.model, plan.local
+    low = lambda *shape: jax.ShapeDtypeStruct(shape, bf16)
+    out_shape = [
+        low(model, plan.attn), low(model, plan.mlp), low(plan.down, model),
+        low(group, model), low(group, model), low(group, model),
+        low(group, local), low(group, local), low(group, local), low(group, local),
+        jax.ShapeDtypeStruct((group, local), f32),
+        low(group, plan.mlp), low(group, plan.mlp), low(group, local), low(group, model),
+    ]
+    scratch = lambda s: pltpu.VMEM(s.shape, s.dtype)
+    dma = pltpu.SemaphoreType.DMA
+    return pl.pallas_call(
+        partial(forward_kernel, plan),
+        in_specs=[any_space] * 6 + [vmem] * 4,
+        out_specs=[any_space] * 15,
+        out_shape=out_shape,
+        scratch_shapes=[scratch(s) for s in out_shape[:3]]
+        + [pltpu.VMEM((n, 16, LANES + plan.out_cols), bf16)]
+        + [scratch(s) for s in out_shape[3:14]]
+        + [dma((6,)), dma((15,)), dma((8 * n,)), dma((8 * n,))]
+        + [dma((2 * line,))] * 4,
+        compiler_params=pltpu.CompilerParams(
+            collective_id=0, has_side_effects=True, vmem_limit_bytes=63 << 20
+        ),
+        cost_estimate=pl.CostEstimate(flops=60 * 10**9, bytes_accessed=80 << 20, transcendentals=0),
+    )(xhat, cot, wa, wm, wd, small, *tables, begin)
+
+
 def after(value, *others):
     return lax.optimization_barrier((value,) + others)[0]
-
-
-def line_gather(own, axis):
-    n = lax.axis_size(axis)
-    me = lax.axis_index(axis)
-    rows = own.shape[0]
-    up, down = [own], [own]
-    for step in range(1, n):
-        up.append(lax.ppermute(up[-1], axis, [(j, j + 1) for j in range(step - 1, n - 1)]))
-        down.append(lax.ppermute(down[-1], axis, [(j, j - 1) for j in range(1, n - step + 1)]))
-    full = jnp.zeros((n * rows,) + own.shape[1:], own.dtype)
-    for step in range(n):
-        part = own if step == 0 else jnp.where(me >= step, up[step], down[n - step])
-        full = lax.dynamic_update_slice_in_dim(full, part, lax.rem(me - step + n, n) * rows, 0)
-    return full, (up[-1], down[-1])
 
 
 def line_scatter(partials, axis):
@@ -218,57 +565,6 @@
 
 def flip(value, axis, bit):
     return lax.ppermute(value, axis, [(j, j ^ bit) for j in range(lax.axis_size(axis))])
-
-
-def low_bit(mask):
-    return mask & -mask
-
-
-def high_bit(mask):
-    return 1 << (mask.bit_length() - 1)
-
-
-def cube_gather(own, axis):
-    n = lax.axis_size(axis)
-    half = own.shape[0] // 2
-    whole = {0: own}
-    parts = {0: (own[:half], own[half:])}
-    for mask in sorted(range(2, n, 2), key=lambda m: m.bit_count()):
-        if mask.bit_count() == 1:
-            whole[mask] = flip(own, axis, mask)
-            parts[mask] = (whole[mask][:half], whole[mask][half:])
-        else:
-            last, other = high_bit(mask), low_bit(mask)
-            parts[mask] = (
-                flip(parts[mask ^ last][0], axis, last),
-                flip(parts[mask ^ other][1], axis, other),
-            )
-    if n > 1:
-        for mask in range(0, n, 2):
-            if mask in whole:
-                whole[mask | 1] = flip(whole[mask], axis, 1)
-            else:
-                parts[mask | 1] = tuple(flip(p, axis, 1) for p in parts[mask])
-    return whole, parts
-
-
-def cube_assemble(gathered, axis, dim):
-    whole, parts = gathered
-    n = lax.axis_size(axis)
-    me = lax.axis_index(axis)
-    shape = list(whole[0].shape)
-    step, half = shape[dim], shape[0] // 2
-    shape[dim] *= n
-    full = jnp.zeros(shape, whole[0].dtype)
-    for mask in range(n):
-        owner = jnp.bitwise_xor(me, mask)
-        pieces = [(0, whole[mask])] if mask in whole else [(0, parts[mask][0]), (half, parts[mask][1])]
-        for row, piece in pieces:
-            start = [0] * len(shape)
-            start[0] = row
-            start[dim] = start[dim] + owner * step
-            full = lax.dynamic_update_slice(full, piece, start)
-    return full
 
 
 def cube_scatter(send, keep, axis):
@@ -357,55 +653,24 @@
     cot_live = out_grad * own_live[:, None]
     cot_low = cot_live.astype(bf16)
 
-    xhat_all, xhat_last = line_gather(xhat.astype(bf16), "tensor")
-    attn_pieces = cube_gather(in_attn, "dp")
-    in_mlp = after(in_mlp, attn_pieces[0][min(2, n_dp - 1)])
-    mlp_pieces = cube_gather(in_mlp, "dp")
-    small = lax.all_gather(
-        jnp.concatenate([column_bias.astype(bf16).reshape(-1), vector_params.astype(bf16).reshape(-1)]),
-        "dp",
-        axis=0,
-    )
+    me = lax.axis_index("dp")
+    plan = Plan(n_dp, n_tensor, own_rows, model, in_rows, local, n_mlp, out_cols)
     n_bias = column_bias.size
-    bias_vals = (
-        small[:, :n_bias].reshape((n_dp,) + column_bias.shape).transpose(1, 0, 2).reshape(widths, local)
-    ).astype(f32)
-    vector_vals = (
-        small[:, n_bias:].reshape((n_dp,) + vector_params.shape).transpose(1, 0, 2).reshape(3, model)
-    ).astype(f32)
-    gain, shift, out_bias = vector_vals[0], vector_vals[1], vector_vals[2]
-
-    cot_low = after(cot_low, *xhat_last)
-    cot_all, _ = line_gather(cot_low, "tensor")
-    down_low = after(down_low, mlp_pieces[0][min(2, n_dp - 1)])
-    down_pieces = cube_gather(down_low, "dp")
-
-    w_attn = cube_assemble(attn_pieces, "dp", 0)
-    w_mlp = cube_assemble(mlp_pieces, "dp", 0)
-    w_down = cube_assemble(down_pieces, "dp", 1)
-
+    lane = lax.rem(me, LANES // plan.bias_cols) * plan.bias_cols
+    bias_tile = lax.dynamic_update_slice(
+        jnp.zeros((16, LANES), bf16), column_bias.astype(bf16), (0, lane)
+    )
+    small = jnp.concatenate([bias_tile, jnp.pad(vector_params.astype(bf16), ((0, 13), (0, 0)))], axis=1)
     tables = rotary_tables(position)
     begin_col = begin[:, None]
-    normed = (xhat_all.astype(f32) * gain + shift).astype(bf16)
-
-    bias_flat = bias_vals.reshape(-1)
-    proj_attn = mm(normed, w_attn) + bias_flat[:attn_width]
-    attended, q_low, k_low, v_low, lse = attend_forward(
-        proj_attn[:, :local],
-        proj_attn[:, local : 2 * local],
-        proj_attn[:, 2 * local :],
-        tables,
-        begin_col,
-    )
-    pre = mm(normed, w_mlp) + bias_flat[attn_width:]
-    hidden, gelu_pull = jax.vjp(partial(jax.nn.gelu, approximate=True), pre)
-    hidden = hidden.astype(bf16)
-    out_part = (mm(attended, w_down[:local]) + mm(hidden, w_down[local:])).astype(bf16)
+    (
+        w_attn, w_mlp, w_down, xhat_all, normed, cot_all, q_low, k_low, v_low, attended, lse,
+        hidden, pre_grad, attn_grad, out_part,
+    ) = forward(plan, xhat.astype(bf16), cot_low, in_attn, in_mlp, down_low, small, tables, begin_col)
+    vector_vals = lax.all_gather(vector_params.astype(bf16), "dp", axis=1, tiled=True).astype(f32)
+    gain, out_bias = vector_vals[0], vector_vals[2]
     mixed = line_scatter(out_part, "tensor")
     block_out = block_input + (mixed + out_bias)
-
-    attn_grad = dot_t(cot_all, w_down[:local]).astype(bf16)
-    pre_grad = gelu_pull(dot_t(cot_all, w_down[local:]))[0].astype(bf16)
 
     keep_masks = list(range(0, n_dp, 2))
     send_masks = [m + 1 for m in keep_masks]

time: 748 us -> 574 us (0.77)
  the two profiles are of different devices: /device:TPU:24 before, /device:TPU:0 now
where the time goes in v2:
time: 574 us; the launch traced here: 566 us
  Pallas kernels  202 us (35%)
  waiting for transfers between devices  76.2 us (13%)
  other arithmetic  70.5 us (12%)
  matrix products  63.5 us (11%)
  local copies, waits for them, and re-layouts  55.2 us (10%)
  starting transfers between devices  54 us (9%)
  blocking collectives  42.1 us (7%)
    pallas_call x1, Pallas kernels, forward(): pl.pallas_call(partial(forward_kernel, plan), in_specs=[any_space] * 6 +...  176 us
    ppermute x15, waiting for transfers between devices, flip(): lax.ppermute(value, axis, [(j, j ^ bit) for j in range(lax.axis_size(axis...  60.1 us
    dot_general x8, matrix products, dot_s(): lax.dot_general(a, b, (((0,), (0,)), ((), ())), preferred_element_type=f32)  39.5 us
    ppermute x6, starting transfers between devices, line_scatter(): lax.ppermute(to_up, axis, [(j, j + 1) for j in range(0, min(step, n - 2)...  33.8 us
    pallas_call x1, Pallas kernels, attend_backward(): pl.pallas_call(attend_backward_kernel, grid=(width // LANES,), in_specs=[...  26.4 us
    dot_general x2, matrix products, dot_t(): lax.dot_general(a, b, (((1,), (1,)), ((), ())), preferred_element_type=f32)  24 us
    unnamed x1, blocking collectives  23.5 us
    convert_element_type x4, other arithmetic, line_scatter(): to_up = (to_up.astype(f32) + up.astype(f32)).astype(bf16)  13.1 us
  transfers between devices with their start and end apart: 27, of which 9 were waited for; matrix products, arithmetic and copies ran while one was open for 23% of the time, Pallas kernels for 0%

profile of v2, /device:TPU:0, one launch (start us, length us, event | category | flops | bytes accessed | tf_op | source)
XLA Modules:
  0.0 565.7 jit_solution(1023184815397572931)
XLA Ops:
  10.9 3.1 concatenate.64.ahead
  31.7 3.8 convert_reduce_fusion.2
  35.5 175.7 %shard_map.254 = (bf16[2048,1536]{1,0:T(8,128)(2,1)}, bf16[2048,2048]{1,0:T(8,128)(2,1)}, bf16[2560,2048]{1,0:T(8,128)(2,1)}, bf16[1024,2048]{1,0:T(8,128)(2,1)}...) custom-call(bf16[256,2048]{1,0:T(8,128)(2,1)} %get-tuple-element.123, ...), custom_call_target="tpu_custom_call" | custom-call | flops 60000002048 | bytes 83886080 | tf_op jit(solution)/shard_map/pallas_call | solution.py:524
  214.3 26.4 %shard_map.255 = (bf16[1024,512]{1,0:T(8,128)(2,1)S(1)}, bf16[1024,512]{1,0:T(8,128)(2,1)S(1)}, bf16[1024,512]{1,0:T(8,128)(2,1)S(1)}) custom-call(bf16[1024,512]{1,0:T(8,128)(2,1)} %get-tuple-element.32.q_in, bf16[1024,512]{1,0:T(8,128)(2,1)} %get-tuple-element.33.k_in, bf16[1024,512]{1,0:T(8,128)(2,1)} %get-tuple-element.34.v_in, ...), custom_call_target="tpu_custom_call" | custom-call | flops 10737418240 | bytes 10485760 | tf_op jit(solution)/shard_map/pallas_call | solution.py:121
  241.0 3.6 constant_dynamic-slice_fusion.15
  244.6 5.0 convolution_convert_fusion
  249.6 6.7 %convolution_convert_fusion.4 = bf16[1024,2048]{1,0:T(8,128)(2,1)} fusion(bf16[1024,2048]{1,0:T(8,128)(2,1)S(1)} %copy-done.18, bf16[1024,256]{1,0:T(8,128)(2,1)S(1)} %get-tuple-element.88, bf16[1024,256]{1,0:T(8,128)(2,1)S(1)} %get-tuple-element.89, bf16[1024,256]{1,0:T(8,128)(2,1)S(1)} %get-tuple-element.90, bf16[1024,256]{1,0:T(8,128)(2,1)S(1)} %get-tuple-element.91), kind=kOutput, calls=%fused_computation.14 | convolution fusion | flops 4305453056 | bytes 10485760 | tf_op jit(solution)/shard_map/dot_general | solution.py:75
  256.9 3.3 constant_dynamic-slice_fusion.19
  262.6 13.9 %fusion.43 = f32[1024,2048]{1,0:T(8,128)} fusion(bf16[1024,2048]{1,0:T(8,128)(2,1)S(1)} %copy-done.19, bf16[2048,2048]{1,0:T(8,128)(2,1)} %get-tuple-element.42), kind=kOutput, calls=%fused_computation.195 | convolution fusion | flops 8589934592 | bytes 20971520 | tf_op jit(solution)/shard_map/dot_general | solution.py:67
  276.5 10.0 %multiply_reduce_fusion = (f32[2048]{0:T(1024)S(1)}, f32[2048]{0:T(1024)S(1)}, bf16[1024,2048]{1,0:T(8,128)(2,1)S(1)}) fusion(bf16[1024,2048]{1,0:T(8,128)(2,1)} %get-tuple-element.47, f32[1024,2048]{1,0:T(8,128)} %fusion.43, bf16[1024,1536]{1,0:T(8,128)(2,1)S(1)} %constant_dynamic-update-slice_fusion, bf16[2048,1536]{1,0:T(8,128)(2,1)S(1)} %bitcast.194), kind=kOutput, calls=%fused_computation | convolution fusion | flops 6455029760 | bytes 26230784 | tf_op jit(solution)/shard_map/dot_general | solution.py:67
  296.3 5.3 convolution_convert_fusion.3
  303.0 5.2 convolution_convert_fusion.2
  313.9 5.2 convolution_convert_fusion.1
  320.1 9.4 %convolution_convert_fusion.5 = bf16[1024,2048]{1,0:T(8,128)(2,1)} fusion(bf16[1024,2048]{1,0:T(8,128)(2,1)} %get-tuple-element.41, bf16[1024,256]{1,0:T(8,128)(2,1)} %get-tuple-element.92, bf16[1024,256]{1,0:T(8,128)(2,1)} %get-tuple-element.93, bf16[1024,256]{1,0:T(8,128)(2,1)} %get-tuple-element.94, bf16[1024,256]{1,0:T(8,128)(2,1)} %get-tuple-element.87), kind=kOutput, calls=%fused_computation.15 | convolution fusion | flops 4305453056 | bytes 10485760 | tf_op jit(solution)/shard_map/dot_general | solution.py:75
  333.6 23.5 %all-reduce.1 = f32[8,1216]{1,0:T(8,128)S(1)} all-reduce(f32[8,1216]{1,0:T(8,128)S(1)} %pad_maximum_fusion.24), channel_id=2, replica_groups=mesh['dp'=8,'tensor'=4] {'dp'}, use_global_device_ids=true, to_apply=%region_12.13.clone | all-reduce | flops 9728 | bytes 77824
  358.6 9.5 %psum.7 = f32[3,256]{1,0:T(4,128)S(1)} all-reduce(f32[3,256]{1,0:T(4,128)S(1)} %reshape.264), channel_id=1, replica_groups=mesh['dp'=8,'tensor'=4] {'tensor'}, use_global_device_ids=true, to_apply=%region_13.14 | all-reduce | flops 768 | bytes 6144 | tf_op jit(solution)/shard_map/psum | solution.py:714
  373.3 3.8 collective-permute-start.1
  377.1 4.1 add_convert_fusion.6
  382.6 5.4 copy.104
  390.6 9.1 %all_gather.3 = bf16[3,2048]{1,0:T(4,128)(2,1)S(1)} all-gather(bf16[3,256]{1,0:T(4,128)(2,1)S(1)} %copy-done.42), channel_id=1, replica_groups=mesh['dp'=8,'tensor'=4] {'dp'}, dimensions={1}, use_global_device_ids=true | all-gather | bytes 13824 | tf_op jit(solution)/shard_map/all_gather | solution.py:670
  399.8 4.1 add_convert_fusion.10
  414.7 16.8 %collective-permute-done.15 = bf16[2,128,1536]{2,1,0:T(8,128)(2,1)S(1)} collective-permute-done((bf16[2,128,1536]{2,1,0:T(8,128)(2,1)S(1)}, bf16[2,128,1536]{2,1,0:T(8,128)(2,1)S(1)}, u32[]{:S(2)}, u32[]{:S(2)}) %collective-permute-start.15) | collective-permute-done | bytes 786464 | tf_op jit(solution)/shard_map/ppermute | solution.py:567
  431.8 21.4 %collective-permute-start.2 = (bf16[256,2048]{1,0:T(8,128)(2,1)}, bf16[256,2048]{1,0:T(8,128)(2,1)S(1)}, u32[]{:S(2)}, u32[]{:S(2)}) collective-permute-start(bf16[256,2048]{1,0:T(8,128)(2,1)} %get-tuple-element.99), channel_id=1, source_target_pairs={{0,1},{1,2},{2,3},{4,5},{5,6},{6,7},{8,9},{9,10},{10,11},{12,13},{... | collective-permute-start | bytes 3145736 | tf_op jit(solution)/shard_map/ppermute | solution.py:561
  458.5 4.1 fusion.4
  463.0 11.7 %collective-permute-done.2 = bf16[256,2048]{1,0:T(8,128)(2,1)S(1)} collective-permute-done((bf16[256,2048]{1,0:T(8,128)(2,1)}, bf16[256,2048]{1,0:T(8,128)(2,1)S(1)}, u32[]{:S(2)}, u32[]{:S(2)}) %collective-permute-start.2) | collective-permute-done | bytes 1048608 | tf_op jit(solution)/shard_map/ppermute | solution.py:561
  475.0 4.4 collective-permute-done.5
  490.8 10.0 %collective-permute-done.20 = bf16[2,128,2048]{2,1,0:T(8,128)(2,1)S(1)} collective-permute-done((bf16[2,128,2048]{2,1,0:T(8,128)(2,1)S(1)}, bf16[2,128,2048]{2,1,0:T(8,128)(2,1)S(1)}, u32[]{:S(2)}, u32[]{:S(2)}) %collective-permute-start.20) | collective-permute-done | bytes 1048608 | tf_op jit(solution)/shard_map/ppermute | solution.py:567
  509.8 7.3 %collective-permute-done.21 = bf16[1,128,2048]{2,1,0:T(8,128)(2,1)} collective-permute-done((bf16[1,128,2048]{2,1,0:T(8,128)(2,1)}, bf16[1,128,2048]{2,1,0:T(8,128)(2,1)}, u32[]{:S(2)}, u32[]{:S(2)}) %collective-permute-start.21) | collective-permute-done | bytes 524320 | tf_op jit(solution)/shard_map/ppermute | solution.py:567
  517.0 19.9 %collective-permute-done.19 = bf16[1,128,2048]{2,1,0:T(8,128)(2,1)} collective-permute-done((bf16[1,128,2048]{2,1,0:T(8,128)(2,1)}, bf16[1,128,2048]{2,1,0:T(8,128)(2,1)}, u32[]{:S(2)}, u32[]{:S(2)}) %collective-permute-start.19) | collective-permute-done | bytes 524320 | tf_op jit(solution)/shard_map/ppermute | solution.py:567
  544.9 5.6 multiply_subtract_fusion
  550.5 5.6 collective-permute-done.26
  560.6 4.6 multiply_subtract_fusion.1
  (283 shorter events, 116.0 us)
Async XLA Ops:
  35.5 175.7 %copy-start = (f32[1024,128]{1,0:T(8,128)S(1)}, f32[1024,128]{1,0:T(8,128)}, u32[]{:S(2)}) copy-start(f32[1024,128]{1,0:T(8,128)} %concatenate.64.ahead) | copy-start | bytes 1572868
  249.6 159.4 %collective-permute-start.12 = (bf16[4,256,1536]{2,1,0:T(8,128)(2,1)}, bf16[4,256,1536]{2,1,0:T(8,128)(2,1)}, u32[]{:S(2)}, u32[]{:S(2)}) collective-permute-start(bf16[4,256,1536]{2,1,0:T(8,128)(2,1)} %bitcast.8), channel_id=1, source_target_pairs={{0,4},{4,0},{8,12},{12,8},{16,20},{20,16},{24,28},{28,24},{1,5},{5... | collective-permute-start | bytes 9437192 | tf_op jit(solution)/shard_map/ppermute | solution.py:567
  256.4 200.3 %collective-permute-start.17 = (bf16[4,256,2048]{2,1,0:T(8,128)(2,1)}, bf16[4,256,2048]{2,1,0:T(8,128)(2,1)}, u32[]{:S(2)}, u32[]{:S(2)}) collective-permute-start(bf16[4,256,2048]{2,1,0:T(8,128)(2,1)} %bitcast.26), channel_id=1, source_target_pairs={{0,4},{4,0},{8,12},{12,8},{16,20},{20,16},{24,28},{28,24},{1,5},{5... | collective-permute-start | bytes 12582920 | tf_op jit(solution)/shard_map/ppermute | solution.py:567
  260.2 108.6 %collective-permute-start = (bf16[256,2048]{1,0:T(8,128)(2,1)}, bf16[256,2048]{1,0:T(8,128)(2,1)}, u32[]{:S(2)}, u32[]{:S(2)}) collective-permute-start(bf16[256,2048]{1,0:T(8,128)(2,1)} %get-tuple-element.101), channel_id=1, source_target_pairs={{0,1},{4,5},{8,9},{12,13},{16,17},{20,21},{24,25},{28,29}} | collective-permute-start | bytes 3145736 | tf_op jit(solution)/shard_map/ppermute | solution.py:561
  288.1 41.4 %collective-permute-start.6 = (bf16[256,2048]{1,0:T(8,128)(2,1)}, bf16[256,2048]{1,0:T(8,128)(2,1)}, u32[]{:S(2)}, u32[]{:S(2)}) collective-permute-start(bf16[256,2048]{1,0:T(8,128)(2,1)} %get-tuple-element.97), channel_id=1, source_target_pairs={{0,1},{4,5},{8,9},{12,13},{16,17},{20,21},{24,25},{28,29}} | collective-permute-start | bytes 3145736 | tf_op jit(solution)/shard_map/ppermute | solution.py:561
  290.6 82.6 %collective-permute-start.9 = (bf16[256,2048]{1,0:T(8,128)(2,1)}, bf16[256,2048]{1,0:T(8,128)(2,1)}, u32[]{:S(2)}, u32[]{:S(2)}) collective-permute-start(bf16[256,2048]{1,0:T(8,128)(2,1)} %get-tuple-element.98), channel_id=1, source_target_pairs={{3,2},{7,6},{11,10},{15,14},{19,18},{23,22},{27,26},{31,30}} | collective-permute-start | bytes 3145736 | tf_op jit(solution)/shard_map/ppermute | solution.py:562
  329.5 39.2 %copy-start.27 = (bf16[256,2048]{1,0:T(8,128)(2,1)S(1)}, bf16[256,2048]{1,0:T(8,128)(2,1)}, u32[]{:S(2)}) copy-start(bf16[256,2048]{1,0:T(8,128)(2,1)} %get-tuple-element.102) | copy-start | bytes 3145732
  331.5 45.5 %collective-permute-start.7 = (bf16[256,2048]{1,0:T(8,128)(2,1)S(1)}, bf16[256,2048]{1,0:T(8,128)(2,1)S(1)}, u32[]{:S(2)}, u32[]{:S(2)}) collective-permute-start(bf16[256,2048]{1,0:T(8,128)(2,1)S(1)} %add_convert_fusion.7), channel_id=1, source_target_pairs={{0,1},{1,2},{4,5},{5,6},{8,9},{9,10},{12,13},{13,14},{16,17},{17,1... | collective-permute-start | bytes 3145736 | tf_op jit(solution)/shard_map/ppermute | solution.py:561
  368.7 31.0 %collective-permute-start.3 = (bf16[256,2048]{1,0:T(8,128)(2,1)S(1)}, bf16[256,2048]{1,0:T(8,128)(2,1)}, u32[]{:S(2)}, u32[]{:S(2)}) collective-permute-start(bf16[256,2048]{1,0:T(8,128)(2,1)S(1)} %copy-done.27), channel_id=1, source_target_pairs={{3,2},{7,6},{11,10},{15,14},{19,18},{23,22},{27,26},{31,30}} | collective-permute-start | bytes 3145736 | tf_op jit(solution)/shard_map/ppermute | solution.py:562
  373.3 26.5 %collective-permute-start.1 = (bf16[256,2048]{1,0:T(8,128)(2,1)}, bf16[256,2048]{1,0:T(8,128)(2,1)}, u32[]{:S(2)}, u32[]{:S(2)}) collective-permute-start(bf16[256,2048]{1,0:T(8,128)(2,1)} %add_convert_fusion.11), channel_id=1, source_target_pairs={{0,1},{1,2},{4,5},{5,6},{8,9},{9,10},{12,13},{13,14},{16,17},{17,1... | collective-permute-start | bytes 3145736 | tf_op jit(solution)/shard_map/ppermute | solution.py:561
  381.2 25.9 %collective-permute-start.10 = (bf16[256,2048]{1,0:T(8,128)(2,1)}, bf16[256,2048]{1,0:T(8,128)(2,1)S(1)}, u32[]{:S(2)}, u32[]{:S(2)}) collective-permute-start(bf16[256,2048]{1,0:T(8,128)(2,1)} %get-tuple-element.96), channel_id=1, source_target_pairs={{2,1},{3,2},{6,5},{7,6},{10,9},{11,10},{14,13},{15,14},{18,17},{19... | collective-permute-start | bytes 3145736 | tf_op jit(solution)/shard_map/ppermute | solution.py:562
  403.9 8.7 %collective-permute-start.4 = (bf16[256,2048]{1,0:T(8,128)(2,1)S(1)}, bf16[256,2048]{1,0:T(8,128)(2,1)S(1)}, u32[]{:S(2)}, u32[]{:S(2)}) collective-permute-start(bf16[256,2048]{1,0:T(8,128)(2,1)S(1)} %get-tuple-element.100), channel_id=1, source_target_pairs={{2,1},{3,2},{6,5},{7,6},{10,9},{11,10},{14,13},{15,14},{18,17},{19... | collective-permute-start | bytes 3145736 | tf_op jit(solution)/shard_map/ppermute | solution.py:562
  404.7 49.3 %collective-permute-start.8 = (bf16[256,2048]{1,0:T(8,128)(2,1)S(1)}, bf16[256,2048]{1,0:T(8,128)(2,1)S(1)}, u32[]{:S(2)}, u32[]{:S(2)}) collective-permute-start(bf16[256,2048]{1,0:T(8,128)(2,1)S(1)} %copy-done.32), channel_id=1, source_target_pairs={{0,1},{1,2},{2,3},{4,5},{5,6},{6,7},{8,9},{9,10},{10,11},{12,13},{... | collective-permute-start | bytes 3145736 | tf_op jit(solution)/shard_map/ppermute | solution.py:561
  407.5 47.8 %collective-permute-start.11 = (bf16[256,2048]{1,0:T(8,128)(2,1)S(1)}, bf16[256,2048]{1,0:T(8,128)(2,1)S(1)}, u32[]{:S(2)}, u32[]{:S(2)}) collective-permute-start(bf16[256,2048]{1,0:T(8,128)(2,1)S(1)} %add_convert_fusion.4), channel_id=1, source_target_pairs={{1,0},{2,1},{3,2},{5,4},{6,5},{7,6},{9,8},{10,9},{11,10},{13,12},{... | collective-permute-start | bytes 3145736 | tf_op jit(solution)/shard_map/ppermute | solution.py:562
  412.0 19.6 %collective-permute-start.15 = (bf16[2,128,1536]{2,1,0:T(8,128)(2,1)S(1)}, bf16[2,128,1536]{2,1,0:T(8,128)(2,1)S(1)}, u32[]{:S(2)}, u32[]{:S(2)}) collective-permute-start(bf16[2,128,1536]{2,1,0:T(8,128)(2,1)S(1)} %pad_maximum_fusion.15), channel_id=1, source_target_pairs={{0,16},{4,20},{8,24},{12,28},{16,0},{20,4},{24,8},{28,12},{1,17},{... | collective-permute-start | bytes 2359304 | tf_op jit(solution)/shard_map/ppermute | solution.py:567
  412.5 43.2 %copy-start.5 = (f32[256,2048]{1,0:T(8,128)S(1)}, f32[256,2048]{1,0:T(8,128)}, u32[]{:S(2)}) copy-start(f32[256,2048]{1,0:T(8,128)} %param.15) | copy-start | bytes 6291460
  412.5 43.2 %copy-start.40 = (f32[256]{0:T(256)S(1)}, f32[256]{0:T(256)}, u32[]{:S(2)}) copy-start(f32[256]{0:T(256)} %copy-done.39) | copy-start | bytes 3076
  412.5 43.2 %copy-start.44 = (f32[256]{0:T(256)S(1)}, f32[256]{0:T(256)}, u32[]{:S(2)}) copy-start(f32[256]{0:T(256)} %copy-done.43) | copy-start | bytes 3076
  412.5 19.3 %collective-permute-start.13 = (bf16[2,128,1536]{2,1,0:T(8,128)(2,1)S(1)}, bf16[2,128,1536]{2,1,0:T(8,128)(2,1)S(1)}, u32[]{:S(2)}, u32[]{:S(2)}) collective-permute-start(bf16[2,128,1536]{2,1,0:T(8,128)(2,1)S(1)} %pad_maximum_fusion.14), channel_id=1, source_target_pairs={{0,8},{4,12},{8,0},{12,4},{16,24},{20,28},{24,16},{28,20},{1,9},{5... | collective-permute-start | bytes 2359304 | tf_op jit(solution)/shard_map/ppermute | solution.py:567
  431.6 52.6 %collective-permute-start.22 = (bf16[4,2560,256]{2,1,0:T(8,128)(2,1)S(1)}, bf16[4,2560,256]{2,1,0:T(8,128)(2,1)S(1)}, u32[]{:S(2)}, u32[]{:S(2)}) collective-permute-start(bf16[4,2560,256]{2,1,0:T(8,128)(2,1)S(1)} %bitcast.180), channel_id=1, source_target_pairs={{0,4},{4,0},{8,12},{12,8},{16,20},{20,16},{24,28},{28,24},{1,5},{5... | collective-permute-start | bytes 15728648 | tf_op jit(solution)/shard_map/ppermute | solution.py:567
  431.8 42.9 %collective-permute-start.2 = (bf16[256,2048]{1,0:T(8,128)(2,1)}, bf16[256,2048]{1,0:T(8,128)(2,1)S(1)}, u32[]{:S(2)}, u32[]{:S(2)}) collective-permute-start(bf16[256,2048]{1,0:T(8,128)(2,1)} %get-tuple-element.99), channel_id=1, source_target_pairs={{0,1},{1,2},{2,3},{4,5},{5,6},{6,7},{8,9},{9,10},{10,11},{12,13},{... | collective-permute-start | bytes 3145736 | tf_op jit(solution)/shard_map/ppermute | solution.py:561
  454.0 25.3 %collective-permute-start.5 = (bf16[256,2048]{1,0:T(8,128)(2,1)S(1)}, bf16[256,2048]{1,0:T(8,128)(2,1)S(1)}, u32[]{:S(2)}, u32[]{:S(2)}) collective-permute-start(bf16[256,2048]{1,0:T(8,128)(2,1)S(1)} %add_convert_fusion.8), channel_id=1, source_target_pairs={{1,0},{2,1},{3,2},{5,4},{6,5},{7,6},{9,8},{10,9},{11,10},{13,12},{... | collective-permute-start | bytes 3145736 | tf_op jit(solution)/shard_map/ppermute | solution.py:562
  455.3 27.3 %collective-permute-start.16 = (bf16[1,128,1536]{2,1,0:T(8,128)(2,1)S(1)}, bf16[1,128,1536]{2,1,0:T(8,128)(2,1)}, u32[]{:S(2)}, u32[]{:S(2)}) collective-permute-start(bf16[1,128,1536]{2,1,0:T(8,128)(2,1)S(1)} %fusion.22), channel_id=1, source_target_pairs={{0,8},{4,12},{8,0},{12,4},{16,24},{20,28},{24,16},{28,20},{1,9},{5... | collective-permute-start | bytes 1179656 | tf_op jit(solution)/shard_map/ppermute | solution.py:567
  456.6 26.0 %collective-permute-start.14 = (bf16[1,128,1536]{2,1,0:T(8,128)(2,1)}, bf16[1,128,1536]{2,1,0:T(8,128)(2,1)}, u32[]{:S(2)}, u32[]{:S(2)}) collective-permute-start(bf16[1,128,1536]{2,1,0:T(8,128)(2,1)} %fusion.21), channel_id=1, source_target_pairs={{0,16},{4,20},{8,24},{12,28},{16,0},{20,4},{24,8},{28,12},{1,17},{... | collective-permute-start | bytes 1179656 | tf_op jit(solution)/shard_map/ppermute | solution.py:567
  474.7 26.1 %collective-permute-start.20 = (bf16[2,128,2048]{2,1,0:T(8,128)(2,1)S(1)}, bf16[2,128,2048]{2,1,0:T(8,128)(2,1)S(1)}, u32[]{:S(2)}, u32[]{:S(2)}) collective-permute-start(bf16[2,128,2048]{2,1,0:T(8,128)(2,1)S(1)} %pad_maximum_fusion.13), channel_id=1, source_target_pairs={{0,16},{4,20},{8,24},{12,28},{16,0},{20,4},{24,8},{28,12},{1,17},{... | collective-permute-start | bytes 3145736 | tf_op jit(solution)/shard_map/ppermute | solution.py:567
  479.4 22.7 %collective-permute-start.18 = (bf16[2,128,2048]{2,1,0:T(8,128)(2,1)S(1)}, bf16[2,128,2048]{2,1,0:T(8,128)(2,1)S(1)}, u32[]{:S(2)}, u32[]{:S(2)}) collective-permute-start(bf16[2,128,2048]{2,1,0:T(8,128)(2,1)S(1)} %pad_maximum_fusion.12), channel_id=1, source_target_pairs={{0,8},{4,12},{8,0},{12,4},{16,24},{20,28},{24,16},{28,20},{1,9},{5... | collective-permute-start | bytes 3145736 | tf_op jit(solution)/shard_map/ppermute | solution.py:567
  489.0 50.3 %collective-permute-start.25 = (bf16[2,1280,256]{2,1,0:T(8,128)(2,1)}, bf16[2,1280,256]{2,1,0:T(8,128)(2,1)}, u32[]{:S(2)}, u32[]{:S(2)}) collective-permute-start(bf16[2,1280,256]{2,1,0:T(8,128)(2,1)} %pad_maximum_fusion.11), channel_id=1, source_target_pairs={{0,16},{4,20},{8,24},{12,28},{16,0},{20,4},{24,8},{28,12},{1,17},{... | collective-permute-start | bytes 3932168 | tf_op jit(solution)/shard_map/ppermute | solution.py:567
  501.9 15.2 %collective-permute-start.21 = (bf16[1,128,2048]{2,1,0:T(8,128)(2,1)}, bf16[1,128,2048]{2,1,0:T(8,128)(2,1)}, u32[]{:S(2)}, u32[]{:S(2)}) collective-permute-start(bf16[1,128,2048]{2,1,0:T(8,128)(2,1)} %fusion.20), channel_id=1, source_target_pairs={{0,8},{4,12},{8,0},{12,4},{16,24},{20,28},{24,16},{28,20},{1,9},{5... | collective-permute-start | bytes 1572872 | tf_op jit(solution)/shard_map/ppermute | solution.py:567
  503.2 33.8 %collective-permute-start.19 = (bf16[1,128,2048]{2,1,0:T(8,128)(2,1)}, bf16[1,128,2048]{2,1,0:T(8,128)(2,1)}, u32[]{:S(2)}, u32[]{:S(2)}) collective-permute-start(bf16[1,128,2048]{2,1,0:T(8,128)(2,1)} %fusion.19), channel_id=1, source_target_pairs={{0,16},{4,20},{8,24},{12,28},{16,0},{20,4},{24,8},{28,12},{1,17},{... | collective-permute-start | bytes 1572872 | tf_op jit(solution)/shard_map/ppermute | solution.py:567
  508.6 34.3 %collective-permute-start.23 = (bf16[2,1280,256]{2,1,0:T(8,128)(2,1)S(1)}, bf16[2,1280,256]{2,1,0:T(8,128)(2,1)S(1)}, u32[]{:S(2)}, u32[]{:S(2)}) collective-permute-start(bf16[2,1280,256]{2,1,0:T(8,128)(2,1)S(1)} %pad_maximum_fusion.10), channel_id=1, source_target_pairs={{0,8},{4,12},{8,0},{12,4},{16,24},{20,28},{24,16},{28,20},{1,9},{5... | collective-permute-start | bytes 3932168 | tf_op jit(solution)/shard_map/ppermute | solution.py:567
  542.5 13.5 %collective-permute-start.26 = (bf16[1,1280,256]{2,1,0:T(8,128)(2,1)S(1)}, bf16[1,1280,256]{2,1,0:T(8,128)(2,1)S(1)}, u32[]{:S(2)}, u32[]{:S(2)}) collective-permute-start(bf16[1,1280,256]{2,1,0:T(8,128)(2,1)S(1)} %add_convert_fusion.12), channel_id=1, source_target_pairs={{0,8},{4,12},{8,0},{12,4},{16,24},{20,28},{24,16},{28,20},{1,9},{5... | collective-permute-start | bytes 1966088 | tf_op jit(solution)/shard_map/ppermute | solution.py:567
  543.1 13.3 %collective-permute-start.24 = (bf16[1,1280,256]{2,1,0:T(8,128)(2,1)S(1)}, bf16[1,1280,256]{2,1,0:T(8,128)(2,1)S(1)}, u32[]{:S(2)}, u32[]{:S(2)}) collective-permute-start(bf16[1,1280,256]{2,1,0:T(8,128)(2,1)S(1)} %add_convert_fusion.14), channel_id=1, source_target_pairs={{0,16},{4,20},{8,24},{12,28},{16,0},{20,4},{24,8},{28,12},{1,17},{... | collective-permute-start | bytes 1966088 | tf_op jit(solution)/shard_map/ppermute | solution.py:567
  (62 other events, 628.3 us)

commit v3 on v2

--- a/solution.py
+++ b/solution.py
@@ -80,56 +80,6 @@
     return x * own + sign * (
         pltpu.roll(x, LANES - half, 1) * ahead + pltpu.roll(x, half, 1) * behind
     )
-
-
-def attend_backward_kernel(q_in, k_in, v_in, grad, lse, own, ahead, behind, begin, dq, dk, dv, k_sum, v_sum):
-    total = q_in.shape[0]
-    rows = min(QUERY_ROWS, total)
-    k_sum[...] = jnp.zeros_like(k_sum)
-    v_sum[...] = jnp.zeros_like(v_sum)
-    scale = HEAD ** (-0.5)
-    for start in range(0, total, rows):
-        stop = start + rows
-        place = pl.ds(start, rows)
-        allowed = attend_mask(begin[place, :], start, rows, stop)
-        q_sum = jnp.zeros((rows, LANES), f32)
-        for head in range(LANES // HEAD):
-            mine = head_lanes(rows, head)
-            query = jnp.where(mine, q_in[place, :], jnp.zeros((rows, LANES), bf16)) * scale
-            query = query.astype(bf16)
-            cot = jnp.where(mine, grad[place, :], jnp.zeros((rows, LANES), bf16))
-            scores = dot_t(query, k_in[:stop, :]) - lse[place, head * HEAD : head * HEAD + 1]
-            probs = jnp.where(allowed, jnp.exp(scores), 0.0)
-            prob_grad = dot_t(cot, v_in[:stop, :])
-            mean = jnp.sum(probs * prob_grad, axis=1, keepdims=True)
-            score_grad = (probs * (prob_grad - mean)).astype(bf16)
-            q_step = dot_n(score_grad, k_in[:stop, :])
-            q_sum = jnp.where(mine, q_step * scale, q_sum)
-            k_sum[:stop, :] += dot_s(score_grad, query)
-            v_sum[:stop, :] += dot_s(probs.astype(bf16), cot)
-        dq[place, :] = turn(
-            q_sum, own[place, :], ahead[place, :], behind[place, :], -1.0
-        ).astype(bf16)
-    dk[...] = turn(k_sum[...], own[...], ahead[...], behind[...], -1.0).astype(bf16)
-    dv[...] = v_sum[...].astype(bf16)
-
-
-def attend_backward(q, k, v, grad, lse, tables, begin):
-    total, width = q.shape
-    tile = pl.BlockSpec((total, LANES), lambda p: (0, p))
-    fixed = pl.BlockSpec((total, LANES), lambda p: (0, 0))
-    return pl.pallas_call(
-        attend_backward_kernel,
-        grid=(width // LANES,),
-        in_specs=[tile] * 5 + [fixed] * 3 + [pl.BlockSpec((total, 1), lambda p: (0, 0))],
-        out_specs=[tile] * 3,
-        out_shape=[jax.ShapeDtypeStruct((total, width), bf16)] * 3,
-        scratch_shapes=[pltpu.VMEM((total, LANES), f32)] * 2,
-        compiler_params=pltpu.CompilerParams(vmem_limit_bytes=48 << 20),
-        cost_estimate=pl.CostEstimate(
-            flops=20 * total * total * width, bytes_accessed=20 * total * width, transcendentals=0
-        ),
-    )(q, k, v, grad, lse, *tables, begin)
 
 
 def low_bit(mask):
@@ -180,9 +130,9 @@
 def forward_kernel(
     plan,
     xhat_in, cot_in, wa_in, wm_in, wd_in, small_in, own, ahead, behind, begin,
-    wa_out, wm_out, wd_out, xhat_out, normed_out, cot_out, q_out, k_out, v_out, att_out, lse_out,
+    wa_out, wm_out, small_out, xhat_out, sums_out, cot_out, q_out, k_out, v_out, att_out, lse_out,
     hidden_out, da_out, do_out, part_out,
-    wa, wm, wd, small, xs, ns, cs, q, k, v, att, lse, hidden, slope, do,
+    wa, wm, wd, small, xs, ns, sums, cs, q, k, v, att, lse, hidden, slope, do,
     own_sem, out_sem, w_send, w_recv, up_send, up_recv, down_send, down_recv,
 ):
     n, line = plan.n_dp, plan.n_line
@@ -308,7 +258,7 @@
         return pl.ds(pl.multiple_of(index * rows, rows), rows)
 
     outs = [
-        (wa, wa_out), (wm, wm_out), (wd, wd_out), (xs, xhat_out), (ns, normed_out), (cs, cot_out),
+        (wa, wa_out), (wm, wm_out), (small, small_out), (xs, xhat_out), (sums, sums_out), (cs, cot_out),
         (q, q_out), (k, k_out), (v, v_out), (att, att_out), (lse, lse_out), (hidden, hidden_out),
         (slope, da_out), (do, do_out), (xs, part_out),
     ]
@@ -392,7 +342,7 @@
             here = pl.ds(start, block)
             allowed = attend_mask(begin[here, :], start, block, stop)
             query = q[here, lanes]
-            results, sums = [], []
+            results, logs = [], []
             for head in range(LANES // HEAD):
                 mine = head_lanes(block, head)
                 chosen = jnp.where(mine, query, jnp.zeros_like(query)) * HEAD ** (-0.5)
@@ -401,10 +351,14 @@
                 weights = jnp.exp(scores - top)
                 total_weight = jnp.sum(weights, axis=1, keepdims=True)
                 results.append(dot_n(weights.astype(bf16), v[:stop, lanes]) / total_weight)
-                sums.append(top + jnp.log(total_weight))
+                logs.append(top + jnp.log(total_weight))
             first = head_lanes(block, 0)
             att[here, lanes] = jnp.where(first, results[0], results[1]).astype(bf16)
-            lse[here, lanes] = jnp.where(first, sums[0], sums[1])
+            which = lax.broadcasted_iota(jnp.int32, (block, LANES), 1)
+            held = lse[here, :]
+            for head in range(LANES // HEAD):
+                held = jnp.where(which == pair * (LANES // HEAD) + head, logs[head], held)
+            lse[here, :] = held
         return carry
 
     tile = min(512, plan.model)
@@ -419,6 +373,7 @@
 
     def back_rows(index):
         at = span(index)
+        sums[0:1, :] += jnp.sum(cs[at, :].astype(f32), axis=0, keepdims=True)
         do[at, :] = dot_t(cs[at, :], wd[:local, :]).astype(bf16)
         for r in range(plan.n_mlp):
             cols = slice(r * local, (r + 1) * local)
@@ -444,7 +399,9 @@
     w_arrive(0, plan.several)
     w_arrive(3, plan.odd)
     w_arrive(0, plan.odd)
-    write(0)
+    write(0, 2)
+    sums[...] = jnp.zeros_like(sums)
+    lse[...] = jnp.zeros_like(lse)
     at_distance(0, attn_rows)
     if line > 2:
         at_distance(1, attn_rows)
@@ -467,7 +424,7 @@
             z_arrive(0, line - 1)
             cot_start(line - 1)
         at_distance(line - 1, lambda c: (attn_rows(c), mlp_rows(c))[0])
-    write(3, 4, 6, 7, 8, 11)
+    write(3, 6, 7, 8, 11)
     pairs = local // LANES
     lax.fori_loop(0, pairs // 2, attend, 0)
     w_arrive(2, plan.single)
@@ -477,7 +434,6 @@
         z_arrive(1, 1)
     w_arrive(2, plan.several)
     w_arrive(2, plan.odd)
-    write(2)
     out_copy(3).wait()
     for step in range(1, line):
         for up in (True, False):
@@ -493,7 +449,7 @@
     for step in range(2, line):
         z_arrive(1, step)
         at_distance(step, back_rows)
-    write(5, 12, 13)
+    write(4, 5, 12, 13)
 
     for flow in range(4):
         for mask in range(1, n):
@@ -513,10 +469,10 @@
     n, line, group, model, local = plan.n_dp, plan.n_line, plan.group, plan.model, plan.local
     low = lambda *shape: jax.ShapeDtypeStruct(shape, bf16)
     out_shape = [
-        low(model, plan.attn), low(model, plan.mlp), low(plan.down, model),
-        low(group, model), low(group, model), low(group, model),
+        low(model, plan.attn), low(model, plan.mlp), low(n, 16, LANES + plan.out_cols),
+        low(group, model), jax.ShapeDtypeStruct((8, model), f32), low(group, model),
         low(group, local), low(group, local), low(group, local), low(group, local),
-        jax.ShapeDtypeStruct((group, local), f32),
+        jax.ShapeDtypeStruct((group, LANES), f32),
         low(group, plan.mlp), low(group, plan.mlp), low(group, local), low(group, model),
     ]
     scratch = lambda s: pltpu.VMEM(s.shape, s.dtype)
@@ -526,9 +482,11 @@
         in_specs=[any_space] * 6 + [vmem] * 4,
         out_specs=[any_space] * 15,
         out_shape=out_shape,
-        scratch_shapes=[scratch(s) for s in out_shape[:3]]
-        + [pltpu.VMEM((n, 16, LANES + plan.out_cols), bf16)]
-        + [scratch(s) for s in out_shape[3:14]]
+        scratch_shapes=[scratch(s) for s in out_shape[:2]]
+        + [pltpu.VMEM((plan.down, model), bf16)]
+        + [scratch(s) for s in out_shape[2:4]]
+        + [pltpu.VMEM((group, model), bf16)]
+        + [scratch(s) for s in out_shape[4:14]]
         + [dma((6,)), dma((15,)), dma((8 * n,)), dma((8 * n,))]
         + [dma((2 * line,))] * 4,
         compiler_params=pltpu.CompilerParams(
@@ -538,54 +496,493 @@
     )(xhat, cot, wa, wm, wd, small, *tables, begin)
 
 
-def after(value, *others):
-    return lax.optimization_barrier((value,) + others)[0]
-
-
-def line_scatter(partials, axis):
-    n = lax.axis_size(axis)
-    me = lax.axis_index(axis)
-    rows = partials.shape[0] // n
-
-    def part(owner):
-        owner = jnp.clip(owner, 0, n - 1)
-        return lax.dynamic_slice_in_dim(partials, owner * rows, rows, 0)
-
-    up = down = None
-    for step in range(n - 1):
-        to_up = part(me + n - 1 - step)
-        to_down = part(me - n + 1 + step)
-        if step:
-            to_up = (to_up.astype(f32) + up.astype(f32)).astype(bf16)
-            to_down = (to_down.astype(f32) + down.astype(f32)).astype(bf16)
-        up = lax.ppermute(to_up, axis, [(j, j + 1) for j in range(0, min(step, n - 2) + 1)])
-        down = lax.ppermute(to_down, axis, [(j, j - 1) for j in range(n - 1 - step, n)])
-    return part(me).astype(f32) + up.astype(f32) + down.astype(f32)
-
-
-def flip(value, axis, bit):
-    return lax.ppermute(value, axis, [(j, j ^ bit) for j in range(lax.axis_size(axis))])
-
-
-def cube_scatter(send, keep, axis):
-    n = lax.axis_size(axis)
-    got = flip(send, axis, 1)
-    total = {2 * j: (keep[j].astype(f32) + got[j].astype(f32)).astype(bf16) for j in range(n // 2)}
-    half = keep.shape[1] // 2
-    bits = [1 << b for b in range(1, n.bit_length() - 1)]
-    results = []
-    for rows, order in ((slice(0, half), bits), (slice(half, None), bits[::-1])):
-        held = {m: t[rows] for m, t in total.items()}
-        for bit in order:
-            away = [m for m in sorted(held) if m & bit]
-            came = flip(jnp.stack([held[m] for m in away]), axis, bit)
-            held = {
-                m ^ bit: held[m ^ bit].astype(f32) + came[j].astype(f32) for j, m in enumerate(away)
-            }
-            if bit != order[-1]:
-                held = {m: t.astype(bf16) for m, t in held.items()}
-        results.append(held[0].astype(f32))
-    return jnp.concatenate(results, axis=0)
+def backward_kernel(
+    plan,
+    xhat_in, cot_in, att_in, hidden_in, da_in, do_in, q_in, k_in, v_in, part_in, wa_in, wm_in,
+    lse, sums_in, own, ahead, behind, begin,
+    down_out, in_out, small_out, part_out, rows_out, dh_out,
+    turned, stage, og, da, qkv, do, k_sum, v_sum, sent, core_in, held, cube_in, up_in, down_in,
+    w_tile, fin, dh_fin, small, small_in, shares,
+    load_sem, stage_sem, tile_sem, fin_sem, dh_sem, core_send, core_recv, cube_send, cube_recv,
+    up_send, up_recv, down_send, down_recv, small_send, small_recv, part_send, part_recv,
+    share_send, share_recv, credit,
+):
+    n, line = plan.n_dp, plan.n_line
+    me, place = lax.axis_index("dp"), lax.axis_index("tensor")
+    rows, local, group, model, in_rows = plan.rows, plan.local, plan.group, plan.model, plan.in_rows
+    MESH = pl.DeviceIdType.MESH
+    half_rows, pairs_n, n_bits = in_rows // 2, n // 2, len(plan.bits)
+    orders = (plan.bits, plan.bits[::-1])
+    n_down, n_mlp = 1 + plan.n_mlp, plan.n_mlp
+    flows = {"down": (n_down, 0, 0), "mlp": (n_mlp, n_down, 3), "attn": (3, 0, 0)}
+
+    def owner(mask):
+        index = me
+        for b in [1] + plan.bits:
+            if mask & b:
+                index = index + b - 2 * b * lax.rem(index // b, 2)
+        return index
+
+    def peer(bit):
+        return {"dp": owner(bit)}
+
+    def position(mask, order):
+        return sum((1 if mask & b else 0) << (n_bits - 1 - p) for p, b in enumerate(order))
+
+    whole = [
+        (att_in, og.at[:, pl.ds(0, local)]),
+        (hidden_in, og.at[:, pl.ds(local, plan.mlp)]),
+        (da_in, da),
+        (q_in, qkv.at[:, pl.ds(0, local)]),
+        (k_in, qkv.at[:, pl.ds(local, local)]),
+        (v_in, qkv.at[:, pl.ds(2 * local, local)]),
+        (do_in, do),
+    ]
+    for j, (a, b) in enumerate(whole):
+        pltpu.make_async_copy(a, b, load_sem.at[j]).start()
+
+    def loaded(*which):
+        for j in which:
+            pltpu.make_async_copy(whole[j][0], whole[j][1], load_sem.at[j]).wait()
+
+    barrier = pltpu.get_barrier_semaphore()
+    for b in [1] + plan.bits:
+        pl.semaphore_signal(barrier, inc=1, device_id=peer(b), device_id_type=MESH)
+    for d in range(1, line):
+        pl.semaphore_signal(
+            barrier, inc=1, device_id={"tensor": lax.rem(place + d, line)}, device_id_type=MESH
+        )
+
+    def part_copy(d, arriving):
+        source = lax.rem(place + line - d, line) if arriving else place
+        target = place if arriving else lax.rem(place + d, line)
+        return pltpu.make_async_remote_copy(
+            src_ref=part_in.at[pl.ds(pl.multiple_of(target * rows, rows), rows), :],
+            dst_ref=part_out.at[source], send_sem=part_send.at[d], recv_sem=part_recv.at[d],
+            device_id={"tensor": lax.rem(place + d, line)}, device_id_type=MESH,
+        )
+
+    def share_copy(d, arriving):
+        source = lax.rem(place + line - d, line) if arriving else place
+        return pltpu.make_async_remote_copy(
+            src_ref=shares, dst_ref=rows_out.at[source],
+            send_sem=share_send.at[d], recv_sem=share_recv.at[d],
+            device_id={"tensor": lax.rem(place + d, line)}, device_id_type=MESH,
+        )
+
+    part_own = pltpu.make_async_copy(
+        part_in.at[pl.ds(pl.multiple_of(place * rows, rows), rows), :], part_out.at[place], part_send.at[0]
+    )
+    share_own = pltpu.make_async_copy(shares, rows_out.at[place], share_send.at[0])
+
+    def turn_columns(source, masks, first, started=False):
+        def fetch(j):
+            at = pl.multiple_of(owner(masks[j]) * in_rows, in_rows)
+            return pltpu.make_async_copy(
+                source.at[:, pl.ds(at, in_rows)], stage.at[j % 2], stage_sem.at[j % 2]
+            )
+
+        fetch(0).start()
+        for j in range(len(masks)):
+            if j + 1 < len(masks):
+                fetch(j + 1).start()
+            fetch(j).wait()
+            turned[pl.ds((first + j) * in_rows, in_rows), :] = stage[j % 2].T
+
+    def core_copy(name, t):
+        return pltpu.make_async_remote_copy(
+            src_ref=sent.at[lax.rem(t, 2)], dst_ref=core_in.at[t],
+            send_sem=core_send.at[lax.rem(t, 2)], recv_sem=core_recv.at[t],
+            device_id=peer(1), device_id_type=MESH,
+        )
+
+    def cube_copy(slot, half, phase):
+        count = pairs_n >> (phase + 1)
+        first = pairs_n - 2 * count
+        at = half * n_bits + phase
+        return pltpu.make_async_remote_copy(
+            src_ref=held.at[slot, half, pl.ds(count, count)],
+            dst_ref=cube_in.at[slot, half, pl.ds(first, count)],
+            send_sem=cube_send.at[slot, at], recv_sem=cube_recv.at[slot, at],
+            device_id=peer(orders[half][phase]), device_id_type=MESH,
+        )
+
+    def operand(name, t):
+        source = {"down": og, "mlp": da, "attn": qkv}[name]
+        return source[:, pl.ds(pl.multiple_of(t * local, local), local)]
+
+    send_rows, keep_rows = pl.ds(0, pairs_n * in_rows), pl.ds(pairs_n * in_rows, pairs_n * in_rows)
+
+    def send_core(name):
+        tiles = flows[name][0]
+        if name != "down":
+            pl.semaphore_wait(credit.at[0], 1)
+
+        def step(t, carry):
+            @pl.when(t >= 2)
+            def _():
+                core_copy(name, t - 2).wait_send()
+            sent[lax.rem(t, 2)] = dot_n(turned[send_rows, :], operand(name, t)).astype(bf16)
+            core_copy(name, t).start()
+            return carry
+
+        lax.fori_loop(0, tiles, step, 0)
+        for t in range(max(tiles - 2, 0), tiles):
+            core_copy(name, t).wait_send()
+
+    def keep_core(name):
+        tiles, base, _ = flows[name]
+
+        def step(t, carry):
+            total = dot_n(turned[keep_rows, :], operand(name, t))
+            core_copy(name, t).wait_recv()
+            total = total + core_in[t].astype(f32)
+            for j in range(pairs_n):
+                for half in range(2):
+                    at = j * in_rows + half * half_rows
+                    held[base + t, half, position(2 * j, orders[half])] = total[at : at + half_rows].astype(bf16)
+            for half in range(2):
+                if n_bits:
+                    cube_copy(base + t, half, 0).start()
+            return carry
+
+        lax.fori_loop(0, tiles, step, 0)
+        if name != "attn":
+            pl.semaphore_signal(credit.at[0], inc=1, device_id=peer(1), device_id_type=MESH)
+
+    def cube_step(name, phase):
+        tiles, base, result = flows[name]
+        count = pairs_n >> (phase + 1)
+        first = pairs_n - 2 * count
+        target = down_out if name == "down" else in_out
+
+        def fin_copy(t):
+            return pltpu.make_async_copy(fin.at[lax.rem(t, 2)], target.at[result + t], fin_sem.at[lax.rem(t, 2)])
+
+        def step(t, carry):
+            slot = base + t
+            if phase == n_bits - 1:
+                @pl.when(t >= 2)
+                def _():
+                    fin_copy(t - 2).wait()
+            for half in range(2):
+                cube_copy(slot, half, phase).wait_recv()
+                total = (
+                    held[slot, half, 0:count].astype(f32)
+                    + cube_in[slot, half, first : first + count].astype(f32)
+                )
+                if phase < n_bits - 1:
+                    held[slot, half, 0:count] = total.astype(bf16)
+                    cube_copy(slot, half, phase + 1).start()
+                else:
+                    fin[lax.rem(t, 2), half * half_rows : (half + 1) * half_rows, :] = total[0]
+            if phase == n_bits - 1:
+                fin_copy(t).start()
+                if name != "down":
+                    weight = w_tile[0 if name == "attn" else 1, 0:in_rows, pl.ds(pl.multiple_of(t * local, local), local)].astype(f32)
+                    product = weight * fin[lax.rem(t, 2)]
+                    extra = weight * small[n_bits + 1, pl.ds(result + t, 1), :]
+                    for g in range(0, local, LANES):
+                        shares[0] += product[:, g : g + LANES]
+                        shares[1] += extra[:, g : g + LANES]
+            return carry
+
+        lax.fori_loop(0, tiles, step, 0)
+        if phase == n_bits - 1:
+            for t in range(max(tiles - 2, 0), tiles):
+                fin_copy(t).wait()
+
+    def cube_sent(name):
+        tiles, base, _ = flows[name]
+
+        def step(t, carry):
+            for half in range(2):
+                for phase in range(n_bits):
+                    cube_copy(base + t, half, phase).wait_send()
+            return carry
+
+        lax.fori_loop(0, tiles, step, 0)
+
+    def attend(pair, carry):
+        block = min(QUERY_ROWS, group)
+        scale = HEAD ** (-0.5)
+        k_sum[...] = jnp.zeros_like(k_sum)
+        v_sum[...] = jnp.zeros_like(v_sum)
+        q_lanes, k_lanes, v_lanes = (
+            pl.ds(pl.multiple_of(pair * LANES + r * local, LANES), LANES) for r in range(3)
+        )
+        lanes = q_lanes
+        which = lax.broadcasted_iota(jnp.int32, (block, LANES), 1)
+        for start in range(0, group, block):
+            stop = start + block
+            here = pl.ds(start, block)
+            allowed = attend_mask(begin[here, :], start, block, stop)
+            q_sum = jnp.zeros((block, LANES), f32)
+            for head in range(LANES // HEAD):
+                mine = head_lanes(block, head)
+                query = jnp.where(mine, qkv[here, q_lanes], jnp.zeros((block, LANES), bf16)) * scale
+                query = query.astype(bf16)
+                cot = jnp.where(mine, do[here, lanes], jnp.zeros((block, LANES), bf16))
+                level = jnp.sum(
+                    jnp.where(which == pair * (LANES // HEAD) + head, lse[here, :], 0.0), axis=1, keepdims=True
+                )
+                scores = dot_t(query, qkv[:stop, k_lanes]) - level
+                probs = jnp.where(allowed, jnp.exp(scores), 0.0)
+                prob_grad = dot_t(cot, qkv[:stop, v_lanes])
+                mean = jnp.sum(probs * prob_grad, axis=1, keepdims=True)
+                score_grad = (probs * (prob_grad - mean)).astype(bf16)
+                q_step = dot_n(score_grad, qkv[:stop, k_lanes])
+                q_sum = jnp.where(mine, q_step * scale, q_sum)
+                k_sum[:stop, :] += dot_s(score_grad, query)
+                v_sum[:stop, :] += dot_s(probs.astype(bf16), cot)
+            qkv[here, q_lanes] = turn(
+                q_sum, own[here, :], ahead[here, :], behind[here, :], -1.0
+            ).astype(bf16)
+        qkv[:, k_lanes] = turn(k_sum[...], own[...], ahead[...], behind[...], -1.0).astype(bf16)
+        qkv[:, v_lanes] = v_sum[...].astype(bf16)
+        return carry
+
+    width = min(256, model)
+    d_tiles = model // width
+
+    def tile_loads(t):
+        at = pl.ds(pl.multiple_of(t * width, width), width)
+        slot = lax.rem(t, 2)
+        return (
+            pltpu.make_async_copy(wa_in.at[at, :], w_tile.at[slot, pl.ds(0, width), pl.ds(0, plan.attn)], tile_sem.at[slot, 0]),
+            pltpu.make_async_copy(wm_in.at[at, :], w_tile.at[slot, pl.ds(0, width), pl.ds(plan.attn, plan.mlp)], tile_sem.at[slot, 1]),
+        )
+
+    def line_copy(t, index, up, arriving=False):
+        at = pl.ds(pl.multiple_of(index * rows, rows), rows)
+        cols = pl.ds(pl.multiple_of(t * width, width), width)
+        return pltpu.make_async_remote_copy(
+            src_ref=og.at[at, cols],
+            dst_ref=(up_in if up else down_in).at[t, index if up else line - 1 - index],
+            send_sem=(up_send if up else down_send).at[t, index],
+            recv_sem=(up_recv if up else down_recv).at[t, index],
+            device_id={"tensor": place + 1 if up != arriving else place - 1}, device_id_type=MESH,
+        )
+
+    def line_first(t):
+        for up in (True, False):
+            @pl.when((place == 0) if up else (place == line - 1))
+            def _():
+                for step in range(line - 1):
+                    line_copy(t, line - 1 - step if up else step, up).start()
+
+    def line_pass(t, step):
+        cols = pl.ds(pl.multiple_of(t * width, width), width)
+        for up in (True, False):
+            index = line - 1 - step if up else step
+            at = pl.ds(index * rows, rows)
+            hears = (place > 0) & (place < index) if up else (place < line - 1) & (place > index)
+
+            @pl.when(hears)
+            def _():
+                line_copy(t, index, up, True).wait_recv()
+                got = (up_in if up else down_in)[t, index if up else line - 1 - index]
+                og[at, cols] = (og[at, cols].astype(f32) + got.astype(f32)).astype(bf16)
+                line_copy(t, index, up).start()
+
+    def line_last(t):
+        cols = pl.ds(pl.multiple_of(t * width, width), width)
+        at = pl.ds(pl.multiple_of(place * rows, rows), rows)
+        slot = lax.rem(t, 2)
+
+        @pl.when(t >= 2)
+        def _():
+            dh_copy(t - 2).wait()
+        dh_fin[slot] = og[at, cols].astype(f32)
+        for up in (True, False):
+            @pl.when((place > 0) if up else (place < line - 1))
+            def _():
+                line_copy(t, place, up, True).wait_recv()
+                buffer = up_in if up else down_in
+                dh_fin[slot] += buffer[t, place if up else line - 1 - place].astype(f32)
+        dh_copy(t).start()
+
+    def dh_copy(t):
+        cols = pl.ds(pl.multiple_of(t * width, width), width)
+        return pltpu.make_async_copy(dh_fin.at[lax.rem(t, 2)], dh_out.at[:, cols], dh_sem.at[lax.rem(t, 2)])
+
+    def line_sent(t):
+        for index in range(line):
+            for up in (True, False):
+                goes = (place < index) if up else (place > index)
+
+                @pl.when(goes)
+                def _():
+                    line_copy(t, index, up).wait_send()
+
+    def dh_tile(t, carry):
+        slot = lax.rem(t, 2)
+        @pl.when(t + 1 < d_tiles)
+        def _():
+            for load in tile_loads(t + 1):
+                load.start()
+        for load in tile_loads(t):
+            load.wait()
+        total = dot_t(qkv[...], w_tile[slot, 0:width, : plan.attn]) + dot_t(da[...], w_tile[slot, 0:width, plan.attn :])
+        og[:, pl.ds(pl.multiple_of(t * width, width), width)] = total.astype(bf16)
+        line_first(t)
+        return carry
+
+    def small_copy(j):
+        return pltpu.make_async_remote_copy(
+            src_ref=small.at[j], dst_ref=small_in.at[j],
+            send_sem=small_send.at[j], recv_sem=small_recv.at[j],
+            device_id=peer(([1] + plan.bits)[j]), device_id_type=MESH,
+        )
+
+    def small_step(j):
+        small_copy(j).wait_recv()
+        small[j + 1] = small[j] + small_in[j]
+        if j < n_bits:
+            small_copy(j + 1).start()
+
+    shares[...] = jnp.zeros_like(shares)
+    small[0] = jnp.zeros_like(small[0])
+    for load in tile_loads(0):
+        load.start()
+    send_masks, keep_masks = [2 * j + 1 for j in range(pairs_n)], [2 * j for j in range(pairs_n)]
+    turn_columns(cot_in, send_masks, 0)
+    pl.semaphore_wait(barrier, 1 + n_bits + line - 1)
+    part_own.start()
+    for d in range(1, line):
+        part_copy(d, False).start()
+    loaded(0, 1)
+    send_core("down")
+    turn_columns(cot_in, keep_masks, pairs_n)
+    keep_core("down")
+    loaded(2)
+    turn_columns(xhat_in, send_masks, 0)
+    send_core("mlp")
+    turn_columns(xhat_in, keep_masks, pairs_n)
+    keep_core("mlp")
+    loaded(3, 4, 5, 6)
+    pairs = local // LANES
+    lax.fori_loop(0, pairs // 2, attend, 0)
+    for phase in range(n_bits - 1):
+        cube_step("down", phase)
+    lax.fori_loop(pairs // 2, pairs, attend, 0)
+    for r in range(3 + n_mlp):
+        block = qkv[:, r * local : (r + 1) * local] if r < 3 else da[:, (r - 3) * local : (r - 2) * local]
+        small[0, r : r + 1, :] = jnp.sum(block.astype(f32), axis=0, keepdims=True)
+    for r in range(model // local):
+        small[0, 8 + r : 9 + r, :] = sums_in[0:1, r * local : (r + 1) * local]
+    small_copy(0).start()
+    lax.fori_loop(0, d_tiles, dh_tile, 0)
+    for phase in range(n_bits - 1):
+        cube_step("mlp", phase)
+    small_step(0)
+    cube_step("down", n_bits - 1)
+    cube_sent("down")
+    for b in plan.bits:
+        pl.semaphore_signal(credit.at[1], inc=1, device_id=peer(b), device_id_type=MESH)
+    small_step(1)
+    send_core("attn")
+    pl.semaphore_wait(credit.at[1], n_bits)
+    keep_core("attn")
+    for j in range(2, n_bits + 1):
+        small_step(j)
+    own_rows = pl.ds(pl.multiple_of(me * in_rows, in_rows), in_rows)
+    weights = [
+        pltpu.make_async_copy(wa_in.at[own_rows, :], w_tile.at[0, pl.ds(0, in_rows), pl.ds(0, plan.attn)], tile_sem.at[0, 0]),
+        pltpu.make_async_copy(wm_in.at[own_rows, :], w_tile.at[1, pl.ds(0, in_rows), pl.ds(0, plan.mlp)], tile_sem.at[1, 0]),
+    ]
+    for w in weights:
+        w.start()
+
+    def passes(first, stop):
+        def step(t, carry):
+            for s in range(line - 1):
+                line_pass(t, s)
+            return carry
+        lax.fori_loop(first, stop, step, 0)
+
+    passes(0, d_tiles // 2)
+    for w in weights:
+        w.wait()
+    cube_step("mlp", n_bits - 1)
+    passes(d_tiles // 2, d_tiles)
+    for phase in range(n_bits):
+        cube_step("attn", phase)
+    share_own.start()
+    for d in range(1, line):
+        share_copy(d, False).start()
+
+    def last(t, carry):
+        line_last(t)
+        return carry
+
+    lax.fori_loop(0, d_tiles, last, 0)
+    for t in range(max(d_tiles - 2, 0), d_tiles):
+        dh_copy(t).wait()
+    small_done = pltpu.make_async_copy(small.at[n_bits + 1], small_out, load_sem.at[0])
+    small_done.start()
+    cube_sent("mlp")
+    cube_sent("attn")
+
+    def sent_all(t, carry):
+        line_sent(t)
+        return carry
+
+    lax.fori_loop(0, d_tiles, sent_all, 0)
+    for j in range(n_bits + 1):
+        small_copy(j).wait_send()
+    part_own.wait()
+    share_own.wait()
+    for d in range(1, line):
+        part_copy(d, False).wait_send()
+        part_copy(d, True).wait_recv()
+        share_copy(d, False).wait_send()
+        share_copy(d, True).wait_recv()
+    small_done.wait()
+
+
+def backward(plan, xhat, cot, att, hidden, da, do, q, k, v, part, wa, wm, lse, sums, tables, begin):
+    any_space = pl.BlockSpec(memory_space=pl.ANY)
+    vmem = pl.BlockSpec(memory_space=pltpu.VMEM)
+    n, line, group, model, local = plan.n_dp, plan.n_line, plan.group, plan.model, plan.local
+    rows, in_rows, n_bits, pairs_n = plan.rows, plan.in_rows, len(plan.bits), n // 2
+    n_down = 1 + plan.n_mlp
+    small_rows = 8 + -(-(model // local) // 8) * 8
+    width = min(256, model)
+    d_tiles = model // width
+    low = lambda *shape: pltpu.VMEM(shape, bf16)
+    full = lambda *shape: pltpu.VMEM(shape, f32)
+    dma = pltpu.SemaphoreType.DMA
+    out = lambda dtype, *shape: jax.ShapeDtypeStruct(shape, dtype)
+    slots = n_down + plan.n_mlp
+    return pl.pallas_call(
+        partial(backward_kernel, plan),
+        in_specs=[any_space] * 12 + [vmem] * 6,
+        out_specs=[any_space] * 6,
+        out_shape=[
+            out(f32, n_down, in_rows, local), out(f32, 3 + plan.n_mlp, in_rows, local),
+            out(f32, small_rows, local), out(bf16, line, rows, model),
+            out(f32, line, 2, in_rows, LANES), out(f32, rows, model),
+        ],
+        scratch_shapes=[
+            low(n * in_rows, group), low(2, group, in_rows), low(group, plan.down), low(group, plan.mlp),
+            low(group, plan.attn), low(group, local), full(group, LANES), full(group, LANES),
+            low(2, pairs_n * in_rows, local), low(n_down, pairs_n * in_rows, local),
+            low(slots, 2, pairs_n, in_rows // 2, local), low(slots, 2, max(pairs_n - 1, 1), in_rows // 2, local),
+            low(d_tiles, line, rows, width), low(d_tiles, line, rows, width),
+            low(2, max(width, in_rows), plan.attn + plan.mlp), full(2, in_rows, local), full(2, rows, width),
+            full(n_bits + 2, small_rows, local), full(n_bits + 1, small_rows, local), full(2, in_rows, LANES),
+            dma((7,)), dma((2,)), dma((2, 2)), dma((2,)), dma((2,)), dma((2,)), dma((n_down,)),
+            dma((slots, max(2 * n_bits, 1))), dma((slots, max(2 * n_bits, 1))),
+            dma((d_tiles, line)), dma((d_tiles, line)), dma((d_tiles, line)), dma((d_tiles, line)),
+            dma((n_bits + 1,)), dma((n_bits + 1,)), dma((line,)), dma((line,)), dma((line,)), dma((line,)),
+            pltpu.SemaphoreType.REGULAR((2,)),
+        ],
+        compiler_params=pltpu.CompilerParams(
+            collective_id=1, has_side_effects=True, vmem_limit_bytes=63 << 20
+        ),
+        cost_estimate=pl.CostEstimate(flops=80 * 10**9, bytes_accessed=80 << 20, transcendentals=0),
+    )(xhat, cot, att, hidden, da, do, q, k, v, part, wa, wm, lse, sums, *tables, begin)
 
 
 def adam_update(weight, moment_one, moment_two, gradient, step_rate, decay_factor):
@@ -597,21 +994,6 @@
         weight - step_rate * (corrected / (spread + adam_eps) + decay_factor * weight),
         first_new,
         second_new,
-    )
-
-
-def mm(a, b):
-    return jnp.dot(a, b, preferred_element_type=f32)
-
-
-def columns_of(full, axis, masks, step):
-    me = lax.axis_index(axis)
-    return jnp.concatenate(
-        [
-            lax.dynamic_slice_in_dim(full, jnp.bitwise_xor(me, m) * step, step, 1)
-            for m in masks
-        ],
-        axis=1,
     )
 
 
@@ -655,7 +1037,6 @@
 
     me = lax.axis_index("dp")
     plan = Plan(n_dp, n_tensor, own_rows, model, in_rows, local, n_mlp, out_cols)
-    n_bias = column_bias.size
     lane = lax.rem(me, LANES // plan.bias_cols) * plan.bias_cols
     bias_tile = lax.dynamic_update_slice(
         jnp.zeros((16, LANES), bf16), column_bias.astype(bf16), (0, lane)
@@ -664,54 +1045,16 @@
     tables = rotary_tables(position)
     begin_col = begin[:, None]
     (
-        w_attn, w_mlp, w_down, xhat_all, normed, cot_all, q_low, k_low, v_low, attended, lse,
+        w_attn, w_mlp, vectors, xhat_all, cot_sums, cot_all, q_low, k_low, v_low, attended, lse,
         hidden, pre_grad, attn_grad, out_part,
     ) = forward(plan, xhat.astype(bf16), cot_low, in_attn, in_mlp, down_low, small, tables, begin_col)
-    vector_vals = lax.all_gather(vector_params.astype(bf16), "dp", axis=1, tiled=True).astype(f32)
+    down_grad, in_grad, small_grad, parts, shares, dh = backward(
+        plan, xhat_all, cot_all, attended, hidden, pre_grad, attn_grad, q_low, k_low, v_low, out_part,
+        w_attn, w_mlp, lse, cot_sums, tables, begin_col,
+    )
+    vector_vals = vectors[:, :3, LANES:].transpose(1, 0, 2).reshape(3, model).astype(f32)
     gain, out_bias = vector_vals[0], vector_vals[2]
-    mixed = line_scatter(out_part, "tensor")
-    block_out = block_input + (mixed + out_bias)
-
-    keep_masks = list(range(0, n_dp, 2))
-    send_masks = [m + 1 for m in keep_masks]
-    cot_send = columns_of(cot_all, "dp", send_masks, out_cols)
-    cot_keep = columns_of(cot_all, "dp", keep_masks, out_cols)
-    normed_send = columns_of(normed, "dp", send_masks, in_rows)
-    normed_keep = columns_of(normed, "dp", keep_masks, in_rows)
-
-    def down_part(cot):
-        parts = jnp.concatenate([dot_s(attended, cot).astype(bf16), dot_s(hidden, cot).astype(bf16)], axis=0)
-        return parts.reshape(parts.shape[0], n_dp // 2, out_cols).transpose(1, 0, 2)
-
-    def in_part(rows, grads):
-        return dot_s(rows, grads).astype(bf16).reshape(n_dp // 2, in_rows, grads.shape[1])
-
-    down_reduced = cube_scatter(down_part(cot_send), down_part(cot_keep), "dp")
-    in_mlp_reduced = cube_scatter(in_part(normed_send, pre_grad), in_part(normed_keep, pre_grad), "dp")
-
-    dq, dk, dv = attend_backward(q_low, k_low, v_low, attn_grad, lse, tables, begin_col)
-    qkv_grad = jnp.concatenate([dq, dk, dv], axis=1)
-    dh_part = dot_t(qkv_grad, w_attn) + dot_t(pre_grad, w_mlp)
-    dh = line_scatter(dh_part.astype(bf16), "tensor")
-    in_attn_reduced = cube_scatter(in_part(normed_send, qkv_grad), in_part(normed_keep, qkv_grad), "dp")
-
-    bias_grad = jnp.concatenate(
-        [jnp.sum(qkv_grad, axis=0, dtype=f32), jnp.sum(pre_grad, axis=0, dtype=f32)]
-    ).reshape(widths, n_dp, column_bias.shape[1])
-    gain_part = jnp.sum(dh_part * xhat_all.astype(f32), axis=0)
-    shift_part = jnp.sum(dh_part, axis=0)
-    outbias_part = jnp.sum(cot_low.astype(f32), axis=0)
-    vector_grad = jnp.stack([gain_part, shift_part, outbias_part]).reshape(3, n_dp, vector_params.shape[1])
-    small_grad = jnp.concatenate(
-        [
-            bias_grad.transpose(1, 0, 2).reshape(n_dp, -1),
-            vector_grad.transpose(1, 0, 2).reshape(n_dp, -1),
-        ],
-        axis=1,
-    )
-    small_reduced = lax.psum_scatter(small_grad, "dp", scatter_dimension=0, tiled=True)[0]
-    bias_reduced = small_reduced[:n_bias].reshape(column_bias.shape)
-    vector_reduced = lax.psum(small_reduced[n_bias:], "tensor").reshape(vector_params.shape)
+    block_out = block_input + (jnp.sum(parts.astype(f32), axis=0) + out_bias)
 
     dxhat = dh * gain
     input_grad = cot_live + inv_scale * (
@@ -720,14 +1063,22 @@
         - xhat * jnp.mean(dxhat * xhat, axis=-1, keepdims=True)
     )
 
-    in_reduced = jnp.concatenate(
+    bias_full = small_grad[:widths]
+    own_vectors = vector_params.astype(bf16).astype(f32)
+    in_reduced = (
+        in_grad * own_vectors[0][None, :, None] + own_vectors[1][None, :, None] * bias_full[:, None, :]
+    ).transpose(1, 0, 2)
+    down_reduced = down_grad.transpose(0, 2, 1)
+    bias_reduced = lax.dynamic_slice_in_dim(bias_full, me * plan.bias_cols, plan.bias_cols, 1)
+    out_sums = small_grad[8 : 8 + model // local].reshape(-1)
+    vector_reduced = jnp.stack(
         [
-            in_attn_reduced.reshape(in_rows, 3, local),
-            in_mlp_reduced.reshape(in_rows, n_mlp, local),
-        ],
-        axis=1,
-    )
-    down_reduced = down_reduced.reshape(down_weight.shape)
+            jnp.sum(shares[:, 0], axis=(0, 2)),
+            jnp.sum(shares[:, 1], axis=(0, 2)),
+            lax.dynamic_slice_in_dim(out_sums, me * out_cols, out_cols, 0),
+        ]
+    )
+
     in_new, in_one, in_two = adam_update(
         in_weight, in_first, in_second, in_reduced, rate_in, weight_decay
     )

time: 574 us -> 483 us (0.84)
  the two profiles are of different devices: /device:TPU:0 before, /device:TPU:24 now
where the time goes in v3:
time: 483 us; the launch traced here: 475 us
  Pallas kernels  401 us (83%)
  other arithmetic  36.2 us (7%)
  local copies, waits for them, and re-layouts  35.8 us (7%)
    pallas_call x1, Pallas kernels, backward(): pl.pallas_call(partial(backward_kernel, plan), in_specs=[any_space] * 12...  228 us
    pallas_call x1, Pallas kernels, forward(): pl.pallas_call(partial(forward_kernel, plan), in_specs=[any_space] * 6 +...  174 us
    unnamed x56, local copies, waits for them, and re-layouts  22.2 us
    sub x4, other arithmetic, adam_update(): weight - step_rate * (corrected / (spread + adam_eps) + decay_factor * we...  19.1 us

profile of v3, /device:TPU:24, one launch (start us, length us, event | category | flops | bytes accessed | tf_op | source)
XLA Modules:
  0.0 474.6 jit_solution(10668712194184767341)
XLA Ops:
  0.7 0.8 convert_element_type.51
  3.6 0.8 reduce-window.8
  4.6 1.8 reduce_sum.83
  6.8 1.2 copy-done.5
  8.0 1.7 multiply_convert_fusion
  9.9 1.9 multiply_sine_fusion
  11.9 1.7 concatenate.24.ahead
  13.6 1.7 concatenate.25.behind
  15.4 1.7 concatenate.23.own
  17.2 1.1 copy.66.begin
  18.2 1.7 slice.49
  20.5 1.4 copy.75.wm_in
  21.9 2.5 slice.48
  24.4 1.4 copy.77
  25.9 1.2 copy.65.wa_in
  27.0 1.2 convert_element_type.50
  28.2 173.8 %shard_map.254 = (bf16[2048,1536]{1,0:T(8,128)(2,1)}, bf16[2048,2048]{1,0:T(8,128)(2,1)}, bf16[8,16,384]{2,1,0:T(8,128)(2,1)}, bf16[1024,2048]{1,0:T(8,128)(2,1)...) custom-call(bf16[256,2048]{1,0:T(8,128)(2,1)} %get-tuple-element.138, ...), custom_call_target="tpu_custom_call" | custom-call | flops 60000002048 | bytes 83886080 | tf_op jit(solution)/shard_map/pallas_call | solution.py:480
  202.1 227.6 %shard_map.255 = (f32[5,256,512]{2,1,0:T(8,128)}, f32[7,256,512]{2,1,0:T(8,128)}, f32[16,512]{1,0:T(8,128)}, bf16[4,256,2048]{2,1,0:T(8,128)(2,1)}, f32[4,2,256,128]{3,2,1,0:T(8,128)}, /*index=5*/f32[256,2048]{1,0:T(8,128)}) custom-call(bf16[1024,2048]{1,0:T(8,128)(2,1)} %get-tuple-element.35.xhat_in, bf16[1024,2048]{1,0:T(8,128)(2,1)} %get-tuple-element.36.cot_in, ...), custom_call_target="tpu_custom_call" | custom-call | flops 80000000000 | bytes 83886080 | tf_op jit(solution)/shard_map/pallas_call | solution.py:958
  429.7 0.7 slice_bitcast_fusion
  430.5 1.3 slice_reduce_fusion.1
  432.5 3.4 copy.68
  435.9 3.4 copy.69
  439.2 2.1 copy.71
  441.3 8.4 %multiply_subtract_fusion.1 = (f32[5,512,256]{1,2,0:T(8,128)}, f32[5,512,256]{1,2,0:T(8,128)}, f32[5,512,256]{1,2,0:T(8,128)S(1)}) fusion(f32[5,512,256]{1,2,0:T(8,128)} %copy.71, f32[5,256,512]{2,1,0:T(8,128)} %get-tuple-element.54, f32[5,512,256]{1,2,0:T(8,128)} %copy.68, f32[5,512,256]{1,2,0:T(8,128)} %copy.69), kind=kLoop, calls=%fused_computation.11 | loop fusion | flops 9830400 | bytes 18350080 | tf_op jit(solution)/shard_map/sub | solution.py:994
  449.7 3.2 copy.72
  452.9 3.2 copy.73
  456.1 2.1 copy.74
  458.2 9.5 %multiply_subtract_fusion = (f32[256,7,512]{2,0,1:T(8,128)}, f32[256,7,512]{2,0,1:T(8,128)}, f32[256,7,512]{2,0,1:T(8,128)}) fusion(f32[256,7,512]{2,0,1:T(8,128)} %param.18, f32[7,512]{1,0:T(8,128)S(1)} %slice.44, f32[256]{0:T(256)S(1)} %bitcast.41, f32[7,256,512]{2,1,0:T(8,128)} %get-tuple-element.52, f32[256]{0:T(256)S(1)} %bitcast.40, ...), kind=kLoop, calls=%fused_computation.6 | loop fusion | flops 16515072 | bytes 25706496 | tf_op jit(solution)/shard_map/sub | solution.py:994
  467.7 0.8 convert_reduce_fusion
  468.6 1.2 convert_bitcast_fusion
  470.8 2.9 multiply_add_fusion.1
  473.7 0.7 multiply_subtract_fusion.3
  (72 shorter events, 5.2 us)
Async XLA Ops:
  0.6 5.8 %copy-start = (f32[256,2048]{1,0:T(8,128)S(1)}, f32[256,2048]{1,0:T(8,128)}, u32[]{:S(2)}) copy-start(f32[256,2048]{1,0:T(8,128)} %param.15) | copy-start | bytes 6291460
  2.4 0.6 copy-start.10
  4.6 5.1 %copy-start.17 = (f32[256]{0:T(256)}, f32[256]{0:T(256)S(1)}, u32[]{:S(2)}) copy-start(f32[256]{0:T(256)S(1)} %dynamic_slice.9) | copy-start | bytes 3076
  6.4 1.6 copy-start.5
  6.4 3.3 copy-start.8
  8.0 1.7 copy-start.13
  21.9 5.1 %copy-start.2 = (f32[5,512,256]{2,1,0:T(8,128)S(1)}, f32[5,512,256]{2,1,0:T(8,128)}, u32[]{:S(2)}) copy-start(f32[5,512,256]{2,1,0:T(8,128)} %param.19) | copy-start | bytes 7864324
  202.0 229.8 %copy-start.15 = (f32[3,256]{1,0:T(4,128)S(1)}, f32[3,256]{1,0:T(4,128)}, u32[]{:S(2)}) copy-start(f32[3,256]{1,0:T(4,128)} %param.21) | copy-start | bytes 9220
  202.1 229.8 %copy-start.19 = (f32[3,256]{1,0:T(4,128)S(1)}, f32[3,256]{1,0:T(4,128)}, u32[]{:S(2)}) copy-start(f32[3,256]{1,0:T(4,128)} %param.28) | copy-start | bytes 9220
  202.1 229.8 %copy-start.20 = (f32[3,256]{1,0:T(4,128)S(1)}, f32[3,256]{1,0:T(4,128)}, u32[]{:S(2)}) copy-start(f32[3,256]{1,0:T(4,128)} %param.29) | copy-start | bytes 9220
  435.9 3.4 copy-start.3
  456.1 2.1 copy-start.12
  456.1 2.1 copy-start.11
  458.2 9.5 %copy-start.7 = (bf16[4,256,2048]{2,1,0:T(8,128)(2,1)S(1)}, bf16[4,256,2048]{2,1,0:T(8,128)(2,1)}, u32[]{:S(2)}) copy-start(bf16[4,256,2048]{2,1,0:T(8,128)(2,1)} %get-tuple-element.49) | copy-start | bytes 12582916
  467.7 2.1 copy-start.1
  467.7 2.2 copy-start.4
  467.7 2.2 copy-start.9
  467.7 2.2 copy-start.14
  468.5 2.3 copy-start.6
  468.5 2.3 copy-start.18
  470.8 2.9 copy-start.16
  470.8 2.9 copy-start.21
  470.8 2.9 copy-start.22

commit v4 on v3

--- a/solution.py
+++ b/solution.py
@@ -2,6 +2,7 @@
 
 import jax
 import jax.numpy as jnp
+import numpy as np
 from jax import lax
 from jax.experimental import pallas as pl
 from jax.experimental.pallas import tpu as pltpu
@@ -27,29 +28,26 @@
 f32 = jnp.float32
 
 
-def layout(lengths, group_size):
-    seq_ends = jnp.cumsum(lengths)
-    places = jnp.arange(group_size, dtype=jnp.int32)
-    segment = jnp.sum((places[:, None] >= seq_ends[None, :]).astype(jnp.int32), axis=1)
-    starts = jnp.concatenate([jnp.zeros((1,), jnp.int32), seq_ends])
-    picked = segment[:, None] == jnp.arange(lengths.shape[0] + 1, dtype=jnp.int32)[None, :]
-    seq_begin = jnp.sum(jnp.where(picked, starts[None, :], 0), axis=1)
-    live_mask = (segment < lengths.shape[0]).astype(f32)
-    return seq_begin, places - seq_begin, live_mask
-
-
-def rotary_tables(position):
+def angle_tables(rows):
     half_rot = ROT // 2
-    frequency = 10000.0 ** (-2.0 * jnp.arange(half_rot, dtype=f32) / ROT)
-    angles = position.astype(f32)[:, None] * frequency[None, :]
-    cosine, sine = jnp.cos(angles), jnp.sin(angles)
-    rows = position.shape[0]
-    none = jnp.zeros((rows, half_rot), f32)
-    rest = jnp.zeros((rows, HEAD - ROT), f32)
-    own = jnp.concatenate([cosine, cosine, rest + 1.0], axis=1)
-    ahead = jnp.concatenate([-sine, none, rest], axis=1)
-    behind = jnp.concatenate([none, sine, rest], axis=1)
-    return tuple(jnp.concatenate([t] * (LANES // HEAD), axis=1) for t in (own, ahead, behind))
+    frequency = 10000.0 ** (-2.0 * (np.arange(LANES) % half_rot) / ROT)
+    angles = np.arange(rows)[:, None] * frequency[None, :]
+    return np.cos(angles).astype(np.float32), np.sin(angles).astype(np.float32)
+
+
+def ends_of(lengths):
+    ends = [jnp.int32(0)]
+    for j in range(lengths.shape[1]):
+        ends.append(ends[-1] + lengths[0, j])
+    return ends
+
+
+def begins_of(lengths, start, rows):
+    places = start + lax.broadcasted_iota(jnp.int32, (rows, 1), 0)
+    begin = jnp.zeros((rows, 1), jnp.int32)
+    for end in ends_of(lengths)[1:]:
+        begin = jnp.where(places >= end, end, begin)
+    return begin
 
 
 def attend_mask(begin, row_start, rows, stop):
@@ -96,6 +94,63 @@
     t = jnp.tanh(root * a * (1.0 + 0.044715 * square))
     half = 0.5 * (1.0 + t)
     return a * half, half + 0.5 * a * (1.0 - t * t) * (root * (1.0 + 3.0 * 0.044715 * square))
+
+
+class LineSum:
+    def __init__(self, place, line, source, landing, sems):
+        self.place, self.line, self.source, self.landing = place, line, source, landing
+        self.up_send, self.up_recv, self.down_send, self.down_recv = sems
+
+    def copy(self, t, index, up, arriving=False):
+        place = self.place
+        slot = index - 1 if up else self.line - 2 - index
+        return pltpu.make_async_remote_copy(
+            src_ref=self.source(t, index),
+            dst_ref=self.landing(t, slot, up),
+            send_sem=(self.up_send if up else self.down_send).at[t, slot],
+            recv_sem=(self.up_recv if up else self.down_recv).at[t, slot],
+            device_id={"tensor": place + 1 if up != arriving else place - 1},
+            device_id_type=pl.DeviceIdType.MESH,
+        )
+
+    def got(self, t, index, up):
+        return self.landing(t, index - 1 if up else self.line - 2 - index, up)[...].astype(f32)
+
+    def first(self, t):
+        for up in (True, False):
+            @pl.when((self.place == 0) if up else (self.place == self.line - 1))
+            def _():
+                for step in range(self.line - 1):
+                    self.copy(t, self.line - 1 - step if up else step, up).start()
+
+    def hand_on(self, t, up):
+        place, line = self.place, self.line
+        for step in range(line - 1):
+            index = line - 1 - step if up else step
+            hears = (place > 0) & (place < index) if up else (place < line - 1) & (place > index)
+
+            @pl.when(hears)
+            def _():
+                self.copy(t, index, up, True).wait_recv()
+                mine = self.source(t, index)
+                mine[...] = (mine[...].astype(f32) + self.got(t, index, up)).astype(bf16)
+                self.copy(t, index, up).start()
+
+    def last(self, t, target):
+        place, line = self.place, self.line
+        target[...] = self.source(t, place)[...].astype(f32)
+        for up in (True, False):
+            @pl.when((place > 0) if up else (place < line - 1))
+            def _():
+                self.copy(t, place, up, True).wait_recv()
+                target[...] += self.got(t, place, up)
+
+    def sent(self, t):
+        for index in range(self.line):
+            for up in (True, False):
+                @pl.when((self.place < index) if up else (self.place > index))
+                def _():
+                    self.copy(t, index, up).wait_send()
 
 
 class Plan:
@@ -107,6 +162,9 @@
         self.attn, self.mlp = 3 * local, n_mlp * local
         self.down = (1 + n_mlp) * local
         self.bias_cols = local // n_dp
+        self.width = min(256, model // 4)
+        self.d_tiles = model // self.width
+        self.early = 3 * self.d_tiles // 4
         self.bits = [1 << b for b in range(1, n_dp.bit_length() - 1)]
         even = range(2, n_dp, 2)
         self.single = [m for m in even if m.bit_count() == 1]
@@ -129,15 +187,17 @@
 
 def forward_kernel(
     plan,
-    xhat_in, cot_in, wa_in, wm_in, wd_in, small_in, own, ahead, behind, begin,
+    x_in, out_grad_in, w_in, wd_in, small_in, lengths, place_cos, place_sin,
     wa_out, wm_out, small_out, xhat_out, sums_out, cot_out, q_out, k_out, v_out, att_out, lse_out,
-    hidden_out, da_out, do_out, part_out,
+    hidden_out, da_out, do_out, part_out, own_out, ahead_out, behind_out, stats_out, mixed_out,
     wa, wm, wd, small, xs, ns, sums, cs, q, k, v, att, lse, hidden, slope, do,
-    own_sem, out_sem, w_send, w_recv, up_send, up_recv, down_send, down_recv,
+    own, ahead, behind, stats, wide, block, tall_block,
+    own_sem, block_sem, out_sem, w_send, w_recv, up_send, up_recv, down_send, down_recv,
+    sum_up_send, sum_up_recv, sum_down_send, sum_down_recv, ready,
 ):
     n, line = plan.n_dp, plan.n_line
     me, place = lax.axis_index("dp"), lax.axis_index("tensor")
-    rows, local = plan.rows, plan.local
+    rows, local, model = plan.rows, plan.local, plan.model
 
     def owner(mask):
         index = me
@@ -257,10 +317,13 @@
     def span(index):
         return pl.ds(pl.multiple_of(index * rows, rows), rows)
 
+    early = plan.early * plan.width
     outs = [
         (wa, wa_out), (wm, wm_out), (small, small_out), (xs, xhat_out), (sums, sums_out), (cs, cot_out),
         (q, q_out), (k, k_out), (v, v_out), (att, att_out), (lse, lse_out), (hidden, hidden_out),
-        (slope, da_out), (do, do_out), (xs, part_out),
+        (slope, da_out), (do, do_out), (xs.at[:, pl.ds(early, model - early)], part_out),
+        (own, own_out), (ahead, ahead_out), (behind, behind_out), (stats, stats_out),
+        (wide.at[:, pl.ds(0, early)], mixed_out),
     ]
 
     def out_copy(j):
@@ -270,16 +333,38 @@
         for j in which:
             out_copy(j).start()
 
-    loads = [
-        pltpu.make_async_copy(xhat_in, chunk(0, place), own_sem.at[0]),
-        pltpu.make_async_copy(wa_in, wa.at[pl.ds(pl.multiple_of(me * plan.in_rows, plan.in_rows), plan.in_rows), :], own_sem.at[1]),
-        pltpu.make_async_copy(small_in, small.at[me], own_sem.at[2]),
-        pltpu.make_async_copy(wm_in, wm.at[pl.ds(pl.multiple_of(me * plan.in_rows, plan.in_rows), plan.in_rows), :], own_sem.at[3]),
-        pltpu.make_async_copy(wd_in, wd.at[:, pl.ds(pl.multiple_of(me * plan.out_cols, plan.out_cols), plan.out_cols)], own_sem.at[4]),
-        pltpu.make_async_copy(cot_in, chunk(1, place), own_sem.at[5]),
-    ]
-    for load in loads:
-        load.start()
+    w_rows = pl.ds(pl.multiple_of(me * plan.in_rows, plan.in_rows), plan.in_rows)
+    w_cols = pl.ds(pl.multiple_of(me * plan.out_cols, plan.out_cols), plan.out_cols)
+    small_load = pltpu.make_async_copy(small_in, small.at[me], own_sem.at[2])
+
+    def in_load(r):
+        return pltpu.make_async_copy(w_in.at[r], block.at[r % 2], block_sem.at[0, r % 2])
+
+    def down_load(r):
+        return pltpu.make_async_copy(wd_in.at[r], tall_block.at[r % 2], block_sem.at[1, r % 2])
+
+    def round_in(first, stop, target, shift):
+        for r in range(first, stop):
+            in_load(r).wait()
+            target[w_rows, (r - shift) * local : (r - shift + 1) * local] = block[r % 2].astype(bf16)
+            if r + 2 < 3 + plan.n_mlp:
+                in_load(r + 2).start()
+
+    def round_down():
+        for r in range(1 + plan.n_mlp):
+            down_load(r).wait()
+            wd[r * local : (r + 1) * local, w_cols] = tall_block[r % 2].astype(bf16)
+            if r + 2 < 1 + plan.n_mlp:
+                down_load(r + 2).start()
+
+    x_load = pltpu.make_async_copy(x_in, wide, own_sem.at[0])
+    cot_load = pltpu.make_async_copy(out_grad_in, wide, own_sem.at[1])
+    x_load.start()
+    small_load.start()
+    in_load(0).start()
+    in_load(1).start()
+    down_load(0).start()
+    down_load(1).start()
     barrier = pltpu.get_barrier_semaphore()
     for b in [1] + plan.bits if n > 1 else []:
         pl.semaphore_signal(barrier, inc=1, device_id={"dp": owner(b)}, device_id_type=pl.DeviceIdType.MESH)
@@ -299,7 +384,7 @@
         at = span(index)
         gain = jnp.concatenate([small[o, 0:1, LANES:] for o in range(n)], axis=1).astype(f32)
         shift = jnp.concatenate([small[o, 1:2, LANES:] for o in range(n)], axis=1).astype(f32)
-        ns[at, :] = (xs[at, :].astype(f32) * gain + shift).astype(bf16)
+        ns[...] = (xs[at, :].astype(f32) * gain + shift).astype(bf16)
 
     def bias_row(r, first, width):
         per = LANES // plan.bias_cols
@@ -315,7 +400,7 @@
         at = span(index)
         normalize_rows(index)
         for r, target in enumerate((q, k, v)):
-            proj = dot_n(ns[at, :], wa[:, r * local : (r + 1) * local]) + bias_row(r, 0, local)
+            proj = dot_n(ns[...], wa[:, r * local : (r + 1) * local]) + bias_row(r, 0, local)
             if r == 2:
                 target[at, :] = proj.astype(bf16)
             else:
@@ -326,9 +411,10 @@
 
     def mlp_rows(index):
         at = span(index)
+        normalize_rows(index)
         for r in range(plan.n_mlp):
             cols = slice(r * local, (r + 1) * local)
-            pre = dot_n(ns[at, :], wm[:, cols]) + bias_row(3 + r, 0, local)
+            pre = dot_n(ns[...], wm[:, cols]) + bias_row(3 + r, 0, local)
             value, grad = gelu_and_slope(pre)
             hidden[at, cols] = value.astype(bf16)
             slope[at, cols] = grad.astype(bf16)
@@ -340,7 +426,7 @@
         for start in range(0, total, block):
             stop = start + block
             here = pl.ds(start, block)
-            allowed = attend_mask(begin[here, :], start, block, stop)
+            allowed = attend_mask(begins_of(lengths, start, block), start, block, stop)
             query = q[here, lanes]
             results, logs = [], []
             for head in range(LANES // HEAD):
@@ -361,15 +447,33 @@
             lse[here, :] = held
         return carry
 
-    tile = min(512, plan.model)
+    width = plan.width
     tall = min(512, plan.group)
 
-    def out_tile(j, carry):
-        cols = pl.ds(pl.multiple_of(lax.rem(j, plan.model // tile) * tile, tile), tile)
-        at = pl.ds(pl.multiple_of((j // (plan.model // tile)) * tall, tall), tall)
-        total = dot_n(att[at, :], wd[:local, cols]) + dot_n(hidden[at, :], wd[local:, cols])
-        xs[at, cols] = total.astype(bf16)
-        return carry
+    def out_tile(t):
+        cols = pl.ds(pl.multiple_of(t * width, width), width)
+
+        def part(j, carry):
+            at = pl.ds(pl.multiple_of(j * tall, tall), tall)
+            total = dot_n(att[at, :], wd[:local, cols]) + dot_n(hidden[at, :], wd[local:, cols])
+            xs[at, cols] = total.astype(bf16)
+            return carry
+
+        lax.fori_loop(0, plan.group // tall, part, 0)
+
+    def tile_source(t, index):
+        return xs.at[span(index), pl.ds(pl.multiple_of(t * width, width), width)]
+
+    def tile_landing(t, slot, up):
+        at = slot * rows + (0 if up else (line - 1) * rows)
+        return wm.at[pl.ds(pl.multiple_of(at, rows), rows), pl.ds(pl.multiple_of(t * width, width), width)]
+
+    out_sum = LineSum(
+        place, line, tile_source, tile_landing, (sum_up_send, sum_up_recv, sum_down_send, sum_down_recv)
+    )
+
+    def early_tiles(fn):
+        lax.fori_loop(0, plan.early, lambda t, carry: (fn(t), carry)[1], 0)
 
     def back_rows(index):
         at = span(index)
@@ -380,28 +484,63 @@
             grad = dot_t(cs[at, :], wd[(1 + r) * local : (2 + r) * local, :])
             slope[at, cols] = (grad * slope[at, cols].astype(f32)).astype(bf16)
 
-    loads[0].wait()
+    def normalize_own():
+        x_load.wait()
+        value = wide[...]
+        mean = jnp.mean(value, axis=1, keepdims=True)
+        centered = value - mean
+        scale = lax.rsqrt(jnp.mean(centered * centered, axis=1, keepdims=True) + norm_eps)
+        xs[span(place), :] = (centered * scale).astype(bf16)
+        stats[0] = jnp.broadcast_to(mean, (rows, LANES))
+        stats[1] = jnp.broadcast_to(scale, (rows, LANES))
+        cot_load.start()
+
+    def mask_cot():
+        cot_load.wait()
+        places = place * rows + lax.broadcasted_iota(jnp.int32, (rows, 1), 0)
+        cs[span(place), :] = jnp.where(places < ends_of(lengths)[-1], wide[...], 0.0).astype(bf16)
+
+    def make_tables():
+        block_rows = min(QUERY_ROWS, plan.group)
+        ends = ends_of(lengths)
+        for start in range(0, plan.group, block_rows):
+            at = pl.ds(start, block_rows)
+            places = start + lax.broadcasted_iota(jnp.int32, (block_rows, LANES), 0)
+            begin_cos, begin_sin = place_cos[0:1, :], place_sin[0:1, :]
+            for end in ends[1:]:
+                row = pl.ds(jnp.minimum(end, plan.group - 1), 1)
+                begin_cos = jnp.where(places >= end, place_cos[row, :], begin_cos)
+                begin_sin = jnp.where(places >= end, place_sin[row, :], begin_sin)
+            cosine = place_cos[at, :] * begin_cos + place_sin[at, :] * begin_sin
+            sine = place_sin[at, :] * begin_cos - place_cos[at, :] * begin_sin
+            lane = lax.rem(lax.broadcasted_iota(jnp.int32, (block_rows, LANES), 1), HEAD)
+            own[at, :] = jnp.where(lane < ROT, cosine, 1.0)
+            ahead[at, :] = jnp.where(lane < ROT // 2, -sine, 0.0)
+            behind[at, :] = jnp.where((lane >= ROT // 2) & (lane < ROT), sine, 0.0)
+
+    normalize_own()
     z_start(0, 1)
-    loads[2].wait()
+    small_load.wait()
     w_start(3)
-    loads[1].wait()
+    round_in(0, 3, wa, 0)
     w_start(0)
-    loads[3].wait()
-    loads[4].wait()
-    loads[5].wait()
+    round_in(3, 3 + plan.n_mlp, wm, 3)
+    mask_cot()
+    round_down()
+    make_tables()
+    sums[...] = jnp.zeros_like(sums)
+    lse[...] = jnp.zeros_like(lse)
+    write(15, 16, 17, 18)
     w_arrive(0, plan.single)
     w_start(1)
     w_arrive(3, plan.single)
-    if line > 1:
-        z_arrive(0, 1)
-        cot_start(1)
+    z_arrive(0, 1)
+    cot_start(1)
     w_arrive(3, plan.several)
     w_arrive(0, plan.several)
     w_arrive(3, plan.odd)
     w_arrive(0, plan.odd)
     write(0, 2)
-    sums[...] = jnp.zeros_like(sums)
-    lse[...] = jnp.zeros_like(lse)
     at_distance(0, attn_rows)
     if line > 2:
         at_distance(1, attn_rows)
@@ -419,21 +558,31 @@
         jnp.maximum(place - near, 0), jnp.minimum(place + near, line - 1) + 1,
         lambda c, carry: (mlp_rows(c), carry)[1], 0,
     )
-    if line > 1:
-        if line > 2:
-            z_arrive(0, line - 1)
-            cot_start(line - 1)
-        at_distance(line - 1, lambda c: (attn_rows(c), mlp_rows(c))[0])
+    if line > 2:
+        z_arrive(0, line - 1)
+        cot_start(line - 1)
+    at_distance(line - 1, lambda c: (attn_rows(c), mlp_rows(c))[0])
     write(3, 6, 7, 8, 11)
     pairs = local // LANES
     lax.fori_loop(0, pairs // 2, attend, 0)
     w_arrive(2, plan.single)
+    out_copy(1).wait()
+    for mask in range(1, n):
+        for half in halves(1):
+            w_copy(1, mask, half).wait_send()
+
+    @pl.when(place < line - 1)
+    def _():
+        pl.semaphore_signal(ready, inc=1, device_id={"tensor": place + 1}, device_id_type=pl.DeviceIdType.MESH)
+
+    @pl.when(place > 0)
+    def _():
+        pl.semaphore_signal(ready, inc=1, device_id={"tensor": place - 1}, device_id_type=pl.DeviceIdType.MESH)
+
     lax.fori_loop(pairs // 2, pairs, attend, 0)
     write(9, 10)
-    if line > 1:
-        z_arrive(1, 1)
+    z_arrive(1, 1)
     w_arrive(2, plan.several)
-    w_arrive(2, plan.odd)
     out_copy(3).wait()
     for step in range(1, line):
         for up in (True, False):
@@ -441,71 +590,104 @@
             @pl.when(left & sends(step, up))
             def _():
                 z_copy(0, step, up).wait_send()
-    lax.fori_loop(0, (plan.model // tile) * (plan.group // tall), out_tile, 0)
+    pl.semaphore_wait(ready, beside)
+    w_arrive(2, plan.odd)
+
+    def first_tile(t):
+        out_tile(t)
+        out_sum.first(t)
+
+    early_tiles(first_tile)
+    lax.fori_loop(plan.early, plan.d_tiles, lambda t, carry: (out_tile(t), carry)[1], 0)
     write(14)
     at_distance(0, back_rows)
-    if line > 1:
+    if line > 2:
         at_distance(1, back_rows)
-    for step in range(2, line):
+    for step in range(2, line - 1):
         z_arrive(1, step)
         at_distance(step, back_rows)
+
+    def running(near_end):
+        for up in (True, False):
+            now = (place < line // 2) if up == near_end else (place >= line // 2)
+
+            @pl.when(now)
+            def _():
+                for step in range(1, line):
+                    z_sent(1, step, up)
+                early_tiles(lambda t: out_sum.hand_on(t, up))
+
+    running(True)
+    if line > 2:
+        z_arrive(1, line - 1)
+    running(False)
+    at_distance(line - 1, back_rows)
     write(4, 5, 12, 13)
-
-    for flow in range(4):
+    early_tiles(lambda t: out_sum.last(t, wide.at[:, pl.ds(pl.multiple_of(t * width, width), width)]))
+    write(19)
+
+    early_tiles(out_sum.sent)
+    for flow in (0, 2, 3):
         for mask in range(1, n):
             for half in halves(flow):
                 w_copy(flow, mask, half).wait_send()
-    for step in range(1, line):
-        for up in (True, False):
-            z_sent(1, step, up)
     for j in range(len(outs)):
-        if j != 3:
+        if j not in (1, 3):
             out_copy(j).wait()
 
 
-def forward(plan, xhat, cot, wa, wm, wd, small, tables, begin):
+def forward(plan, x, out_grad, w, wd, small, lengths):
     any_space = pl.BlockSpec(memory_space=pl.ANY)
     vmem = pl.BlockSpec(memory_space=pltpu.VMEM)
-    n, line, group, model, local = plan.n_dp, plan.n_line, plan.group, plan.model, plan.local
+    n, line, group, model, local, rows = (
+        plan.n_dp, plan.n_line, plan.group, plan.model, plan.local, plan.rows
+    )
     low = lambda *shape: jax.ShapeDtypeStruct(shape, bf16)
+    full = lambda *shape: jax.ShapeDtypeStruct(shape, f32)
+    early = plan.early * plan.width
     out_shape = [
         low(model, plan.attn), low(model, plan.mlp), low(n, 16, LANES + plan.out_cols),
-        low(group, model), jax.ShapeDtypeStruct((8, model), f32), low(group, model),
+        low(group, model), full(8, model), low(group, model),
         low(group, local), low(group, local), low(group, local), low(group, local),
-        jax.ShapeDtypeStruct((group, LANES), f32),
-        low(group, plan.mlp), low(group, plan.mlp), low(group, local), low(group, model),
+        full(group, LANES),
+        low(group, plan.mlp), low(group, plan.mlp), low(group, local), low(group, model - early),
+        full(group, LANES), full(group, LANES), full(group, LANES), full(2, rows, LANES), full(rows, early),
     ]
     scratch = lambda s: pltpu.VMEM(s.shape, s.dtype)
     dma = pltpu.SemaphoreType.DMA
     return pl.pallas_call(
         partial(forward_kernel, plan),
-        in_specs=[any_space] * 6 + [vmem] * 4,
-        out_specs=[any_space] * 15,
+        in_specs=[any_space] * 5 + [pl.BlockSpec(memory_space=pltpu.SMEM)] + [vmem] * 2,
+        out_specs=[any_space] * 20,
         out_shape=out_shape,
         scratch_shapes=[scratch(s) for s in out_shape[:2]]
         + [pltpu.VMEM((plan.down, model), bf16)]
         + [scratch(s) for s in out_shape[2:4]]
-        + [pltpu.VMEM((group, model), bf16)]
+        + [pltpu.VMEM((rows, model), bf16)]
         + [scratch(s) for s in out_shape[4:14]]
-        + [dma((6,)), dma((15,)), dma((8 * n,)), dma((8 * n,))]
-        + [dma((2 * line,))] * 4,
+        + [scratch(s) for s in out_shape[15:19]]
+        + [pltpu.VMEM((rows, model), f32), pltpu.VMEM((2,) + w.shape[1:], f32), pltpu.VMEM((2,) + wd.shape[1:], f32)]
+        + [dma((3,)), dma((2, 2)), dma((20,)), dma((8 * n,)), dma((8 * n,))]
+        + [dma((2 * line,))] * 4
+        + [dma((plan.early, max(line - 1, 1)))] * 4
+        + [pltpu.SemaphoreType.REGULAR],
         compiler_params=pltpu.CompilerParams(
             collective_id=0, has_side_effects=True, vmem_limit_bytes=63 << 20
         ),
         cost_estimate=pl.CostEstimate(flops=60 * 10**9, bytes_accessed=80 << 20, transcendentals=0),
-    )(xhat, cot, wa, wm, wd, small, *tables, begin)
+    )(x, out_grad, w, wd, small, lengths, *angle_tables(group))
 
 
 def backward_kernel(
     plan,
     xhat_in, cot_in, att_in, hidden_in, da_in, do_in, q_in, k_in, v_in, part_in, wa_in, wm_in,
-    lse, sums_in, own, ahead, behind, begin,
-    down_out, in_out, small_out, part_out, rows_out, dh_out,
+    lse, sums_in, own, ahead, behind, lengths,
+    down_out, in_out, small_out, mixed_out, rows_out, dh_out,
     turned, stage, og, da, qkv, do, k_sum, v_sum, sent, core_in, held, cube_in, up_in, down_in,
-    w_tile, fin, dh_fin, small, small_in, shares,
+    part, part_up, part_down, w_tile, fin, fin_turned, dh_fin, small, small_in, shares,
     load_sem, stage_sem, tile_sem, fin_sem, dh_sem, core_send, core_recv, cube_send, cube_recv,
-    up_send, up_recv, down_send, down_recv, small_send, small_recv, part_send, part_recv,
-    share_send, share_recv, credit,
+    up_send, up_recv, down_send, down_recv, part_up_send, part_up_recv, part_down_send, part_down_recv,
+    small_send, small_recv, share_send, share_recv, credit,
 ):
     n, line = plan.n_dp, plan.n_line
     me, place = lax.axis_index("dp"), lax.axis_index("tensor")
@@ -537,6 +719,7 @@
         (k_in, qkv.at[:, pl.ds(local, local)]),
         (v_in, qkv.at[:, pl.ds(2 * local, local)]),
         (do_in, do),
+        (part_in, part),
     ]
     for j, (a, b) in enumerate(whole):
         pltpu.make_async_copy(a, b, load_sem.at[j]).start()
@@ -553,15 +736,6 @@
             barrier, inc=1, device_id={"tensor": lax.rem(place + d, line)}, device_id_type=MESH
         )
 
-    def part_copy(d, arriving):
-        source = lax.rem(place + line - d, line) if arriving else place
-        target = place if arriving else lax.rem(place + d, line)
-        return pltpu.make_async_remote_copy(
-            src_ref=part_in.at[pl.ds(pl.multiple_of(target * rows, rows), rows), :],
-            dst_ref=part_out.at[source], send_sem=part_send.at[d], recv_sem=part_recv.at[d],
-            device_id={"tensor": lax.rem(place + d, line)}, device_id_type=MESH,
-        )
-
     def share_copy(d, arriving):
         source = lax.rem(place + line - d, line) if arriving else place
         return pltpu.make_async_remote_copy(
@@ -570,9 +744,6 @@
             device_id={"tensor": lax.rem(place + d, line)}, device_id_type=MESH,
         )
 
-    part_own = pltpu.make_async_copy(
-        part_in.at[pl.ds(pl.multiple_of(place * rows, rows), rows), :], part_out.at[place], part_send.at[0]
-    )
     share_own = pltpu.make_async_copy(shares, rows_out.at[place], share_send.at[0])
 
     def turn_columns(source, masks, first, started=False):
@@ -611,7 +782,7 @@
         source = {"down": og, "mlp": da, "attn": qkv}[name]
         return source[:, pl.ds(pl.multiple_of(t * local, local), local)]
 
-    send_rows, keep_rows = pl.ds(0, pairs_n * in_rows), pl.ds(pairs_n * in_rows, pairs_n * in_rows)
+    piece = min(2, pairs_n) * in_rows
 
     def send_core(name):
         tiles = flows[name][0]
@@ -622,7 +793,10 @@
             @pl.when(t >= 2)
             def _():
                 core_copy(name, t - 2).wait_send()
-            sent[lax.rem(t, 2)] = dot_n(turned[send_rows, :], operand(name, t)).astype(bf16)
+            for at in range(0, pairs_n * in_rows, piece):
+                sent[lax.rem(t, 2), at : at + piece, :] = dot_n(
+                    turned[at : at + piece, :], operand(name, t)
+                ).astype(bf16)
             core_copy(name, t).start()
             return carry
 
@@ -634,12 +808,13 @@
         tiles, base, _ = flows[name]
 
         def step(t, carry):
-            total = dot_n(turned[keep_rows, :], operand(name, t))
             core_copy(name, t).wait_recv()
-            total = total + core_in[t].astype(f32)
-            for j in range(pairs_n):
-                for half in range(2):
-                    at = j * in_rows + half * half_rows
+            for first in range(0, pairs_n * in_rows, piece):
+                kept = pairs_n * in_rows + first
+                total = dot_n(turned[kept : kept + piece, :], operand(name, t))
+                total = total + core_in[t, first : first + piece, :].astype(f32)
+                for at in range(0, piece, half_rows):
+                    j, half = divmod((first + at) // half_rows, 2)
                     held[base + t, half, position(2 * j, orders[half])] = total[at : at + half_rows].astype(bf16)
             for half in range(2):
                 if n_bits:
@@ -654,17 +829,18 @@
         tiles, base, result = flows[name]
         count = pairs_n >> (phase + 1)
         first = pairs_n - 2 * count
-        target = down_out if name == "down" else in_out
+        target, depth = (down_out, 1) if name == "down" else (in_out, 2)
 
         def fin_copy(t):
-            return pltpu.make_async_copy(fin.at[lax.rem(t, 2)], target.at[result + t], fin_sem.at[lax.rem(t, 2)])
+            source = fin_turned if name == "down" else fin.at[lax.rem(t, 2)]
+            return pltpu.make_async_copy(source, target.at[result + t], fin_sem.at[lax.rem(t, 2)])
 
         def step(t, carry):
             slot = base + t
             if phase == n_bits - 1:
-                @pl.when(t >= 2)
+                @pl.when(t >= depth)
                 def _():
-                    fin_copy(t - 2).wait()
+                    fin_copy(t - depth).wait()
             for half in range(2):
                 cube_copy(slot, half, phase).wait_recv()
                 total = (
@@ -677,6 +853,8 @@
                 else:
                     fin[lax.rem(t, 2), half * half_rows : (half + 1) * half_rows, :] = total[0]
             if phase == n_bits - 1:
+                if name == "down":
+                    fin_turned[...] = fin[lax.rem(t, 2)].T
                 fin_copy(t).start()
                 if name != "down":
                     weight = w_tile[0 if name == "attn" else 1, 0:in_rows, pl.ds(pl.multiple_of(t * local, local), local)].astype(f32)
@@ -689,7 +867,7 @@
 
         lax.fori_loop(0, tiles, step, 0)
         if phase == n_bits - 1:
-            for t in range(max(tiles - 2, 0), tiles):
+            for t in range(max(tiles - depth, 0), tiles):
                 fin_copy(t).wait()
 
     def cube_sent(name):
@@ -716,7 +894,7 @@
         for start in range(0, group, block):
             stop = start + block
             here = pl.ds(start, block)
-            allowed = attend_mask(begin[here, :], start, block, stop)
+            allowed = attend_mask(begins_of(lengths, start, block), start, block, stop)
             q_sum = jnp.zeros((block, LANES), f32)
             for head in range(LANES // HEAD):
                 mine = head_lanes(block, head)
@@ -742,8 +920,7 @@
         qkv[:, v_lanes] = v_sum[...].astype(bf16)
         return carry
 
-    width = min(256, model)
-    d_tiles = model // width
+    width, d_tiles = plan.width, plan.d_tiles
 
     def tile_loads(t):
         at = pl.ds(pl.multiple_of(t * width, width), width)
@@ -753,69 +930,50 @@
             pltpu.make_async_copy(wm_in.at[at, :], w_tile.at[slot, pl.ds(0, width), pl.ds(plan.attn, plan.mlp)], tile_sem.at[slot, 1]),
         )
 
-    def line_copy(t, index, up, arriving=False):
-        at = pl.ds(pl.multiple_of(index * rows, rows), rows)
+    def tile_of(buffer):
+        def source(t, index):
+            return buffer.at[
+                pl.ds(pl.multiple_of(index * rows, rows), rows),
+                pl.ds(pl.multiple_of(t * width, width), width),
+            ]
+        return source
+
+    dh_sum = LineSum(
+        place, line, tile_of(og), lambda t, slot, up: (up_in if up else down_in).at[t, slot],
+        (up_send, up_recv, down_send, down_recv),
+    )
+    late = d_tiles - plan.early
+    out_sum = LineSum(
+        place, line, tile_of(part), lambda t, slot, up: (part_up if up else part_down).at[t, slot],
+        (part_up_send, part_up_recv, part_down_send, part_down_recv),
+    )
+
+    def sum_copy(target, t):
         cols = pl.ds(pl.multiple_of(t * width, width), width)
-        return pltpu.make_async_remote_copy(
-            src_ref=og.at[at, cols],
-            dst_ref=(up_in if up else down_in).at[t, index if up else line - 1 - index],
-            send_sem=(up_send if up else down_send).at[t, index],
-            recv_sem=(up_recv if up else down_recv).at[t, index],
-            device_id={"tensor": place + 1 if up != arriving else place - 1}, device_id_type=MESH,
-        )
-
-    def line_first(t):
-        for up in (True, False):
-            @pl.when((place == 0) if up else (place == line - 1))
+        return pltpu.make_async_copy(dh_fin.at[lax.rem(t, 2)], target.at[:, cols], dh_sem.at[lax.rem(t, 2)])
+
+    def finish(flow, target, count):
+        def step(t):
+            @pl.when(t >= 2)
             def _():
-                for step in range(line - 1):
-                    line_copy(t, line - 1 - step if up else step, up).start()
-
-    def line_pass(t, step):
-        cols = pl.ds(pl.multiple_of(t * width, width), width)
-        for up in (True, False):
-            index = line - 1 - step if up else step
-            at = pl.ds(index * rows, rows)
-            hears = (place > 0) & (place < index) if up else (place < line - 1) & (place > index)
-
-            @pl.when(hears)
-            def _():
-                line_copy(t, index, up, True).wait_recv()
-                got = (up_in if up else down_in)[t, index if up else line - 1 - index]
-                og[at, cols] = (og[at, cols].astype(f32) + got.astype(f32)).astype(bf16)
-                line_copy(t, index, up).start()
-
-    def line_last(t):
-        cols = pl.ds(pl.multiple_of(t * width, width), width)
-        at = pl.ds(pl.multiple_of(place * rows, rows), rows)
-        slot = lax.rem(t, 2)
-
-        @pl.when(t >= 2)
-        def _():
-            dh_copy(t - 2).wait()
-        dh_fin[slot] = og[at, cols].astype(f32)
-        for up in (True, False):
-            @pl.when((place > 0) if up else (place < line - 1))
-            def _():
-                line_copy(t, place, up, True).wait_recv()
-                buffer = up_in if up else down_in
-                dh_fin[slot] += buffer[t, place if up else line - 1 - place].astype(f32)
-        dh_copy(t).start()
-
-    def dh_copy(t):
-        cols = pl.ds(pl.multiple_of(t * width, width), width)
-        return pltpu.make_async_copy(dh_fin.at[lax.rem(t, 2)], dh_out.at[:, cols], dh_sem.at[lax.rem(t, 2)])
-
-    def line_sent(t):
-        for index in range(line):
+                sum_copy(target, t - 2).wait()
+            flow.last(t, dh_fin.at[lax.rem(t, 2)])
+            sum_copy(target, t).start()
+
+        tiles(0, count, step)
+        for t in range(max(count - 2, 0), count):
+            sum_copy(target, t).wait()
+
+    def tiles(first, stop, fn):
+        lax.fori_loop(first, stop, lambda t, carry: (fn(t), carry)[1], 0)
+
+    def hand_on(flow):
+        def step(t):
             for up in (True, False):
-                goes = (place < index) if up else (place > index)
-
-                @pl.when(goes)
-                def _():
-                    line_copy(t, index, up).wait_send()
-
-    def dh_tile(t, carry):
+                flow.hand_on(t, up)
+        return step
+
+    def dh_tile(t):
         slot = lax.rem(t, 2)
         @pl.when(t + 1 < d_tiles)
         def _():
@@ -825,8 +983,7 @@
             load.wait()
         total = dot_t(qkv[...], w_tile[slot, 0:width, : plan.attn]) + dot_t(da[...], w_tile[slot, 0:width, plan.attn :])
         og[:, pl.ds(pl.multiple_of(t * width, width), width)] = total.astype(bf16)
-        line_first(t)
-        return carry
+        dh_sum.first(t)
 
     def small_copy(j):
         return pltpu.make_async_remote_copy(
@@ -848,23 +1005,16 @@
     send_masks, keep_masks = [2 * j + 1 for j in range(pairs_n)], [2 * j for j in range(pairs_n)]
     turn_columns(cot_in, send_masks, 0)
     pl.semaphore_wait(barrier, 1 + n_bits + line - 1)
-    part_own.start()
-    for d in range(1, line):
-        part_copy(d, False).start()
+    loaded(7)
+    tiles(0, late, out_sum.first)
     loaded(0, 1)
     send_core("down")
     turn_columns(cot_in, keep_masks, pairs_n)
     keep_core("down")
-    loaded(2)
-    turn_columns(xhat_in, send_masks, 0)
-    send_core("mlp")
-    turn_columns(xhat_in, keep_masks, pairs_n)
-    keep_core("mlp")
-    loaded(3, 4, 5, 6)
+    loaded(2, 3, 4, 5, 6)
     pairs = local // LANES
     lax.fori_loop(0, pairs // 2, attend, 0)
-    for phase in range(n_bits - 1):
-        cube_step("down", phase)
+    tiles(0, late, hand_on(out_sum))
     lax.fori_loop(pairs // 2, pairs, attend, 0)
     for r in range(3 + n_mlp):
         block = qkv[:, r * local : (r + 1) * local] if r < 3 else da[:, (r - 3) * local : (r - 2) * local]
@@ -872,9 +1022,17 @@
     for r in range(model // local):
         small[0, 8 + r : 9 + r, :] = sums_in[0:1, r * local : (r + 1) * local]
     small_copy(0).start()
-    lax.fori_loop(0, d_tiles, dh_tile, 0)
+    some = min(3, d_tiles)
+    tiles(0, some, dh_tile)
     for phase in range(n_bits - 1):
-        cube_step("mlp", phase)
+        cube_step("down", phase)
+    turn_columns(xhat_in, send_masks, 0)
+    send_core("mlp")
+    turn_columns(xhat_in, keep_masks, pairs_n)
+    keep_core("mlp")
+    finish(out_sum, mixed_out, late)
+    tiles(some, d_tiles, dh_tile)
+    tiles(0, d_tiles // 4, hand_on(dh_sum))
     small_step(0)
     cube_step("down", n_bits - 1)
     cube_sent("down")
@@ -893,63 +1051,44 @@
     ]
     for w in weights:
         w.start()
-
-    def passes(first, stop):
-        def step(t, carry):
-            for s in range(line - 1):
-                line_pass(t, s)
-            return carry
-        lax.fori_loop(first, stop, step, 0)
-
-    passes(0, d_tiles // 2)
+    tiles(d_tiles // 4, d_tiles // 2, hand_on(dh_sum))
+    for phase in range(n_bits - 1):
+        cube_step("mlp", phase)
+    tiles(d_tiles // 2, 3 * d_tiles // 4, hand_on(dh_sum))
     for w in weights:
         w.wait()
     cube_step("mlp", n_bits - 1)
-    passes(d_tiles // 2, d_tiles)
+    tiles(3 * d_tiles // 4, d_tiles, hand_on(dh_sum))
     for phase in range(n_bits):
         cube_step("attn", phase)
     share_own.start()
     for d in range(1, line):
         share_copy(d, False).start()
-
-    def last(t, carry):
-        line_last(t)
-        return carry
-
-    lax.fori_loop(0, d_tiles, last, 0)
-    for t in range(max(d_tiles - 2, 0), d_tiles):
-        dh_copy(t).wait()
+    finish(dh_sum, dh_out, d_tiles)
     small_done = pltpu.make_async_copy(small.at[n_bits + 1], small_out, load_sem.at[0])
     small_done.start()
     cube_sent("mlp")
     cube_sent("attn")
-
-    def sent_all(t, carry):
-        line_sent(t)
-        return carry
-
-    lax.fori_loop(0, d_tiles, sent_all, 0)
+    tiles(0, d_tiles, dh_sum.sent)
+    tiles(0, late, out_sum.sent)
     for j in range(n_bits + 1):
         small_copy(j).wait_send()
-    part_own.wait()
     share_own.wait()
     for d in range(1, line):
-        part_copy(d, False).wait_send()
-        part_copy(d, True).wait_recv()
         share_copy(d, False).wait_send()
         share_copy(d, True).wait_recv()
     small_done.wait()
 
 
-def backward(plan, xhat, cot, att, hidden, da, do, q, k, v, part, wa, wm, lse, sums, tables, begin):
+def backward(plan, xhat, cot, att, hidden, da, do, q, k, v, part, wa, wm, lse, sums, tables, lengths):
     any_space = pl.BlockSpec(memory_space=pl.ANY)
     vmem = pl.BlockSpec(memory_space=pltpu.VMEM)
     n, line, group, model, local = plan.n_dp, plan.n_line, plan.group, plan.model, plan.local
     rows, in_rows, n_bits, pairs_n = plan.rows, plan.in_rows, len(plan.bits), n // 2
     n_down = 1 + plan.n_mlp
     small_rows = 8 + -(-(model // local) // 8) * 8
-    width = min(256, model)
-    d_tiles = model // width
+    width, d_tiles, steps = plan.width, plan.d_tiles, max(line - 1, 1)
+    late = d_tiles - plan.early
     low = lambda *shape: pltpu.VMEM(shape, bf16)
     full = lambda *shape: pltpu.VMEM(shape, f32)
     dma = pltpu.SemaphoreType.DMA
@@ -957,11 +1096,11 @@
     slots = n_down + plan.n_mlp
     return pl.pallas_call(
         partial(backward_kernel, plan),
-        in_specs=[any_space] * 12 + [vmem] * 6,
+        in_specs=[any_space] * 12 + [vmem] * 5 + [pl.BlockSpec(memory_space=pltpu.SMEM)],
         out_specs=[any_space] * 6,
         out_shape=[
-            out(f32, n_down, in_rows, local), out(f32, 3 + plan.n_mlp, in_rows, local),
-            out(f32, small_rows, local), out(bf16, line, rows, model),
+            out(f32, n_down, local, in_rows), out(f32, 3 + plan.n_mlp, in_rows, local),
+            out(f32, small_rows, local), out(f32, rows, late * width),
             out(f32, line, 2, in_rows, LANES), out(f32, rows, model),
         ],
         scratch_shapes=[
@@ -969,20 +1108,22 @@
             low(group, plan.attn), low(group, local), full(group, LANES), full(group, LANES),
             low(2, pairs_n * in_rows, local), low(n_down, pairs_n * in_rows, local),
             low(slots, 2, pairs_n, in_rows // 2, local), low(slots, 2, max(pairs_n - 1, 1), in_rows // 2, local),
-            low(d_tiles, line, rows, width), low(d_tiles, line, rows, width),
-            low(2, max(width, in_rows), plan.attn + plan.mlp), full(2, in_rows, local), full(2, rows, width),
+            low(d_tiles, steps, rows, width), low(d_tiles, steps, rows, width),
+            low(group, late * width), low(late, steps, rows, width), low(late, steps, rows, width),
+            low(2, max(width, in_rows), plan.attn + plan.mlp), full(2, in_rows, local), full(local, in_rows), full(2, rows, width),
             full(n_bits + 2, small_rows, local), full(n_bits + 1, small_rows, local), full(2, in_rows, LANES),
-            dma((7,)), dma((2,)), dma((2, 2)), dma((2,)), dma((2,)), dma((2,)), dma((n_down,)),
+            dma((8,)), dma((2,)), dma((2, 2)), dma((2,)), dma((2,)), dma((2,)), dma((n_down,)),
             dma((slots, max(2 * n_bits, 1))), dma((slots, max(2 * n_bits, 1))),
-            dma((d_tiles, line)), dma((d_tiles, line)), dma((d_tiles, line)), dma((d_tiles, line)),
-            dma((n_bits + 1,)), dma((n_bits + 1,)), dma((line,)), dma((line,)), dma((line,)), dma((line,)),
+            dma((d_tiles, steps)), dma((d_tiles, steps)), dma((d_tiles, steps)), dma((d_tiles, steps)),
+            dma((late, steps)), dma((late, steps)), dma((late, steps)), dma((late, steps)),
+            dma((n_bits + 1,)), dma((n_bits + 1,)), dma((line,)), dma((line,)),
             pltpu.SemaphoreType.REGULAR((2,)),
         ],
         compiler_params=pltpu.CompilerParams(
             collective_id=1, has_side_effects=True, vmem_limit_bytes=63 << 20
         ),
         cost_estimate=pl.CostEstimate(flops=80 * 10**9, bytes_accessed=80 << 20, transcendentals=0),
-    )(xhat, cot, att, hidden, da, do, q, k, v, part, wa, wm, lse, sums, *tables, begin)
+    )(xhat, cot, att, hidden, da, do, q, k, v, part, wa, wm, lse, sums, *tables, lengths)
 
 
 def adam_update(weight, moment_one, moment_two, gradient, step_rate, decay_factor):
@@ -1023,38 +1164,29 @@
     n_mlp = widths - 3
     attn_width, mlp_width = 3 * local, n_mlp * local
 
-    in_attn = in_weight[:, :3].astype(bf16).reshape(in_rows, attn_width)
-    in_mlp = in_weight[:, 3:].astype(bf16).reshape(in_rows, mlp_width)
-    down_low = down_weight.astype(bf16).reshape(widths_down(down_weight), out_cols)
-
-    centered = block_input - jnp.mean(block_input, axis=-1, keepdims=True)
-    inv_scale = lax.rsqrt(jnp.mean(centered * centered, axis=-1, keepdims=True) + norm_eps)
-    xhat = centered * inv_scale
-    begin, position, live = layout(seq_lengths[0], group)
-    own_live = lax.dynamic_slice_in_dim(live, lax.axis_index("tensor") * own_rows, own_rows)
-    cot_live = out_grad * own_live[:, None]
-    cot_low = cot_live.astype(bf16)
-
     me = lax.axis_index("dp")
     plan = Plan(n_dp, n_tensor, own_rows, model, in_rows, local, n_mlp, out_cols)
-    lane = lax.rem(me, LANES // plan.bias_cols) * plan.bias_cols
-    bias_tile = lax.dynamic_update_slice(
-        jnp.zeros((16, LANES), bf16), column_bias.astype(bf16), (0, lane)
-    )
-    small = jnp.concatenate([bias_tile, jnp.pad(vector_params.astype(bf16), ((0, 13), (0, 0)))], axis=1)
-    tables = rotary_tables(position)
-    begin_col = begin[:, None]
+    share = LANES // plan.bias_cols
+    lane = lax.broadcasted_iota(jnp.int32, (widths, LANES), 1) // plan.bias_cols
+    bias_tile = jnp.where(lane == lax.rem(me, share), jnp.tile(column_bias, (1, share)), 0.0)
+    small = jnp.concatenate(
+        [jnp.pad(bias_tile, ((0, 16 - widths), (0, 0))), jnp.pad(vector_params, ((0, 13), (0, 0)))], axis=1
+    ).astype(bf16)
     (
         w_attn, w_mlp, vectors, xhat_all, cot_sums, cot_all, q_low, k_low, v_low, attended, lse,
-        hidden, pre_grad, attn_grad, out_part,
-    ) = forward(plan, xhat.astype(bf16), cot_low, in_attn, in_mlp, down_low, small, tables, begin_col)
-    down_grad, in_grad, small_grad, parts, shares, dh = backward(
+        hidden, pre_grad, attn_grad, out_part, own, ahead, behind, stats, mixed_early,
+    ) = forward(plan, block_input, out_grad, in_weight.transpose(1, 0, 2), down_weight, small, seq_lengths)
+    down_grad, in_grad, small_grad, mixed_late, shares, dh = backward(
         plan, xhat_all, cot_all, attended, hidden, pre_grad, attn_grad, q_low, k_low, v_low, out_part,
-        w_attn, w_mlp, lse, cot_sums, tables, begin_col,
+        w_attn, w_mlp, lse, cot_sums, (own, ahead, behind), seq_lengths,
     )
     vector_vals = vectors[:, :3, LANES:].transpose(1, 0, 2).reshape(3, model).astype(f32)
     gain, out_bias = vector_vals[0], vector_vals[2]
-    block_out = block_input + (jnp.sum(parts.astype(f32), axis=0) + out_bias)
+    block_out = block_input + (jnp.concatenate([mixed_early, mixed_late], axis=1) + out_bias)
+    mean, inv_scale = stats[0, :, :1], stats[1, :, :1]
+    xhat = (block_input - mean) * inv_scale
+    places = lax.axis_index("tensor") * own_rows + lax.broadcasted_iota(jnp.int32, (own_rows, 1), 0)
+    cot_live = jnp.where(places < jnp.sum(seq_lengths), out_grad, 0.0)
 
     dxhat = dh * gain
     input_grad = cot_live + inv_scale * (
@@ -1068,7 +1200,7 @@
     in_reduced = (
         in_grad * own_vectors[0][None, :, None] + own_vectors[1][None, :, None] * bias_full[:, None, :]
     ).transpose(1, 0, 2)
-    down_reduced = down_grad.transpose(0, 2, 1)
+    down_reduced = down_grad
     bias_reduced = lax.dynamic_slice_in_dim(bias_full, me * plan.bias_cols, plan.bias_cols, 1)
     out_sums = small_grad[8 : 8 + model // local].reshape(-1)
     vector_reduced = jnp.stack(

time: 483 us -> 456 us (0.944)
  local copies, waits for them, and re-layouts: 35.8 us -> 2.77 us
  Pallas kernels: 401 us -> 416 us
  other arithmetic: 36.2 us -> 27.4 us
    unnamed x56 -> x40, local copies, waits for them, and re-layouts: 22.2 us -> 0.22 us
    pallas_call x1, Pallas kernels: 174 us -> 194 us  [forward(): pl.pallas_call(partial(forward_kernel, plan), in_specs=[any_space] * 5 +...]
    sub x4, other arithmetic: 19.1 us -> 13.6 us  [adam_update(): weight - step_rate * (corrected / (spread + adam_eps) + decay_factor * we...]
    concatenate x3 -> x0, local copies, waits for them, and re-layouts: 5.24 us -> none  [rotary_tables(): jnp.concatenate([t] * (LANES // HEAD), axis=1)]
    pallas_call x1, Pallas kernels: 228 us -> 223 us  [backward(): pl.pallas_call(partial(backward_kernel, plan), in_specs=[any_space] * 12...]
where the time goes in v4:
time: 456 us; the launch traced here: 448 us
  Pallas kernels  416 us (91%)
  other arithmetic  27.4 us (6%)
    pallas_call x1, Pallas kernels, backward(): pl.pallas_call(partial(backward_kernel, plan), in_specs=[any_space] * 12...  223 us
    pallas_call x1, Pallas kernels, forward(): pl.pallas_call(partial(forward_kernel, plan), in_specs=[any_space] * 5 +...  194 us
    sub x4, other arithmetic, adam_update(): weight - step_rate * (corrected / (spread + adam_eps) + decay_factor * we...  13.6 us

profile of v4, /device:TPU:24, one launch (start us, length us, event | category | flops | bytes accessed | tf_op | source)
XLA Modules:
  0.0 447.8 jit_solution(3805107600259415595)
XLA Ops:
  0.7 1.3 reduce_sum.45
  1.9 0.7 add_compare_fusion
  2.6 0.7 convert.12
  3.3 0.6 fusion.15
  3.9 0.7 tile.4
  4.6 0.1 tile.10
  4.7 0.6 fusion.6.small_in
  5.3 193.6 %shard_map.272 = (bf16[2048,1536]{1,0:T(8,128)(2,1)}, bf16[2048,2048]{1,0:T(8,128)(2,1)}, bf16[8,16,384]{2,1,0:T(8,128)(2,1)}, bf16[1024,2048]{1,0:T(8,128)(2,1)...) custom-call(f32[256,2048]{1,0:T(8,128)} %x_in.1, ...), custom_call_target="tpu_custom_call" | custom-call | flops 60000002048 | bytes 83886080 | tf_op jit(solution)/shard_map/pallas_call | solution.py:658
  198.9 1.1 slice_reduce_fusion.3
  200.0 0.8 convert_bitcast_fusion
  200.8 222.7 %shard_map.273 = (f32[5,512,256]{2,1,0:T(8,128)}, f32[7,256,512]{2,1,0:T(8,128)}, f32[16,512]{1,0:T(8,128)}, f32[256,512]{1,0:T(8,128)}, f32[4,2,256,128]{3,2,1,0:T(8,128)}, /*index=5*/f32[256,2048]{1,0:T(8,128)}) custom-call(bf16[1024,2048]{1,0:T(8,128)(2,1)} %get-tuple-element.41.xhat_in, bf16[1024,2048]{1,0:T(8,128)(2,1)} %get-tuple-element.42.cot_in, ...), custom_call_target="tpu_custom_call" | custom-call | flops 80000000000 | bytes 83886080 | tf_op jit(solution)/shard_map/pallas_call | solution.py:1097
  423.6 0.0 copy-start
  423.6 1.5 slice_reduce_fusion.1
  425.1 3.0 multiply_reduce_fusion.1
  428.1 0.0 copy-start.11
  428.1 0.0 copy-start.15
  428.2 0.0 copy-start.16
  428.2 0.0 copy-start.12
  428.2 0.0 copy-start.17
  428.2 0.0 copy-start.18
  428.2 0.0 copy-start.2
  428.2 0.0 copy-start.3
  428.2 0.0 copy-start.4
  428.2 0.0 copy-start.13
  428.3 0.0 copy-start.14
  428.3 5.2 %multiply_add_fusion.2 = (f32[256,2048]{1,0:T(8,128)}, f32[256,2048]{1,0:T(8,128)}) fusion(f32[256,2048]{1,0:T(8,128)} %out_grad_in.1, f32[256,2048]{1,0:T(8,128)S(1)} %copy-done, f32[256,2048]{1,0:T(8,128)S(1)} %copy-done.1, f32[256]{0:T(256)S(1)} %broadcast_multiply_fusion, f32[256]{0:T(256)S(1)} %get-tuple-element.71, ...), kind=kLoop, calls=%fused_computation.12 | loop fusion | flops 6291456 | bytes 12603648 | tf_op jit(solution)/shard_map/add | solution.py:1192
  433.5 0.1 dynamic_slice.7
  433.6 0.6 multiply_subtract_fusion.2
  434.3 0.7 multiply_subtract_fusion.3
  435.0 0.1 copy-done.4
  435.1 7.8 %multiply_subtract_fusion = (f32[256,7,512]{2,0,1:T(8,128)}, f32[256,7,512]{2,0,1:T(8,128)}, f32[256,7,512]{2,0,1:T(8,128)}) fusion(f32[256,7,512]{2,0,1:T(8,128)S(1)} %copy-done.2, f32[7,512]{1,0:T(8,128)S(1)} %slice.42, f32[256]{0:T(256)S(1)} %bitcast.26, f32[7,256,512]{2,1,0:T(8,128)} %get-tuple-element.62, f32[256]{0:T(256)S(1)} %bitcast.25, ...), kind=kLoop, calls=%fused_computation.5 | loop fusion | flops 16515072 | bytes 25706496 | tf_op jit(solution)/shard_map/sub | solution.py:1135
  442.9 4.5 %multiply_subtract_fusion.1 = (f32[5,512,256]{2,1,0:T(8,128)}, f32[5,512,256]{2,1,0:T(8,128)}, f32[5,512,256]{2,1,0:T(8,128)}) fusion(f32[5,512,256]{2,1,0:T(8,128)S(1)} %copy-done.5, f32[5,512,256]{2,1,0:T(8,128)S(1)} %copy-done.8, f32[5,512,256]{2,1,0:T(8,128)S(1)} %copy-done.6, f32[5,512,256]{2,1,0:T(8,128)S(1)} %copy-done.7), kind=kLoop, calls=%fused_computation.8 | loop fusion | flops 9830400 | bytes 18350080 | tf_op jit(solution)/shard_map/sub | solution.py:1135
  (34 shorter events, 0.1 us)
Async XLA Ops:
  423.6 4.5 %copy-start = (f32[256,2048]{1,0:T(8,128)S(1)}, f32[256,2048]{1,0:T(8,128)}, u32[]{:S(2)}) copy-start(f32[256,2048]{1,0:T(8,128)} %x_in.1) | copy-start | bytes 6291460
  423.6 4.5 %copy-start.1 = (f32[256,2048]{1,0:T(8,128)S(1)}, f32[256,2048]{1,0:T(8,128)}, u32[]{:S(2)}) copy-start(f32[256,2048]{1,0:T(8,128)} %get-tuple-element.61) | copy-start | bytes 6291460
  423.6 4.5 %copy-start.9 = (f32[256,512]{1,0:T(8,128)S(1)}, f32[256,512]{1,0:T(8,128)}, u32[]{:S(2)}) copy-start(f32[256,512]{1,0:T(8,128)} %get-tuple-element.58) | copy-start | bytes 1572868
  428.1 5.4 %copy-start.10 = (f32[16,512]{1,0:T(8,128)S(1)}, f32[16,512]{1,0:T(8,128)}, u32[]{:S(2)}) copy-start(f32[16,512]{1,0:T(8,128)} %get-tuple-element.63) | copy-start | bytes 98308
  428.1 5.5 %copy-start.11 = (f32[3,256]{1,0:T(4,128)S(1)}, f32[3,256]{1,0:T(4,128)}, u32[]{:S(2)}) copy-start(f32[3,256]{1,0:T(4,128)} %param.23) | copy-start | bytes 9220
  428.1 5.5 %copy-start.15 = (f32[3,256]{1,0:T(4,128)S(1)}, f32[3,256]{1,0:T(4,128)}, u32[]{:S(2)}) copy-start(f32[3,256]{1,0:T(4,128)} %param.30) | copy-start | bytes 9220
  428.2 5.5 %copy-start.16 = (f32[3,256]{1,0:T(4,128)S(1)}, f32[3,256]{1,0:T(4,128)}, u32[]{:S(2)}) copy-start(f32[3,256]{1,0:T(4,128)} %param.31) | copy-start | bytes 9220
  428.2 6.1 %copy-start.12 = (f32[7,64]{1,0:T(8,128)S(1)}, f32[7,64]{1,0:T(8,128)}, u32[]{:S(2)}) copy-start(f32[7,64]{1,0:T(8,128)} %param.22) | copy-start | bytes 5380
  428.2 6.1 %copy-start.17 = (f32[7,64]{1,0:T(8,128)S(1)}, f32[7,64]{1,0:T(8,128)}, u32[]{:S(2)}) copy-start(f32[7,64]{1,0:T(8,128)} %param.28) | copy-start | bytes 5380
  428.2 6.1 %copy-start.18 = (f32[7,64]{1,0:T(8,128)S(1)}, f32[7,64]{1,0:T(8,128)}, u32[]{:S(2)}) copy-start(f32[7,64]{1,0:T(8,128)} %param.29) | copy-start | bytes 5380
  428.2 6.7 %copy-start.2 = (f32[256,7,512]{2,0,1:T(8,128)S(1)}, f32[256,7,512]{2,0,1:T(8,128)}, u32[]{:S(2)}) copy-start(f32[256,7,512]{2,0,1:T(8,128)} %param.20) | copy-start | bytes 11010052
  428.2 6.7 %copy-start.3 = (f32[256,7,512]{2,0,1:T(8,128)S(1)}, f32[256,7,512]{2,0,1:T(8,128)}, u32[]{:S(2)}) copy-start(f32[256,7,512]{2,0,1:T(8,128)} %param.24) | copy-start | bytes 11010052
  428.2 6.8 %copy-start.4 = (f32[256,7,512]{2,0,1:T(8,128)S(1)}, f32[256,7,512]{2,0,1:T(8,128)}, u32[]{:S(2)}) copy-start(f32[256,7,512]{2,0,1:T(8,128)} %param.25) | copy-start | bytes 11010052
  428.2 6.8 %copy-start.13 = (f32[1,256]{1,0:T(1,128)S(1)}, f32[1,256]{1,0:T(1,128)}, u32[]{:S(2)}) copy-start(f32[1,256]{1,0:T(1,128)} %get-tuple-element.88) | copy-start | bytes 3076
  428.3 6.8 %copy-start.14 = (f32[1,256]{1,0:T(1,128)S(1)}, f32[1,256]{1,0:T(1,128)}, u32[]{:S(2)}) copy-start(f32[1,256]{1,0:T(1,128)} %get-tuple-element.89) | copy-start | bytes 3076
  435.1 7.8 %copy-start.5 = (f32[5,512,256]{2,1,0:T(8,128)S(1)}, f32[5,512,256]{2,1,0:T(8,128)}, u32[]{:S(2)}) copy-start(f32[5,512,256]{2,1,0:T(8,128)} %wd_in.1) | copy-start | bytes 7864324
  435.1 7.8 %copy-start.6 = (f32[5,512,256]{2,1,0:T(8,128)S(1)}, f32[5,512,256]{2,1,0:T(8,128)}, u32[]{:S(2)}) copy-start(f32[5,512,256]{2,1,0:T(8,128)} %param.26) | copy-start | bytes 7864324
  435.1 7.8 %copy-start.7 = (f32[5,512,256]{2,1,0:T(8,128)S(1)}, f32[5,512,256]{2,1,0:T(8,128)}, u32[]{:S(2)}) copy-start(f32[5,512,256]{2,1,0:T(8,128)} %param.27) | copy-start | bytes 7864324
  435.1 7.8 %copy-start.8 = (f32[5,512,256]{2,1,0:T(8,128)S(1)}, f32[5,512,256]{2,1,0:T(8,128)}, u32[]{:S(2)}) copy-start(f32[5,512,256]{2,1,0:T(8,128)} %get-tuple-element.64) | copy-start | bytes 7864324

commit v5 on v4

--- a/solution.py
+++ b/solution.py
@@ -136,6 +136,19 @@
                 mine[...] = (mine[...].astype(f32) + self.got(t, index, up)).astype(bf16)
                 self.copy(t, index, up).start()
 
+    def both_ways(self, first, stop, count, lag=2):
+        def step(t, carry):
+            for up in (True, False):
+                far = 2 * self.place // self.line
+                index = t - lag * (far if up else 1 - far)
+
+                @pl.when((index >= 0) & (index < count))
+                def _():
+                    self.hand_on(index, up)
+            return carry
+
+        lax.fori_loop(first, stop + (lag if stop == count else 0), step, 0)
+
     def last(self, t, target):
         place, line = self.place, self.line
         target[...] = self.source(t, place)[...].astype(f32)
@@ -162,8 +175,8 @@
         self.attn, self.mlp = 3 * local, n_mlp * local
         self.down = (1 + n_mlp) * local
         self.bias_cols = local // n_dp
-        self.width = min(256, model // 4)
-        self.d_tiles = model // self.width
+        self.width = out_cols
+        self.d_tiles = model // out_cols
         self.early = 3 * self.d_tiles // 4
         self.bits = [1 << b for b in range(1, n_dp.bit_length() - 1)]
         even = range(2, n_dp, 2)
@@ -191,13 +204,13 @@
     wa_out, wm_out, small_out, xhat_out, sums_out, cot_out, q_out, k_out, v_out, att_out, lse_out,
     hidden_out, da_out, do_out, part_out, own_out, ahead_out, behind_out, stats_out, mixed_out,
     wa, wm, wd, small, xs, ns, sums, cs, q, k, v, att, lse, hidden, slope, do,
-    own, ahead, behind, stats, wide, block, tall_block,
-    own_sem, block_sem, out_sem, w_send, w_recv, up_send, up_recv, down_send, down_recv,
-    sum_up_send, sum_up_recv, sum_down_send, sum_down_recv, ready,
+    own, ahead, behind, stats, land_up, land_down, wide, mixed, block, tall_block,
+    mixed_sem, own_sem, block_sem, out_sem, w_send, w_recv, up_send, up_recv, down_send, down_recv,
+    sum_up_send, sum_up_recv, sum_down_send, sum_down_recv,
 ):
     n, line = plan.n_dp, plan.n_line
     me, place = lax.axis_index("dp"), lax.axis_index("tensor")
-    rows, local, model = plan.rows, plan.local, plan.model
+    rows, local, model, width = plan.rows, plan.local, plan.model, plan.width
 
     def owner(mask):
         index = me
@@ -213,8 +226,7 @@
             return (wa, wm)[flow].at[pl.ds(at, step), :]
         if flow == 2:
             step = plan.down // 2
-            at = pl.multiple_of(index * plan.out_cols, plan.out_cols)
-            return wd.at[pl.ds(half * step, step), pl.ds(at, plan.out_cols)]
+            return wd.at[index, pl.ds(half * step, step), :]
         return small.at[index]
 
     def halves(flow):
@@ -247,7 +259,7 @@
                     w_copy(flow, target, half).start()
 
     def chunk(flow, index):
-        return (xs, cs)[flow].at[pl.ds(pl.multiple_of(index * rows, rows), rows), :]
+        return (xs, cs)[flow].at[:, pl.ds(pl.multiple_of(index * rows, rows), rows), :]
 
     def z_copy(flow, step, up):
         piece = chunk(flow, place - (step - 1) if up else place + (step - 1))
@@ -317,13 +329,11 @@
     def span(index):
         return pl.ds(pl.multiple_of(index * rows, rows), rows)
 
-    early = plan.early * plan.width
     outs = [
         (wa, wa_out), (wm, wm_out), (small, small_out), (xs, xhat_out), (sums, sums_out), (cs, cot_out),
         (q, q_out), (k, k_out), (v, v_out), (att, att_out), (lse, lse_out), (hidden, hidden_out),
-        (slope, da_out), (do, do_out), (xs.at[:, pl.ds(early, model - early)], part_out),
+        (slope, da_out), (do, do_out), (xs.at[pl.ds(plan.early, plan.d_tiles - plan.early)], part_out),
         (own, own_out), (ahead, ahead_out), (behind, behind_out), (stats, stats_out),
-        (wide.at[:, pl.ds(0, early)], mixed_out),
     ]
 
     def out_copy(j):
@@ -334,37 +344,58 @@
             out_copy(j).start()
 
     w_rows = pl.ds(pl.multiple_of(me * plan.in_rows, plan.in_rows), plan.in_rows)
-    w_cols = pl.ds(pl.multiple_of(me * plan.out_cols, plan.out_cols), plan.out_cols)
     small_load = pltpu.make_async_copy(small_in, small.at[me], own_sem.at[2])
 
-    def in_load(r):
-        return pltpu.make_async_copy(w_in.at[r], block.at[r % 2], block_sem.at[0, r % 2])
-
-    def down_load(r):
-        return pltpu.make_async_copy(wd_in.at[r], tall_block.at[r % 2], block_sem.at[1, r % 2])
-
-    def round_in(first, stop, target, shift):
-        for r in range(first, stop):
-            in_load(r).wait()
-            target[w_rows, (r - shift) * local : (r - shift + 1) * local] = block[r % 2].astype(bf16)
-            if r + 2 < 3 + plan.n_mlp:
-                in_load(r + 2).start()
+    half_rows, half_cols = plan.in_rows // 2, local // 2
+
+    def in_load(i):
+        return pltpu.make_async_copy(
+            w_in.at[i // 2, pl.ds(i % 2 * half_rows, half_rows), :], block.at[i % 2], block_sem.at[0, i % 2]
+        )
+
+    def down_load(i):
+        return pltpu.make_async_copy(
+            wd_in.at[i // 2, pl.ds(i % 2 * half_cols, half_cols), :], tall_block.at[i % 2], block_sem.at[1, i % 2]
+        )
+
+    def round_in(first, stop, target):
+        for i in range(2 * first, 2 * stop):
+            r, half = divmod(i, 2)
+            in_load(i).wait()
+            to = pl.ds(pl.multiple_of(me * plan.in_rows + half * half_rows, half_rows), half_rows)
+            target[to, (r - first) * local : (r - first + 1) * local] = block[half].astype(bf16)
+            if i + 2 < 2 * (3 + plan.n_mlp):
+                in_load(i + 2).start()
 
     def round_down():
-        for r in range(1 + plan.n_mlp):
-            down_load(r).wait()
-            wd[r * local : (r + 1) * local, w_cols] = tall_block[r % 2].astype(bf16)
-            if r + 2 < 1 + plan.n_mlp:
-                down_load(r + 2).start()
-
-    x_load = pltpu.make_async_copy(x_in, wide, own_sem.at[0])
-    cot_load = pltpu.make_async_copy(out_grad_in, wide, own_sem.at[1])
-    x_load.start()
+        for i in range(2 * (1 + plan.n_mlp)):
+            down_load(i).wait()
+            wd[me, i * half_cols : (i + 1) * half_cols, :] = tall_block[i % 2].astype(bf16)
+            if i + 2 < 2 * (1 + plan.n_mlp):
+                down_load(i + 2).start()
+
+    strip_rows = min(64, rows)
+    strip_count = rows // strip_rows
+
+    def row_load(j):
+        source = x_in if j < strip_count else out_grad_in
+        first = j % strip_count * strip_rows
+        return pltpu.make_async_copy(
+            source.at[pl.ds(first, strip_rows), :], wide.at[j % 2], own_sem.at[j % 2]
+        )
+
+    row_load(0).start()
+    row_load(1).start()
     small_load.start()
     in_load(0).start()
     in_load(1).start()
     down_load(0).start()
     down_load(1).start()
+    table_loads = [
+        pltpu.make_async_copy(place_cos, own, own_sem.at[3]), pltpu.make_async_copy(place_sin, ahead, own_sem.at[4])
+    ]
+    for load in table_loads:
+        load.start()
     barrier = pltpu.get_barrier_semaphore()
     for b in [1] + plan.bits if n > 1 else []:
         pl.semaphore_signal(barrier, inc=1, device_id={"dp": owner(b)}, device_id_type=pl.DeviceIdType.MESH)
@@ -382,9 +413,9 @@
 
     def normalize_rows(index):
         at = span(index)
-        gain = jnp.concatenate([small[o, 0:1, LANES:] for o in range(n)], axis=1).astype(f32)
-        shift = jnp.concatenate([small[o, 1:2, LANES:] for o in range(n)], axis=1).astype(f32)
-        ns[...] = (xs[at, :].astype(f32) * gain + shift).astype(bf16)
+        for o in range(n):
+            gain, shift = small[o, 0:1, LANES:].astype(f32), small[o, 1:2, LANES:].astype(f32)
+            ns[:, o * width : (o + 1) * width] = (xs[o, at, :].astype(f32) * gain + shift).astype(bf16)
 
     def bias_row(r, first, width):
         per = LANES // plan.bias_cols
@@ -447,26 +478,22 @@
             lse[here, :] = held
         return carry
 
-    width = plan.width
     tall = min(512, plan.group)
 
     def out_tile(t):
-        cols = pl.ds(pl.multiple_of(t * width, width), width)
-
         def part(j, carry):
             at = pl.ds(pl.multiple_of(j * tall, tall), tall)
-            total = dot_n(att[at, :], wd[:local, cols]) + dot_n(hidden[at, :], wd[local:, cols])
-            xs[at, cols] = total.astype(bf16)
+            total = dot_n(att[at, :], wd[t, :local, :]) + dot_n(hidden[at, :], wd[t, local:, :])
+            xs[t, at, :] = total.astype(bf16)
             return carry
 
         lax.fori_loop(0, plan.group // tall, part, 0)
 
     def tile_source(t, index):
-        return xs.at[span(index), pl.ds(pl.multiple_of(t * width, width), width)]
+        return xs.at[t, span(index), :]
 
     def tile_landing(t, slot, up):
-        at = slot * rows + (0 if up else (line - 1) * rows)
-        return wm.at[pl.ds(pl.multiple_of(at, rows), rows), pl.ds(pl.multiple_of(t * width, width), width)]
+        return (land_up if up else land_down).at[t, slot]
 
     out_sum = LineSum(
         place, line, tile_source, tile_landing, (sum_up_send, sum_up_recv, sum_down_send, sum_down_recv)
@@ -477,54 +504,87 @@
 
     def back_rows(index):
         at = span(index)
-        sums[0:1, :] += jnp.sum(cs[at, :].astype(f32), axis=0, keepdims=True)
-        do[at, :] = dot_t(cs[at, :], wd[:local, :]).astype(bf16)
-        for r in range(plan.n_mlp):
-            cols = slice(r * local, (r + 1) * local)
-            grad = dot_t(cs[at, :], wd[(1 + r) * local : (2 + r) * local, :])
-            slope[at, cols] = (grad * slope[at, cols].astype(f32)).astype(bf16)
+        for o in range(n):
+            sums[0:1, o * width : (o + 1) * width] += jnp.sum(cs[o, at, :].astype(f32), axis=0, keepdims=True)
+        for r in range(1 + plan.n_mlp):
+            grad = dot_t(cs[0, at, :], wd[0, r * local : (r + 1) * local, :])
+            for o in range(1, n):
+                grad = grad + dot_t(cs[o, at, :], wd[o, r * local : (r + 1) * local, :])
+            if r == 0:
+                do[at, :] = grad.astype(bf16)
+            else:
+                cols = slice((r - 1) * local, r * local)
+                slope[at, cols] = (grad * slope[at, cols].astype(f32)).astype(bf16)
 
     def normalize_own():
-        x_load.wait()
-        value = wide[...]
-        mean = jnp.mean(value, axis=1, keepdims=True)
-        centered = value - mean
-        scale = lax.rsqrt(jnp.mean(centered * centered, axis=1, keepdims=True) + norm_eps)
-        xs[span(place), :] = (centered * scale).astype(bf16)
-        stats[0] = jnp.broadcast_to(mean, (rows, LANES))
-        stats[1] = jnp.broadcast_to(scale, (rows, LANES))
-        cot_load.start()
+        for j in range(strip_count):
+            row_load(j).wait()
+            at = slice(j * strip_rows, (j + 1) * strip_rows)
+            value = wide[j % 2]
+            mean = jnp.mean(value, axis=1, keepdims=True)
+            centered = value - mean
+            scale = lax.rsqrt(jnp.mean(centered * centered, axis=1, keepdims=True) + norm_eps)
+            normed = (centered * scale).astype(bf16)
+            to = pl.ds(pl.multiple_of(place * rows + j * strip_rows, strip_rows), strip_rows)
+            for o in range(n):
+                xs[o, to, :] = normed[:, o * width : (o + 1) * width]
+            stats[0, at, :] = jnp.broadcast_to(mean, (strip_rows, LANES))
+            stats[1, at, :] = jnp.broadcast_to(scale, (strip_rows, LANES))
+            if j + 2 < 2 * strip_count:
+                row_load(j + 2).start()
 
     def mask_cot():
-        cot_load.wait()
-        places = place * rows + lax.broadcasted_iota(jnp.int32, (rows, 1), 0)
-        cs[span(place), :] = jnp.where(places < ends_of(lengths)[-1], wide[...], 0.0).astype(bf16)
+        for j in range(strip_count, 2 * strip_count):
+            row_load(j).wait()
+            first = place * rows + (j - strip_count) * strip_rows
+            places = first + lax.broadcasted_iota(jnp.int32, (strip_rows, 1), 0)
+            masked = jnp.where(places < ends_of(lengths)[-1], wide[j % 2], 0.0).astype(bf16)
+            to = pl.ds(pl.multiple_of(first, strip_rows), strip_rows)
+            for o in range(n):
+                cs[o, to, :] = masked[:, o * width : (o + 1) * width]
+            if j + 2 < 2 * strip_count:
+                row_load(j + 2).start()
 
     def make_tables():
+        for load in table_loads:
+            load.wait()
         block_rows = min(QUERY_ROWS, plan.group)
         ends = ends_of(lengths)
+        at_ends = [pl.ds(jnp.minimum(end, plan.group - 1), 1) for end in ends]
+        cosines, sines = [own[row, :] for row in at_ends], [ahead[row, :] for row in at_ends]
         for start in range(0, plan.group, block_rows):
             at = pl.ds(start, block_rows)
             places = start + lax.broadcasted_iota(jnp.int32, (block_rows, LANES), 0)
-            begin_cos, begin_sin = place_cos[0:1, :], place_sin[0:1, :]
-            for end in ends[1:]:
-                row = pl.ds(jnp.minimum(end, plan.group - 1), 1)
-                begin_cos = jnp.where(places >= end, place_cos[row, :], begin_cos)
-                begin_sin = jnp.where(places >= end, place_sin[row, :], begin_sin)
-            cosine = place_cos[at, :] * begin_cos + place_sin[at, :] * begin_sin
-            sine = place_sin[at, :] * begin_cos - place_cos[at, :] * begin_sin
+            begin_cos, begin_sin = cosines[0], sines[0]
+            for end, end_cos, end_sin in zip(ends[1:], cosines[1:], sines[1:]):
+                begin_cos = jnp.where(places >= end, end_cos, begin_cos)
+                begin_sin = jnp.where(places >= end, end_sin, begin_sin)
+            place_c, place_s = own[at, :], ahead[at, :]
+            cosine = place_c * begin_cos + place_s * begin_sin
+            sine = place_s * begin_cos - place_c * begin_sin
             lane = lax.rem(lax.broadcasted_iota(jnp.int32, (block_rows, LANES), 1), HEAD)
             own[at, :] = jnp.where(lane < ROT, cosine, 1.0)
             ahead[at, :] = jnp.where(lane < ROT // 2, -sine, 0.0)
             behind[at, :] = jnp.where((lane >= ROT // 2) & (lane < ROT), sine, 0.0)
 
+    def mixed_copy(t):
+        cols = pl.ds(pl.multiple_of(t * width, width), width)
+        return pltpu.make_async_copy(mixed.at[lax.rem(t, 2)], mixed_out.at[:, cols], mixed_sem.at[lax.rem(t, 2)])
+
+    def finish_tile(t):
+        @pl.when(t >= 2)
+        def _():
+            mixed_copy(t - 2).wait()
+        out_sum.last(t, mixed.at[lax.rem(t, 2)])
+        mixed_copy(t).start()
+
     normalize_own()
     z_start(0, 1)
     small_load.wait()
     w_start(3)
-    round_in(0, 3, wa, 0)
+    round_in(0, 3, wa)
     w_start(0)
-    round_in(3, 3 + plan.n_mlp, wm, 3)
+    round_in(3, 3 + plan.n_mlp, wm)
     mask_cot()
     round_down()
     make_tables()
@@ -566,19 +626,6 @@
     pairs = local // LANES
     lax.fori_loop(0, pairs // 2, attend, 0)
     w_arrive(2, plan.single)
-    out_copy(1).wait()
-    for mask in range(1, n):
-        for half in halves(1):
-            w_copy(1, mask, half).wait_send()
-
-    @pl.when(place < line - 1)
-    def _():
-        pl.semaphore_signal(ready, inc=1, device_id={"tensor": place + 1}, device_id_type=pl.DeviceIdType.MESH)
-
-    @pl.when(place > 0)
-    def _():
-        pl.semaphore_signal(ready, inc=1, device_id={"tensor": place - 1}, device_id_type=pl.DeviceIdType.MESH)
-
     lax.fori_loop(pairs // 2, pairs, attend, 0)
     write(9, 10)
     z_arrive(1, 1)
@@ -590,7 +637,6 @@
             @pl.when(left & sends(step, up))
             def _():
                 z_copy(0, step, up).wait_send()
-    pl.semaphore_wait(ready, beside)
     w_arrive(2, plan.odd)
 
     def first_tile(t):
@@ -623,22 +669,22 @@
     running(False)
     at_distance(line - 1, back_rows)
     write(4, 5, 12, 13)
-    early_tiles(lambda t: out_sum.last(t, wide.at[:, pl.ds(pl.multiple_of(t * width, width), width)]))
-    write(19)
+    early_tiles(finish_tile)
+    for t in range(max(plan.early - 2, 0), plan.early):
+        mixed_copy(t).wait()
 
     early_tiles(out_sum.sent)
-    for flow in (0, 2, 3):
+    for flow in range(4):
         for mask in range(1, n):
             for half in halves(flow):
                 w_copy(flow, mask, half).wait_send()
     for j in range(len(outs)):
-        if j not in (1, 3):
+        if j != 3:
             out_copy(j).wait()
 
 
 def forward(plan, x, out_grad, w, wd, small, lengths):
     any_space = pl.BlockSpec(memory_space=pl.ANY)
-    vmem = pl.BlockSpec(memory_space=pltpu.VMEM)
     n, line, group, model, local, rows = (
         plan.n_dp, plan.n_line, plan.group, plan.model, plan.local, plan.rows
     )
@@ -647,30 +693,34 @@
     early = plan.early * plan.width
     out_shape = [
         low(model, plan.attn), low(model, plan.mlp), low(n, 16, LANES + plan.out_cols),
-        low(group, model), full(8, model), low(group, model),
+        low(n, group, plan.width), full(8, model), low(n, group, plan.width),
         low(group, local), low(group, local), low(group, local), low(group, local),
         full(group, LANES),
-        low(group, plan.mlp), low(group, plan.mlp), low(group, local), low(group, model - early),
+        low(group, plan.mlp), low(group, plan.mlp), low(group, local),
+        low(plan.d_tiles - plan.early, group, plan.width),
         full(group, LANES), full(group, LANES), full(group, LANES), full(2, rows, LANES), full(rows, early),
     ]
     scratch = lambda s: pltpu.VMEM(s.shape, s.dtype)
     dma = pltpu.SemaphoreType.DMA
     return pl.pallas_call(
         partial(forward_kernel, plan),
-        in_specs=[any_space] * 5 + [pl.BlockSpec(memory_space=pltpu.SMEM)] + [vmem] * 2,
+        in_specs=[any_space] * 5 + [pl.BlockSpec(memory_space=pltpu.SMEM)] + [any_space] * 2,
         out_specs=[any_space] * 20,
         out_shape=out_shape,
         scratch_shapes=[scratch(s) for s in out_shape[:2]]
-        + [pltpu.VMEM((plan.down, model), bf16)]
+        + [pltpu.VMEM((n, plan.down, plan.out_cols), bf16)]
         + [scratch(s) for s in out_shape[2:4]]
         + [pltpu.VMEM((rows, model), bf16)]
         + [scratch(s) for s in out_shape[4:14]]
         + [scratch(s) for s in out_shape[15:19]]
-        + [pltpu.VMEM((rows, model), f32), pltpu.VMEM((2,) + w.shape[1:], f32), pltpu.VMEM((2,) + wd.shape[1:], f32)]
-        + [dma((3,)), dma((2, 2)), dma((20,)), dma((8 * n,)), dma((8 * n,))]
+        + [pltpu.VMEM((plan.early, max(line - 1, 1), rows, plan.width), bf16)] * 2
+        + [
+            pltpu.VMEM((2, min(64, rows), model), f32), pltpu.VMEM((2, rows, plan.width), f32),
+            pltpu.VMEM((2, plan.in_rows // 2, local), f32), pltpu.VMEM((2, local // 2, plan.out_cols), f32),
+        ]
+        + [dma((2,)), dma((5,)), dma((2, 2)), dma((19,)), dma((8 * n,)), dma((8 * n,))]
         + [dma((2 * line,))] * 4
-        + [dma((plan.early, max(line - 1, 1)))] * 4
-        + [pltpu.SemaphoreType.REGULAR],
+        + [dma((plan.early, max(line - 1, 1)))] * 4,
         compiler_params=pltpu.CompilerParams(
             collective_id=0, has_side_effects=True, vmem_limit_bytes=63 << 20
         ),
@@ -711,9 +761,13 @@
     def position(mask, order):
         return sum((1 if mask & b else 0) << (n_bits - 1 - p) for p, b in enumerate(order))
 
+    width, d_tiles = plan.width, plan.d_tiles
+    sub = local // width
+
+    def strip(source, j):
+        return source.at[:, pl.ds(j * width, width)]
+
     whole = [
-        (att_in, og.at[:, pl.ds(0, local)]),
-        (hidden_in, og.at[:, pl.ds(local, plan.mlp)]),
         (da_in, da),
         (q_in, qkv.at[:, pl.ds(0, local)]),
         (k_in, qkv.at[:, pl.ds(local, local)]),
@@ -721,6 +775,10 @@
         (do_in, do),
         (part_in, part),
     ]
+    whole = whole + [
+        (strip(att_in, j) if j < sub else strip(hidden_in, j - sub), og.at[j]) for j in range(n_down * sub)
+    ]
+    strips = range(6, len(whole))
     for j, (a, b) in enumerate(whole):
         pltpu.make_async_copy(a, b, load_sem.at[j]).start()
 
@@ -746,19 +804,16 @@
 
     share_own = pltpu.make_async_copy(shares, rows_out.at[place], share_send.at[0])
 
-    def turn_columns(source, masks, first, started=False):
+    def turn_columns(source, masks):
         def fetch(j):
-            at = pl.multiple_of(owner(masks[j]) * in_rows, in_rows)
-            return pltpu.make_async_copy(
-                source.at[:, pl.ds(at, in_rows)], stage.at[j % 2], stage_sem.at[j % 2]
-            )
+            return pltpu.make_async_copy(source.at[owner(masks[j])], stage.at[j % 2], stage_sem.at[j % 2])
 
         fetch(0).start()
         for j in range(len(masks)):
             if j + 1 < len(masks):
                 fetch(j + 1).start()
             fetch(j).wait()
-            turned[pl.ds((first + j) * in_rows, in_rows), :] = stage[j % 2].T
+            turned[pl.ds(j * in_rows, in_rows), :] = stage[j % 2].T
 
     def core_copy(name, t):
         return pltpu.make_async_remote_copy(
@@ -778,50 +833,61 @@
             device_id=peer(orders[half][phase]), device_id_type=MESH,
         )
 
-    def operand(name, t):
-        source = {"down": og, "mlp": da, "attn": qkv}[name]
-        return source[:, pl.ds(pl.multiple_of(t * local, local), local)]
+    def product(name, at, count, t):
+        if name == "down":
+            return [dot_n(turned[at : at + count, :], og[t * sub + j]) for j in range(sub)]
+        source = da if name == "mlp" else qkv
+        return [dot_n(turned[at : at + count, :], source[:, pl.ds(pl.multiple_of(t * local, local), local)])]
 
     piece = min(2, pairs_n) * in_rows
 
-    def send_core(name):
-        tiles = flows[name][0]
+    def send_core(name, t):
+        @pl.when(t >= 2)
+        def _():
+            core_copy(name, t - 2).wait_send()
+        for at in range(0, pairs_n * in_rows, piece):
+            strips_of = product(name, at, piece, t)
+            step = local // len(strips_of)
+            for j, value in enumerate(strips_of):
+                sent[lax.rem(t, 2), at : at + piece, j * step : (j + 1) * step] = value.astype(bf16)
+        core_copy(name, t).start()
+
+    def keep_core(name, t):
+        base = flows[name][1]
+        core_copy(name, t).wait_recv()
+        for first in range(0, pairs_n * in_rows, piece):
+            strips_of = product(name, pairs_n * in_rows + first, piece, t)
+            step = local // len(strips_of)
+            for i, value in enumerate(strips_of):
+                cols = slice(i * step, (i + 1) * step)
+                total = value + core_in[t, first : first + piece, cols].astype(f32)
+                for at in range(0, piece, half_rows):
+                    j, half = divmod((first + at) // half_rows, 2)
+                    held[base + t, half, position(2 * j, orders[half]), :, cols] = total[at : at + half_rows].astype(bf16)
+        for half in range(2):
+            if n_bits:
+                cube_copy(base + t, half, 0).start()
+
+    def scatter(name):
+        tiles_n = flows[name][0]
         if name != "down":
             pl.semaphore_wait(credit.at[0], 1)
+        if name == "attn":
+            pl.semaphore_wait(credit.at[1], n_bits)
 
         def step(t, carry):
-            @pl.when(t >= 2)
+            @pl.when(t < tiles_n)
             def _():
-                core_copy(name, t - 2).wait_send()
-            for at in range(0, pairs_n * in_rows, piece):
-                sent[lax.rem(t, 2), at : at + piece, :] = dot_n(
-                    turned[at : at + piece, :], operand(name, t)
-                ).astype(bf16)
-            core_copy(name, t).start()
+                send_core(name, t)
+
+            @pl.when(t >= 1)
+            def _():
+                keep_core(name, t - 1)
             return carry
 
-        lax.fori_loop(0, tiles, step, 0)
-        for t in range(max(tiles - 2, 0), tiles):
+        lax.fori_loop(0, tiles_n + 1, step, 0)
+        for t in range(max(tiles_n - 2, 0), tiles_n):
             core_copy(name, t).wait_send()
-
-    def keep_core(name):
-        tiles, base, _ = flows[name]
-
-        def step(t, carry):
-            core_copy(name, t).wait_recv()
-            for first in range(0, pairs_n * in_rows, piece):
-                kept = pairs_n * in_rows + first
-                total = dot_n(turned[kept : kept + piece, :], operand(name, t))
-                total = total + core_in[t, first : first + piece, :].astype(f32)
-                for at in range(0, piece, half_rows):
-                    j, half = divmod((first + at) // half_rows, 2)
-                    held[base + t, half, position(2 * j, orders[half])] = total[at : at + half_rows].astype(bf16)
-            for half in range(2):
-                if n_bits:
-                    cube_copy(base + t, half, 0).start()
-            return carry
-
-        lax.fori_loop(0, tiles, step, 0)
         if name != "attn":
             pl.semaphore_signal(credit.at[0], inc=1, device_id=peer(1), device_id_type=MESH)
 
@@ -920,8 +986,6 @@
         qkv[:, v_lanes] = v_sum[...].astype(bf16)
         return carry
 
-    width, d_tiles = plan.width, plan.d_tiles
-
     def tile_loads(t):
         at = pl.ds(pl.multiple_of(t * width, width), width)
         slot = lax.rem(t, 2)
@@ -932,10 +996,7 @@
 
     def tile_of(buffer):
         def source(t, index):
-            return buffer.at[
-                pl.ds(pl.multiple_of(index * rows, rows), rows),
-                pl.ds(pl.multiple_of(t * width, width), width),
-            ]
+            return buffer.at[t, pl.ds(pl.multiple_of(index * rows, rows), rows), :]
         return source
 
     dh_sum = LineSum(
@@ -966,12 +1027,6 @@
 
     def tiles(first, stop, fn):
         lax.fori_loop(first, stop, lambda t, carry: (fn(t), carry)[1], 0)
-
-    def hand_on(flow):
-        def step(t):
-            for up in (True, False):
-                flow.hand_on(t, up)
-        return step
 
     def dh_tile(t):
         slot = lax.rem(t, 2)
@@ -982,7 +1037,7 @@
         for load in tile_loads(t):
             load.wait()
         total = dot_t(qkv[...], w_tile[slot, 0:width, : plan.attn]) + dot_t(da[...], w_tile[slot, 0:width, plan.attn :])
-        og[:, pl.ds(pl.multiple_of(t * width, width), width)] = total.astype(bf16)
+        og[t] = total.astype(bf16)
         dh_sum.first(t)
 
     def small_copy(j):
@@ -1002,19 +1057,17 @@
     small[0] = jnp.zeros_like(small[0])
     for load in tile_loads(0):
         load.start()
-    send_masks, keep_masks = [2 * j + 1 for j in range(pairs_n)], [2 * j for j in range(pairs_n)]
-    turn_columns(cot_in, send_masks, 0)
+    masks = [2 * j + 1 for j in range(pairs_n)] + [2 * j for j in range(pairs_n)]
+    turn_columns(cot_in, masks)
     pl.semaphore_wait(barrier, 1 + n_bits + line - 1)
-    loaded(7)
+    loaded(5)
     tiles(0, late, out_sum.first)
-    loaded(0, 1)
-    send_core("down")
-    turn_columns(cot_in, keep_masks, pairs_n)
-    keep_core("down")
-    loaded(2, 3, 4, 5, 6)
+    loaded(*strips)
+    scatter("down")
+    loaded(0, 1, 2, 3, 4)
     pairs = local // LANES
     lax.fori_loop(0, pairs // 2, attend, 0)
-    tiles(0, late, hand_on(out_sum))
+    out_sum.both_ways(0, late, late)
     lax.fori_loop(pairs // 2, pairs, attend, 0)
     for r in range(3 + n_mlp):
         block = qkv[:, r * local : (r + 1) * local] if r < 3 else da[:, (r - 3) * local : (r - 2) * local]
@@ -1026,22 +1079,18 @@
     tiles(0, some, dh_tile)
     for phase in range(n_bits - 1):
         cube_step("down", phase)
-    turn_columns(xhat_in, send_masks, 0)
-    send_core("mlp")
-    turn_columns(xhat_in, keep_masks, pairs_n)
-    keep_core("mlp")
+    turn_columns(xhat_in, masks)
+    scatter("mlp")
     finish(out_sum, mixed_out, late)
     tiles(some, d_tiles, dh_tile)
-    tiles(0, d_tiles // 4, hand_on(dh_sum))
+    dh_sum.both_ways(0, d_tiles // 4, d_tiles)
     small_step(0)
     cube_step("down", n_bits - 1)
     cube_sent("down")
     for b in plan.bits:
         pl.semaphore_signal(credit.at[1], inc=1, device_id=peer(b), device_id_type=MESH)
     small_step(1)
-    send_core("attn")
-    pl.semaphore_wait(credit.at[1], n_bits)
-    keep_core("attn")
+    scatter("attn")
     for j in range(2, n_bits + 1):
         small_step(j)
     own_rows = pl.ds(pl.multiple_of(me * in_rows, in_rows), in_rows)
@@ -1051,14 +1100,14 @@
     ]
     for w in weights:
         w.start()
-    tiles(d_tiles // 4, d_tiles // 2, hand_on(dh_sum))
+    dh_sum.both_ways(d_tiles // 4, d_tiles // 2, d_tiles)
     for phase in range(n_bits - 1):
         cube_step("mlp", phase)
-    tiles(d_tiles // 2, 3 * d_tiles // 4, hand_on(dh_sum))
+    dh_sum.both_ways(d_tiles // 2, 3 * d_tiles // 4, d_tiles)
     for w in weights:
         w.wait()
     cube_step("mlp", n_bits - 1)
-    tiles(3 * d_tiles // 4, d_tiles, hand_on(dh_sum))
+    dh_sum.both_ways(3 * d_tiles // 4, d_tiles, d_tiles)
     for phase in range(n_bits):
         cube_step("attn", phase)
     share_own.start()
@@ -1104,15 +1153,16 @@
             out(f32, line, 2, in_rows, LANES), out(f32, rows, model),
         ],
         scratch_shapes=[
-            low(n * in_rows, group), low(2, group, in_rows), low(group, plan.down), low(group, plan.mlp),
+            low(n * in_rows, group), low(2, group, in_rows),
+            low(max(d_tiles, plan.down // width), group, width), low(group, plan.mlp),
             low(group, plan.attn), low(group, local), full(group, LANES), full(group, LANES),
             low(2, pairs_n * in_rows, local), low(n_down, pairs_n * in_rows, local),
             low(slots, 2, pairs_n, in_rows // 2, local), low(slots, 2, max(pairs_n - 1, 1), in_rows // 2, local),
             low(d_tiles, steps, rows, width), low(d_tiles, steps, rows, width),
-            low(group, late * width), low(late, steps, rows, width), low(late, steps, rows, width),
+            low(late, group, width), low(late, steps, rows, width), low(late, steps, rows, width),
             low(2, max(width, in_rows), plan.attn + plan.mlp), full(2, in_rows, local), full(local, in_rows), full(2, rows, width),
             full(n_bits + 2, small_rows, local), full(n_bits + 1, small_rows, local), full(2, in_rows, LANES),
-            dma((8,)), dma((2,)), dma((2, 2)), dma((2,)), dma((2,)), dma((2,)), dma((n_down,)),
+            dma((6 + plan.down // width,)), dma((2,)), dma((2, 2)), dma((2,)), dma((2,)), dma((2,)), dma((n_down,)),
             dma((slots, max(2 * n_bits, 1))), dma((slots, max(2 * n_bits, 1))),
             dma((d_tiles, steps)), dma((d_tiles, steps)), dma((d_tiles, steps)), dma((d_tiles, steps)),
             dma((late, steps)), dma((late, steps)), dma((late, steps)), dma((late, steps)),

time: 456 us -> 425 us (0.932)
  the two profiles are of different devices: /device:TPU:24 before, /device:TPU:0 now
where the time goes in v5:
time: 425 us; the launch traced here: 417 us
  Pallas kernels  386 us (91%)
  other arithmetic  27.4 us (6%)
    pallas_call x1, Pallas kernels, backward(): pl.pallas_call(partial(backward_kernel, plan), in_specs=[any_space] * 12...  193 us
    pallas_call x1, Pallas kernels, forward(): pl.pallas_call(partial(forward_kernel, plan), in_specs=[any_space] * 5 +...  193 us
    sub x4, other arithmetic, adam_update(): weight - step_rate * (corrected / (spread + adam_eps) + decay_factor * we...  13.6 us

profile of v5, /device:TPU:0, one launch (start us, length us, event | category | flops | bytes accessed | tf_op | source)
XLA Modules:
  0.0 417.1 jit_solution(447915833712773015)
XLA Ops:
  0.7 1.3 reduce_sum.45
  1.9 0.7 add_compare_fusion
  2.6 0.7 convert.12
  3.3 0.6 fusion.15
  3.9 0.7 tile.4
  4.6 0.1 tile.10
  4.7 0.6 fusion.6.small_in
  5.3 192.7 %shard_map.272 = (bf16[2048,1536]{1,0:T(8,128)(2,1)}, bf16[2048,2048]{1,0:T(8,128)(2,1)}, bf16[8,16,384]{2,1,0:T(8,128)(2,1)}, bf16[8,1024,256]{2,1,0:T(8,128)(2...) custom-call(f32[256,2048]{1,0:T(8,128)} %x_in.1, ...), custom_call_target="tpu_custom_call" | custom-call | flops 60000002048 | bytes 83886080 | tf_op jit(solution)/shard_map/pallas_call | solution.py:705
  198.0 1.1 slice_reduce_fusion.3
  199.1 0.8 convert_bitcast_fusion
  199.9 193.0 %shard_map.273 = (f32[5,512,256]{2,1,0:T(8,128)}, f32[7,256,512]{2,1,0:T(8,128)}, f32[16,512]{1,0:T(8,128)}, f32[256,512]{1,0:T(8,128)}, f32[4,2,256,128]{3,2,1,0:T(8,128)}, /*index=5*/f32[256,2048]{1,0:T(8,128)}) custom-call(bf16[8,1024,256]{2,1,0:T(8,128)(2,1)} %get-tuple-element.41.xhat_in, bf16[8,1024,256]{2,1,0:T(8,128)(2,1)} %get-tuple-element.42.cot_in, ...), custom_call_target="tpu_custom_call" | custom-call | flops 80000000000 | bytes 83886080 | tf_op jit(solution)/shard_map/pallas_call | solution.py:1146
  392.9 0.0 copy-start
  392.9 1.5 slice_reduce_fusion.1
  394.4 3.0 multiply_reduce_fusion.1
  397.4 0.0 copy-start.11
  397.4 0.0 copy-start.15
  397.5 0.0 copy-start.16
  397.5 0.0 copy-start.12
  397.5 0.0 copy-start.17
  397.5 0.0 copy-start.18
  397.5 0.0 copy-start.2
  397.5 0.0 copy-start.3
  397.5 0.0 copy-start.4
  397.5 0.0 copy-start.13
  397.6 5.2 %multiply_add_fusion.2 = (f32[256,2048]{1,0:T(8,128)}, f32[256,2048]{1,0:T(8,128)}) fusion(f32[256,2048]{1,0:T(8,128)} %out_grad_in.1, f32[256,2048]{1,0:T(8,128)S(1)} %copy-done, f32[256,2048]{1,0:T(8,128)S(1)} %copy-done.1, f32[256]{0:T(256)S(1)} %broadcast_multiply_fusion, f32[256]{0:T(256)S(1)} %get-tuple-element.71, ...), kind=kLoop, calls=%fused_computation.12 | loop fusion | flops 6291456 | bytes 12603648 | tf_op jit(solution)/shard_map/add | solution.py:1242
  402.8 0.1 dynamic_slice.7
  402.9 0.6 multiply_subtract_fusion.2
  403.6 0.7 multiply_subtract_fusion.3
  404.3 0.1 copy-done.4
  404.4 0.0 copy-start.7
  404.4 7.8 %multiply_subtract_fusion = (f32[256,7,512]{2,0,1:T(8,128)}, f32[256,7,512]{2,0,1:T(8,128)}, f32[256,7,512]{2,0,1:T(8,128)}) fusion(f32[256,7,512]{2,0,1:T(8,128)S(1)} %copy-done.2, f32[7,512]{1,0:T(8,128)S(1)} %slice.42, f32[256]{0:T(256)S(1)} %bitcast.26, f32[7,256,512]{2,1,0:T(8,128)} %get-tuple-element.62, f32[256]{0:T(256)S(1)} %bitcast.25, ...), kind=kLoop, calls=%fused_computation.5 | loop fusion | flops 16515072 | bytes 25706496 | tf_op jit(solution)/shard_map/sub | solution.py:1185
  412.2 4.5 %multiply_subtract_fusion.1 = (f32[5,512,256]{2,1,0:T(8,128)}, f32[5,512,256]{2,1,0:T(8,128)}, f32[5,512,256]{2,1,0:T(8,128)}) fusion(f32[5,512,256]{2,1,0:T(8,128)S(1)} %copy-done.5, f32[5,512,256]{2,1,0:T(8,128)S(1)} %copy-done.8, f32[5,512,256]{2,1,0:T(8,128)S(1)} %copy-done.6, f32[5,512,256]{2,1,0:T(8,128)S(1)} %copy-done.7), kind=kLoop, calls=%fused_computation.8 | loop fusion | flops 9830400 | bytes 18350080 | tf_op jit(solution)/shard_map/sub | solution.py:1185
  (34 shorter events, 0.1 us)
Async XLA Ops:
  392.9 4.5 %copy-start = (f32[256,2048]{1,0:T(8,128)S(1)}, f32[256,2048]{1,0:T(8,128)}, u32[]{:S(2)}) copy-start(f32[256,2048]{1,0:T(8,128)} %x_in.1) | copy-start | bytes 6291460
  392.9 4.5 %copy-start.1 = (f32[256,2048]{1,0:T(8,128)S(1)}, f32[256,2048]{1,0:T(8,128)}, u32[]{:S(2)}) copy-start(f32[256,2048]{1,0:T(8,128)} %get-tuple-element.61) | copy-start | bytes 6291460
  392.9 4.5 %copy-start.9 = (f32[256,512]{1,0:T(8,128)S(1)}, f32[256,512]{1,0:T(8,128)}, u32[]{:S(2)}) copy-start(f32[256,512]{1,0:T(8,128)} %get-tuple-element.58) | copy-start | bytes 1572868
  397.4 5.4 %copy-start.10 = (f32[16,512]{1,0:T(8,128)S(1)}, f32[16,512]{1,0:T(8,128)}, u32[]{:S(2)}) copy-start(f32[16,512]{1,0:T(8,128)} %get-tuple-element.63) | copy-start | bytes 98308
  397.4 5.5 %copy-start.11 = (f32[3,256]{1,0:T(4,128)S(1)}, f32[3,256]{1,0:T(4,128)}, u32[]{:S(2)}) copy-start(f32[3,256]{1,0:T(4,128)} %param.23) | copy-start | bytes 9220
  397.4 5.5 %copy-start.15 = (f32[3,256]{1,0:T(4,128)S(1)}, f32[3,256]{1,0:T(4,128)}, u32[]{:S(2)}) copy-start(f32[3,256]{1,0:T(4,128)} %param.30) | copy-start | bytes 9220
  397.5 5.5 %copy-start.16 = (f32[3,256]{1,0:T(4,128)S(1)}, f32[3,256]{1,0:T(4,128)}, u32[]{:S(2)}) copy-start(f32[3,256]{1,0:T(4,128)} %param.31) | copy-start | bytes 9220
  397.5 6.1 %copy-start.12 = (f32[7,64]{1,0:T(8,128)S(1)}, f32[7,64]{1,0:T(8,128)}, u32[]{:S(2)}) copy-start(f32[7,64]{1,0:T(8,128)} %param.22) | copy-start | bytes 5380
  397.5 6.1 %copy-start.17 = (f32[7,64]{1,0:T(8,128)S(1)}, f32[7,64]{1,0:T(8,128)}, u32[]{:S(2)}) copy-start(f32[7,64]{1,0:T(8,128)} %param.28) | copy-start | bytes 5380
  397.5 6.1 %copy-start.18 = (f32[7,64]{1,0:T(8,128)S(1)}, f32[7,64]{1,0:T(8,128)}, u32[]{:S(2)}) copy-start(f32[7,64]{1,0:T(8,128)} %param.29) | copy-start | bytes 5380
  397.5 6.7 %copy-start.2 = (f32[256,7,512]{2,0,1:T(8,128)S(1)}, f32[256,7,512]{2,0,1:T(8,128)}, u32[]{:S(2)}) copy-start(f32[256,7,512]{2,0,1:T(8,128)} %param.20) | copy-start | bytes 11010052
  397.5 6.7 %copy-start.3 = (f32[256,7,512]{2,0,1:T(8,128)S(1)}, f32[256,7,512]{2,0,1:T(8,128)}, u32[]{:S(2)}) copy-start(f32[256,7,512]{2,0,1:T(8,128)} %param.24) | copy-start | bytes 11010052
  397.5 6.8 %copy-start.4 = (f32[256,7,512]{2,0,1:T(8,128)S(1)}, f32[256,7,512]{2,0,1:T(8,128)}, u32[]{:S(2)}) copy-start(f32[256,7,512]{2,0,1:T(8,128)} %param.25) | copy-start | bytes 11010052
  397.5 6.8 %copy-start.13 = (f32[1,256]{1,0:T(1,128)S(1)}, f32[1,256]{1,0:T(1,128)}, u32[]{:S(2)}) copy-start(f32[1,256]{1,0:T(1,128)} %get-tuple-element.88) | copy-start | bytes 3076
  397.6 6.8 %copy-start.14 = (f32[1,256]{1,0:T(1,128)S(1)}, f32[1,256]{1,0:T(1,128)}, u32[]{:S(2)}) copy-start(f32[1,256]{1,0:T(1,128)} %get-tuple-element.89) | copy-start | bytes 3076
  404.4 7.8 %copy-start.5 = (f32[5,512,256]{2,1,0:T(8,128)S(1)}, f32[5,512,256]{2,1,0:T(8,128)}, u32[]{:S(2)}) copy-start(f32[5,512,256]{2,1,0:T(8,128)} %wd_in.1) | copy-start | bytes 7864324
  404.4 7.8 %copy-start.6 = (f32[5,512,256]{2,1,0:T(8,128)S(1)}, f32[5,512,256]{2,1,0:T(8,128)}, u32[]{:S(2)}) copy-start(f32[5,512,256]{2,1,0:T(8,128)} %param.26) | copy-start | bytes 7864324
  404.4 7.8 %copy-start.7 = (f32[5,512,256]{2,1,0:T(8,128)S(1)}, f32[5,512,256]{2,1,0:T(8,128)}, u32[]{:S(2)}) copy-start(f32[5,512,256]{2,1,0:T(8,128)} %param.27) | copy-start | bytes 7864324
  404.4 7.8 %copy-start.8 = (f32[5,512,256]{2,1,0:T(8,128)S(1)}, f32[5,512,256]{2,1,0:T(8,128)}, u32[]{:S(2)}) copy-start(f32[5,512,256]{2,1,0:T(8,128)} %get-tuple-element.64) | copy-start | bytes 7864324

commit v6 on v5

--- a/solution.py
+++ b/solution.py
@@ -103,10 +103,10 @@
 
     def copy(self, t, index, up, arriving=False):
         place = self.place
-        slot = index - 1 if up else self.line - 2 - index
+        slot = self.slot(index, up)
         return pltpu.make_async_remote_copy(
             src_ref=self.source(t, index),
-            dst_ref=self.landing(t, slot, up),
+            dst_ref=self.landing(t, slot),
             send_sem=(self.up_send if up else self.down_send).at[t, slot],
             recv_sem=(self.up_recv if up else self.down_recv).at[t, slot],
             device_id={"tensor": place + 1 if up != arriving else place - 1},
@@ -114,7 +114,10 @@
         )
 
     def got(self, t, index, up):
-        return self.landing(t, index - 1 if up else self.line - 2 - index, up)[...].astype(f32)
+        return self.landing(t, self.slot(index, up))[...].astype(f32)
+
+    def slot(self, index, up):
+        return index - 1 if up else lax.rem(self.line - 1 + index, self.line + 1)
 
     def first(self, t):
         for up in (True, False):
@@ -177,7 +180,6 @@
         self.bias_cols = local // n_dp
         self.width = out_cols
         self.d_tiles = model // out_cols
-        self.early = 3 * self.d_tiles // 4
         self.bits = [1 << b for b in range(1, n_dp.bit_length() - 1)]
         even = range(2, n_dp, 2)
         self.single = [m for m in even if m.bit_count() == 1]
@@ -201,10 +203,10 @@
 def forward_kernel(
     plan,
     x_in, out_grad_in, w_in, wd_in, small_in, lengths, place_cos, place_sin,
-    wa_out, wm_out, small_out, xhat_out, sums_out, cot_out, q_out, k_out, v_out, att_out, lse_out,
-    hidden_out, da_out, do_out, part_out, own_out, ahead_out, behind_out, stats_out, mixed_out,
-    wa, wm, wd, small, xs, ns, sums, cs, q, k, v, att, lse, hidden, slope, do,
-    own, ahead, behind, stats, land_up, land_down, wide, mixed, block, tall_block,
+    wa_out, wm_out, small_out, xhat_out, sums_out, cot_out, q_out, k_out, v_out, att_out,
+    hidden_out, da_out, dh_out, stats_out, mixed_out,
+    wa, wm, wd, small, xs, ns, sums, cs, q, k, v, att, lse, hidden, slope, k_sum, v_sum,
+    own, ahead, behind, stats, land, wide, mixed, block, tall_block,
     mixed_sem, own_sem, block_sem, out_sem, w_send, w_recv, up_send, up_recv, down_send, down_recv,
     sum_up_send, sum_up_recv, sum_down_send, sum_down_recv,
 ):
@@ -331,9 +333,8 @@
 
     outs = [
         (wa, wa_out), (wm, wm_out), (small, small_out), (xs, xhat_out), (sums, sums_out), (cs, cot_out),
-        (q, q_out), (k, k_out), (v, v_out), (att, att_out), (lse, lse_out), (hidden, hidden_out),
-        (slope, da_out), (do, do_out), (xs.at[pl.ds(plan.early, plan.d_tiles - plan.early)], part_out),
-        (own, own_out), (ahead, ahead_out), (behind, behind_out), (stats, stats_out),
+        (q, q_out), (k, k_out), (v, v_out), (att, att_out), (hidden, hidden_out),
+        (slope, da_out), (cs, dh_out), (stats, stats_out),
     ]
 
     def out_copy(j):
@@ -346,35 +347,35 @@
     w_rows = pl.ds(pl.multiple_of(me * plan.in_rows, plan.in_rows), plan.in_rows)
     small_load = pltpu.make_async_copy(small_in, small.at[me], own_sem.at[2])
 
-    half_rows, half_cols = plan.in_rows // 2, local // 2
+    some_rows, some_cols = plan.in_rows // 4, local // 4
 
     def in_load(i):
         return pltpu.make_async_copy(
-            w_in.at[i // 2, pl.ds(i % 2 * half_rows, half_rows), :], block.at[i % 2], block_sem.at[0, i % 2]
+            w_in.at[i // 4, pl.ds(i % 4 * some_rows, some_rows), :], block.at[i % 2], block_sem.at[0, i % 2]
         )
 
     def down_load(i):
         return pltpu.make_async_copy(
-            wd_in.at[i // 2, pl.ds(i % 2 * half_cols, half_cols), :], tall_block.at[i % 2], block_sem.at[1, i % 2]
+            wd_in.at[i // 4, pl.ds(i % 4 * some_cols, some_cols), :], tall_block.at[i % 2], block_sem.at[1, i % 2]
         )
 
     def round_in(first, stop, target):
-        for i in range(2 * first, 2 * stop):
-            r, half = divmod(i, 2)
+        for i in range(4 * first, 4 * stop):
+            r, part = divmod(i, 4)
             in_load(i).wait()
-            to = pl.ds(pl.multiple_of(me * plan.in_rows + half * half_rows, half_rows), half_rows)
-            target[to, (r - first) * local : (r - first + 1) * local] = block[half].astype(bf16)
-            if i + 2 < 2 * (3 + plan.n_mlp):
+            to = pl.ds(pl.multiple_of(me * plan.in_rows + part * some_rows, some_rows), some_rows)
+            target[to, (r - first) * local : (r - first + 1) * local] = block[i % 2].astype(bf16)
+            if i + 2 < 4 * (3 + plan.n_mlp):
                 in_load(i + 2).start()
 
     def round_down():
-        for i in range(2 * (1 + plan.n_mlp)):
+        for i in range(4 * (1 + plan.n_mlp)):
             down_load(i).wait()
-            wd[me, i * half_cols : (i + 1) * half_cols, :] = tall_block[i % 2].astype(bf16)
-            if i + 2 < 2 * (1 + plan.n_mlp):
+            wd[me, i * some_cols : (i + 1) * some_cols, :] = tall_block[i % 2].astype(bf16)
+            if i + 2 < 4 * (1 + plan.n_mlp):
                 down_load(i + 2).start()
 
-    strip_rows = min(64, rows)
+    strip_rows = min(32, rows)
     strip_count = rows // strip_rows
 
     def row_load(j):
@@ -492,15 +493,15 @@
     def tile_source(t, index):
         return xs.at[t, span(index), :]
 
-    def tile_landing(t, slot, up):
-        return (land_up if up else land_down).at[t, slot]
+    def tile_landing(t, slot):
+        return land.at[t, slot]
 
     out_sum = LineSum(
         place, line, tile_source, tile_landing, (sum_up_send, sum_up_recv, sum_down_send, sum_down_recv)
     )
 
-    def early_tiles(fn):
-        lax.fori_loop(0, plan.early, lambda t, carry: (fn(t), carry)[1], 0)
+    def all_tiles(fn):
+        lax.fori_loop(0, plan.d_tiles, lambda t, carry: (fn(t), carry)[1], 0)
 
     def back_rows(index):
         at = span(index)
@@ -511,10 +512,53 @@
             for o in range(1, n):
                 grad = grad + dot_t(cs[o, at, :], wd[o, r * local : (r + 1) * local, :])
             if r == 0:
-                do[at, :] = grad.astype(bf16)
+                att[at, :] = grad.astype(bf16)
             else:
                 cols = slice((r - 1) * local, r * local)
                 slope[at, cols] = (grad * slope[at, cols].astype(f32)).astype(bf16)
+
+    def attend_back(pair, carry):
+        block = min(QUERY_ROWS, plan.group)
+        scale = HEAD ** (-0.5)
+        k_sum[...] = jnp.zeros_like(k_sum)
+        v_sum[...] = jnp.zeros_like(v_sum)
+        lanes = pl.ds(pl.multiple_of(pair * LANES, LANES), LANES)
+        which = lax.broadcasted_iota(jnp.int32, (block, LANES), 1)
+        for start in range(0, plan.group, block):
+            stop = start + block
+            here = pl.ds(start, block)
+            allowed = attend_mask(begins_of(lengths, start, block), start, block, stop)
+            q_sum = jnp.zeros((block, LANES), f32)
+            for head in range(LANES // HEAD):
+                mine = head_lanes(block, head)
+                query = jnp.where(mine, q[here, lanes], jnp.zeros((block, LANES), bf16)) * scale
+                query = query.astype(bf16)
+                cot = jnp.where(mine, att[here, lanes], jnp.zeros((block, LANES), bf16))
+                level = jnp.sum(
+                    jnp.where(which == pair * (LANES // HEAD) + head, lse[here, :], 0.0), axis=1, keepdims=True
+                )
+                scores = dot_t(query, k[:stop, lanes]) - level
+                probs = jnp.where(allowed, jnp.exp(scores), 0.0)
+                prob_grad = dot_t(cot, v[:stop, lanes])
+                mean = jnp.sum(probs * prob_grad, axis=1, keepdims=True)
+                score_grad = (probs * (prob_grad - mean)).astype(bf16)
+                q_step = dot_n(score_grad, k[:stop, lanes])
+                q_sum = jnp.where(mine, q_step * scale, q_sum)
+                k_sum[:stop, :] += dot_s(score_grad, query)
+                v_sum[:stop, :] += dot_s(probs.astype(bf16), cot)
+            q[here, lanes] = turn(
+                q_sum, own[here, :], ahead[here, :], behind[here, :], -1.0
+            ).astype(bf16)
+        k[:, lanes] = turn(k_sum[...], own[...], ahead[...], behind[...], -1.0).astype(bf16)
+        v[:, lanes] = v_sum[...].astype(bf16)
+        return carry
+
+    def dh_tile(t):
+        at = pl.ds(pl.multiple_of(t * width, width), width)
+        total = dot_t(slope[...], wm[at, :])
+        for r, grad in enumerate((q, k, v)):
+            total = total + dot_t(grad[...], wa[at, r * local : (r + 1) * local])
+        cs[t] = total.astype(bf16)
 
     def normalize_own():
         for j in range(strip_count):
@@ -578,19 +622,19 @@
         out_sum.last(t, mixed.at[lax.rem(t, 2)])
         mixed_copy(t).start()
 
-    normalize_own()
-    z_start(0, 1)
     small_load.wait()
     w_start(3)
     round_in(0, 3, wa)
     w_start(0)
+    normalize_own()
+    z_start(0, 1)
     round_in(3, 3 + plan.n_mlp, wm)
     mask_cot()
     round_down()
     make_tables()
     sums[...] = jnp.zeros_like(sums)
     lse[...] = jnp.zeros_like(lse)
-    write(15, 16, 17, 18)
+    write(13)
     w_arrive(0, plan.single)
     w_start(1)
     w_arrive(3, plan.single)
@@ -622,12 +666,12 @@
         z_arrive(0, line - 1)
         cot_start(line - 1)
     at_distance(line - 1, lambda c: (attn_rows(c), mlp_rows(c))[0])
-    write(3, 6, 7, 8, 11)
+    write(3, 10)
     pairs = local // LANES
     lax.fori_loop(0, pairs // 2, attend, 0)
     w_arrive(2, plan.single)
     lax.fori_loop(pairs // 2, pairs, attend, 0)
-    write(9, 10)
+    write(9)
     z_arrive(1, 1)
     w_arrive(2, plan.several)
     out_copy(3).wait()
@@ -643,9 +687,8 @@
         out_tile(t)
         out_sum.first(t)
 
-    early_tiles(first_tile)
-    lax.fori_loop(plan.early, plan.d_tiles, lambda t, carry: (out_tile(t), carry)[1], 0)
-    write(14)
+    all_tiles(first_tile)
+    out_copy(9).wait()
     at_distance(0, back_rows)
     if line > 2:
         at_distance(1, back_rows)
@@ -661,25 +704,30 @@
             def _():
                 for step in range(1, line):
                     z_sent(1, step, up)
-                early_tiles(lambda t: out_sum.hand_on(t, up))
+                all_tiles(lambda t: out_sum.hand_on(t, up))
 
     running(True)
     if line > 2:
         z_arrive(1, line - 1)
     running(False)
     at_distance(line - 1, back_rows)
-    write(4, 5, 12, 13)
-    early_tiles(finish_tile)
-    for t in range(max(plan.early - 2, 0), plan.early):
+    write(4, 5, 11)
+    lax.fori_loop(0, pairs, attend_back, 0)
+    write(6, 7, 8)
+    out_copy(5).wait()
+    all_tiles(dh_tile)
+    write(12)
+    all_tiles(finish_tile)
+    for t in range(max(plan.d_tiles - 2, 0), plan.d_tiles):
         mixed_copy(t).wait()
 
-    early_tiles(out_sum.sent)
+    all_tiles(out_sum.sent)
     for flow in range(4):
         for mask in range(1, n):
             for half in halves(flow):
                 w_copy(flow, mask, half).wait_send()
     for j in range(len(outs)):
-        if j != 3:
+        if j not in (3, 5, 9):
             out_copy(j).wait()
 
 
@@ -690,37 +738,37 @@
     )
     low = lambda *shape: jax.ShapeDtypeStruct(shape, bf16)
     full = lambda *shape: jax.ShapeDtypeStruct(shape, f32)
-    early = plan.early * plan.width
     out_shape = [
         low(model, plan.attn), low(model, plan.mlp), low(n, 16, LANES + plan.out_cols),
         low(n, group, plan.width), full(8, model), low(n, group, plan.width),
         low(group, local), low(group, local), low(group, local), low(group, local),
-        full(group, LANES),
-        low(group, plan.mlp), low(group, plan.mlp), low(group, local),
-        low(plan.d_tiles - plan.early, group, plan.width),
-        full(group, LANES), full(group, LANES), full(group, LANES), full(2, rows, LANES), full(rows, early),
+        low(group, plan.mlp), low(group, plan.mlp), low(n, group, plan.width), full(2, rows, LANES),
+        full(rows, model),
     ]
     scratch = lambda s: pltpu.VMEM(s.shape, s.dtype)
     dma = pltpu.SemaphoreType.DMA
     return pl.pallas_call(
         partial(forward_kernel, plan),
         in_specs=[any_space] * 5 + [pl.BlockSpec(memory_space=pltpu.SMEM)] + [any_space] * 2,
-        out_specs=[any_space] * 20,
+        out_specs=[any_space] * 15,
         out_shape=out_shape,
         scratch_shapes=[scratch(s) for s in out_shape[:2]]
         + [pltpu.VMEM((n, plan.down, plan.out_cols), bf16)]
         + [scratch(s) for s in out_shape[2:4]]
         + [pltpu.VMEM((rows, model), bf16)]
-        + [scratch(s) for s in out_shape[4:14]]
-        + [scratch(s) for s in out_shape[15:19]]
-        + [pltpu.VMEM((plan.early, max(line - 1, 1), rows, plan.width), bf16)] * 2
+        + [scratch(s) for s in out_shape[4:10]]
+        + [pltpu.VMEM((group, LANES), f32)]
+        + [scratch(s) for s in out_shape[10:12]]
+        + [pltpu.VMEM((group, LANES), f32)] * 5
+        + [scratch(out_shape[13])]
+        + [pltpu.VMEM((plan.d_tiles, line + 1, rows, plan.width), bf16)]
         + [
-            pltpu.VMEM((2, min(64, rows), model), f32), pltpu.VMEM((2, rows, plan.width), f32),
-            pltpu.VMEM((2, plan.in_rows // 2, local), f32), pltpu.VMEM((2, local // 2, plan.out_cols), f32),
+            pltpu.VMEM((2, min(32, rows), model), f32), pltpu.VMEM((2, rows, plan.width), f32),
+            pltpu.VMEM((2, plan.in_rows // 4, local), f32), pltpu.VMEM((2, local // 4, plan.out_cols), f32),
         ]
-        + [dma((2,)), dma((5,)), dma((2, 2)), dma((19,)), dma((8 * n,)), dma((8 * n,))]
+        + [dma((2,)), dma((5,)), dma((2, 2)), dma((14,)), dma((8 * n,)), dma((8 * n,))]
         + [dma((2 * line,))] * 4
-        + [dma((plan.early, max(line - 1, 1)))] * 4,
+        + [dma((plan.d_tiles, line + 1))] * 4,
         compiler_params=pltpu.CompilerParams(
             collective_id=0, has_side_effects=True, vmem_limit_bytes=63 << 20
         ),
@@ -730,13 +778,12 @@
 
 def backward_kernel(
     plan,
-    xhat_in, cot_in, att_in, hidden_in, da_in, do_in, q_in, k_in, v_in, part_in, wa_in, wm_in,
-    lse, sums_in, own, ahead, behind, lengths,
-    down_out, in_out, small_out, mixed_out, rows_out, dh_out,
-    turned, stage, og, da, qkv, do, k_sum, v_sum, sent, core_in, held, cube_in, up_in, down_in,
-    part, part_up, part_down, w_tile, fin, fin_turned, dh_fin, small, small_in, shares,
-    load_sem, stage_sem, tile_sem, fin_sem, dh_sem, core_send, core_recv, cube_send, cube_recv,
-    up_send, up_recv, down_send, down_recv, part_up_send, part_up_recv, part_down_send, part_down_recv,
+    xhat_in, cot_in, att_in, hidden_in, da_in, q_in, k_in, v_in, dh_in, wa_in, wm_in, sums_in,
+    down_out, in_out, small_out, rows_out, dh_out,
+    turned, stage, og, da, qkv, dh, sent, core_in, held, cube_in, land,
+    w_own, fin, fin_turned, dh_fin, small, small_in, shares,
+    load_sem, stage_sem, fin_sem, dh_sem, core_send, core_recv, cube_send, cube_recv,
+    up_send, up_recv, down_send, down_recv,
     small_send, small_recv, share_send, share_recv, credit,
 ):
     n, line = plan.n_dp, plan.n_line
@@ -763,6 +810,7 @@
 
     width, d_tiles = plan.width, plan.d_tiles
     sub = local // width
+    own_rows = pl.ds(pl.multiple_of(me * in_rows, in_rows), in_rows)
 
     def strip(source, j):
         return source.at[:, pl.ds(j * width, width)]
@@ -772,13 +820,14 @@
         (q_in, qkv.at[:, pl.ds(0, local)]),
         (k_in, qkv.at[:, pl.ds(local, local)]),
         (v_in, qkv.at[:, pl.ds(2 * local, local)]),
-        (do_in, do),
-        (part_in, part),
+        (dh_in, dh),
+        (wa_in.at[own_rows, :], w_own.at[:, pl.ds(0, plan.attn)]),
+        (wm_in.at[own_rows, :], w_own.at[:, pl.ds(plan.attn, plan.mlp)]),
     ]
     whole = whole + [
         (strip(att_in, j) if j < sub else strip(hidden_in, j - sub), og.at[j]) for j in range(n_down * sub)
     ]
-    strips = range(6, len(whole))
+    strips = range(7, len(whole))
     for j, (a, b) in enumerate(whole):
         pltpu.make_async_copy(a, b, load_sem.at[j]).start()
 
@@ -923,7 +972,7 @@
                     fin_turned[...] = fin[lax.rem(t, 2)].T
                 fin_copy(t).start()
                 if name != "down":
-                    weight = w_tile[0 if name == "attn" else 1, 0:in_rows, pl.ds(pl.multiple_of(t * local, local), local)].astype(f32)
+                    weight = w_own[:, pl.ds(pl.multiple_of((result + t) * local, local), local)].astype(f32)
                     product = weight * fin[lax.rem(t, 2)]
                     extra = weight * small[n_bits + 1, pl.ds(result + t, 1), :]
                     for g in range(0, local, LANES):
@@ -947,68 +996,15 @@
 
         lax.fori_loop(0, tiles, step, 0)
 
-    def attend(pair, carry):
-        block = min(QUERY_ROWS, group)
-        scale = HEAD ** (-0.5)
-        k_sum[...] = jnp.zeros_like(k_sum)
-        v_sum[...] = jnp.zeros_like(v_sum)
-        q_lanes, k_lanes, v_lanes = (
-            pl.ds(pl.multiple_of(pair * LANES + r * local, LANES), LANES) for r in range(3)
-        )
-        lanes = q_lanes
-        which = lax.broadcasted_iota(jnp.int32, (block, LANES), 1)
-        for start in range(0, group, block):
-            stop = start + block
-            here = pl.ds(start, block)
-            allowed = attend_mask(begins_of(lengths, start, block), start, block, stop)
-            q_sum = jnp.zeros((block, LANES), f32)
-            for head in range(LANES // HEAD):
-                mine = head_lanes(block, head)
-                query = jnp.where(mine, qkv[here, q_lanes], jnp.zeros((block, LANES), bf16)) * scale
-                query = query.astype(bf16)
-                cot = jnp.where(mine, do[here, lanes], jnp.zeros((block, LANES), bf16))
-                level = jnp.sum(
-                    jnp.where(which == pair * (LANES // HEAD) + head, lse[here, :], 0.0), axis=1, keepdims=True
-                )
-                scores = dot_t(query, qkv[:stop, k_lanes]) - level
-                probs = jnp.where(allowed, jnp.exp(scores), 0.0)
-                prob_grad = dot_t(cot, qkv[:stop, v_lanes])
-                mean = jnp.sum(probs * prob_grad, axis=1, keepdims=True)
-                score_grad = (probs * (prob_grad - mean)).astype(bf16)
-                q_step = dot_n(score_grad, qkv[:stop, k_lanes])
-                q_sum = jnp.where(mine, q_step * scale, q_sum)
-                k_sum[:stop, :] += dot_s(score_grad, query)
-                v_sum[:stop, :] += dot_s(probs.astype(bf16), cot)
-            qkv[here, q_lanes] = turn(
-                q_sum, own[here, :], ahead[here, :], behind[here, :], -1.0
-            ).astype(bf16)
-        qkv[:, k_lanes] = turn(k_sum[...], own[...], ahead[...], behind[...], -1.0).astype(bf16)
-        qkv[:, v_lanes] = v_sum[...].astype(bf16)
-        return carry
-
-    def tile_loads(t):
-        at = pl.ds(pl.multiple_of(t * width, width), width)
-        slot = lax.rem(t, 2)
-        return (
-            pltpu.make_async_copy(wa_in.at[at, :], w_tile.at[slot, pl.ds(0, width), pl.ds(0, plan.attn)], tile_sem.at[slot, 0]),
-            pltpu.make_async_copy(wm_in.at[at, :], w_tile.at[slot, pl.ds(0, width), pl.ds(plan.attn, plan.mlp)], tile_sem.at[slot, 1]),
-        )
-
     def tile_of(buffer):
         def source(t, index):
             return buffer.at[t, pl.ds(pl.multiple_of(index * rows, rows), rows), :]
         return source
 
     dh_sum = LineSum(
-        place, line, tile_of(og), lambda t, slot, up: (up_in if up else down_in).at[t, slot],
+        place, line, tile_of(dh), lambda t, slot: land.at[t, slot],
         (up_send, up_recv, down_send, down_recv),
     )
-    late = d_tiles - plan.early
-    out_sum = LineSum(
-        place, line, tile_of(part), lambda t, slot, up: (part_up if up else part_down).at[t, slot],
-        (part_up_send, part_up_recv, part_down_send, part_down_recv),
-    )
-
     def sum_copy(target, t):
         cols = pl.ds(pl.multiple_of(t * width, width), width)
         return pltpu.make_async_copy(dh_fin.at[lax.rem(t, 2)], target.at[:, cols], dh_sem.at[lax.rem(t, 2)])
@@ -1028,18 +1024,6 @@
     def tiles(first, stop, fn):
         lax.fori_loop(first, stop, lambda t, carry: (fn(t), carry)[1], 0)
 
-    def dh_tile(t):
-        slot = lax.rem(t, 2)
-        @pl.when(t + 1 < d_tiles)
-        def _():
-            for load in tile_loads(t + 1):
-                load.start()
-        for load in tile_loads(t):
-            load.wait()
-        total = dot_t(qkv[...], w_tile[slot, 0:width, : plan.attn]) + dot_t(da[...], w_tile[slot, 0:width, plan.attn :])
-        og[t] = total.astype(bf16)
-        dh_sum.first(t)
-
     def small_copy(j):
         return pltpu.make_async_remote_copy(
             src_ref=small.at[j], dst_ref=small_in.at[j],
@@ -1055,71 +1039,52 @@
 
     shares[...] = jnp.zeros_like(shares)
     small[0] = jnp.zeros_like(small[0])
-    for load in tile_loads(0):
-        load.start()
     masks = [2 * j + 1 for j in range(pairs_n)] + [2 * j for j in range(pairs_n)]
+    pl.semaphore_wait(barrier, 1 + n_bits + line - 1)
+    loaded(4)
+    tiles(0, d_tiles, dh_sum.first)
     turn_columns(cot_in, masks)
-    pl.semaphore_wait(barrier, 1 + n_bits + line - 1)
-    loaded(5)
-    tiles(0, late, out_sum.first)
     loaded(*strips)
     scatter("down")
-    loaded(0, 1, 2, 3, 4)
-    pairs = local // LANES
-    lax.fori_loop(0, pairs // 2, attend, 0)
-    out_sum.both_ways(0, late, late)
-    lax.fori_loop(pairs // 2, pairs, attend, 0)
+    dh_sum.both_ways(0, d_tiles // 4, d_tiles)
+    turn_columns(xhat_in, masks)
+    loaded(0, 1, 2, 3)
+    scatter("mlp")
+    dh_sum.both_ways(d_tiles // 4, d_tiles // 2, d_tiles)
     for r in range(3 + n_mlp):
         block = qkv[:, r * local : (r + 1) * local] if r < 3 else da[:, (r - 3) * local : (r - 2) * local]
         small[0, r : r + 1, :] = jnp.sum(block.astype(f32), axis=0, keepdims=True)
     for r in range(model // local):
         small[0, 8 + r : 9 + r, :] = sums_in[0:1, r * local : (r + 1) * local]
     small_copy(0).start()
-    some = min(3, d_tiles)
-    tiles(0, some, dh_tile)
     for phase in range(n_bits - 1):
         cube_step("down", phase)
-    turn_columns(xhat_in, masks)
-    scatter("mlp")
-    finish(out_sum, mixed_out, late)
-    tiles(some, d_tiles, dh_tile)
-    dh_sum.both_ways(0, d_tiles // 4, d_tiles)
     small_step(0)
+    dh_sum.both_ways(d_tiles // 2, 3 * d_tiles // 4, d_tiles)
+    small_step(1)
+    for phase in range(n_bits - 1):
+        cube_step("mlp", phase)
     cube_step("down", n_bits - 1)
     cube_sent("down")
     for b in plan.bits:
         pl.semaphore_signal(credit.at[1], inc=1, device_id=peer(b), device_id_type=MESH)
-    small_step(1)
     scatter("attn")
     for j in range(2, n_bits + 1):
         small_step(j)
-    own_rows = pl.ds(pl.multiple_of(me * in_rows, in_rows), in_rows)
-    weights = [
-        pltpu.make_async_copy(wa_in.at[own_rows, :], w_tile.at[0, pl.ds(0, in_rows), pl.ds(0, plan.attn)], tile_sem.at[0, 0]),
-        pltpu.make_async_copy(wm_in.at[own_rows, :], w_tile.at[1, pl.ds(0, in_rows), pl.ds(0, plan.mlp)], tile_sem.at[1, 0]),
-    ]
-    for w in weights:
-        w.start()
-    dh_sum.both_ways(d_tiles // 4, d_tiles // 2, d_tiles)
-    for phase in range(n_bits - 1):
-        cube_step("mlp", phase)
-    dh_sum.both_ways(d_tiles // 2, 3 * d_tiles // 4, d_tiles)
-    for w in weights:
-        w.wait()
+    dh_sum.both_ways(3 * d_tiles // 4, d_tiles, d_tiles)
+    loaded(5, 6)
     cube_step("mlp", n_bits - 1)
-    dh_sum.both_ways(3 * d_tiles // 4, d_tiles, d_tiles)
+    finish(dh_sum, dh_out, d_tiles)
     for phase in range(n_bits):
         cube_step("attn", phase)
     share_own.start()
     for d in range(1, line):
         share_copy(d, False).start()
-    finish(dh_sum, dh_out, d_tiles)
     small_done = pltpu.make_async_copy(small.at[n_bits + 1], small_out, load_sem.at[0])
     small_done.start()
     cube_sent("mlp")
     cube_sent("attn")
     tiles(0, d_tiles, dh_sum.sent)
-    tiles(0, late, out_sum.sent)
     for j in range(n_bits + 1):
         small_copy(j).wait_send()
     share_own.wait()
@@ -1129,15 +1094,14 @@
     small_done.wait()
 
 
-def backward(plan, xhat, cot, att, hidden, da, do, q, k, v, part, wa, wm, lse, sums, tables, lengths):
+def backward(plan, xhat, cot, att, hidden, da, q, k, v, dh, wa, wm, sums):
     any_space = pl.BlockSpec(memory_space=pl.ANY)
     vmem = pl.BlockSpec(memory_space=pltpu.VMEM)
     n, line, group, model, local = plan.n_dp, plan.n_line, plan.group, plan.model, plan.local
     rows, in_rows, n_bits, pairs_n = plan.rows, plan.in_rows, len(plan.bits), n // 2
     n_down = 1 + plan.n_mlp
     small_rows = 8 + -(-(model // local) // 8) * 8
-    width, d_tiles, steps = plan.width, plan.d_tiles, max(line - 1, 1)
-    late = d_tiles - plan.early
+    width, d_tiles = plan.width, plan.d_tiles
     low = lambda *shape: pltpu.VMEM(shape, bf16)
     full = lambda *shape: pltpu.VMEM(shape, f32)
     dma = pltpu.SemaphoreType.DMA
@@ -1145,27 +1109,25 @@
     slots = n_down + plan.n_mlp
     return pl.pallas_call(
         partial(backward_kernel, plan),
-        in_specs=[any_space] * 12 + [vmem] * 5 + [pl.BlockSpec(memory_space=pltpu.SMEM)],
-        out_specs=[any_space] * 6,
+        in_specs=[any_space] * 11 + [vmem],
+        out_specs=[any_space] * 5,
         out_shape=[
             out(f32, n_down, local, in_rows), out(f32, 3 + plan.n_mlp, in_rows, local),
-            out(f32, small_rows, local), out(f32, rows, late * width),
+            out(f32, small_rows, local),
             out(f32, line, 2, in_rows, LANES), out(f32, rows, model),
         ],
         scratch_shapes=[
             low(n * in_rows, group), low(2, group, in_rows),
             low(max(d_tiles, plan.down // width), group, width), low(group, plan.mlp),
-            low(group, plan.attn), low(group, local), full(group, LANES), full(group, LANES),
+            low(group, plan.attn), low(d_tiles, group, width),
             low(2, pairs_n * in_rows, local), low(n_down, pairs_n * in_rows, local),
             low(slots, 2, pairs_n, in_rows // 2, local), low(slots, 2, max(pairs_n - 1, 1), in_rows // 2, local),
-            low(d_tiles, steps, rows, width), low(d_tiles, steps, rows, width),
-            low(late, group, width), low(late, steps, rows, width), low(late, steps, rows, width),
-            low(2, max(width, in_rows), plan.attn + plan.mlp), full(2, in_rows, local), full(local, in_rows), full(2, rows, width),
+            low(d_tiles, line + 1, rows, width),
+            low(in_rows, plan.attn + plan.mlp), full(2, in_rows, local), full(local, in_rows), full(2, rows, width),
             full(n_bits + 2, small_rows, local), full(n_bits + 1, small_rows, local), full(2, in_rows, LANES),
-            dma((6 + plan.down // width,)), dma((2,)), dma((2, 2)), dma((2,)), dma((2,)), dma((2,)), dma((n_down,)),
+            dma((7 + plan.down // width,)), dma((2,)), dma((2,)), dma((2,)), dma((2,)), dma((n_down,)),
             dma((slots, max(2 * n_bits, 1))), dma((slots, max(2 * n_bits, 1))),
-            dma((d_tiles, steps)), dma((d_tiles, steps)), dma((d_tiles, steps)), dma((d_tiles, steps)),
-            dma((late, steps)), dma((late, steps)), dma((late, steps)), dma((late, steps)),
+            dma((d_tiles, line + 1)), dma((d_tiles, line + 1)), dma((d_tiles, line + 1)), dma((d_tiles, line + 1)),
             dma((n_bits + 1,)), dma((n_bits + 1,)), dma((line,)), dma((line,)),
             pltpu.SemaphoreType.REGULAR((2,)),
         ],
@@ -1173,7 +1135,7 @@
             collective_id=1, has_side_effects=True, vmem_limit_bytes=63 << 20
         ),
         cost_estimate=pl.CostEstimate(flops=80 * 10**9, bytes_accessed=80 << 20, transcendentals=0),
-    )(xhat, cot, att, hidden, da, do, q, k, v, part, wa, wm, lse, sums, *tables, lengths)
+    )(xhat, cot, att, hidden, da, q, k, v, dh, wa, wm, sums)
 
 
 def adam_update(weight, moment_one, moment_two, gradient, step_rate, decay_factor):
@@ -1223,16 +1185,16 @@
         [jnp.pad(bias_tile, ((0, 16 - widths), (0, 0))), jnp.pad(vector_params, ((0, 13), (0, 0)))], axis=1
     ).astype(bf16)
     (
-        w_attn, w_mlp, vectors, xhat_all, cot_sums, cot_all, q_low, k_low, v_low, attended, lse,
-        hidden, pre_grad, attn_grad, out_part, own, ahead, behind, stats, mixed_early,
+        w_attn, w_mlp, vectors, xhat_all, cot_sums, cot_all, q_grad, k_grad, v_grad, attended,
+        hidden, pre_grad, dh_part, stats, mixed,
     ) = forward(plan, block_input, out_grad, in_weight.transpose(1, 0, 2), down_weight, small, seq_lengths)
-    down_grad, in_grad, small_grad, mixed_late, shares, dh = backward(
-        plan, xhat_all, cot_all, attended, hidden, pre_grad, attn_grad, q_low, k_low, v_low, out_part,
-        w_attn, w_mlp, lse, cot_sums, (own, ahead, behind), seq_lengths,
+    down_grad, in_grad, small_grad, shares, dh = backward(
+        plan, xhat_all, cot_all, attended, hidden, pre_grad, q_grad, k_grad, v_grad, dh_part,
+        w_attn, w_mlp, cot_sums,
     )
     vector_vals = vectors[:, :3, LANES:].transpose(1, 0, 2).reshape(3, model).astype(f32)
     gain, out_bias = vector_vals[0], vector_vals[2]
-    block_out = block_input + (jnp.concatenate([mixed_early, mixed_late], axis=1) + out_bias)
+    block_out = block_input + (mixed + out_bias)
     mean, inv_scale = stats[0, :, :1], stats[1, :, :1]
     xhat = (block_input - mean) * inv_scale
     places = lax.axis_index("tensor") * own_rows + lax.broadcasted_iota(jnp.int32, (own_rows, 1), 0)

time: 425 us -> 439 us (1.033)
  the two profiles are of different devices: /device:TPU:0 before, /device:TPU:24 now
where the time goes in v6:
time: 439 us; the launch traced here: 431 us
  Pallas kernels  399 us (91%)
  other arithmetic  27.6 us (6%)
    pallas_call x1, Pallas kernels, forward(): pl.pallas_call(partial(forward_kernel, plan), in_specs=[any_space] * 5 +...  226 us
    pallas_call x1, Pallas kernels, backward(): pl.pallas_call(partial(backward_kernel, plan), in_specs=[any_space] * 11...  173 us
    sub x4, other arithmetic, adam_update(): weight - step_rate * (corrected / (spread + adam_eps) + decay_factor * we...  13.7 us

profile of v6, /device:TPU:24, one launch (start us, length us, event | category | flops | bytes accessed | tf_op | source)
XLA Modules:
  0.0 430.6 jit_solution(4503839804382685299)
XLA Ops:
  0.7 1.3 reduce_sum.45
  1.9 0.7 add_compare_fusion
  2.6 0.7 convert.12
  3.3 0.6 fusion.14
  3.9 0.7 tile.4
  4.6 0.1 tile.10
  4.7 0.6 fusion.5.small_in
  5.3 226.4 %shard_map.272 = (bf16[2048,1536]{1,0:T(8,128)(2,1)}, bf16[2048,2048]{1,0:T(8,128)(2,1)}, bf16[8,16,384]{2,1,0:T(8,128)(2,1)}, bf16[8,1024,256]{2,1,0:T(8,128)(2...) custom-call(f32[256,2048]{1,0:T(8,128)} %x_in.1, ...), custom_call_target="tpu_custom_call" | custom-call | flops 60000002048 | bytes 83886080 | tf_op jit(solution)/shard_map/pallas_call | solution.py:750
  231.7 1.1 slice_reduce_fusion.3
  232.8 0.8 convert_bitcast_fusion
  233.6 172.5 %shard_map.273 = (f32[5,512,256]{2,1,0:T(8,128)}, f32[7,256,512]{2,1,0:T(8,128)}, f32[16,512]{1,0:T(8,128)}, f32[4,2,256,128]{3,2,1,0:T(8,128)}, f32[256,2048]{1,0:T(8,128)}) custom-call(bf16[8,1024,256]{2,1,0:T(8,128)(2,1)} %get-tuple-element.37.xhat_in, bf16[8,1024,256]{2,1,0:T(8,128)(2,1)} %get-tuple-element.38.cot_in, ...), custom_call_target="tpu_custom_call" | custom-call | flops 80000000000 | bytes 83886080 | tf_op jit(solution)/shard_map/pallas_call | solution.py:1110
  406.1 0.0 copy-start
  406.2 1.5 slice_reduce_fusion.1
  407.7 2.8 multiply_reduce_fusion.1
  410.6 0.0 copy-start.10
  410.6 0.0 copy-start.14
  410.6 0.0 copy-start.15
  410.6 0.0 copy-start.11
  410.6 0.0 copy-start.16
  410.6 0.0 copy-start.17
  410.6 0.0 copy-start.2
  410.6 0.0 copy-start.3
  410.6 0.0 copy-start.4
  410.7 0.0 copy-start.12
  410.7 5.5 %multiply_add_fusion.2 = (f32[256,2048]{1,0:T(8,128)}, f32[256,2048]{1,0:T(8,128)}) fusion(f32[256,2048]{1,0:T(8,128)} %out_grad_in.1, f32[256,2048]{1,0:T(8,128)S(1)} %copy-done, f32[256,2048]{1,0:T(8,128)S(1)} %copy-done.1, f32[256]{0:T(256)S(1)} %broadcast_multiply_fusion, f32[256]{0:T(256)S(1)} %get-tuple-element.59, ...), kind=kLoop, calls=%fused_computation.10 | loop fusion | flops 5767168 | bytes 12603648 | tf_op jit(solution)/shard_map/add | solution.py:1204
  416.2 0.1 dynamic_slice.7
  416.3 0.6 multiply_subtract_fusion.2
  417.0 0.7 multiply_subtract_fusion.3
  417.7 0.0 copy-start.6
  417.7 0.0 copy-start.7
  417.7 7.8 %multiply_subtract_fusion = (f32[256,7,512]{2,0,1:T(8,128)}, f32[256,7,512]{2,0,1:T(8,128)}, f32[256,7,512]{2,0,1:T(8,128)}) fusion(f32[256,7,512]{2,0,1:T(8,128)S(1)} %copy-done.2, f32[7,512]{1,0:T(8,128)S(1)} %slice.42, f32[256]{0:T(256)S(1)} %bitcast.26, f32[7,256,512]{2,1,0:T(8,128)} %get-tuple-element.50, f32[256]{0:T(256)S(1)} %bitcast.25, ...), kind=kLoop, calls=%fused_computation.5 | loop fusion | flops 16515072 | bytes 25706496 | tf_op jit(solution)/shard_map/sub | solution.py:1147
  425.5 4.6 %multiply_subtract_fusion.1 = (f32[5,512,256]{2,1,0:T(8,128)}, f32[5,512,256]{2,1,0:T(8,128)}, f32[5,512,256]{2,1,0:T(8,128)}) fusion(f32[5,512,256]{2,1,0:T(8,128)S(1)} %copy-done.5, f32[5,512,256]{2,1,0:T(8,128)S(1)} %copy-done.8, f32[5,512,256]{2,1,0:T(8,128)S(1)} %copy-done.6, f32[5,512,256]{2,1,0:T(8,128)S(1)} %copy-done.7), kind=kLoop, calls=%fused_computation.8 | loop fusion | flops 9830400 | bytes 18350080 | tf_op jit(solution)/shard_map/sub | solution.py:1147
  (32 shorter events, 0.1 us)
Async XLA Ops:
  406.1 4.4 %copy-start = (f32[256,2048]{1,0:T(8,128)S(1)}, f32[256,2048]{1,0:T(8,128)}, u32[]{:S(2)}) copy-start(f32[256,2048]{1,0:T(8,128)} %x_in.1) | copy-start | bytes 6291460
  406.2 4.4 %copy-start.1 = (f32[256,2048]{1,0:T(8,128)S(1)}, f32[256,2048]{1,0:T(8,128)}, u32[]{:S(2)}) copy-start(f32[256,2048]{1,0:T(8,128)} %get-tuple-element.49) | copy-start | bytes 6291460
  410.5 5.7 %copy-start.9 = (f32[16,512]{1,0:T(8,128)S(1)}, f32[16,512]{1,0:T(8,128)}, u32[]{:S(2)}) copy-start(f32[16,512]{1,0:T(8,128)} %get-tuple-element.51) | copy-start | bytes 98308
  410.6 5.8 %copy-start.10 = (f32[3,256]{1,0:T(4,128)S(1)}, f32[3,256]{1,0:T(4,128)}, u32[]{:S(2)}) copy-start(f32[3,256]{1,0:T(4,128)} %param.23) | copy-start | bytes 9220
  410.6 5.8 %copy-start.14 = (f32[3,256]{1,0:T(4,128)S(1)}, f32[3,256]{1,0:T(4,128)}, u32[]{:S(2)}) copy-start(f32[3,256]{1,0:T(4,128)} %param.30) | copy-start | bytes 9220
  410.6 5.7 %copy-start.15 = (f32[3,256]{1,0:T(4,128)S(1)}, f32[3,256]{1,0:T(4,128)}, u32[]{:S(2)}) copy-start(f32[3,256]{1,0:T(4,128)} %param.31) | copy-start | bytes 9220
  410.6 6.4 %copy-start.11 = (f32[7,64]{1,0:T(8,128)S(1)}, f32[7,64]{1,0:T(8,128)}, u32[]{:S(2)}) copy-start(f32[7,64]{1,0:T(8,128)} %param.22) | copy-start | bytes 5380
  410.6 6.4 %copy-start.16 = (f32[7,64]{1,0:T(8,128)S(1)}, f32[7,64]{1,0:T(8,128)}, u32[]{:S(2)}) copy-start(f32[7,64]{1,0:T(8,128)} %param.28) | copy-start | bytes 5380
  410.6 6.3 %copy-start.17 = (f32[7,64]{1,0:T(8,128)S(1)}, f32[7,64]{1,0:T(8,128)}, u32[]{:S(2)}) copy-start(f32[7,64]{1,0:T(8,128)} %param.29) | copy-start | bytes 5380
  410.6 7.0 %copy-start.2 = (f32[256,7,512]{2,0,1:T(8,128)S(1)}, f32[256,7,512]{2,0,1:T(8,128)}, u32[]{:S(2)}) copy-start(f32[256,7,512]{2,0,1:T(8,128)} %param.20) | copy-start | bytes 11010052
  410.6 7.0 %copy-start.3 = (f32[256,7,512]{2,0,1:T(8,128)S(1)}, f32[256,7,512]{2,0,1:T(8,128)}, u32[]{:S(2)}) copy-start(f32[256,7,512]{2,0,1:T(8,128)} %param.24) | copy-start | bytes 11010052
  410.6 7.0 %copy-start.4 = (f32[256,7,512]{2,0,1:T(8,128)S(1)}, f32[256,7,512]{2,0,1:T(8,128)}, u32[]{:S(2)}) copy-start(f32[256,7,512]{2,0,1:T(8,128)} %param.25) | copy-start | bytes 11010052
  410.7 7.0 %copy-start.12 = (f32[1,256]{1,0:T(1,128)S(1)}, f32[1,256]{1,0:T(1,128)}, u32[]{:S(2)}) copy-start(f32[1,256]{1,0:T(1,128)} %get-tuple-element.76) | copy-start | bytes 3076
  410.7 7.0 %copy-start.13 = (f32[1,256]{1,0:T(1,128)S(1)}, f32[1,256]{1,0:T(1,128)}, u32[]{:S(2)}) copy-start(f32[1,256]{1,0:T(1,128)} %get-tuple-element.77) | copy-start | bytes 3076
  417.7 7.8 %copy-start.5 = (f32[5,512,256]{2,1,0:T(8,128)S(1)}, f32[5,512,256]{2,1,0:T(8,128)}, u32[]{:S(2)}) copy-start(f32[5,512,256]{2,1,0:T(8,128)} %wd_in.1) | copy-start | bytes 7864324
  417.7 7.8 %copy-start.6 = (f32[5,512,256]{2,1,0:T(8,128)S(1)}, f32[5,512,256]{2,1,0:T(8,128)}, u32[]{:S(2)}) copy-start(f32[5,512,256]{2,1,0:T(8,128)} %param.26) | copy-start | bytes 7864324
  417.7 7.8 %copy-start.7 = (f32[5,512,256]{2,1,0:T(8,128)S(1)}, f32[5,512,256]{2,1,0:T(8,128)}, u32[]{:S(2)}) copy-start(f32[5,512,256]{2,1,0:T(8,128)} %param.27) | copy-start | bytes 7864324
  417.7 7.8 %copy-start.8 = (f32[5,512,256]{2,1,0:T(8,128)S(1)}, f32[5,512,256]{2,1,0:T(8,128)}, u32[]{:S(2)}) copy-start(f32[5,512,256]{2,1,0:T(8,128)} %get-tuple-element.52) | copy-start | bytes 7864324

commit v7 on v6

--- a/solution.py
+++ b/solution.py
@@ -73,11 +73,11 @@
     return lax.dot_general(a, b, (((0,), (0,)), ((), ())), preferred_element_type=f32)
 
 
-def turn(x, own, ahead, behind, sign):
+def turn(x, own, sines, sign):
     half = ROT // 2
-    return x * own + sign * (
-        pltpu.roll(x, LANES - half, 1) * ahead + pltpu.roll(x, half, 1) * behind
-    )
+    lane = lax.rem(lax.broadcasted_iota(jnp.int32, x.shape, 1), HEAD)
+    other = jnp.where(lane < half, pltpu.roll(x, LANES - half, 1), pltpu.roll(x, half, 1))
+    return x * own + sign * (other * sines)
 
 
 def low_bit(mask):
@@ -139,18 +139,18 @@
                 mine[...] = (mine[...].astype(f32) + self.got(t, index, up)).astype(bf16)
                 self.copy(t, index, up).start()
 
-    def both_ways(self, first, stop, count, lag=2):
+    def one_way(self, first, stop, near):
         def step(t, carry):
             for up in (True, False):
                 far = 2 * self.place // self.line
-                index = t - lag * (far if up else 1 - far)
-
-                @pl.when((index >= 0) & (index < count))
+                late = far if up else 1 - far
+
+                @pl.when(late == (0 if near else 1))
                 def _():
-                    self.hand_on(index, up)
+                    self.hand_on(t, up)
             return carry
 
-        lax.fori_loop(first, stop + (lag if stop == count else 0), step, 0)
+        lax.fori_loop(first, stop, step, 0)
 
     def last(self, t, target):
         place, line = self.place, self.line
@@ -203,11 +203,10 @@
 def forward_kernel(
     plan,
     x_in, out_grad_in, w_in, wd_in, small_in, lengths, place_cos, place_sin,
-    wa_out, wm_out, small_out, xhat_out, sums_out, cot_out, q_out, k_out, v_out, att_out,
-    hidden_out, da_out, dh_out, stats_out, mixed_out,
+    wa_out, wm_out, small_out, sums_out, stats_out, dh_out, tiles_out, xhat_out, cot_out, mixed_out,
     wa, wm, wd, small, xs, ns, sums, cs, q, k, v, att, lse, hidden, slope, k_sum, v_sum,
-    own, ahead, behind, stats, land, wide, mixed, block, tall_block,
-    mixed_sem, own_sem, block_sem, out_sem, w_send, w_recv, up_send, up_recv, down_send, down_recv,
+    own, sines, stats, land, wide, mixed,
+    turn_sem, mixed_sem, own_sem, block_sem, out_sem, w_send, w_recv, up_send, up_recv, down_send, down_recv,
     sum_up_send, sum_up_recv, sum_down_send, sum_down_recv,
 ):
     n, line = plan.n_dp, plan.n_line
@@ -332,10 +331,17 @@
         return pl.ds(pl.multiple_of(index * rows, rows), rows)
 
     outs = [
-        (wa, wa_out), (wm, wm_out), (small, small_out), (xs, xhat_out), (sums, sums_out), (cs, cot_out),
-        (q, q_out), (k, k_out), (v, v_out), (att, att_out), (hidden, hidden_out),
-        (slope, da_out), (cs, dh_out), (stats, stats_out),
+        (wa, wa_out), (wm, wm_out), (small, small_out), (sums, sums_out), (stats, stats_out), (cs, dh_out),
+        (att, tiles_out.at[0]),
     ]
+    for first, source in ((1, hidden), (1 + plan.n_mlp, slope)):
+        outs = outs + [
+            (source.at[:, pl.ds(r * local, local)], tiles_out.at[first + r]) for r in range(plan.n_mlp)
+        ]
+    outs = outs + [(source, tiles_out.at[1 + 2 * plan.n_mlp + r]) for r, source in enumerate((q, k, v))]
+    hidden_at, da_at, qkv_at = (
+        range(7, 7 + plan.n_mlp), range(7 + plan.n_mlp, 7 + 2 * plan.n_mlp), range(7 + 2 * plan.n_mlp, 10 + 2 * plan.n_mlp)
+    )
 
     def out_copy(j):
         return pltpu.make_async_copy(outs[j][0], outs[j][1], out_sem.at[j])
@@ -347,33 +353,47 @@
     w_rows = pl.ds(pl.multiple_of(me * plan.in_rows, plan.in_rows), plan.in_rows)
     small_load = pltpu.make_async_copy(small_in, small.at[me], own_sem.at[2])
 
-    some_rows, some_cols = plan.in_rows // 4, local // 4
-
-    def in_load(i):
-        return pltpu.make_async_copy(
-            w_in.at[i // 4, pl.ds(i % 4 * some_rows, some_rows), :], block.at[i % 2], block_sem.at[0, i % 2]
-        )
-
-    def down_load(i):
-        return pltpu.make_async_copy(
-            wd_in.at[i // 4, pl.ds(i % 4 * some_cols, some_cols), :], tall_block.at[i % 2], block_sem.at[1, i % 2]
-        )
+    stages = (k_sum, v_sum)
+
+    def block_copies(i):
+        source = w_in.at[i] if i < 3 + plan.n_mlp else wd_in.at[i - 3 - plan.n_mlp]
+        height, wide_cols = source.shape
+        strip = min(LANES, wide_cols)
+        return [
+            (
+                g, strip, height,
+                pltpu.make_async_copy(
+                    source.at[:, pl.ds(g * strip, strip)],
+                    stages[i % 2].at[pl.ds(g * height, height), pl.ds(0, strip)],
+                    block_sem.at[i % 2, g],
+                ),
+            )
+            for g in range(wide_cols // strip)
+        ]
+
+    def block_start(i):
+        if i < 4 + 2 * plan.n_mlp:
+            for part in block_copies(i):
+                part[3].start()
+
+    def round_blocks(first, stop, store):
+        for i in range(first, stop):
+            for g, strip, height, copy in block_copies(i):
+                copy.wait()
+                store(i - first, g * strip, strip, stages[i % 2][g * height : (g + 1) * height, :strip].astype(bf16))
+            block_start(i + 2)
 
     def round_in(first, stop, target):
-        for i in range(4 * first, 4 * stop):
-            r, part = divmod(i, 4)
-            in_load(i).wait()
-            to = pl.ds(pl.multiple_of(me * plan.in_rows + part * some_rows, some_rows), some_rows)
-            target[to, (r - first) * local : (r - first + 1) * local] = block[i % 2].astype(bf16)
-            if i + 2 < 4 * (3 + plan.n_mlp):
-                in_load(i + 2).start()
+        def store(r, at, strip, value):
+            target[w_rows, r * local + at : r * local + at + strip] = value
+
+        round_blocks(first, stop, store)
 
     def round_down():
-        for i in range(4 * (1 + plan.n_mlp)):
-            down_load(i).wait()
-            wd[me, i * some_cols : (i + 1) * some_cols, :] = tall_block[i % 2].astype(bf16)
-            if i + 2 < 4 * (1 + plan.n_mlp):
-                down_load(i + 2).start()
+        def store(r, at, strip, value):
+            wd[me, r * local : (r + 1) * local, at : at + strip] = value
+
+        round_blocks(3 + plan.n_mlp, 4 + 2 * plan.n_mlp, store)
 
     strip_rows = min(32, rows)
     strip_count = rows // strip_rows
@@ -388,12 +408,10 @@
     row_load(0).start()
     row_load(1).start()
     small_load.start()
-    in_load(0).start()
-    in_load(1).start()
-    down_load(0).start()
-    down_load(1).start()
+    block_start(0)
+    block_start(1)
     table_loads = [
-        pltpu.make_async_copy(place_cos, own, own_sem.at[3]), pltpu.make_async_copy(place_sin, ahead, own_sem.at[4])
+        pltpu.make_async_copy(place_cos, own, own_sem.at[3]), pltpu.make_async_copy(place_sin, sines, own_sem.at[4])
     ]
     for load in table_loads:
         load.start()
@@ -416,7 +434,7 @@
         at = span(index)
         for o in range(n):
             gain, shift = small[o, 0:1, LANES:].astype(f32), small[o, 1:2, LANES:].astype(f32)
-            ns[:, o * width : (o + 1) * width] = (xs[o, at, :].astype(f32) * gain + shift).astype(bf16)
+            ns[0:rows, o * width : (o + 1) * width] = (xs[o, at, :].astype(f32) * gain + shift).astype(bf16)
 
     def bias_row(r, first, width):
         per = LANES // plan.bias_cols
@@ -428,17 +446,33 @@
             groups.append(total)
         return jnp.concatenate(groups, axis=1)
 
+    def turn_rows(source, target, index):
+        def staged(o):
+            return ns.at[pl.ds(0, width), pl.ds(o % 2 * rows, rows)]
+
+        def copy(o):
+            return pltpu.make_async_copy(staged(o), target.at[o, :, span(index)], turn_sem.at[o % 2])
+
+        for o in range(n):
+            if o >= 2:
+                copy(o - 2).wait()
+            staged(o)[...] = source[o, span(index), :].T
+            copy(o).start()
+        for o in range(max(n - 2, 0), n):
+            copy(o).wait()
+
     def attn_rows(index):
         at = span(index)
+        turn_rows(xs, xhat_out, index)
         normalize_rows(index)
         for r, target in enumerate((q, k, v)):
-            proj = dot_n(ns[...], wa[:, r * local : (r + 1) * local]) + bias_row(r, 0, local)
+            proj = dot_n(ns[0:rows, :], wa[:, r * local : (r + 1) * local]) + bias_row(r, 0, local)
             if r == 2:
                 target[at, :] = proj.astype(bf16)
             else:
                 for g in range(0, local, LANES):
                     target[at, g : g + LANES] = turn(
-                        proj[:, g : g + LANES], own[at, :], ahead[at, :], behind[at, :], 1.0
+                        proj[:, g : g + LANES], own[at, :], sines[at, :], 1.0
                     ).astype(bf16)
 
     def mlp_rows(index):
@@ -446,7 +480,7 @@
         normalize_rows(index)
         for r in range(plan.n_mlp):
             cols = slice(r * local, (r + 1) * local)
-            pre = dot_n(ns[...], wm[:, cols]) + bias_row(3 + r, 0, local)
+            pre = dot_n(ns[0:rows, :], wm[:, cols]) + bias_row(3 + r, 0, local)
             value, grad = gelu_and_slope(pre)
             hidden[at, cols] = value.astype(bf16)
             slope[at, cols] = grad.astype(bf16)
@@ -505,6 +539,7 @@
 
     def back_rows(index):
         at = span(index)
+        turn_rows(cs, cot_out, index)
         for o in range(n):
             sums[0:1, o * width : (o + 1) * width] += jnp.sum(cs[o, at, :].astype(f32), axis=0, keepdims=True)
         for r in range(1 + plan.n_mlp):
@@ -547,9 +582,9 @@
                 k_sum[:stop, :] += dot_s(score_grad, query)
                 v_sum[:stop, :] += dot_s(probs.astype(bf16), cot)
             q[here, lanes] = turn(
-                q_sum, own[here, :], ahead[here, :], behind[here, :], -1.0
+                q_sum, own[here, :], sines[here, :], -1.0
             ).astype(bf16)
-        k[:, lanes] = turn(k_sum[...], own[...], ahead[...], behind[...], -1.0).astype(bf16)
+        k[:, lanes] = turn(k_sum[...], own[...], sines[...], -1.0).astype(bf16)
         v[:, lanes] = v_sum[...].astype(bf16)
         return carry
 
@@ -572,8 +607,8 @@
             to = pl.ds(pl.multiple_of(place * rows + j * strip_rows, strip_rows), strip_rows)
             for o in range(n):
                 xs[o, to, :] = normed[:, o * width : (o + 1) * width]
-            stats[0, at, :] = jnp.broadcast_to(mean, (strip_rows, LANES))
-            stats[1, at, :] = jnp.broadcast_to(scale, (strip_rows, LANES))
+            first = lax.broadcasted_iota(jnp.int32, (strip_rows, LANES), 1) == 0
+            stats[at, :] = jnp.where(first, mean, scale)
             if j + 2 < 2 * strip_count:
                 row_load(j + 2).start()
 
@@ -595,21 +630,20 @@
         block_rows = min(QUERY_ROWS, plan.group)
         ends = ends_of(lengths)
         at_ends = [pl.ds(jnp.minimum(end, plan.group - 1), 1) for end in ends]
-        cosines, sines = [own[row, :] for row in at_ends], [ahead[row, :] for row in at_ends]
+        end_cosines, end_sines = [own[row, :] for row in at_ends], [sines[row, :] for row in at_ends]
         for start in range(0, plan.group, block_rows):
             at = pl.ds(start, block_rows)
             places = start + lax.broadcasted_iota(jnp.int32, (block_rows, LANES), 0)
-            begin_cos, begin_sin = cosines[0], sines[0]
-            for end, end_cos, end_sin in zip(ends[1:], cosines[1:], sines[1:]):
+            begin_cos, begin_sin = end_cosines[0], end_sines[0]
+            for end, end_cos, end_sin in zip(ends[1:], end_cosines[1:], end_sines[1:]):
                 begin_cos = jnp.where(places >= end, end_cos, begin_cos)
                 begin_sin = jnp.where(places >= end, end_sin, begin_sin)
-            place_c, place_s = own[at, :], ahead[at, :]
+            place_c, place_s = own[at, :], sines[at, :]
             cosine = place_c * begin_cos + place_s * begin_sin
             sine = place_s * begin_cos - place_c * begin_sin
             lane = lax.rem(lax.broadcasted_iota(jnp.int32, (block_rows, LANES), 1), HEAD)
             own[at, :] = jnp.where(lane < ROT, cosine, 1.0)
-            ahead[at, :] = jnp.where(lane < ROT // 2, -sine, 0.0)
-            behind[at, :] = jnp.where((lane >= ROT // 2) & (lane < ROT), sine, 0.0)
+            sines[at, :] = jnp.where(lane < ROT // 2, -sine, jnp.where(lane < ROT, sine, 0.0))
 
     def mixed_copy(t):
         cols = pl.ds(pl.multiple_of(t * width, width), width)
@@ -634,7 +668,7 @@
     make_tables()
     sums[...] = jnp.zeros_like(sums)
     lse[...] = jnp.zeros_like(lse)
-    write(13)
+    write(4)
     w_arrive(0, plan.single)
     w_start(1)
     w_arrive(3, plan.single)
@@ -666,15 +700,14 @@
         z_arrive(0, line - 1)
         cot_start(line - 1)
     at_distance(line - 1, lambda c: (attn_rows(c), mlp_rows(c))[0])
-    write(3, 10)
+    write(*hidden_at)
     pairs = local // LANES
     lax.fori_loop(0, pairs // 2, attend, 0)
     w_arrive(2, plan.single)
     lax.fori_loop(pairs // 2, pairs, attend, 0)
-    write(9)
+    write(6)
     z_arrive(1, 1)
     w_arrive(2, plan.several)
-    out_copy(3).wait()
     for step in range(1, line):
         for up in (True, False):
             left = place != step - 1 if up else place != line - step
@@ -688,7 +721,7 @@
         out_sum.first(t)
 
     all_tiles(first_tile)
-    out_copy(9).wait()
+    out_copy(6).wait()
     at_distance(0, back_rows)
     if line > 2:
         at_distance(1, back_rows)
@@ -696,29 +729,36 @@
         z_arrive(1, step)
         at_distance(step, back_rows)
 
-    def running(near_end):
+    def settle(near):
         for up in (True, False):
-            now = (place < line // 2) if up == near_end else (place >= line // 2)
+            now = (place < line // 2) if up == near else (place >= line // 2)
 
             @pl.when(now)
             def _():
                 for step in range(1, line):
                     z_sent(1, step, up)
-                all_tiles(lambda t: out_sum.hand_on(t, up))
-
-    running(True)
+
+    quarter, count = plan.d_tiles // 4, plan.d_tiles
+    settle(True)
+    out_sum.one_way(0, quarter, True)
     if line > 2:
         z_arrive(1, line - 1)
-    running(False)
     at_distance(line - 1, back_rows)
-    write(4, 5, 11)
-    lax.fori_loop(0, pairs, attend_back, 0)
-    write(6, 7, 8)
-    out_copy(5).wait()
+    write(3, *da_at)
+    settle(False)
+    lax.fori_loop(0, pairs // 2, attend_back, 0)
+    out_sum.one_way(quarter, 2 * quarter, True)
+    out_sum.one_way(0, quarter, False)
+    lax.fori_loop(pairs // 2, pairs, attend_back, 0)
+    write(*qkv_at)
+    out_sum.one_way(2 * quarter, 3 * quarter, True)
+    out_sum.one_way(quarter, 2 * quarter, False)
     all_tiles(dh_tile)
-    write(12)
+    write(5)
+    out_sum.one_way(3 * quarter, count, True)
+    out_sum.one_way(2 * quarter, count, False)
     all_tiles(finish_tile)
-    for t in range(max(plan.d_tiles - 2, 0), plan.d_tiles):
+    for t in range(max(count - 2, 0), count):
         mixed_copy(t).wait()
 
     all_tiles(out_sum.sent)
@@ -727,7 +767,7 @@
             for half in halves(flow):
                 w_copy(flow, mask, half).wait_send()
     for j in range(len(outs)):
-        if j not in (3, 5, 9):
+        if j != 6:
             out_copy(j).wait()
 
 
@@ -738,35 +778,32 @@
     )
     low = lambda *shape: jax.ShapeDtypeStruct(shape, bf16)
     full = lambda *shape: jax.ShapeDtypeStruct(shape, f32)
+    tiles = 4 + 2 * plan.n_mlp
     out_shape = [
         low(model, plan.attn), low(model, plan.mlp), low(n, 16, LANES + plan.out_cols),
-        low(n, group, plan.width), full(8, model), low(n, group, plan.width),
-        low(group, local), low(group, local), low(group, local), low(group, local),
-        low(group, plan.mlp), low(group, plan.mlp), low(n, group, plan.width), full(2, rows, LANES),
-        full(rows, model),
+        full(8, model), full(rows, LANES), low(n, group, plan.width), low(tiles, group, local),
+        low(n, plan.width, group), low(n, plan.width, group), full(rows, model),
     ]
+    act = pltpu.VMEM((n, group, plan.width), bf16)
+    head = pltpu.VMEM((group, local), bf16)
+    hide = pltpu.VMEM((group, plan.mlp), bf16)
+    lane = pltpu.VMEM((group, LANES), f32)
     scratch = lambda s: pltpu.VMEM(s.shape, s.dtype)
     dma = pltpu.SemaphoreType.DMA
     return pl.pallas_call(
         partial(forward_kernel, plan),
         in_specs=[any_space] * 5 + [pl.BlockSpec(memory_space=pltpu.SMEM)] + [any_space] * 2,
-        out_specs=[any_space] * 15,
+        out_specs=[any_space] * 10,
         out_shape=out_shape,
         scratch_shapes=[scratch(s) for s in out_shape[:2]]
-        + [pltpu.VMEM((n, plan.down, plan.out_cols), bf16)]
-        + [scratch(s) for s in out_shape[2:4]]
-        + [pltpu.VMEM((rows, model), bf16)]
-        + [scratch(s) for s in out_shape[4:10]]
-        + [pltpu.VMEM((group, LANES), f32)]
-        + [scratch(s) for s in out_shape[10:12]]
-        + [pltpu.VMEM((group, LANES), f32)] * 5
-        + [scratch(out_shape[13])]
+        + [pltpu.VMEM((n, plan.down, plan.out_cols), bf16), scratch(out_shape[2]), act]
+        + [pltpu.VMEM((max(rows, plan.width), model), bf16), scratch(out_shape[3]), act, head, head, head, head, lane]
+        + [hide, hide] + [lane] * 4 + [scratch(out_shape[4])]
         + [pltpu.VMEM((plan.d_tiles, line + 1, rows, plan.width), bf16)]
         + [
             pltpu.VMEM((2, min(32, rows), model), f32), pltpu.VMEM((2, rows, plan.width), f32),
-            pltpu.VMEM((2, plan.in_rows // 4, local), f32), pltpu.VMEM((2, local // 4, plan.out_cols), f32),
         ]
-        + [dma((2,)), dma((5,)), dma((2, 2)), dma((14,)), dma((8 * n,)), dma((8 * n,))]
+        + [dma((2,)), dma((2,)), dma((5,)), dma((2, 4)), dma((6 + tiles,)), dma((8 * n,)), dma((8 * n,))]
         + [dma((2 * line,))] * 4
         + [dma((plan.d_tiles, line + 1))] * 4,
         compiler_params=pltpu.CompilerParams(
@@ -778,11 +815,11 @@
 
 def backward_kernel(
     plan,
-    xhat_in, cot_in, att_in, hidden_in, da_in, q_in, k_in, v_in, dh_in, wa_in, wm_in, sums_in,
+    xhat_in, cot_in, tiles_in, dh_in, wa_in, wm_in, sums_in,
     down_out, in_out, small_out, rows_out, dh_out,
-    turned, stage, og, da, qkv, dh, sent, core_in, held, cube_in, land,
+    turned, operand, dh, sent, core_in, held, cube_in, land,
     w_own, fin, fin_turned, dh_fin, small, small_in, shares,
-    load_sem, stage_sem, fin_sem, dh_sem, core_send, core_recv, cube_send, cube_recv,
+    load_sem, turn_sem, operand_sem, fin_sem, dh_sem, core_send, core_recv, cube_send, cube_recv,
     up_send, up_recv, down_send, down_recv,
     small_send, small_recv, share_send, share_recv, credit,
 ):
@@ -793,8 +830,6 @@
     half_rows, pairs_n, n_bits = in_rows // 2, n // 2, len(plan.bits)
     orders = (plan.bits, plan.bits[::-1])
     n_down, n_mlp = 1 + plan.n_mlp, plan.n_mlp
-    flows = {"down": (n_down, 0, 0), "mlp": (n_mlp, n_down, 3), "attn": (3, 0, 0)}
-
     def owner(mask):
         index = me
         for b in [1] + plan.bits:
@@ -809,25 +844,13 @@
         return sum((1 if mask & b else 0) << (n_bits - 1 - p) for p, b in enumerate(order))
 
     width, d_tiles = plan.width, plan.d_tiles
-    sub = local // width
     own_rows = pl.ds(pl.multiple_of(me * in_rows, in_rows), in_rows)
 
-    def strip(source, j):
-        return source.at[:, pl.ds(j * width, width)]
-
     whole = [
-        (da_in, da),
-        (q_in, qkv.at[:, pl.ds(0, local)]),
-        (k_in, qkv.at[:, pl.ds(local, local)]),
-        (v_in, qkv.at[:, pl.ds(2 * local, local)]),
         (dh_in, dh),
         (wa_in.at[own_rows, :], w_own.at[:, pl.ds(0, plan.attn)]),
         (wm_in.at[own_rows, :], w_own.at[:, pl.ds(plan.attn, plan.mlp)]),
     ]
-    whole = whole + [
-        (strip(att_in, j) if j < sub else strip(hidden_in, j - sub), og.at[j]) for j in range(n_down * sub)
-    ]
-    strips = range(7, len(whole))
     for j, (a, b) in enumerate(whole):
         pltpu.make_async_copy(a, b, load_sem.at[j]).start()
 
@@ -853,21 +876,31 @@
 
     share_own = pltpu.make_async_copy(shares, rows_out.at[place], share_send.at[0])
 
-    def turn_columns(source, masks):
-        def fetch(j):
-            return pltpu.make_async_copy(source.at[owner(masks[j])], stage.at[j % 2], stage_sem.at[j % 2])
-
-        fetch(0).start()
-        for j in range(len(masks)):
-            if j + 1 < len(masks):
-                fetch(j + 1).start()
-            fetch(j).wait()
-            turned[pl.ds(j * in_rows, in_rows), :] = stage[j % 2].T
-
-    def core_copy(name, t):
+    masks = [2 * j + 1 for j in range(pairs_n)] + [2 * j for j in range(pairs_n)]
+
+    def turned_copy(source, j):
+        return pltpu.make_async_copy(
+            source.at[owner(masks[j])], turned.at[pl.ds(j * in_rows, in_rows), :], turn_sem.at[j]
+        )
+
+    def turned_start(source):
+        for j in range(n):
+            turned_copy(source, j).start()
+
+    def turned_wait(source):
+        for j in range(n):
+            turned_copy(source, j).wait()
+
+    tiles_n = n_down + n_mlp + 3
+
+    def operand_copy(t):
+        slot = lax.rem(t, 3)
+        return pltpu.make_async_copy(tiles_in.at[t], operand.at[slot], operand_sem.at[slot])
+
+    def core_copy(t, base):
         return pltpu.make_async_remote_copy(
-            src_ref=sent.at[lax.rem(t, 2)], dst_ref=core_in.at[t],
-            send_sem=core_send.at[lax.rem(t, 2)], recv_sem=core_recv.at[t],
+            src_ref=sent.at[lax.rem(t, 2)], dst_ref=core_in.at[t - base],
+            send_sem=core_send.at[lax.rem(t, 2)], recv_sem=core_recv.at[t - base],
             device_id=peer(1), device_id_type=MESH,
         )
 
@@ -882,78 +915,70 @@
             device_id=peer(orders[half][phase]), device_id_type=MESH,
         )
 
-    def product(name, at, count, t):
-        if name == "down":
-            return [dot_n(turned[at : at + count, :], og[t * sub + j]) for j in range(sub)]
-        source = da if name == "mlp" else qkv
-        return [dot_n(turned[at : at + count, :], source[:, pl.ds(pl.multiple_of(t * local, local), local)])]
-
     piece = min(2, pairs_n) * in_rows
 
-    def send_core(name, t):
-        @pl.when(t >= 2)
+    def send_core(t, base):
+        @pl.when(t >= base + 2)
         def _():
-            core_copy(name, t - 2).wait_send()
+            core_copy(t - 2, base).wait_send()
+        slot = lax.rem(t, 3)
         for at in range(0, pairs_n * in_rows, piece):
-            strips_of = product(name, at, piece, t)
-            step = local // len(strips_of)
-            for j, value in enumerate(strips_of):
-                sent[lax.rem(t, 2), at : at + piece, j * step : (j + 1) * step] = value.astype(bf16)
-        core_copy(name, t).start()
-
-    def keep_core(name, t):
-        base = flows[name][1]
-        core_copy(name, t).wait_recv()
+            sent[lax.rem(t, 2), at : at + piece, :] = dot_n(turned[at : at + piece, :], operand[slot]).astype(bf16)
+        core_copy(t, base).start()
+        if base:
+            row = lax.rem(t - base + 3, n_mlp + 3)
+            small[0, pl.ds(row, 1), :] = jnp.sum(operand[slot].astype(f32), axis=0, keepdims=True)
+
+    def keep_core(t, base):
+        core_copy(t, base).wait_recv()
         for first in range(0, pairs_n * in_rows, piece):
-            strips_of = product(name, pairs_n * in_rows + first, piece, t)
-            step = local // len(strips_of)
-            for i, value in enumerate(strips_of):
-                cols = slice(i * step, (i + 1) * step)
-                total = value + core_in[t, first : first + piece, cols].astype(f32)
-                for at in range(0, piece, half_rows):
-                    j, half = divmod((first + at) // half_rows, 2)
-                    held[base + t, half, position(2 * j, orders[half]), :, cols] = total[at : at + half_rows].astype(bf16)
+            kept = pairs_n * in_rows + first
+            total = dot_n(turned[kept : kept + piece, :], operand[lax.rem(t, 3)])
+            total = total + core_in[t - base, first : first + piece, :].astype(f32)
+            for at in range(0, piece, half_rows):
+                j, half = divmod((first + at) // half_rows, 2)
+                held[t, half, position(2 * j, orders[half])] = total[at : at + half_rows].astype(bf16)
         for half in range(2):
             if n_bits:
-                cube_copy(base + t, half, 0).start()
-
-    def scatter(name):
-        tiles_n = flows[name][0]
-        if name != "down":
-            pl.semaphore_wait(credit.at[0], 1)
-        if name == "attn":
-            pl.semaphore_wait(credit.at[1], n_bits)
-
+                cube_copy(t, half, 0).start()
+
+    def scatter(base, stop):
         def step(t, carry):
-            @pl.when(t < tiles_n)
+            operand_copy(t).wait()
+
+            @pl.when(t + 1 < tiles_n)
             def _():
-                send_core(name, t)
-
-            @pl.when(t >= 1)
+                operand_copy(t + 1).start()
+            send_core(t, base)
+
+            @pl.when(t >= base + 1)
             def _():
-                keep_core(name, t - 1)
+                keep_core(t - 1, base)
             return carry
 
-        lax.fori_loop(0, tiles_n + 1, step, 0)
-        for t in range(max(tiles_n - 2, 0), tiles_n):
-            core_copy(name, t).wait_send()
-        if name != "attn":
-            pl.semaphore_signal(credit.at[0], inc=1, device_id=peer(1), device_id_type=MESH)
-
-    def cube_step(name, phase):
-        tiles, base, result = flows[name]
+        lax.fori_loop(base, stop, step, 0)
+        keep_core(stop - 1, base)
+        for t in range(max(stop - 2, base), stop):
+            core_copy(t, base).wait_send()
+
+    def cube_step(base, stop, phase):
         count = pairs_n >> (phase + 1)
         first = pairs_n - 2 * count
-        target, depth = (down_out, 1) if name == "down" else (in_out, 2)
+        down = base == 0
+        depth = 1 if down else 2
+
+        def result(t):
+            return t if down else lax.rem(t - n_down + 3, n_mlp + 3)
 
         def fin_copy(t):
-            source = fin_turned if name == "down" else fin.at[lax.rem(t, 2)]
-            return pltpu.make_async_copy(source, target.at[result + t], fin_sem.at[lax.rem(t, 2)])
+            source = fin_turned if down else fin.at[lax.rem(t, 2)]
+            target = down_out if down else in_out
+            return pltpu.make_async_copy(source, target.at[result(t)], fin_sem.at[lax.rem(t, 2)])
 
         def step(t, carry):
-            slot = base + t
+            slot = t
             if phase == n_bits - 1:
-                @pl.when(t >= depth)
+                @pl.when(t >= base + depth)
                 def _():
                     fin_copy(t - depth).wait()
             for half in range(2):
@@ -968,33 +993,27 @@
                 else:
                     fin[lax.rem(t, 2), half * half_rows : (half + 1) * half_rows, :] = total[0]
             if phase == n_bits - 1:
-                if name == "down":
+                if down:
                     fin_turned[...] = fin[lax.rem(t, 2)].T
                 fin_copy(t).start()
-                if name != "down":
-                    weight = w_own[:, pl.ds(pl.multiple_of((result + t) * local, local), local)].astype(f32)
+                if not down:
+                    weight = w_own[:, pl.ds(pl.multiple_of(result(t) * local, local), local)].astype(f32)
                     product = weight * fin[lax.rem(t, 2)]
-                    extra = weight * small[n_bits + 1, pl.ds(result + t, 1), :]
+                    extra = weight * small[n_bits + 1, pl.ds(result(t), 1), :]
                     for g in range(0, local, LANES):
                         shares[0] += product[:, g : g + LANES]
                         shares[1] += extra[:, g : g + LANES]
             return carry
 
-        lax.fori_loop(0, tiles, step, 0)
+        lax.fori_loop(base, stop, step, 0)
         if phase == n_bits - 1:
-            for t in range(max(tiles - depth, 0), tiles):
+            for t in range(max(stop - depth, base), stop):
                 fin_copy(t).wait()
 
-    def cube_sent(name):
-        tiles, base, _ = flows[name]
-
-        def step(t, carry):
-            for half in range(2):
-                for phase in range(n_bits):
-                    cube_copy(base + t, half, phase).wait_send()
-            return carry
-
-        lax.fori_loop(0, tiles, step, 0)
+    def cube_sent(t):
+        for half in range(2):
+            for phase in range(n_bits):
+                cube_copy(t, half, phase).wait_send()
 
     def tile_of(buffer):
         def source(t, index):
@@ -1037,53 +1056,52 @@
         if j < n_bits:
             small_copy(j + 1).start()
 
+    turned_start(cot_in)
+    operand_copy(0).start()
     shares[...] = jnp.zeros_like(shares)
     small[0] = jnp.zeros_like(small[0])
-    masks = [2 * j + 1 for j in range(pairs_n)] + [2 * j for j in range(pairs_n)]
-    pl.semaphore_wait(barrier, 1 + n_bits + line - 1)
-    loaded(4)
-    tiles(0, d_tiles, dh_sum.first)
-    turn_columns(cot_in, masks)
-    loaded(*strips)
-    scatter("down")
-    dh_sum.both_ways(0, d_tiles // 4, d_tiles)
-    turn_columns(xhat_in, masks)
-    loaded(0, 1, 2, 3)
-    scatter("mlp")
-    dh_sum.both_ways(d_tiles // 4, d_tiles // 2, d_tiles)
-    for r in range(3 + n_mlp):
-        block = qkv[:, r * local : (r + 1) * local] if r < 3 else da[:, (r - 3) * local : (r - 2) * local]
-        small[0, r : r + 1, :] = jnp.sum(block.astype(f32), axis=0, keepdims=True)
     for r in range(model // local):
         small[0, 8 + r : 9 + r, :] = sums_in[0:1, r * local : (r + 1) * local]
+    pl.semaphore_wait(barrier, 1 + n_bits + line - 1)
+    loaded(0)
+    tiles(0, d_tiles, dh_sum.first)
+    turned_wait(cot_in)
+    quarter = d_tiles // 4
+    scatter(0, n_down)
+    pl.semaphore_signal(credit, inc=1, device_id=peer(1), device_id_type=MESH)
+    turned_start(xhat_in)
+    dh_sum.one_way(0, quarter, True)
+    turned_wait(xhat_in)
+    pl.semaphore_wait(credit, 1)
+    scatter(n_down, tiles_n)
     small_copy(0).start()
+    dh_sum.one_way(quarter, 2 * quarter, True)
+    dh_sum.one_way(0, quarter, False)
     for phase in range(n_bits - 1):
-        cube_step("down", phase)
+        cube_step(0, n_down, phase)
     small_step(0)
-    dh_sum.both_ways(d_tiles // 2, 3 * d_tiles // 4, d_tiles)
-    small_step(1)
+    dh_sum.one_way(2 * quarter, 3 * quarter, True)
+    dh_sum.one_way(quarter, 2 * quarter, False)
+    for j in range(1, n_bits + 1):
+        small_step(j)
+    loaded(1, 2)
     for phase in range(n_bits - 1):
-        cube_step("mlp", phase)
-    cube_step("down", n_bits - 1)
-    cube_sent("down")
-    for b in plan.bits:
-        pl.semaphore_signal(credit.at[1], inc=1, device_id=peer(b), device_id_type=MESH)
-    scatter("attn")
-    for j in range(2, n_bits + 1):
-        small_step(j)
-    dh_sum.both_ways(3 * d_tiles // 4, d_tiles, d_tiles)
-    loaded(5, 6)
-    cube_step("mlp", n_bits - 1)
+        cube_step(n_down, n_down + n_mlp, phase)
+    dh_sum.one_way(3 * quarter, d_tiles, True)
+    dh_sum.one_way(2 * quarter, 3 * quarter, False)
+    cube_step(0, n_down, n_bits - 1)
+    dh_sum.one_way(3 * quarter, d_tiles, False)
+    for phase in range(n_bits - 1):
+        cube_step(n_down + n_mlp, tiles_n, phase)
     finish(dh_sum, dh_out, d_tiles)
-    for phase in range(n_bits):
-        cube_step("attn", phase)
+    cube_step(n_down, n_down + n_mlp, n_bits - 1)
+    cube_step(n_down + n_mlp, tiles_n, n_bits - 1)
     share_own.start()
     for d in range(1, line):
         share_copy(d, False).start()
     small_done = pltpu.make_async_copy(small.at[n_bits + 1], small_out, load_sem.at[0])
     small_done.start()
-    cube_sent("mlp")
-    cube_sent("attn")
+    tiles(0, tiles_n, cube_sent)
     tiles(0, d_tiles, dh_sum.sent)
     for j in range(n_bits + 1):
         small_copy(j).wait_send()
@@ -1094,7 +1112,7 @@
     small_done.wait()
 
 
-def backward(plan, xhat, cot, att, hidden, da, q, k, v, dh, wa, wm, sums):
+def backward(plan, xhat, cot, tiles, dh, wa, wm, sums):
     any_space = pl.BlockSpec(memory_space=pl.ANY)
     vmem = pl.BlockSpec(memory_space=pltpu.VMEM)
     n, line, group, model, local = plan.n_dp, plan.n_line, plan.group, plan.model, plan.local
@@ -1106,10 +1124,10 @@
     full = lambda *shape: pltpu.VMEM(shape, f32)
     dma = pltpu.SemaphoreType.DMA
     out = lambda dtype, *shape: jax.ShapeDtypeStruct(shape, dtype)
-    slots = n_down + plan.n_mlp
+    slots = n_down + plan.n_mlp + 3
     return pl.pallas_call(
         partial(backward_kernel, plan),
-        in_specs=[any_space] * 11 + [vmem],
+        in_specs=[any_space] * 6 + [vmem],
         out_specs=[any_space] * 5,
         out_shape=[
             out(f32, n_down, local, in_rows), out(f32, 3 + plan.n_mlp, in_rows, local),
@@ -1117,25 +1135,23 @@
             out(f32, line, 2, in_rows, LANES), out(f32, rows, model),
         ],
         scratch_shapes=[
-            low(n * in_rows, group), low(2, group, in_rows),
-            low(max(d_tiles, plan.down // width), group, width), low(group, plan.mlp),
-            low(group, plan.attn), low(d_tiles, group, width),
-            low(2, pairs_n * in_rows, local), low(n_down, pairs_n * in_rows, local),
+            low(n * in_rows, group), low(3, group, local), low(d_tiles, group, width),
+            low(2, pairs_n * in_rows, local), low(3 + plan.n_mlp, pairs_n * in_rows, local),
             low(slots, 2, pairs_n, in_rows // 2, local), low(slots, 2, max(pairs_n - 1, 1), in_rows // 2, local),
             low(d_tiles, line + 1, rows, width),
             low(in_rows, plan.attn + plan.mlp), full(2, in_rows, local), full(local, in_rows), full(2, rows, width),
             full(n_bits + 2, small_rows, local), full(n_bits + 1, small_rows, local), full(2, in_rows, LANES),
-            dma((7 + plan.down // width,)), dma((2,)), dma((2,)), dma((2,)), dma((2,)), dma((n_down,)),
+            dma((3,)), dma((n,)), dma((3,)), dma((2,)), dma((2,)), dma((2,)), dma((3 + plan.n_mlp,)),
             dma((slots, max(2 * n_bits, 1))), dma((slots, max(2 * n_bits, 1))),
             dma((d_tiles, line + 1)), dma((d_tiles, line + 1)), dma((d_tiles, line + 1)), dma((d_tiles, line + 1)),
             dma((n_bits + 1,)), dma((n_bits + 1,)), dma((line,)), dma((line,)),
-            pltpu.SemaphoreType.REGULAR((2,)),
+            pltpu.SemaphoreType.REGULAR,
         ],
         compiler_params=pltpu.CompilerParams(
             collective_id=1, has_side_effects=True, vmem_limit_bytes=63 << 20
         ),
         cost_estimate=pl.CostEstimate(flops=80 * 10**9, bytes_accessed=80 << 20, transcendentals=0),
-    )(xhat, cot, att, hidden, da, q, k, v, dh, wa, wm, sums)
+    )(xhat, cot, tiles, dh, wa, wm, sums)
 
 
 def adam_update(weight, moment_one, moment_two, gradient, step_rate, decay_factor):
@@ -1185,17 +1201,15 @@
         [jnp.pad(bias_tile, ((0, 16 - widths), (0, 0))), jnp.pad(vector_params, ((0, 13), (0, 0)))], axis=1
     ).astype(bf16)
     (
-        w_attn, w_mlp, vectors, xhat_all, cot_sums, cot_all, q_grad, k_grad, v_grad, attended,
-        hidden, pre_grad, dh_part, stats, mixed,
+        w_attn, w_mlp, vectors, cot_sums, stats, dh_part, tiles, xhat_turned, cot_turned, mixed,
     ) = forward(plan, block_input, out_grad, in_weight.transpose(1, 0, 2), down_weight, small, seq_lengths)
     down_grad, in_grad, small_grad, shares, dh = backward(
-        plan, xhat_all, cot_all, attended, hidden, pre_grad, q_grad, k_grad, v_grad, dh_part,
-        w_attn, w_mlp, cot_sums,
+        plan, xhat_turned, cot_turned, tiles, dh_part, w_attn, w_mlp, cot_sums
     )
     vector_vals = vectors[:, :3, LANES:].transpose(1, 0, 2).reshape(3, model).astype(f32)
     gain, out_bias = vector_vals[0], vector_vals[2]
     block_out = block_input + (mixed + out_bias)
-    mean, inv_scale = stats[0, :, :1], stats[1, :, :1]
+    mean, inv_scale = stats[:, :1], stats[:, 1:2]
     xhat = (block_input - mean) * inv_scale
     places = lax.axis_index("tensor") * own_rows + lax.broadcasted_iota(jnp.int32, (own_rows, 1), 0)
     cot_live = jnp.where(places < jnp.sum(seq_lengths), out_grad, 0.0)

time: 439 us -> 431 us (0.982)
  Pallas kernels: 399 us -> 391 us
    pallas_call x1, Pallas kernels: 173 us -> 145 us  [backward(): pl.pallas_call(partial(backward_kernel, plan), in_specs=[any_space] * 6 +...]
    pallas_call x1, Pallas kernels: 226 us -> 246 us  [forward(): pl.pallas_call(partial(forward_kernel, plan), in_specs=[any_space] * 5 +...]
where the time goes in v7:
time: 431 us; the launch traced here: 423 us
  Pallas kernels  391 us (91%)
  other arithmetic  27.6 us (6%)
    pallas_call x1, Pallas kernels, forward(): pl.pallas_call(partial(forward_kernel, plan), in_specs=[any_space] * 5 +...  246 us
    pallas_call x1, Pallas kernels, backward(): pl.pallas_call(partial(backward_kernel, plan), in_specs=[any_space] * 6 +...  145 us
    sub x4, other arithmetic, adam_update(): weight - step_rate * (corrected / (spread + adam_eps) + decay_factor * we...  13.7 us

profile of v7, /device:TPU:24, one launch (start us, length us, event | category | flops | bytes accessed | tf_op | source)
XLA Modules:
  0.0 422.9 jit_solution(4801531984828414203)
XLA Ops:
  0.7 1.3 reduce_sum.45
  1.9 0.7 add_compare_fusion
  2.6 0.7 convert.12
  3.3 0.6 fusion.14
  3.9 0.7 tile.4
  4.6 0.1 tile.10
  4.7 0.6 fusion.5.small_in
  5.3 246.0 %shard_map.272 = (bf16[2048,1536]{1,0:T(8,128)(2,1)}, bf16[2048,2048]{1,0:T(8,128)(2,1)}, bf16[8,16,384]{2,1,0:T(8,128)(2,1)}, f32[8,2048]{1,0:T(8,128)}, f32[25...) custom-call(f32[256,2048]{1,0:T(8,128)} %x_in.1, ...), custom_call_target="tpu_custom_call" | custom-call | flops 60000002048 | bytes 83886080 | tf_op jit(solution)/shard_map/pallas_call | solution.py:793
  251.3 1.2 slice_reduce_fusion.3
  252.5 0.8 convert_bitcast_fusion
  253.3 145.2 %shard_map.273 = (f32[5,512,256]{2,1,0:T(8,128)}, f32[7,256,512]{2,1,0:T(8,128)}, f32[16,512]{1,0:T(8,128)}, f32[4,2,256,128]{3,2,1,0:T(8,128)}, f32[256,2048]{1,0:T(8,128)}) custom-call(bf16[8,256,1024]{2,1,0:T(8,128)(2,1)} %get-tuple-element.32.xhat_in, bf16[8,256,1024]{2,1,0:T(8,128)(2,1)} %get-tuple-element.33.cot_in, ...), custom_call_target="tpu_custom_call" | custom-call | flops 80000000000 | bytes 83886080 | tf_op jit(solution)/shard_map/pallas_call | solution.py:1128
  398.5 0.0 copy-start
  398.5 1.5 slice_reduce_fusion.1
  400.0 2.8 multiply_reduce_fusion.1
  402.9 0.0 copy-start.10
  402.9 0.0 copy-start.14
  402.9 0.0 copy-start.15
  402.9 0.0 copy-start.11
  402.9 0.0 copy-start.16
  403.0 0.0 copy-start.17
  403.0 0.0 copy-start.2
  403.0 0.0 copy-start.3
  403.0 0.0 copy-start.4
  403.0 0.0 copy-start.12
  403.0 0.0 copy-start.13
  403.0 5.5 %multiply_add_fusion.2 = (f32[256,2048]{1,0:T(8,128)}, f32[256,2048]{1,0:T(8,128)}) fusion(f32[256,2048]{1,0:T(8,128)} %out_grad_in.1, f32[256,2048]{1,0:T(8,128)S(1)} %copy-done, f32[256,2048]{1,0:T(8,128)S(1)} %copy-done.1, f32[256]{0:T(256)S(1)} %broadcast_multiply_fusion, f32[256]{0:T(256)S(1)} %get-tuple-element.49, ...), kind=kLoop, calls=%fused_computation.10 | loop fusion | flops 5767168 | bytes 12603648 | tf_op jit(solution)/shard_map/add | solution.py:1218
  408.6 0.1 dynamic_slice.7
  408.7 0.6 multiply_subtract_fusion.2
  409.3 0.7 multiply_subtract_fusion.3
  410.0 0.0 copy-start.5
  410.1 7.7 %multiply_subtract_fusion = (f32[256,7,512]{2,0,1:T(8,128)}, f32[256,7,512]{2,0,1:T(8,128)}, f32[256,7,512]{2,0,1:T(8,128)}) fusion(f32[256,7,512]{2,0,1:T(8,128)S(1)} %copy-done.2, f32[7,512]{1,0:T(8,128)S(1)} %slice.42, f32[256]{0:T(256)S(1)} %bitcast.26, f32[7,256,512]{2,1,0:T(8,128)} %get-tuple-element.40, f32[256]{0:T(256)S(1)} %bitcast.25, ...), kind=kLoop, calls=%fused_computation.5 | loop fusion | flops 16515072 | bytes 25706496 | tf_op jit(solution)/shard_map/sub | solution.py:1163
  417.8 4.6 %multiply_subtract_fusion.1 = (f32[5,512,256]{2,1,0:T(8,128)}, f32[5,512,256]{2,1,0:T(8,128)}, f32[5,512,256]{2,1,0:T(8,128)}) fusion(f32[5,512,256]{2,1,0:T(8,128)S(1)} %copy-done.5, f32[5,512,256]{2,1,0:T(8,128)S(1)} %copy-done.8, f32[5,512,256]{2,1,0:T(8,128)S(1)} %copy-done.6, f32[5,512,256]{2,1,0:T(8,128)S(1)} %copy-done.7), kind=kLoop, calls=%fused_computation.8 | loop fusion | flops 9830400 | bytes 18350080 | tf_op jit(solution)/shard_map/sub | solution.py:1163
  (32 shorter events, 0.1 us)
Async XLA Ops:
  398.5 4.4 %copy-start = (f32[256,2048]{1,0:T(8,128)S(1)}, f32[256,2048]{1,0:T(8,128)}, u32[]{:S(2)}) copy-start(f32[256,2048]{1,0:T(8,128)} %x_in.1) | copy-start | bytes 6291460
  398.5 4.4 %copy-start.1 = (f32[256,2048]{1,0:T(8,128)S(1)}, f32[256,2048]{1,0:T(8,128)}, u32[]{:S(2)}) copy-start(f32[256,2048]{1,0:T(8,128)} %get-tuple-element.39) | copy-start | bytes 6291460
  402.9 5.7 %copy-start.9 = (f32[16,512]{1,0:T(8,128)S(1)}, f32[16,512]{1,0:T(8,128)}, u32[]{:S(2)}) copy-start(f32[16,512]{1,0:T(8,128)} %get-tuple-element.41) | copy-start | bytes 98308
  402.9 5.8 %copy-start.10 = (f32[3,256]{1,0:T(4,128)S(1)}, f32[3,256]{1,0:T(4,128)}, u32[]{:S(2)}) copy-start(f32[3,256]{1,0:T(4,128)} %param.23) | copy-start | bytes 9220
  402.9 5.8 %copy-start.14 = (f32[3,256]{1,0:T(4,128)S(1)}, f32[3,256]{1,0:T(4,128)}, u32[]{:S(2)}) copy-start(f32[3,256]{1,0:T(4,128)} %param.30) | copy-start | bytes 9220
  402.9 5.7 %copy-start.15 = (f32[3,256]{1,0:T(4,128)S(1)}, f32[3,256]{1,0:T(4,128)}, u32[]{:S(2)}) copy-start(f32[3,256]{1,0:T(4,128)} %param.31) | copy-start | bytes 9220
  402.9 6.4 %copy-start.11 = (f32[7,64]{1,0:T(8,128)S(1)}, f32[7,64]{1,0:T(8,128)}, u32[]{:S(2)}) copy-start(f32[7,64]{1,0:T(8,128)} %param.22) | copy-start | bytes 5380
  402.9 6.4 %copy-start.16 = (f32[7,64]{1,0:T(8,128)S(1)}, f32[7,64]{1,0:T(8,128)}, u32[]{:S(2)}) copy-start(f32[7,64]{1,0:T(8,128)} %param.28) | copy-start | bytes 5380
  403.0 6.3 %copy-start.17 = (f32[7,64]{1,0:T(8,128)S(1)}, f32[7,64]{1,0:T(8,128)}, u32[]{:S(2)}) copy-start(f32[7,64]{1,0:T(8,128)} %param.29) | copy-start | bytes 5380
  403.0 7.0 %copy-start.2 = (f32[256,7,512]{2,0,1:T(8,128)S(1)}, f32[256,7,512]{2,0,1:T(8,128)}, u32[]{:S(2)}) copy-start(f32[256,7,512]{2,0,1:T(8,128)} %param.20) | copy-start | bytes 11010052
  403.0 7.0 %copy-start.3 = (f32[256,7,512]{2,0,1:T(8,128)S(1)}, f32[256,7,512]{2,0,1:T(8,128)}, u32[]{:S(2)}) copy-start(f32[256,7,512]{2,0,1:T(8,128)} %param.24) | copy-start | bytes 11010052
  403.0 7.0 %copy-start.4 = (f32[256,7,512]{2,0,1:T(8,128)S(1)}, f32[256,7,512]{2,0,1:T(8,128)}, u32[]{:S(2)}) copy-start(f32[256,7,512]{2,0,1:T(8,128)} %param.25) | copy-start | bytes 11010052
  403.0 7.0 %copy-start.12 = (f32[1,256]{1,0:T(1,128)S(1)}, f32[1,256]{1,0:T(1,128)}, u32[]{:S(2)}) copy-start(f32[1,256]{1,0:T(1,128)} %get-tuple-element.66) | copy-start | bytes 3076
  403.0 7.0 %copy-start.13 = (f32[1,256]{1,0:T(1,128)S(1)}, f32[1,256]{1,0:T(1,128)}, u32[]{:S(2)}) copy-start(f32[1,256]{1,0:T(1,128)} %get-tuple-element.67) | copy-start | bytes 3076
  410.0 7.8 %copy-start.5 = (f32[5,512,256]{2,1,0:T(8,128)S(1)}, f32[5,512,256]{2,1,0:T(8,128)}, u32[]{:S(2)}) copy-start(f32[5,512,256]{2,1,0:T(8,128)} %wd_in.1) | copy-start | bytes 7864324
  410.0 7.8 %copy-start.6 = (f32[5,512,256]{2,1,0:T(8,128)S(1)}, f32[5,512,256]{2,1,0:T(8,128)}, u32[]{:S(2)}) copy-start(f32[5,512,256]{2,1,0:T(8,128)} %param.26) | copy-start | bytes 7864324
  410.1 7.8 %copy-start.7 = (f32[5,512,256]{2,1,0:T(8,128)S(1)}, f32[5,512,256]{2,1,0:T(8,128)}, u32[]{:S(2)}) copy-start(f32[5,512,256]{2,1,0:T(8,128)} %param.27) | copy-start | bytes 7864324
  410.1 7.8 %copy-start.8 = (f32[5,512,256]{2,1,0:T(8,128)S(1)}, f32[5,512,256]{2,1,0:T(8,128)}, u32[]{:S(2)}) copy-start(f32[5,512,256]{2,1,0:T(8,128)} %get-tuple-element.42) | copy-start | bytes 7864324

commit v8 on v7

--- a/solution.py
+++ b/solution.py
@@ -218,6 +218,12 @@
         for b in [1] + plan.bits:
             if mask & b:
                 index = index + b - 2 * b * lax.rem(index // b, 2)
+        return index
+
+    def owner_of(j):
+        index = 0
+        for b in [1] + plan.bits:
+            index = index + b * lax.rem(me // b + j // b, 2)
         return index
 
     def slot(flow, index, half):
@@ -516,9 +522,11 @@
     tall = min(512, plan.group)
 
     def out_tile(t):
+        o = owner_of(t)
+
         def part(j, carry):
             at = pl.ds(pl.multiple_of(j * tall, tall), tall)
-            total = dot_n(att[at, :], wd[t, :local, :]) + dot_n(hidden[at, :], wd[t, local:, :])
+            total = dot_n(att[at, :], wd[o, :local, :]) + dot_n(hidden[at, :], wd[o, local:, :])
             xs[t, at, :] = total.astype(bf16)
             return carry
 
@@ -537,11 +545,14 @@
     def all_tiles(fn):
         lax.fori_loop(0, plan.d_tiles, lambda t, carry: (fn(t), carry)[1], 0)
 
-    def back_rows(index):
+    def cot_rows(index):
         at = span(index)
         turn_rows(cs, cot_out, index)
         for o in range(n):
             sums[0:1, o * width : (o + 1) * width] += jnp.sum(cs[o, at, :].astype(f32), axis=0, keepdims=True)
+
+    def back_rows(index):
+        at = span(index)
         for r in range(1 + plan.n_mlp):
             grad = dot_t(cs[0, at, :], wd[0, r * local : (r + 1) * local, :])
             for o in range(1, n):
@@ -646,7 +657,7 @@
             sines[at, :] = jnp.where(lane < ROT // 2, -sine, jnp.where(lane < ROT, sine, 0.0))
 
     def mixed_copy(t):
-        cols = pl.ds(pl.multiple_of(t * width, width), width)
+        cols = pl.ds(pl.multiple_of(owner_of(t) * width, width), width)
         return pltpu.make_async_copy(mixed.at[lax.rem(t, 2)], mixed_out.at[:, cols], mixed_sem.at[lax.rem(t, 2)])
 
     def finish_tile(t):
@@ -679,6 +690,7 @@
     w_arrive(3, plan.odd)
     w_arrive(0, plan.odd)
     write(0, 2)
+    at_distance(0, cot_rows)
     at_distance(0, attn_rows)
     if line > 2:
         at_distance(1, attn_rows)
@@ -696,6 +708,7 @@
         jnp.maximum(place - near, 0), jnp.minimum(place + near, line - 1) + 1,
         lambda c, carry: (mlp_rows(c), carry)[1], 0,
     )
+    w_arrive(2, plan.single)
     if line > 2:
         z_arrive(0, line - 1)
         cot_start(line - 1)
@@ -703,31 +716,41 @@
     write(*hidden_at)
     pairs = local // LANES
     lax.fori_loop(0, pairs // 2, attend, 0)
-    w_arrive(2, plan.single)
+    w_arrive(2, plan.several)
+    z_arrive(1, 1)
     lax.fori_loop(pairs // 2, pairs, attend, 0)
     write(6)
-    z_arrive(1, 1)
-    w_arrive(2, plan.several)
+    if line > 2:
+        at_distance(1, cot_rows)
     for step in range(1, line):
         for up in (True, False):
             left = place != step - 1 if up else place != line - step
             @pl.when(left & sends(step, up))
             def _():
                 z_copy(0, step, up).wait_send()
-    w_arrive(2, plan.odd)
-
-    def first_tile(t):
-        out_tile(t)
-        out_sum.first(t)
-
-    all_tiles(first_tile)
+
+    def some_tiles(first, stop):
+        def step(t, carry):
+            out_tile(t)
+            out_sum.first(t)
+            return carry
+
+        lax.fori_loop(first, stop, step, 0)
+
+    split = min(6, n)
+    w_arrive(2, [m for m in plan.odd if m < 2])
+    some_tiles(0, min(2, n))
+    w_arrive(2, [m for m in plan.odd if 2 <= m < split])
+    some_tiles(min(2, n), split)
+    w_arrive(2, [m for m in plan.odd if m >= split])
+    some_tiles(split, n)
     out_copy(6).wait()
     at_distance(0, back_rows)
     if line > 2:
         at_distance(1, back_rows)
     for step in range(2, line - 1):
         z_arrive(1, step)
-        at_distance(step, back_rows)
+        at_distance(step, lambda c: (cot_rows(c), back_rows(c))[0])
 
     def settle(near):
         for up in (True, False):
@@ -743,7 +766,7 @@
     out_sum.one_way(0, quarter, True)
     if line > 2:
         z_arrive(1, line - 1)
-    at_distance(line - 1, back_rows)
+    at_distance(line - 1, lambda c: (cot_rows(c), back_rows(c))[0])
     write(3, *da_at)
     settle(False)
     lax.fori_loop(0, pairs // 2, attend_back, 0)

time: 431 us -> 438 us (1.016)
  Pallas kernels: 391 us -> 397 us
    pallas_call x1, Pallas kernels: 246 us -> 252 us  [forward(): pl.pallas_call(partial(forward_kernel, plan), in_specs=[any_space] * 5 +...]
where the time goes in v8:
time: 438 us; the launch traced here: 429 us
  Pallas kernels  397 us (91%)
  other arithmetic  27.6 us (6%)
    pallas_call x1, Pallas kernels, forward(): pl.pallas_call(partial(forward_kernel, plan), in_specs=[any_space] * 5 +...  252 us
    pallas_call x1, Pallas kernels, backward(): pl.pallas_call(partial(backward_kernel, plan), in_specs=[any_space] * 6 +...  145 us
    sub x4, other arithmetic, adam_update(): weight - step_rate * (corrected / (spread + adam_eps) + decay_factor * we...  13.7 us

profile of v8, /device:TPU:24, one launch (start us, length us, event | category | flops | bytes accessed | tf_op | source)
XLA Modules:
  0.0 429.1 jit_solution(6140093162851541248)
XLA Ops:
  0.7 1.3 reduce_sum.45
  1.9 0.7 add_compare_fusion
  2.6 0.7 convert.12
  3.3 0.6 fusion.14
  3.9 0.7 tile.4
  4.6 0.1 tile.10
  4.7 0.6 fusion.5.small_in
  5.3 252.0 %shard_map.272 = (bf16[2048,1536]{1,0:T(8,128)(2,1)}, bf16[2048,2048]{1,0:T(8,128)(2,1)}, bf16[8,16,384]{2,1,0:T(8,128)(2,1)}, f32[8,2048]{1,0:T(8,128)}, f32[25...) custom-call(f32[256,2048]{1,0:T(8,128)} %x_in.1, ...), custom_call_target="tpu_custom_call" | custom-call | flops 60000002048 | bytes 83886080 | tf_op jit(solution)/shard_map/pallas_call | solution.py:816
  257.3 1.2 slice_reduce_fusion.3
  258.5 0.8 convert_bitcast_fusion
  259.3 145.3 %shard_map.273 = (f32[5,512,256]{2,1,0:T(8,128)}, f32[7,256,512]{2,1,0:T(8,128)}, f32[16,512]{1,0:T(8,128)}, f32[4,2,256,128]{3,2,1,0:T(8,128)}, f32[256,2048]{1,0:T(8,128)}) custom-call(bf16[8,256,1024]{2,1,0:T(8,128)(2,1)} %get-tuple-element.32.xhat_in, bf16[8,256,1024]{2,1,0:T(8,128)(2,1)} %get-tuple-element.33.cot_in, ...), custom_call_target="tpu_custom_call" | custom-call | flops 80000000000 | bytes 83886080 | tf_op jit(solution)/shard_map/pallas_call | solution.py:1151
  404.6 0.0 copy-start
  404.7 1.5 slice_reduce_fusion.1
  406.2 2.8 multiply_reduce_fusion.1
  409.0 0.0 copy-start.10
  409.1 0.0 copy-start.14
  409.1 0.0 copy-start.15
  409.1 0.0 copy-start.11
  409.1 0.0 copy-start.16
  409.1 0.0 copy-start.17
  409.1 0.0 copy-start.2
  409.1 0.0 copy-start.3
  409.1 0.0 copy-start.4
  409.2 0.0 copy-start.12
  409.2 5.5 %multiply_add_fusion.2 = (f32[256,2048]{1,0:T(8,128)}, f32[256,2048]{1,0:T(8,128)}) fusion(f32[256,2048]{1,0:T(8,128)} %out_grad_in.1, f32[256,2048]{1,0:T(8,128)S(1)} %copy-done, f32[256,2048]{1,0:T(8,128)S(1)} %copy-done.1, f32[256]{0:T(256)S(1)} %broadcast_multiply_fusion, f32[256]{0:T(256)S(1)} %get-tuple-element.49, ...), kind=kLoop, calls=%fused_computation.10 | loop fusion | flops 5767168 | bytes 12603648 | tf_op jit(solution)/shard_map/add | solution.py:1241
  414.7 0.1 dynamic_slice.7
  414.8 0.6 multiply_subtract_fusion.2
  415.4 0.7 multiply_subtract_fusion.3
  416.2 0.0 copy-start.6
  416.2 0.0 copy-start.7
  416.2 7.7 %multiply_subtract_fusion = (f32[256,7,512]{2,0,1:T(8,128)}, f32[256,7,512]{2,0,1:T(8,128)}, f32[256,7,512]{2,0,1:T(8,128)}) fusion(f32[256,7,512]{2,0,1:T(8,128)S(1)} %copy-done.2, f32[7,512]{1,0:T(8,128)S(1)} %slice.42, f32[256]{0:T(256)S(1)} %bitcast.26, f32[7,256,512]{2,1,0:T(8,128)} %get-tuple-element.40, f32[256]{0:T(256)S(1)} %bitcast.25, ...), kind=kLoop, calls=%fused_computation.5 | loop fusion | flops 16515072 | bytes 25706496 | tf_op jit(solution)/shard_map/sub | solution.py:1186
  424.0 4.6 %multiply_subtract_fusion.1 = (f32[5,512,256]{2,1,0:T(8,128)}, f32[5,512,256]{2,1,0:T(8,128)}, f32[5,512,256]{2,1,0:T(8,128)}) fusion(f32[5,512,256]{2,1,0:T(8,128)S(1)} %copy-done.5, f32[5,512,256]{2,1,0:T(8,128)S(1)} %copy-done.8, f32[5,512,256]{2,1,0:T(8,128)S(1)} %copy-done.6, f32[5,512,256]{2,1,0:T(8,128)S(1)} %copy-done.7), kind=kLoop, calls=%fused_computation.8 | loop fusion | flops 9830400 | bytes 18350080 | tf_op jit(solution)/shard_map/sub | solution.py:1186
  (32 shorter events, 0.1 us)
Async XLA Ops:
  404.6 4.4 %copy-start = (f32[256,2048]{1,0:T(8,128)S(1)}, f32[256,2048]{1,0:T(8,128)}, u32[]{:S(2)}) copy-start(f32[256,2048]{1,0:T(8,128)} %x_in.1) | copy-start | bytes 6291460
  404.6 4.4 %copy-start.1 = (f32[256,2048]{1,0:T(8,128)S(1)}, f32[256,2048]{1,0:T(8,128)}, u32[]{:S(2)}) copy-start(f32[256,2048]{1,0:T(8,128)} %get-tuple-element.39) | copy-start | bytes 6291460
  409.0 5.7 %copy-start.9 = (f32[16,512]{1,0:T(8,128)S(1)}, f32[16,512]{1,0:T(8,128)}, u32[]{:S(2)}) copy-start(f32[16,512]{1,0:T(8,128)} %get-tuple-element.41) | copy-start | bytes 98308
  409.0 5.8 %copy-start.10 = (f32[3,256]{1,0:T(4,128)S(1)}, f32[3,256]{1,0:T(4,128)}, u32[]{:S(2)}) copy-start(f32[3,256]{1,0:T(4,128)} %param.23) | copy-start | bytes 9220
  409.1 5.8 %copy-start.14 = (f32[3,256]{1,0:T(4,128)S(1)}, f32[3,256]{1,0:T(4,128)}, u32[]{:S(2)}) copy-start(f32[3,256]{1,0:T(4,128)} %param.30) | copy-start | bytes 9220
  409.1 5.7 %copy-start.15 = (f32[3,256]{1,0:T(4,128)S(1)}, f32[3,256]{1,0:T(4,128)}, u32[]{:S(2)}) copy-start(f32[3,256]{1,0:T(4,128)} %param.31) | copy-start | bytes 9220
  409.1 6.4 %copy-start.11 = (f32[7,64]{1,0:T(8,128)S(1)}, f32[7,64]{1,0:T(8,128)}, u32[]{:S(2)}) copy-start(f32[7,64]{1,0:T(8,128)} %param.22) | copy-start | bytes 5380
  409.1 6.4 %copy-start.16 = (f32[7,64]{1,0:T(8,128)S(1)}, f32[7,64]{1,0:T(8,128)}, u32[]{:S(2)}) copy-start(f32[7,64]{1,0:T(8,128)} %param.28) | copy-start | bytes 5380
  409.1 6.3 %copy-start.17 = (f32[7,64]{1,0:T(8,128)S(1)}, f32[7,64]{1,0:T(8,128)}, u32[]{:S(2)}) copy-start(f32[7,64]{1,0:T(8,128)} %param.29) | copy-start | bytes 5380
  409.1 7.0 %copy-start.2 = (f32[256,7,512]{2,0,1:T(8,128)S(1)}, f32[256,7,512]{2,0,1:T(8,128)}, u32[]{:S(2)}) copy-start(f32[256,7,512]{2,0,1:T(8,128)} %param.20) | copy-start | bytes 11010052
  409.1 7.0 %copy-start.3 = (f32[256,7,512]{2,0,1:T(8,128)S(1)}, f32[256,7,512]{2,0,1:T(8,128)}, u32[]{:S(2)}) copy-start(f32[256,7,512]{2,0,1:T(8,128)} %param.24) | copy-start | bytes 11010052
  409.1 7.0 %copy-start.4 = (f32[256,7,512]{2,0,1:T(8,128)S(1)}, f32[256,7,512]{2,0,1:T(8,128)}, u32[]{:S(2)}) copy-start(f32[256,7,512]{2,0,1:T(8,128)} %param.25) | copy-start | bytes 11010052
  409.2 7.0 %copy-start.12 = (f32[1,256]{1,0:T(1,128)S(1)}, f32[1,256]{1,0:T(1,128)}, u32[]{:S(2)}) copy-start(f32[1,256]{1,0:T(1,128)} %get-tuple-element.66) | copy-start | bytes 3076
  409.2 7.0 %copy-start.13 = (f32[1,256]{1,0:T(1,128)S(1)}, f32[1,256]{1,0:T(1,128)}, u32[]{:S(2)}) copy-start(f32[1,256]{1,0:T(1,128)} %get-tuple-element.67) | copy-start | bytes 3076
  416.2 7.8 %copy-start.5 = (f32[5,512,256]{2,1,0:T(8,128)S(1)}, f32[5,512,256]{2,1,0:T(8,128)}, u32[]{:S(2)}) copy-start(f32[5,512,256]{2,1,0:T(8,128)} %wd_in.1) | copy-start | bytes 7864324
  416.2 7.8 %copy-start.6 = (f32[5,512,256]{2,1,0:T(8,128)S(1)}, f32[5,512,256]{2,1,0:T(8,128)}, u32[]{:S(2)}) copy-start(f32[5,512,256]{2,1,0:T(8,128)} %param.26) | copy-start | bytes 7864324
  416.2 7.8 %copy-start.7 = (f32[5,512,256]{2,1,0:T(8,128)S(1)}, f32[5,512,256]{2,1,0:T(8,128)}, u32[]{:S(2)}) copy-start(f32[5,512,256]{2,1,0:T(8,128)} %param.27) | copy-start | bytes 7864324
  416.2 7.8 %copy-start.8 = (f32[5,512,256]{2,1,0:T(8,128)S(1)}, f32[5,512,256]{2,1,0:T(8,128)}, u32[]{:S(2)}) copy-start(f32[5,512,256]{2,1,0:T(8,128)} %get-tuple-element.42) | copy-start | bytes 7864324
